TPU v7x, 32 devices: a whole 2x2x4 slice. The times are simulated.
32 devices in a mesh: expert: 8 (over z, y), tensor: 4 (over x, core).
Axes of the slice: x: 2, y: 2, z: 4, core: 2. Of those that a mesh axis runs over, the one named last changes fastest.
Arguments:
- block_in: bfloat16 [17336, 1024], P('expert'), may hold values from -6 to 6
- norm_one: float32 [1024], replicated, may hold values from 0.5 to 1.5
- head_in: bfloat16 [3, 1024, 1024], P(None, None, 'tensor'), may hold values from -0.1875 to 0.1875
- head_out: bfloat16 [1024, 1024], P('tensor'), may hold values from -0.5 to 0.5
- norm_two: float32 [1024], replicated, may hold values from 0.5 to 1.5
- router: bfloat16 [1024, 8], replicated, may hold values from -0.125 to 0.125
- expert_in: bfloat16 [8, 1024, 4096], P('expert', None, 'tensor'), may hold values from -0.1875 to 0.1875
- expert_out: bfloat16 [8, 4096, 1024], P('expert', 'tensor'), may hold values from -0.09375 to 0.09375
- expert_ids: int32 [17336, 2], P('expert'), may hold values from 0 to 7, all different within a row; in each aligned block of 2167 rows (0 to 2166, 2167 to 4333, ...) at most 880 rows name the same one
- route_noise: float32 [17336, 2], P('expert'), may hold values from -3 to 3
- cotangent: bfloat16 [17336, 1024], P('expert'), may hold values from -6 to 6
Outputs:
- block_out: bfloat16 [17336, 1024], P('expert')
- input_grad: float32 [17336, 1024], P('expert')
- norm_one_grad: float32 [1024], replicated
- head_in_grad: float32 [3, 1024, 1024], P(None, None, 'tensor')
- head_out_grad: float32 [1024, 1024], P('tensor')
- norm_two_grad: float32 [1024], replicated
- router_grad: float32 [1024, 8], replicated
- expert_in_grad: float32 [8, 1024, 4096], P('expert', None, 'tensor')
- expert_out_grad: float32 [8, 4096, 1024], P('expert', 'tensor')
Inputs may be any that keep to these rules, and one draw needn't show every extreme that they name: `expert_ids`: each row names 2 different experts, and every expert is named somewhere. In each aligned block of 2167 rows no expert is named by more than 880 rows, and in every draw some block has an expert named by exactly 880 rows.
All inputs are finite; a program needn't handle non-finite values.
Results may differ from a plain program's by a relative error of at most 0.019.
Values may be sent and summed in bfloat16 or wider, within the bound.
No kernel may reach another device: no remote copies, remote signals or barrier semaphores. Data moves between devices by JAX's collectives and lax.ppermute only.
A program may use at most 320 MiB of HBM per device.

v0:
```python
import jax
import jax.numpy as jnp
from jax import lax
from jax.sharding import PartitionSpec as P

HD = 64
SEQ = 197


EPSILON = 1e-06


def normalize(field, gain_vec):
    centre = field - jnp.mean(field, -1, keepdims=True)
    spread = lax.rsqrt(jnp.mean(centre * centre, -1, keepdims=True) + EPSILON)
    scaled = centre * spread
    return (scaled * gain_vec, scaled, spread)


def norm_back(upstream, gain_vec, scaled, spread):
    gain_grad = jnp.sum(upstream * scaled, 0)
    weighted = upstream * gain_vec
    field_grad = spread * (
        weighted
        - jnp.mean(weighted, -1, keepdims=True)
        - scaled * jnp.mean(weighted * scaled, -1, keepdims=True)
    )
    return (field_grad, gain_grad)


def head_total(partial_value):
    return lax.psum(partial_value, "tensor")


def to_owner(buffer):
    return lax.all_to_all(buffer, "expert", split_axis=0, concat_axis=0, tiled=True)


def to_source(partial_value):
    reduced = lax.psum_scatter(
        partial_value.astype(jnp.bfloat16), "tensor", scatter_dimension=1, tiled=True
    )
    arrived_piece = lax.all_to_all(reduced, "expert", split_axis=0, concat_axis=0, tiled=True)
    return lax.all_gather(arrived_piece, "tensor", axis=1, tiled=True)


def shards(
    block_in,
    norm_one,
    head_in,
    head_out,
    norm_two,
    router,
    expert_in,
    expert_out,
    expert_ids,
    route_noise,
    cotangent,
):
    rows_here, model_width = block_in.shape
    local_cols = head_in.shape[2]
    heads_here = local_cols // HD
    images = rows_here // SEQ
    experts = router.shape[1]
    experts_here = expert_in.shape[0]
    top_count = expert_ids.shape[1]
    capacity = (rows_here * top_count * 8 // (5 * experts) + 15) // 16 * 16
    groups = lax.axis_size("expert")
    score_scale = HD ** (-0.5)
    inputs = block_in.astype(jnp.float32)
    normed_one, scaled_one, spread_one = normalize(inputs, norm_one)
    first_in = normed_one.astype(jnp.bfloat16)
    projected = jnp.einsum(
        "rd,kdc->krc", first_in, head_in, preferred_element_type=jnp.float32
    ).astype(jnp.bfloat16)
    shaped = projected.reshape(3, images, SEQ, heads_here, HD)
    queries, keys, values = (shaped[0], shaped[1], shaped[2])
    scores = (
        jnp.einsum("ishd,ithd->ihst", queries, keys, preferred_element_type=jnp.float32)
        * score_scale
    )
    highest = jnp.max(scores, -1, keepdims=True)
    weights = jnp.exp(scores - highest)
    totals = jnp.sum(weights, -1, keepdims=True)
    probs = weights / totals
    log_norm = highest + jnp.log(totals)
    mixed_heads = jnp.einsum(
        "ihst,ithd->ishd", probs.astype(jnp.bfloat16), values, preferred_element_type=jnp.float32
    )
    mixed_heads = mixed_heads.astype(jnp.bfloat16).reshape(rows_here, local_cols)
    attended = head_total(jnp.dot(mixed_heads, head_out, preferred_element_type=jnp.float32))
    middle = inputs + attended
    normed_two, scaled_two, spread_two = normalize(middle, norm_two)
    second_in = normed_two.astype(jnp.bfloat16)
    logits = jnp.dot(second_in, router, preferred_element_type=jnp.float32)
    selector = (expert_ids[:, :, None] == jnp.arange(experts, dtype=jnp.int32)).astype(jnp.float32)
    chosen = jnp.sum(selector * logits[:, None, :], -1) + route_noise
    top_logit = jnp.max(chosen, -1, keepdims=True)
    gate_raw = jnp.exp(chosen - top_logit)
    gate_values = gate_raw / jnp.sum(gate_raw, -1, keepdims=True)
    flat_ids = expert_ids.reshape(-1)
    member = (flat_ids[:, None] == jnp.arange(experts, dtype=jnp.int32)).astype(jnp.int32)
    earlier = jnp.cumsum(member, 0) - member
    positions = flat_ids * capacity + jnp.sum(earlier * member, -1)
    slot_count = experts * capacity

    def pack_rows(row_values):
        return jnp.zeros((slot_count, model_width), jnp.bfloat16).at[positions].set(row_values)

    outgoing = pack_rows(
        jnp.broadcast_to(second_in[:, None, :], (rows_here, top_count, model_width)).reshape(
            -1, model_width
        )
    )
    upstream = cotangent.astype(jnp.float32)
    dispatched = to_owner(outgoing).reshape(groups, experts_here, capacity, model_width)
    hidden = jnp.einsum("sjcd,jdf->sjcf", dispatched, expert_in, preferred_element_type=jnp.float32)
    active = jax.nn.gelu(hidden, approximate=False).astype(jnp.bfloat16)
    partial_value = jnp.einsum(
        "sjcf,jfd->sjcd", active, expert_out, preferred_element_type=jnp.float32
    ).reshape(-1, model_width)
    returned = to_source(partial_value)
    picked = returned[positions].reshape(rows_here, top_count, model_width).astype(jnp.float32)
    gate_grad = jnp.sum(upstream[:, None, :] * picked, -1)
    back_rows = (
        (gate_values[:, :, None] * upstream[:, None, :])
        .astype(jnp.bfloat16)
        .reshape(-1, model_width)
    )
    owner_grad = to_owner(pack_rows(back_rows)).reshape(groups, experts_here, capacity, model_width)
    expert_out_grad = jnp.einsum(
        "sjcf,sjcd->jfd", active, owner_grad, preferred_element_type=jnp.float32
    )
    active_grad = jnp.einsum(
        "sjcd,jfd->sjcf", owner_grad, expert_out, preferred_element_type=jnp.float32
    )
    unused_value, gelu_pull = jax.vjp(
        lambda hidden_in: jax.nn.gelu(hidden_in, approximate=False), hidden
    )
    hidden_grad = gelu_pull(active_grad)[0].astype(jnp.bfloat16)
    expert_in_grad = jnp.einsum(
        "sjcd,sjcf->jdf", dispatched, hidden_grad, preferred_element_type=jnp.float32
    )
    row_grad = jnp.einsum(
        "sjcf,jdf->sjcd", hidden_grad, expert_in, preferred_element_type=jnp.float32
    ).reshape(-1, model_width)
    source_grad = to_source(row_grad)
    combined = jnp.sum(gate_values[:, :, None] * picked, 1)
    block_out = (middle + combined).astype(jnp.bfloat16)
    routed_grad = jnp.sum(
        source_grad[positions].reshape(rows_here, top_count, model_width).astype(jnp.float32), 1
    )
    mean_term = jnp.sum(gate_values * gate_grad, -1, keepdims=True)
    chosen_grad = gate_values * (gate_grad - mean_term)
    logit_grad = jnp.sum(selector * chosen_grad[:, :, None], 1).astype(jnp.bfloat16)
    router_grad = lax.dot_general(
        second_in, logit_grad, (((0,), (0,)), ((), ())), preferred_element_type=jnp.float32
    )
    second_grad = routed_grad + jnp.dot(logit_grad, router.T, preferred_element_type=jnp.float32)
    middle_part, norm_two_grad = norm_back(second_grad, norm_two, scaled_two, spread_two)
    middle_grad = upstream + middle_part
    attended_grad = middle_grad.astype(jnp.bfloat16)
    head_out_grad = lax.dot_general(
        mixed_heads, attended_grad, (((0,), (0,)), ((), ())), preferred_element_type=jnp.float32
    )
    mixed_grad = jnp.dot(attended_grad, head_out.T, preferred_element_type=jnp.float32).astype(
        jnp.bfloat16
    )
    mixed_grad = mixed_grad.reshape(images, SEQ, heads_here, HD)
    probs_again = jnp.exp(
        jnp.einsum("ishd,ithd->ihst", queries, keys, preferred_element_type=jnp.float32)
        * score_scale
        - log_norm
    )
    prob_grad = jnp.einsum(
        "ishd,ithd->ihst", mixed_grad, values, preferred_element_type=jnp.float32
    )
    values_grad = jnp.einsum(
        "ihst,ishd->ithd",
        probs_again.astype(jnp.bfloat16),
        mixed_grad,
        preferred_element_type=jnp.float32,
    ).astype(jnp.bfloat16)
    score_grad = (
        probs_again * (prob_grad - jnp.sum(probs_again * prob_grad, -1, keepdims=True))
    ).astype(jnp.bfloat16)
    queries_grad = (
        jnp.einsum("ihst,ithd->ishd", score_grad, keys, preferred_element_type=jnp.float32)
        * score_scale
    ).astype(jnp.bfloat16)
    keys_grad = (
        jnp.einsum("ihst,ishd->ithd", score_grad, queries, preferred_element_type=jnp.float32)
        * score_scale
    ).astype(jnp.bfloat16)
    stacked = jnp.stack([queries_grad, keys_grad, values_grad]).reshape(3, rows_here, local_cols)
    head_in_grad = jnp.einsum("rd,krc->kdc", first_in, stacked, preferred_element_type=jnp.float32)
    first_grad = head_total(
        jnp.einsum("krc,kdc->rd", stacked, head_in, preferred_element_type=jnp.float32)
    )
    input_part, norm_one_grad = norm_back(first_grad, norm_one, scaled_one, spread_one)
    input_grad = middle_grad + input_part
    summed = (
        lax.psum(norm_one_grad.astype(jnp.bfloat16), "expert").astype(jnp.float32),
        lax.psum(head_in_grad.astype(jnp.bfloat16), "expert").astype(jnp.float32),
        lax.psum(head_out_grad.astype(jnp.bfloat16), "expert").astype(jnp.float32),
        lax.psum(norm_two_grad.astype(jnp.bfloat16), "expert").astype(jnp.float32),
        lax.psum(router_grad.astype(jnp.bfloat16), "expert").astype(jnp.float32),
    )
    return (
        block_out,
        input_grad,
        summed[0],
        summed[1],
        summed[2],
        summed[3],
        summed[4],
        expert_in_grad,
        expert_out_grad,
    )


def solution(mesh):
    in_specs = (
        P("expert", None),
        P(),
        P(None, None, "tensor"),
        P("tensor", None),
        P(),
        P(),
        P("expert", None, "tensor"),
        P("expert", "tensor", None),
        P("expert", None),
        P("expert", None),
        P("expert", None),
    )
    out_specs = (
        P("expert", None),
        P("expert", None),
        P(),
        P(None, None, "tensor"),
        P("tensor", None),
        P(),
        P(),
        P("expert", None, "tensor"),
        P("expert", "tensor", None),
    )
    return jax.shard_map(shards, mesh=mesh, in_specs=in_specs, out_specs=out_specs, check_vma=False)
```

profile of v0, /device:TPU:0, one launch (start us, length us, event | category | flops | bytes accessed | tf_op | source)
XLA Modules:
  0.0 1849.1 jit_solution(874290821535785502)
XLA Ops:
  7.2 3.1 convert_reduce_fusion
  10.3 3.6 fusion.38
  13.9 7.1 fusion.51
  22.6 3.2 reshape.271
  25.9 4.7 copy.106
  30.6 4.7 reshape.270
  35.3 5.1 copy.105
  40.5 4.5 reshape.269
  44.9 5.1 copy.107
  50.1 2.9 multiply_reduce_fusion.8
  59.6 3.6 reshape.216
  63.2 6.4 fusion.100
  77.2 156.4 %all-reduce.7.cloned.1.call-done = f32[2167,1024]{1,0:T(8,128)} async-done(((f32[2167,1024]{1,0:T(8,128)}), f32[2167,1024]{1,0:T(8,128)}) %all-reduce.7.cloned.1.call-update) | async-done | bytes 8876048 | tf_op jit(solution)/shard_map/psum | solution.py:32
  233.6 5.7 fusion.98
  240.9 3.5 multiply_convert_fusion.3
  244.4 7.1 broadcast_in_dim.2
  251.5 19.0 %reshape.248 = bf16[4334,1024]{1,0:T(8,128)(2,1)} reshape(bf16[2167,2,1024]{2,1,0:T(2,128)(2,1)} %broadcast_in_dim.2) | data formatting | bytes 17752064 | tf_op jit(solution)/shard_map/reshape | solution.py:111
  270.4 32.0 %scatter_custom_fusion = bf16[7040,1024]{1,0:T(8,128)(2,1)} fusion(s32[4334]{0:T(1024)S(1)} %fusion.88, bf16[4334,1024]{1,0:T(8,128)(2,1)} %reshape.248, bf16[]{:T(256)} %constant.16.clone.1), kind=kCustom, calls=%fused_computation.76 | custom fusion | bytes 14418432 | tf_op jit(solution)/shard_map/scatter | solution.py:108
  302.5 5.6 all-to-all-start
  308.0 7.8 mul.265
  315.8 22.0 %mul.266 = f32[4334,1024]{1,0:T(8,128)} reshape(f32[2167,2,1024]{2,1,0:T(2,128)} %mul.265) | data formatting | bytes 35504128 | tf_op jit(solution)/shard_map/mul | solution.py:126
  337.8 3.5 fusion.101
  343.6 45.5 %scatter_custom_fusion.1 = bf16[7040,1024]{1,0:T(8,128)(2,1)} fusion(s32[4334]{0:T(1024)S(1)} %fusion.88, f32[4334,1024]{1,0:T(8,128)} %mul.266, f32[4334]{0:T(1024)S(1)} %mul.263, bf16[]{:T(256)} %constant.16.clone.1), kind=kCustom, calls=%fused_computation.62 | custom fusion | flops 8876032 | bytes 32190466 | tf_op jit(solution)/shard_map/scatter | solution.py:108
  389.1 231.5 %all-to-all-done = bf16[8,880,1024]{2,1,0:T(8,128)(2,1)} async-done(((bf16[8,880,1024]{2,1,0:T(8,128)(2,1)}), bf16[8,880,1024]{2,1,0:T(8,128)(2,1)}, u32[]{:S(2)}, u32[]{:S(2)}) %all-to-all-start) | async-done | bytes 14417952 | tf_op jit(solution)/shard_map/all_to_all | solution.py:36
  620.6 5.5 all-to-all-start.2
  626.1 24.2 %fusion.62 = f32[8,880,1024]{2,1,0:T(8,128)} fusion(bf16[8,880,1024]{2,1,0:T(8,128)(2,1)} %all-to-all-done, bf16[1,1024,1024]{2,1,0:T(8,128)(2,1)} %param.17), kind=kOutput, calls=%fused_computation.99 | convolution fusion | flops 14763950080 | bytes 45350912 | tf_op jit(solution)/shard_map/sjcd,jdf->sjcf/dot_general | solution.py:117
  650.3 77.1 %convolution_convert_fusion = bf16[8,880,1024]{2,1,0:T(8,128)(2,1)} fusion(bf16[1,1024,1024]{2,1,0:T(8,128)(2,1)S(1)} %copy-done, f32[8,880,1024]{2,1,0:T(8,128)} %fusion.62), kind=kOutput, calls=%fused_computation.49 | convolution fusion | flops 15239741440 | bytes 45350912 | tf_op jit(solution)/shard_map/sjcf,jfd->sjcd/dot_general | solution.py:119
  727.9 209.8 %all-to-all-done.2 = bf16[8,880,1024]{2,1,0:T(8,128)(2,1)} async-done(((bf16[8,880,1024]{2,1,0:T(8,128)(2,1)}), bf16[8,880,1024]{2,1,0:T(8,128)(2,1)}, u32[]{:S(2)}, u32[]{:S(2)}) %all-to-all-start.2) | async-done | bytes 14417952 | tf_op jit(solution)/shard_map/all_to_all | solution.py:36
  937.8 82.5 %fusion.6 = bf16[8,1,880,1024]{3,2,0,1:T(8,128)(2,1)} fusion(f32[8,880,1024]{2,1,0:T(8,128)} %fusion.62, bf16[8,880,1024]{2,1,0:T(8,128)(2,1)} %all-to-all-done.2, bf16[1,1024,1024]{2,1,0:T(8,128)(2,1)S(1)} %copy-done), kind=kOutput, calls=%fused_computation.13 | convolution fusion | flops 15282995200 | bytes 59768832 | tf_op jit(solution)/shard_map/sjcd,jfd->sjcf/dot_general | solution.py:134
  1020.2 22.9 %fusion.29 = bf16[8,880,1024]{2,1,0:T(8,128)(2,1)} fusion(bf16[8,1,880,1024]{3,2,0,1:T(8,128)(2,1)} %fusion.6, bf16[1,1024,1024]{2,1,0:T(8,128)(2,1)S(1)} %copy-done.53), kind=kOutput, calls=%fused_computation.48 | convolution fusion | flops 14771159040 | bytes 30932992 | tf_op jit(solution)/shard_map/sjcf,jdf->sjcd/dot_general | solution.py:144
  1043.2 84.8 %all_to_all.42 = bf16[8,880,256]{2,1,0:T(8,128)(2,1)} all-to-all(bf16[8,880,256]{2,1,0:T(8,128)(2,1)} %bitcast.228), channel_id=1, replica_groups=mesh['expert'=8,'tensor'=4] {'expert'}, dimensions={0} | all-to-all | bytes 7208960 | tf_op jit(solution)/shard_map/all_to_all | solution.py:43
  1128.1 24.6 %reduce-scatter.5.cloned.1.call-done = bf16[7040,256]{1,0:T(8,128)(2,1)} async-done(((bf16[7040,1024]{1,0:T(8,128)(2,1)}), bf16[7040,256]{1,0:T(8,128)(2,1)}) %reduce-scatter.5.cloned.1.call-update) | async-done | bytes 3604496 | tf_op jit(solution)/shard_map/reduce_scatter | solution.py:40
  1152.7 86.3 %all_to_all.43 = bf16[8,880,256]{2,1,0:T(8,128)(2,1)} all-to-all(bf16[8,880,256]{2,1,0:T(8,128)(2,1)} %bitcast.229), channel_id=1, replica_groups=mesh['expert'=8,'tensor'=4] {'expert'}, dimensions={0} | all-to-all | bytes 7208960 | tf_op jit(solution)/shard_map/all_to_all | solution.py:43
  1239.0 6.8 convert_element_type.175
  1248.6 26.8 %gather_fusion = bf16[4334,1024]{1,0:T(8,128)(2,1)} fusion(bf16[7040,1024]{1,0:T(8,128)(2,1)} %all-gather.3.cloned.1.call-done, s32[5120]{0:T(1024)S(1)} %pad_clamp_fusion), kind=kCustom, calls=%fused_computation | custom fusion | bytes 17769400 | tf_op jit(solution)/shard_map/gather | solution.py:123
  1275.3 20.1 %reshape.226 = f32[2167,2,1024]{2,1,0:T(2,128)} reshape(bf16[4334,1024]{1,0:T(8,128)(2,1)} %gather_fusion) | data formatting | bytes 26628096 | tf_op jit(solution)/shard_map/convert_element_type | solution.py:123
  1295.4 43.8 %multiply_reduce_fusion = (f32[2167,2]{1,0:T(8,128)S(1)}, f32[2167,1024]{1,0:T(8,128)}) fusion(f32[2167,2,1024]{2,1,0:T(2,128)} %reshape.226, f32[2167,1024]{1,0:T(8,128)} %convert_element_type.175, f32[2167,2]{1,0:T(8,128)S(1)} %copy-done.13), kind=kLoop, calls=%fused_computation.32 | loop fusion | flops 15528722 | bytes 35538800 | tf_op jit(solution)/shard_map/reduce_sum | solution.py:124
  1339.8 4.7 all-gather.5.cloned.1.call-done
  1344.5 26.6 %gather_fusion.1 = bf16[4334,1024]{1,0:T(8,128)(2,1)} fusion(bf16[7040,1024]{1,0:T(8,128)(2,1)} %all-gather.5.cloned.1.call-done, s32[5120]{0:T(1024)S(1)} %pad_clamp_fusion), kind=kCustom, calls=%fused_computation.1 | custom fusion | bytes 17769400 | tf_op jit(solution)/shard_map/gather | solution.py:151
  1371.0 19.9 %reshape.227 = f32[2167,2,1024]{2,1,0:T(2,128)} reshape(bf16[4334,1024]{1,0:T(8,128)(2,1)} %gather_fusion.1) | data formatting | bytes 26628096 | tf_op jit(solution)/shard_map/convert_element_type | solution.py:151
  1391.0 26.7 %reduce_sum.192 = f32[2167,1024]{1,0:T(8,128)} reduce(f32[2167,2,1024]{2,1,0:T(2,128)} %reshape.227, f32[]{:T(128)} %constant.40.clone.1), dimensions={1}, to_apply=%region_18.19 | reduce | flops 2219008 | bytes 26628100 | tf_op jit(solution)/shard_map/reduce_sum | solution.py:150
  1417.7 9.1 multiply_reduce_fusion.3
  1426.8 10.2 multiply_add_fusion
  1442.1 3.2 reshape.272
  1445.4 4.2 copy.118
  1449.6 6.4 fusion.77
  1456.0 7.2 multiply_reduce_fusion.2
  1463.3 10.7 multiply_convert_fusion.1
  1474.0 5.1 fusion.81
  1481.1 5.2 copy.139
  1486.3 3.6 reshape.268
  1490.0 5.2 copy.137
  1495.2 4.4 reshape.266
  1499.6 3.4 copy.138
  1503.0 3.6 reshape.267
  1509.9 8.0 fusion.74
  1518.0 9.4 convolution_bitcast_fusion
  1527.4 79.5 %convolution_bitcast_fusion.1 = f32[1,1024,1024]{2,1,0:T(8,128)} fusion(bf16[8,880,1024]{2,1,0:T(8,128)(2,1)} %all-to-all-done.2, f32[8,880,1024]{2,1,0:T(8,128)} %fusion.62), kind=kOutput, calls=%fused_computation.95 | convolution fusion | flops 15232532480 | bytes 47448064 | tf_op jit(solution)/shard_map/sjcf,sjcd->jfd/dot_general | solution.py:131
  1606.9 21.6 %fusion.56 = f32[1,1024,1024]{2,1,0:T(8,128)} fusion(bf16[8,880,1024]{2,1,0:T(8,128)(2,1)} %all-to-all-done, bf16[8,1,880,1024]{3,2,0,1:T(8,128)(2,1)} %fusion.6), kind=kOutput, calls=%fused_computation.94 | convolution fusion | flops 14763950080 | bytes 33030144 | tf_op jit(solution)/shard_map/sjcd,sjcf->jdf/dot_general | solution.py:141
  1631.4 3.1 copy.132
  1634.5 149.3 %all-reduce.9.cloned.1.call-done = f32[2167,1024]{1,0:T(8,128)} async-done(((f32[2167,1024]{1,0:T(8,128)}), f32[2167,1024]{1,0:T(8,128)}) %all-reduce.9.cloned.1.call-update) | async-done | bytes 8876048 | tf_op jit(solution)/shard_map/psum | solution.py:32
  1783.7 7.1 fusion.37
  1790.8 37.1 %all-reduce.1 = (bf16[1024]{0:T(1024)(128)(2,1)S(1)}, bf16[1024]{0:T(1024)(128)(2,1)S(1)}, bf16[1024,8]{0,1:T(8,128)(2,1)S(1)}) all-reduce(bf16[1024]{0:T(1024)(128)(2,1)S(1)} %get-tuple-element.49, bf16[1024]{0:T(1024)(128)(2,1)S(1)} %copy-done.52, ...), channel_id=1, replica_groups=mesh['expert'=8,'tensor'=4] {'expert'}, use_global_device_ids=true, to_apply=%region_29.30 | all-reduce | flops 10240 | bytes 40960 | tf_op jit(solution)/shard_map/psum | solution.py:203
  1829.8 12.3 fusion.36
  (180 shorter events, 38.6 us)
Async XLA Ops:
  7.2 643.1 %copy-start = (bf16[1,1024,1024]{2,1,0:T(8,128)(2,1)S(1)}, bf16[1,1024,1024]{2,1,0:T(8,128)(2,1)}, u32[]{:S(2)}) copy-start(bf16[1,1024,1024]{2,1,0:T(8,128)(2,1)} %param.18) | copy-start | bytes 6291460
  7.2 226.4 %all-reduce.7.cloned.1.call-start = ((), (), s32[]{:S(2)}) async-start(), calls=%async_computation.6 | async-start | bytes 17760256 | tf_op jit(solution)/shard_map/psum | solution.py:32
  10.3 10.7 copy-start.35
  13.9 7.2 copy-start.40
  30.6 22.4 %copy-start.7 = (bf16[11,197,4,64]{1,3,2,0:T(8,128)(2,1)}, bf16[11,197,4,64]{1,3,2,0:T(8,128)(2,1)S(1)}, u32[]{:S(2)}) copy-start(bf16[11,197,4,64]{1,3,2,0:T(8,128)(2,1)S(1)} %copy.106) | copy-start | bytes 3328516
  50.1 4.9 copy-start.15
  53.0 4.3 copy-start.2
  53.0 4.3 copy-start.20
  55.0 2.4 copy-start.38
  63.2 6.4 copy-start.10
  63.2 6.4 copy-start.29
  77.2 266.4 %copy-start.43 = (s32[4334]{0:T(1024)}, s32[4334]{0:T(1024)S(1)}, u32[]{:S(2)}) copy-start(s32[4334]{0:T(1024)S(1)} %fusion.88) | copy-start | bytes 52012
  77.2 163.6 %copy-start.47 = (f32[1024]{0:T(1024)S(1)}, f32[1024]{0:T(1024)}, u32[]{:S(2)}) copy-start(f32[1024]{0:T(1024)} %param.15) | copy-start | bytes 12292
  239.4 5.0 copy-start.3
  239.4 1.5 copy-start.27
  240.9 10.6 copy-start.33
  302.5 318.1 %all-to-all-start = ((bf16[8,880,1024]{2,1,0:T(8,128)(2,1)}), bf16[8,880,1024]{2,1,0:T(8,128)(2,1)}, u32[]{:S(2)}, u32[]{:S(2)}) async-start(bf16[8,880,1024]{2,1,0:T(8,128)(2,1)} %bitcast.220), calls=%async_computation | async-start | bytes 28835840 | tf_op jit(solution)/shard_map/all_to_all | solution.py:36
  315.8 22.0 %copy-start.45 = (bf16[1024,8]{0,1:T(8,128)(2,1)S(1)}, bf16[1024,8]{0,1:T(8,128)(2,1)}, u32[]{:S(2)}) copy-start(bf16[1024,8]{0,1:T(8,128)(2,1)} %param.16) | copy-start | bytes 49156
  315.8 25.6 %copy-start.49 = (f32[2167,2]{0,1:T(2,128)S(1)}, f32[2167,2]{0,1:T(2,128)}, u32[]{:S(2)}) copy-start(f32[2167,2]{0,1:T(2,128)} %param.20) | copy-start | bytes 52012
  341.4 0.6 copy-start.18
  341.4 0.6 copy-start.25
  343.1 46.1 %copy-start.12 = (f32[2167,2]{1,0:T(8,128)}, f32[2167,2]{1,0:T(8,128)S(1)}, u32[]{:S(2)}) copy-start(f32[2167,2]{1,0:T(8,128)S(1)} %copy.110) | copy-start | bytes 52012
  620.6 317.2 %all-to-all-start.2 = ((bf16[8,880,1024]{2,1,0:T(8,128)(2,1)}), bf16[8,880,1024]{2,1,0:T(8,128)(2,1)}, u32[]{:S(2)}, u32[]{:S(2)}) async-start(bf16[8,880,1024]{2,1,0:T(8,128)(2,1)} %bitcast.221), calls=%async_computation.3 | async-start | bytes 28835840 | tf_op jit(solution)/shard_map/all_to_all | solution.py:36
  626.1 417.1 %reduce-scatter.3.cloned.1.call-start = ((), (), s32[]{:S(2)}) async-start(), calls=%async_computation.7 | async-start | bytes 18022400 | tf_op jit(solution)/shard_map/reduce_scatter | solution.py:40
  727.5 425.2 %reduce-scatter.5.cloned.1.call-start = ((), (), s32[]{:S(2)}) async-start(), calls=%async_computation.9 | async-start | bytes 18022400 | tf_op jit(solution)/shard_map/reduce_scatter | solution.py:40
  937.7 82.5 %copy-start.53 = (bf16[1,1024,1024]{2,1,0:T(8,128)(2,1)S(1)}, bf16[1,1024,1024]{2,1,0:T(8,128)(2,1)}, u32[]{:S(2)}) copy-start(bf16[1,1024,1024]{2,1,0:T(8,128)(2,1)} %param.17) | copy-start | bytes 6291460
  1043.2 205.4 %all-gather.3.cloned.1.call-start = ((), (), s32[]{:S(2)}) async-start(), calls=%async_computation.8 | async-start | bytes 18022400 | tf_op jit(solution)/shard_map/all_gather | solution.py:44
  1128.1 216.4 %all-gather.5.cloned.1.call-start = ((), (), s32[]{:S(2)}) async-start(), calls=%async_computation.10 | async-start | bytes 18022400 | tf_op jit(solution)/shard_map/all_gather | solution.py:44
  1238.9 6.8 copy-start.44
  1238.9 6.9 copy-start.21
  1238.9 6.9 copy-start.39
  1239.0 390.3 %all-reduce.11.cloned.1.call-start = ((), (), s32[]{:S(2)}) async-start(), calls=%async_computation.12 | async-start | bytes 4194304 | tf_op jit(solution)/shard_map/psum | solution.py:204
  1275.3 20.1 %copy-start.13 = (f32[2167,2]{1,0:T(8,128)S(1)}, f32[2167,2]{1,0:T(8,128)}, u32[]{:S(2)}) copy-start(f32[2167,2]{1,0:T(8,128)} %copy-done.12) | copy-start | bytes 52012
  1295.4 44.2 %copy-start.19 = (f32[2167,2]{0,1:T(2,128)S(1)}, f32[2167,2]{0,1:T(2,128)}, u32[]{:S(2)}) copy-start(f32[2167,2]{0,1:T(2,128)} %copy-done.18) | copy-start | bytes 52012
  1295.4 44.2 %copy-start.26 = (f32[2167]{0:T(1024)S(1)}, f32[2167]{0:T(1024)}, u32[]{:S(2)}) copy-start(f32[2167]{0:T(1024)} %copy-done.25) | copy-start | bytes 26008
  1295.4 44.2 %copy-start.32 = (f32[2167]{0:T(1024)S(1)}, f32[2167]{0:T(1024)}, u32[]{:S(2)}) copy-start(f32[2167]{0:T(1024)} %copy-done.31) | copy-start | bytes 26008
  1295.4 44.3 %copy-start.30 = (s32[2167,2]{0,1:T(2,128)S(1)}, s32[2167,2]{0,1:T(2,128)}, u32[]{:S(2)}) copy-start(s32[2167,2]{0,1:T(2,128)} %param.19) | copy-start | bytes 52012
  1339.8 77.9 %copy-start.23 = (bf16[2167,8]{0,1:T(8,128)(2,1)}, bf16[2167,8]{0,1:T(8,128)(2,1)S(1)}, u32[]{:S(2)}) copy-start(bf16[2167,8]{0,1:T(8,128)(2,1)S(1)} %select_reduce_fusion) | copy-start | bytes 104020
  1391.0 26.7 %copy-start.28 = (f32[2167]{0:T(1024)S(1)}, f32[2167]{0:T(1024)}, u32[]{:S(2)}) copy-start(f32[2167]{0:T(1024)} %copy-done.27) | copy-start | bytes 26008
  1391.0 26.7 %copy-start.34 = (f32[2167]{0:T(1024)S(1)}, f32[2167]{0:T(1024)}, u32[]{:S(2)}) copy-start(f32[2167]{0:T(1024)} %copy-done.33) | copy-start | bytes 26008
  1391.0 26.7 %copy-start.46 = (bf16[1024,8]{0,1:T(8,128)(2,1)S(1)}, bf16[1024,8]{0,1:T(8,128)(2,1)}, u32[]{:S(2)}) copy-start(bf16[1024,8]{0,1:T(8,128)(2,1)} %param.16) | copy-start | bytes 49156
  1391.0 26.8 %copy-start.48 = (f32[1024]{0:T(1024)S(1)}, f32[1024]{0:T(1024)}, u32[]{:S(2)}) copy-start(f32[1024]{0:T(1024)} %param.15) | copy-start | bytes 12292
  1391.0 35.8 %slice-start = ((s8[4440064]{0:T(1024)(128)(4,1)}), s8[245760]{0:T(1024)(128)(4,1)S(1)}, s32[]{:S(2)}) async-start(s8[4440064]{0:T(1024)(128)(4,1)} %bitcast.222), calls=%async_computation.13 | async-start | bytes 491520
  1417.7 9.1 slice-start.1
  1426.8 10.2 copy-start.11
  1437.0 3.7 copy-start.4
  1437.0 3.7 copy-start.17
  1442.1 13.9 copy-start.16
  1463.3 10.7 copy-start.9
  1463.3 15.8 copy-start.8
  1474.0 5.1 copy-start.6
  1479.1 20.5 %copy-start.14 = (bf16[11,197,4,64]{1,3,2,0:T(8,128)(2,1)S(1)}, bf16[11,197,4,64]{1,3,2,0:T(8,128)(2,1)}, u32[]{:S(2)}) copy-start(bf16[11,197,4,64]{1,3,2,0:T(8,128)(2,1)} %fusion.81) | copy-start | bytes 3328516
  1495.2 14.7 copy-start.36
  1495.2 14.7 copy-start.41
  1495.2 14.7 copy-start.50
  1508.2 1.7 copy-start.22
  1517.9 265.8 %all-reduce.9.cloned.1.call-start = ((), (), s32[]{:S(2)}) async-start(), calls=%async_computation.11 | async-start | bytes 17760256 | tf_op jit(solution)/shard_map/psum | solution.py:32
  1606.9 21.6 %copy-start.5 = (bf16[2167,1024]{1,0:T(8,128)(2,1)S(1)}, bf16[2167,1024]{1,0:T(8,128)(2,1)}, u32[]{:S(2)}) copy-start(bf16[2167,1024]{1,0:T(8,128)(2,1)} %multiply_convert_fusion.3) | copy-start | bytes 13314052
  1606.9 21.6 %copy-start.24 = (bf16[2167,8]{0,1:T(8,128)(2,1)S(1)}, bf16[2167,8]{0,1:T(8,128)(2,1)}, u32[]{:S(2)}) copy-start(bf16[2167,8]{0,1:T(8,128)(2,1)} %copy-done.23) | copy-start | bytes 104020
  1628.6 155.2 %copy-start.37 = (f32[2167]{0:T(1024)S(1)}, f32[2167]{0:T(1024)}, u32[]{:S(2)}) copy-start(f32[2167]{0:T(1024)} %copy-done.35) | copy-start | bytes 26008
  1628.6 155.2 %copy-start.42 = (f32[2167]{0:T(1024)S(1)}, f32[2167]{0:T(1024)}, u32[]{:S(2)}) copy-start(f32[2167]{0:T(1024)} %copy-done.40) | copy-start | bytes 26008
  1628.6 155.2 %copy-start.51 = (f32[1024]{0:T(1024)S(1)}, f32[1024]{0:T(1024)}, u32[]{:S(2)}) copy-start(f32[1024]{0:T(1024)} %param.12) | copy-start | bytes 12292
  1631.4 159.4 %copy-start.52 = (bf16[1024]{0:T(1024)(128)(2,1)S(1)}, bf16[1024]{0:T(1024)(128)(2,1)}, u32[]{:S(2)}) copy-start(bf16[1024]{0:T(1024)(128)(2,1)} %get-tuple-element.45) | copy-start | bytes 6148
  1829.1 13.0 copy-start.1
  (1 other events, 0.6 us)
Sparse Core Ops, SparseCore 0:
  69.7 163.8 all-reduce.6
  727.6 111.5 reduce-scatter.2
  1043.3 109.3 reduce-scatter.4
  1154.1 94.4 all-gather.2
  1250.0 94.4 all-gather.4
  1518.1 102.1 all-reduce.10
  1622.8 160.9 all-reduce.8
where the time goes:
time: 1860 us; the launch traced here: 1850 us
  waiting for transfers between devices  779 us (42%)
  matrix products  382 us (21%)
  local copies, waits for them, and re-layouts  264 us (14%)
  blocking collectives  208 us (11%)
  other arithmetic  189 us (10%)
    all_to_all x2, waiting for transfers between devices, to_owner(): lax.all_to_all(buffer, 'expert', split_axis=0, concat_axis=0, tiled=True)  441 us
    psum x2, waiting for transfers between devices, head_total(): return lax.psum(partial_value, 'tensor')  306 us
    all_to_all x2, blocking collectives, to_source(): lax.all_to_all(reduced, 'expert', split_axis=0, concat_axis=0, tiled=True)  171 us
    dot_general x1, matrix products, shards(): jnp.einsum('sjcd,jfd->sjcf', owner_grad, expert_out, preferred_element_ty...  82.5 us
    dot_general x1, matrix products, shards(): jnp.einsum('sjcf,sjcd->jfd', active, owner_grad, preferred_element_type=j...  79.5 us
    dot_general x1, matrix products, shards(): jnp.einsum('sjcf,jfd->sjcd', active, expert_out, preferred_element_type=j...  77.1 us
    scatter x1, other arithmetic, pack_rows(): jnp.zeros((slot_count, model_width), jnp.bfloat16).at[positions]  45.5 us
    reduce_sum x1, other arithmetic, shards(): gate_grad = jnp.sum(upstream[:, None, :] * picked, -1)  43.8 us
  transfers between devices with their start and end apart: 9, of which 7 were waited for; matrix products, arithmetic and copies ran while one was open for 27% of the time, Pallas kernels for 0%

commit v1 on v0

v1 whole, which is shorter than its diff:
```python
import functools

import jax
import jax.numpy as jnp
from jax import lax
from jax.experimental import pallas as pl
from jax.experimental.pallas import tpu as pltpu
from jax.sharding import PartitionSpec as P

HD = 64
SEQ = 197
LANES = 128
EPSILON = 1e-06
CHUNKS = 1
BF = jnp.bfloat16
F32 = jnp.float32


def up_to(value, unit):
    return -(-value // unit) * unit


def params(mib=48):
    return pltpu.CompilerParams(vmem_limit_bytes=mib * 1024 * 1024)


def dot(a, b, da=1, db=0):
    return lax.dot_general(a, b, (((da,), (db,)), ((), ())), preferred_element_type=F32)


def iota(rows, cols, dim):
    return lax.broadcasted_iota(jnp.int32, (rows, cols), dim)


def flag(mask):
    return jnp.where(mask, 1.0, 0.0)


def whole(shape, once=False):
    zeros = (0,) * len(shape)
    mode = pl.Buffered(1) if once else None
    return pl.BlockSpec(shape, lambda *_: zeros, pipeline_mode=mode)


def image(*shape):
    return pl.BlockSpec((1,) + shape, lambda i: (i,) + (0,) * len(shape))


def fill(x_ref, tail_ref, rows_ref):
    full = x_ref.shape[0] // 16 * 16
    rows_ref[0:full, :] = x_ref[0:full, :]
    rows_ref[full : full + 16, :] = tail_ref[...]
    rest = rows_ref.shape[0] - full - 16
    if rest:
        rows_ref[full + 16 :, :] = jnp.zeros((rest, rows_ref.shape[1]), BF)


def norm_parts(field):
    centre = field - jnp.mean(field, -1, keepdims=True)
    spread = lax.rsqrt(jnp.mean(centre * centre, -1, keepdims=True) + EPSILON)
    return centre * spread, spread


def norm_field_back(upstream, gain, scaled, spread):
    weighted = upstream * gain
    return spread * (
        weighted
        - jnp.mean(weighted, -1, keepdims=True)
        - scaled * jnp.mean(weighted * scaled, -1, keepdims=True)
    )


def head_masks():
    lane = iota(1, LANES, 1)
    return [(flag(lane // HD == h)).astype(BF) for h in range(2)]


def attend_kernel(images, x_ref, tail_ref, gain_ref, w_ref, mixed_ref, first_ref, qkv_ref, log_ref, rows):
    i = pl.program_id(0)

    @pl.when(i == 0)
    def _():
        fill(x_ref, tail_ref, rows)

    height = first_ref.shape[1]
    window = height + 16
    start = jnp.minimum(i, images - 1) * SEQ
    aligned = start // 16 * 16
    r, c = iota(height, window, 0), iota(height, window, 1)
    limit = jnp.where(i < images, SEQ, 0)
    shift = flag((c == r + (start - aligned)) & (r < limit)).astype(BF)
    field = dot(shift, rows[pl.ds(pl.multiple_of(aligned, 16), window), :])
    scaled, _ = norm_parts(field)
    first = (scaled * gain_ref[...]).astype(BF)
    first_ref[0] = first
    for k in range(3):
        qkv_ref[k, 0] = dot(first, w_ref[k]).astype(BF)
    masks = head_masks()
    lane = iota(1, LANES, 1)
    key_lane = iota(1, height, 1)
    logs = jnp.zeros((height, LANES), F32)
    for pair in range(mixed_ref.shape[2] // LANES):
        cols = slice(pair * LANES, (pair + 1) * LANES)
        queries, keys, values = (qkv_ref[k, 0, :, cols] for k in range(3))
        total = jnp.zeros((height, LANES), F32)
        for h in range(2):
            scores = dot(queries * masks[h], keys, 1, 1) * HD ** (-0.5)
            scores = jnp.where(key_lane < SEQ, scores, -1e30)
            highest = jnp.max(scores, -1, keepdims=True)
            weights = jnp.exp(scores - highest)
            sums = jnp.sum(weights, -1, keepdims=True)
            probs = (weights * (1.0 / sums)).astype(BF)
            total += dot(probs, values * masks[h])
            logs = jnp.where(lane == pair * 2 + h, highest + jnp.log(sums), logs)
        mixed_ref[0, :, cols] = total.astype(BF)
    log_ref[0] = logs


def attend(block_in, tail, gain, head_in, images, image_slots, height):
    rows, width = block_in.shape
    cols = head_in.shape[2]
    return pl.pallas_call(
        functools.partial(attend_kernel, images),
        grid=(image_slots,),
        in_specs=[whole((rows, width), True), whole((16, width)), whole((1, width)), whole(head_in.shape, True)],
        out_specs=[
            image(height, cols),
            image(height, width),
            pl.BlockSpec((3, 1, height, cols), lambda i: (0, i, 0, 0)),
            image(height, LANES),
        ],
        out_shape=[
            jax.ShapeDtypeStruct((image_slots, height, cols), BF),
            jax.ShapeDtypeStruct((image_slots, height, width), BF),
            jax.ShapeDtypeStruct((3, image_slots, height, cols), BF),
            jax.ShapeDtypeStruct((image_slots, height, LANES), F32),
        ],
        scratch_shapes=[pltpu.VMEM((rows // 16 * 16 + 48, width), BF)],
        compiler_params=params(),
        name="attend",
    )(block_in, tail, gain, head_in)


def attend_back_kernel(dmix_ref, qkv_ref, log_ref, first_ref, w_ref, fg_ref, hg_ref, acc, grads):
    i = pl.program_id(0)
    height = first_ref.shape[1]
    masks = head_masks()
    lane = iota(1, LANES, 1)
    key_lane = iota(1, height, 1)
    scale = HD ** (-0.5)
    logs = log_ref[0]
    for pair in range(dmix_ref.shape[2] // LANES):
        cols = slice(pair * LANES, (pair + 1) * LANES)
        queries, keys, values = (qkv_ref[k, 0, :, cols] for k in range(3))
        out_grad = dmix_ref[0, :, cols]
        dq = jnp.zeros((height, LANES), F32)
        dk = jnp.zeros((height, LANES), F32)
        dv = jnp.zeros((height, LANES), F32)
        for h in range(2):
            q_h = queries * masks[h]
            o_h = out_grad * masks[h]
            log_h = jnp.sum(jnp.where(lane == pair * 2 + h, logs, 0.0), -1, keepdims=True)
            probs = jnp.exp(dot(q_h, keys, 1, 1) * scale - log_h)
            probs = jnp.where(key_lane < SEQ, probs, 0.0)
            prob_grad = dot(o_h, values, 1, 1)
            dv += dot(probs.astype(BF), o_h, 0, 0)
            delta = jnp.sum(probs * prob_grad, -1, keepdims=True)
            score_grad = (probs * (prob_grad - delta)).astype(BF)
            dq += dot(score_grad, keys * masks[h])
            dk += dot(score_grad, q_h, 0, 0)
        grads[0, :, cols] = (dq * scale).astype(BF)
        grads[1, :, cols] = (dk * scale).astype(BF)
        grads[2, :, cols] = dv.astype(BF)

    @pl.when(i == 0)
    def _():
        acc[...] = jnp.zeros_like(acc)

    first = first_ref[0]
    total = None
    for k in range(3):
        part = dot(grads[k], w_ref[k], 1, 1)
        total = part if total is None else total + part
        acc[k] += dot(first, grads[k], 0, 0)
    fg_ref[0] = total.astype(BF)

    @pl.when(i == pl.num_programs(0) - 1)
    def _():
        hg_ref[...] = acc[...].astype(BF)


def attend_back(dmix, qkv, logs, first, head_in):
    image_slots, height, cols = dmix.shape
    width = first.shape[2]
    return pl.pallas_call(
        attend_back_kernel,
        grid=(image_slots,),
        in_specs=[
            image(height, cols),
            pl.BlockSpec((3, 1, height, cols), lambda i: (0, i, 0, 0)),
            image(height, LANES),
            image(height, width),
            whole(head_in.shape, True),
        ],
        out_specs=[image(height, width), whole(head_in.shape)],
        out_shape=[
            jax.ShapeDtypeStruct((image_slots, height, width), BF),
            jax.ShapeDtypeStruct(head_in.shape, BF),
        ],
        scratch_shapes=[pltpu.VMEM(head_in.shape, F32), pltpu.VMEM((3, height, cols), BF)],
        compiler_params=params(),
        name="attend_back",
    )(dmix, qkv, logs, first, head_in)


def pack_first_kernel(slots, base, x_ref, tail_ref, lp_ref, side_ref, out_ref, rows):
    e = pl.program_id(0)

    @pl.when(e == 0)
    def _():
        fill(x_ref, tail_ref, rows)

    j = base + e * slots + iota(slots, rows.shape[0], 0)
    picks = [flag(lp_ref[c : c + 1, :] == j) for c in range(2)]
    width = x_ref.shape[1]
    out_ref[0, :, 0:width] = dot((picks[0] + picks[1]).astype(BF), rows[...]).astype(BF)
    out_ref[0, :, width:] = (
        dot(picks[0].astype(BF), side_ref[0]) + dot(picks[1].astype(BF), side_ref[1])
    ).astype(BF)


def pack_first(x, tail, lp, side, experts, slots, base):
    rows, width = x.shape
    padded = lp.shape[1]
    return pl.pallas_call(
        functools.partial(pack_first_kernel, slots, base),
        grid=(experts,),
        in_specs=[whole((rows, width), True), whole((16, width)), whole(lp.shape), whole(side.shape)],
        out_specs=image(slots, width + LANES),
        out_shape=jax.ShapeDtypeStruct((experts, slots, width + LANES), BF),
        scratch_shapes=[pltpu.VMEM((padded, width), BF)],
        compiler_params=params(),
        name="pack_cotangent",
    )(x, tail, lp, side)


def pack_kernel(slots, base, x_ref, lp_ref, out_ref):
    j = base + pl.program_id(0) * slots + iota(slots, x_ref.shape[0], 0)
    picks = flag((lp_ref[0:1, :] == j) | (lp_ref[1:2, :] == j)).astype(BF)
    out_ref[0] = dot(picks, x_ref[...]).astype(BF)


def pack(x, lp, experts, slots, base):
    rows, width = x.shape
    return pl.pallas_call(
        functools.partial(pack_kernel, slots, base),
        grid=(experts,),
        in_specs=[whole((rows, width), True), whole(lp.shape)],
        out_specs=image(slots, width),
        out_shape=jax.ShapeDtypeStruct((experts, slots, width), BF),
        compiler_params=params(),
        name="pack_rows",
    )(x, lp)


def unpack_kernel(count, lp_ref, *refs):
    row_refs, gg_refs, out_ref = refs[:count], refs[count:-1], refs[-1]
    lp = lp_ref[0]
    height = lp.shape[0]
    width = row_refs[0].shape[1]
    total = jnp.zeros((height, width), F32)
    extra = [jnp.zeros((height, 1), F32) for _ in range(2)]
    for n in range(count):
        slots = row_refs[n].shape[0]
        j = n * slots + iota(1, slots, 1)
        hits = [lp[:, c : c + 1] == j for c in range(2)]
        total += dot(flag(hits[0] | hits[1]).astype(BF), row_refs[n][...])
        if gg_refs:
            for c in range(2):
                extra[c] += jnp.sum(jnp.where(hits[c], gg_refs[n][...], 0.0), -1, keepdims=True)
    out_ref[0, :, 0:width] = total.astype(BF)
    if gg_refs:
        lane = iota(1, LANES, 1)
        tail = jnp.zeros((height, LANES), F32)
        for c in range(2):
            high = extra[c].astype(BF).astype(F32)
            tail = jnp.where(lane == c, high, tail)
            tail = jnp.where(lane == 2 + c, extra[c] - high, tail)
        out_ref[0, :, width:] = tail.astype(BF)


def unpack(lp, rows, gate_grads=()):
    image_slots, height, _ = lp.shape
    count = len(rows)
    width = rows[0].shape[1]
    out_width = width + (LANES if gate_grads else 0)
    return pl.pallas_call(
        functools.partial(unpack_kernel, count),
        grid=(image_slots,),
        in_specs=[image(height, 2)]
        + [whole(item.shape, True) for item in rows]
        + [whole(item.shape) for item in gate_grads],
        out_specs=image(height, out_width),
        out_shape=jax.ShapeDtypeStruct((image_slots, height, out_width), BF),
        compiler_params=params(),
        name="unpack_rows",
    )(lp, *rows, *gate_grads)


def middle_kernel(mixed_ref, wo_ref, x_ref, gain_ref, router_ref, ids_ref, noise_ref, mid_ref, second_ref, gates_ref):
    middle = x_ref[0].astype(F32)
    for t in range(wo_ref.shape[0]):
        middle += dot(mixed_ref[t, 0], wo_ref[t])
    mid_ref[0] = middle
    scaled, _ = norm_parts(middle)
    second = (scaled * gain_ref[...]).astype(BF)
    second_ref[0] = second
    logits = dot(second, router_ref[...])
    lane = iota(1, LANES, 1)
    chosen = [
        jnp.sum(jnp.where(lane == ids_ref[0, :, c : c + 1], logits, 0.0), -1, keepdims=True)
        + noise_ref[0, :, c : c + 1]
        for c in range(2)
    ]
    top = jnp.maximum(chosen[0], chosen[1])
    raw = [jnp.exp(item - top) for item in chosen]
    inverse = 1.0 / (raw[0] + raw[1])
    gates_ref[0] = jnp.where(lane == 0, raw[0] * inverse, 0.0) + jnp.where(lane == 1, raw[1] * inverse, 0.0)


def middle_of(mixed, head_out, x_own, gain, router, ids, noise):
    parts, own, height, cols = mixed.shape
    width = x_own.shape[2]
    return pl.pallas_call(
        middle_kernel,
        grid=(own,),
        in_specs=[
            pl.BlockSpec((parts, 1, height, cols), lambda i: (0, i, 0, 0)),
            whole(head_out.shape, True),
            image(height, width),
            whole((1, width)),
            whole(router.shape),
            image(height, 2),
            image(height, 2),
        ],
        out_specs=[image(height, width), image(height, width), image(height, LANES)],
        out_shape=[
            jax.ShapeDtypeStruct((own, height, width), F32),
            jax.ShapeDtypeStruct((own, height, width), BF),
            jax.ShapeDtypeStruct((own, height, LANES), F32),
        ],
        compiler_params=params(),
        name="middle",
    )(mixed, head_out, x_own, gain, router, ids, noise)


def middle_back_kernel(
    rs_ref, mid_ref, second_ref, gates_ref, ids_ref, up_ref, mixed_ref, wo_ref, gain_ref, router_ref,
    mg_ref, dmix_ref, hog_ref, rg_ref, ng_ref, hog_acc,
):
    i = pl.program_id(0)

    @pl.when(i == 0)
    def _():
        hog_acc[...] = jnp.zeros_like(hog_acc)
        rg_ref[...] = jnp.zeros_like(rg_ref)
        ng_ref[...] = jnp.zeros_like(ng_ref)

    width = up_ref.shape[2]
    lane = iota(1, LANES, 1)
    tail = rs_ref[0, :, width:].astype(F32)
    gates = gates_ref[0]
    gate, grad = [], []
    for c in range(2):
        gate.append(jnp.sum(jnp.where(lane == c, gates, 0.0), -1, keepdims=True))
        grad.append(jnp.sum(jnp.where((lane == c) | (lane == 2 + c), tail, 0.0), -1, keepdims=True))
    mean_term = gate[0] * grad[0] + gate[1] * grad[1]
    logit_grad = jnp.zeros((up_ref.shape[1], LANES), F32)
    for c in range(2):
        logit_grad = jnp.where(lane == ids_ref[0, :, c : c + 1], gate[c] * (grad[c] - mean_term), logit_grad)
    logit_grad = logit_grad.astype(BF)
    second_grad = rs_ref[0, :, 0:width].astype(F32) + dot(logit_grad, router_ref[...], 1, 1)
    rg_ref[...] += dot(logit_grad, second_ref[0], 0, 0)
    scaled, spread = norm_parts(mid_ref[0])
    ng_ref[...] += jnp.sum(second_grad * scaled, 0, keepdims=True)
    middle_grad = up_ref[0].astype(F32) + norm_field_back(second_grad, gain_ref[...], scaled, spread)
    mg_ref[0] = middle_grad
    rounded = middle_grad.astype(BF)
    for t in range(wo_ref.shape[0]):
        dmix_ref[t, 0] = dot(rounded, wo_ref[t], 1, 1).astype(BF)
        hog_acc[t] += dot(mixed_ref[t, 0], rounded, 0, 0)

    @pl.when(i == pl.num_programs(0) - 1)
    def _():
        hog_ref[...] = hog_acc[...].astype(BF)


def middle_back(rs, middle, second, gates, ids, up, mixed, head_out, gain, router):
    parts, own, height, cols = mixed.shape
    width = up.shape[2]
    by_part = pl.BlockSpec((parts, 1, height, cols), lambda i: (0, i, 0, 0))
    return pl.pallas_call(
        middle_back_kernel,
        grid=(own,),
        in_specs=[
            image(height, rs.shape[2]),
            image(height, width),
            image(height, width),
            image(height, LANES),
            image(height, 2),
            image(height, width),
            by_part,
            whole(head_out.shape, True),
            whole((1, width)),
            whole(router.shape),
        ],
        out_specs=[image(height, width), by_part, whole(head_out.shape), whole((LANES, width)), whole((1, width))],
        out_shape=[
            jax.ShapeDtypeStruct((own, height, width), F32),
            jax.ShapeDtypeStruct((parts, own, height, cols), BF),
            jax.ShapeDtypeStruct(head_out.shape, BF),
            jax.ShapeDtypeStruct((LANES, width), F32),
            jax.ShapeDtypeStruct((1, width), F32),
        ],
        scratch_shapes=[pltpu.VMEM(head_out.shape, F32)],
        compiler_params=params(),
        name="middle_back",
    )(rs, middle, second, gates, ids, up, mixed, head_out, gain, router)


def input_back_kernel(fg_ref, x_ref, mg_ref, gain_ref, out_ref, ng_ref):
    @pl.when(pl.program_id(0) == 0)
    def _():
        ng_ref[...] = jnp.zeros_like(ng_ref)

    scaled, spread = norm_parts(x_ref[0].astype(F32))
    first_grad = fg_ref[0].astype(F32)
    ng_ref[...] += jnp.sum(first_grad * scaled, 0, keepdims=True)
    out_ref[0] = (mg_ref[0] + norm_field_back(first_grad, gain_ref[...], scaled, spread)).astype(BF)


def input_back(first_grad, x_own, middle_grad, gain):
    own, height, width = x_own.shape
    return pl.pallas_call(
        input_back_kernel,
        grid=(own,),
        in_specs=[image(height, width)] * 3 + [whole((1, width))],
        out_specs=[image(height, width), whole((1, width))],
        out_shape=[
            jax.ShapeDtypeStruct((own, height, width), BF),
            jax.ShapeDtypeStruct((1, width), F32),
        ],
        compiler_params=params(),
        name="input_back",
    )(first_grad, x_own, middle_grad, gain)


def gelu_parts(v):
    x = jnp.abs(v) * 0.7071067811865476
    t = 1.0 / (1.0 + 0.3275911 * x)
    bell = jnp.exp(-x * x)
    poly = ((((1.061405429 * t - 1.453152027) * t + 1.421413741) * t - 0.284496736) * t + 0.254829592) * t
    below = 0.5 * poly * bell
    share = jnp.where(v < 0.0, below, 1.0 - below)
    return v * share, share + v * bell * 0.3989422804014327


def expert_kernel(x_ref, g_ref, router_ref, w1_ref, w2_ref, back_ref, act_ref, hg_ref, rg_ref, dx_ref, gg_ref):
    width = x_ref.shape[1]
    rows = x_ref[...]
    lane = iota(1, LANES, 1)
    side = g_ref[:, width:].astype(F32)

    def column(*lanes):
        keep = lane == lanes[0]
        for other in lanes[1:]:
            keep = keep | (lane == other)
        return jnp.sum(jnp.where(keep, side, 0.0), -1, keepdims=True)

    logits = dot(rows, router_ref[...])
    lane_f = lane.astype(F32)
    mine = jnp.sum(jnp.where(lane_f == column(4), logits, 0.0), -1, keepdims=True)
    other = jnp.sum(jnp.where(lane_f == column(0), logits, 0.0), -1, keepdims=True)
    gate = 1.0 / (1.0 + jnp.exp(other - mine - column(1, 2, 3)))
    upstream = g_ref[:, 0:width].astype(F32)
    rows_grad = (gate * upstream).astype(BF)
    rg_ref[...] = rows_grad
    parts, _, hidden_here = w1_ref.shape
    step = min(512, hidden_here)
    for t in range(parts):
        for at in range(0, hidden_here, step):
            cols = slice(at, at + step)
            place = slice(t * hidden_here + at, t * hidden_here + at + step)
            hidden = dot(rows, w1_ref[t, :, cols])
            active_grad = dot(rows_grad, w2_ref[t, cols, :], 1, 1)
            active, slope = gelu_parts(hidden)
            act_ref[:, place] = active.astype(BF)
            hg_ref[:, place] = (active_grad * slope).astype(BF)
    out = None
    grad = None
    for t in range(parts):
        place = slice(t * hidden_here, (t + 1) * hidden_here)
        part = dot(act_ref[:, place], w2_ref[t])
        out = part if out is None else out + part
        part = dot(hg_ref[:, place], w1_ref[t], 1, 1)
        grad = part if grad is None else grad + part
    dx_ref[...] = grad.astype(BF)
    back_ref[...] = (gate * out).astype(BF)
    gate_grad = jnp.sum(upstream * out.astype(BF).astype(F32), -1, keepdims=True)
    gg_ref[...] = jnp.where(lane == 0, gate_grad, 0.0)


def expert(x, g, router, w1, w2):
    rows, width = x.shape
    total = w1.shape[0] * w1.shape[2]
    tile = next(size for size in (256, 224, 192, 128, 64, 32, 16) if rows % size == 0)

    def tiled(cols):
        return pl.BlockSpec((tile, cols), lambda i: (i, 0))

    flops = 8 * rows * width * total
    return pl.pallas_call(
        expert_kernel,
        grid=(rows // tile,),
        in_specs=[tiled(width), tiled(g.shape[1]), whole(router.shape), whole(w1.shape, True), whole(w2.shape, True)],
        out_specs=[tiled(width), tiled(total), tiled(total), tiled(width), tiled(width), tiled(LANES)],
        out_shape=[
            jax.ShapeDtypeStruct((rows, width), BF),
            jax.ShapeDtypeStruct((rows, total), BF),
            jax.ShapeDtypeStruct((rows, total), BF),
            jax.ShapeDtypeStruct((rows, width), BF),
            jax.ShapeDtypeStruct((rows, width), BF),
            jax.ShapeDtypeStruct((rows, LANES), F32),
        ],
        compiler_params=params(56),
        cost_estimate=pl.CostEstimate(flops=flops, bytes_accessed=rows * total * 6, transcendentals=rows * total * 2),
        name="expert",
    )(x, g, router, w1, w2)


def weight_kernel(count, *refs):
    ins, (out_ref,) = refs[:-1], refs[-1:]
    total = None
    for n in range(count):
        part = dot(ins[2 * n][...], ins[2 * n + 1][...], 0, 0)
        total = part if total is None else total + part
    out_ref[0] = total.astype(BF)


def weight_grad(columns, rows, parts):
    count = len(columns)
    total = columns[0].shape[1]
    width = rows[0].shape[1]
    here = total // parts
    step = min(512, here)
    per = here // step
    specs, args = [], []
    for a, b in zip(columns, rows):
        specs += [pl.BlockSpec((a.shape[0], step), lambda i: (0, i)), whole(b.shape, True)]
        args += [a, b]
    return pl.pallas_call(
        functools.partial(weight_kernel, count),
        grid=(total // step,),
        in_specs=specs,
        out_specs=pl.BlockSpec((1, step, width), lambda i: (i // per, i % per, 0)),
        out_shape=jax.ShapeDtypeStruct((parts, here, width), BF),
        compiler_params=params(),
        cost_estimate=pl.CostEstimate(
            flops=2 * sum(b.shape[0] for b in rows) * width * total, bytes_accessed=4 * total * width, transcendentals=0
        ),
        name="weight_grad",
    )(*args)


def shards(
    block_in,
    norm_one,
    head_in,
    head_out,
    norm_two,
    router,
    expert_in,
    expert_out,
    expert_ids,
    route_noise,
    cotangent,
):
    rows_here, width = block_in.shape
    parts = lax.axis_size("tensor")
    groups = lax.axis_size("expert")
    me = lax.axis_index("tensor")
    images = rows_here // SEQ
    own = -(-images // parts)
    image_slots = own * parts
    height = up_to(SEQ, 16)
    experts = router.shape[1]
    capacity = (rows_here * 2 * 8 // (5 * experts) + 15) // 16 * 16
    share = -(-capacity // parts)
    slots = up_to(share, 16 * CHUNKS) // CHUNKS
    chunk_rows = experts * slots
    full = rows_here // 16 * 16

    def tail_of(x):
        return jnp.pad(x[full:], ((0, 16 - (rows_here - full)), (0, 0)))

    def gathered(x):
        return lax.all_gather(x, "tensor", axis=0, tiled=False)

    def to_images(x, value):
        x = x.reshape(images, SEQ, x.shape[-1])
        return jnp.pad(
            x, ((0, image_slots - images), (0, height - SEQ), (0, 0)), constant_values=value
        )

    def own_images(x):
        pieces = []
        for n in range(own):
            at = jnp.minimum(me * own + n, images - 1) * SEQ
            piece = lax.dynamic_slice(x, (at, 0), (SEQ, x.shape[1]))
            pieces.append(jnp.pad(piece, ((0, height - SEQ), (0, 0))))
        return jnp.stack(pieces)

    def swap(x, axis):
        return lax.all_to_all(x, axis, split_axis=0, concat_axis=0, tiled=True)

    names = jnp.arange(experts, dtype=jnp.int32)
    member = [(expert_ids[:, c : c + 1] == names).astype(jnp.int32) for c in range(2)]
    both = member[0] + member[1]
    earlier = jnp.cumsum(both, 0) - both
    slot = jnp.stack([jnp.sum(earlier * item, -1) for item in member], 1)
    local = slot - me * share
    chunk = local // slots
    place = chunk * chunk_rows + expert_ids * slots + local % slots
    place = jnp.where((local >= 0) & (local < share), place, -1)
    place_flat = jnp.pad(place.T, ((0, 0), (0, full + 16 - rows_here)), constant_values=-1)
    place_images = to_images(place, -1)
    place_lanes = place_images.reshape(image_slots * height, 2).T
    ids_images = to_images(expert_ids, -1)
    noise_images = to_images(route_noise, 0.0)
    ids_own = lax.dynamic_slice_in_dim(ids_images, me * own, own, 0)
    noise_own = lax.dynamic_slice_in_dim(noise_images, me * own, own, 0)

    sides = []
    for c in range(2):
        gap = route_noise[:, c] - route_noise[:, 1 - c]
        high = gap.astype(BF)
        left = gap - high.astype(F32)
        mid = left.astype(BF)
        low = (left - mid.astype(F32)).astype(BF)
        columns = [expert_ids[:, 1 - c].astype(BF), high, mid, low, expert_ids[:, c].astype(BF)]
        sides.append(jnp.stack(columns, 1))
    side = jnp.pad(jnp.stack(sides), ((0, 0), (0, full + 16 - rows_here), (0, LANES - 5)))

    router_wide = jnp.pad(router, ((0, 0), (0, LANES - experts)))
    gain_one, gain_two = norm_one[None, :], norm_two[None, :]
    head_out_all = gathered(head_out)
    w1 = gathered(expert_in[0])

    tail = tail_of(cotangent)
    signals = [
        swap(pack_first(cotangent, tail, place_flat, side, experts, slots, n * chunk_rows), "expert")
        for n in range(CHUNKS)
    ]

    mixed, first_in, qkv, logs = attend(
        block_in, tail_of(block_in), gain_one, head_in, images, image_slots, height
    )
    mixed_rows = swap(mixed, "tensor").reshape(parts, own, height, mixed.shape[2])
    x_own = own_images(block_in)
    valid = (me * own + jnp.arange(own) < images)[:, None, None]
    up_own = jnp.where(valid, own_images(cotangent), 0)
    middle, second_in, gates = middle_of(
        mixed_rows, head_out_all, x_own, gain_two, router_wide, ids_own, noise_own
    )
    second_all = gathered(second_in).reshape(image_slots * height, width)
    second_all, late_out = lax.optimization_barrier((second_all, expert_out[0]))
    w2 = gathered(late_out)

    backs, actives, hidden_grads, rows_grads, arrived, returned, gate_grads = [], [], [], [], [], [], []
    for n in range(CHUNKS):
        x = swap(pack(second_all, place_lanes, experts, slots, n * chunk_rows), "expert")
        x = x.reshape(groups * slots, width)
        signal = signals[n].reshape(groups * slots, width + LANES)
        back, active, hidden_grad, rows_grad, row_grad, gate_grad = expert(x, signal, router_wide, w1, w2)
        arrived.append(x)
        actives.append(active)
        hidden_grads.append(hidden_grad)
        rows_grads.append(rows_grad)
        backs.append(back)
        returned.append(swap(row_grad.reshape(experts, slots, width), "expert").reshape(chunk_rows, width))
        gate_grads.append(swap(gate_grad[:, 0].reshape(experts, slots), "expert").reshape(1, chunk_rows))

    out_grad = lax.psum_scatter(weight_grad(actives, rows_grads, parts), "tensor", scatter_dimension=0)
    in_grad_parts = weight_grad(hidden_grads, arrived, parts)

    second_sum = lax.psum_scatter(
        unpack(place_images, returned, gate_grads), "tensor", scatter_dimension=0, tiled=True
    )
    middle_grad, mixed_grad, head_out_part, router_part, norm_two_part = middle_back(
        second_sum, middle, second_in, gates, ids_own, up_own, mixed_rows, head_out_all, gain_two, router_wide
    )
    mixed_grad = swap(mixed_grad.reshape(image_slots, height, mixed.shape[2]), "tensor")
    in_grad_parts, mixed_grad = lax.optimization_barrier((in_grad_parts, mixed_grad))
    in_grad = lax.psum_scatter(in_grad_parts, "tensor", scatter_dimension=0)
    mixed_grad, *backs = lax.optimization_barrier((mixed_grad, *backs))
    combined = [swap(item.reshape(experts, slots, width), "expert").reshape(chunk_rows, width) for item in backs]
    first_part, head_in_part = attend_back(mixed_grad, qkv, logs, first_in, head_in)
    first_grad = lax.psum_scatter(first_part, "tensor", scatter_dimension=0, tiled=True)
    input_part, norm_one_part = input_back(first_grad, x_own, middle_grad, gain_one)

    def to_rows(x):
        return x[:images, :SEQ].reshape(rows_here, width)

    input_grad = to_rows(gathered(input_part).reshape(image_slots, height, width)).astype(F32)
    out_sum = lax.psum_scatter(unpack(place_images, combined), "tensor", scatter_dimension=0, tiled=True)
    block_own = (middle + out_sum.astype(F32)).astype(BF)
    block_out = to_rows(gathered(block_own).reshape(image_slots, height, width))

    head_in_grad = lax.psum(head_in_part, "expert").astype(F32)
    head_out_grad = lax.psum(lax.psum_scatter(head_out_part, "tensor", scatter_dimension=0), "expert").astype(F32)
    small = lax.psum(
        jnp.concatenate([norm_one_part, norm_two_part, router_part[:experts]], 0), ("expert", "tensor")
    )
    return (
        block_out,
        input_grad,
        small[0],
        head_in_grad,
        head_out_grad,
        small[1],
        small[2:].T,
        in_grad.astype(F32).T[None],
        out_grad.astype(F32)[None],
    )


def solution(mesh):
    in_specs = (
        P("expert", None),
        P(),
        P(None, None, "tensor"),
        P("tensor", None),
        P(),
        P(),
        P("expert", None, "tensor"),
        P("expert", "tensor", None),
        P("expert", None),
        P("expert", None),
        P("expert", None),
    )
    out_specs = (
        P("expert", None),
        P("expert", None),
        P(),
        P(None, None, "tensor"),
        P("tensor", None),
        P(),
        P(),
        P("expert", None, "tensor"),
        P("expert", "tensor", None),
    )
    return jax.shard_map(shards, mesh=mesh, in_specs=in_specs, out_specs=out_specs, check_vma=False)
```

time: 1860 us -> 1130 us (0.61)
  matrix products: 382 us -> 0 us
  Pallas kernels: 0 us -> 275 us
  waiting for transfers between devices: 779 us -> 576 us
  local copies, waits for them, and re-layouts: 264 us -> 64.4 us
  other arithmetic: 189 us -> 29.3 us
  blocking collectives: 208 us -> 139 us
    dot_general x21 -> x0, matrix products: 382 us -> none  [the longest x1 82.5 us: shards(): jnp.einsum('sjcd,jfd->sjcf', owner_grad, expert_out, preferred_element_ty...]
    pallas_call x0 -> x12, Pallas kernels: none -> 275 us  [the longest x1 85.5 us: expert(): pl.pallas_call(expert_kernel, grid=(rows // tile,), in_specs=[tiled(width...]
    psum x3 -> x1, waiting for transfers between devices: 306 us -> 101 us  [shards(): head_in_grad = lax.psum(head_in_part, 'expert').astype(F32)]
    all_to_all x2 -> x5, waiting for transfers between devices: 441 us -> 240 us  [swap(): return lax.all_to_all(x, axis, split_axis=0, concat_axis=0, tiled=True)]
    reduce_scatter x2 -> x6, waiting for transfers between devices: 24.6 us -> 170 us  [the longest x1 70.7 us: shards(): lax.psum_scatter(weight_grad(actives, rows_grads, parts), 'tensor', scatt...]
    reduce_sum x13 -> x1, other arithmetic: 93.2 us -> 0.06 us  [shards(): slot = jnp.stack([jnp.sum(earlier * item, -1) for item in member], 1)]
    all_to_all x2, blocking collectives: 171 us -> 97.9 us  [swap(): return lax.all_to_all(x, axis, split_axis=0, concat_axis=0, tiled=True)]
    all_gather x2 -> x6, waiting for transfers between devices: 7.42 us -> 62.1 us  [gathered(): return lax.all_gather(x, 'tensor', axis=0, tiled=False)]
  transfers between devices with their start and end apart: 9 -> 18, of which waited for: 7 -> 12; matrix products, arithmetic and copies ran while one was open for 27% -> 5% of each run, Pallas kernels for 0% -> 13%
where the time goes in v1:
time: 1130 us; the launch traced here: 1120 us
  waiting for transfers between devices  576 us (51%)
  Pallas kernels  275 us (24%)
  blocking collectives  139 us (12%)
  local copies, waits for them, and re-layouts  64.4 us (6%)
  other arithmetic  29.3 us (3%)
  starting transfers between devices  25.6 us (2%)
  between operations  14.8 us (1%)
    all_to_all x5, waiting for transfers between devices, swap(): return lax.all_to_all(x, axis, split_axis=0, concat_axis=0, tiled=True)  240 us
    psum x1, waiting for transfers between devices, shards(): head_in_grad = lax.psum(head_in_part, 'expert').astype(F32)  101 us
    all_to_all x2, blocking collectives, swap(): return lax.all_to_all(x, axis, split_axis=0, concat_axis=0, tiled=True)  97.9 us
    pallas_call x1, Pallas kernels, expert(): pl.pallas_call(expert_kernel, grid=(rows // tile,), in_specs=[tiled(width...  85.5 us
    reduce_scatter x1, waiting for transfers between devices, shards(): lax.psum_scatter(weight_grad(actives, rows_grads, parts), 'tensor', scatt...  70.7 us
    all_gather x6, waiting for transfers between devices, gathered(): return lax.all_gather(x, 'tensor', axis=0, tiled=False)  62.1 us
    reduce_scatter x1, waiting for transfers between devices, shards(): lax.psum_scatter(unpack(place_images, returned, gate_grads), 'tensor', sc...  50 us
    psum x1, blocking collectives, shards(): lax.psum(jnp.concatenate([norm_one_part, norm_two_part, router_part[:expe...  40.7 us
  transfers between devices with their start and end apart: 18, of which 12 were waited for; matrix products, arithmetic and copies ran while one was open for 5% of the time, Pallas kernels for 13%

profile of v1, /device:TPU:0, one launch (start us, length us, event | category | flops | bytes accessed | tf_op | source)
XLA Modules:
  0.0 1123.7 jit_solution(11975616859354104406)
XLA Ops:
  8.6 1.4 copy-done.3
  10.7 28.2 %attend.1 = (bf16[12,208,256]{2,1,0:T(8,128)(2,1)S(1)}, bf16[12,208,1024]{2,1,0:T(8,128)(2,1)}, bf16[3,12,208,256]{3,2,1,0:T(8,128)(2,1)}, f32[12,208,128]{2,1,0:T(8,128)S(1)}) custom-call(bf16[2167,1024]{1,0:T(8,128)(2,1)} %x_ref.2, bf16[16,1024]{1,0:T(8,128)(2,1)S(1)} %pad.52.tail_ref, f32[1,1024]{1,0:T(1,128)S(1)} %bitcast.69, ...), custom_call_target="tpu_custom_call" | custom-call | tf_op jit(solution)/shard_map/attend/pallas_call | solution.py:122
  41.0 4.3 all-to-all-start
  45.9 1.4 copy.58
  47.6 1.3 copy-done.23
  49.0 1.6 constant_dynamic-slice_fusion.5
  50.8 11.4 %all-to-all-done = bf16[12,208,256]{2,1,0:T(8,128)(2,1)S(1)} async-done(((bf16[12,208,256]{2,1,0:T(8,128)(2,1)}), bf16[12,208,256]{2,1,0:T(8,128)(2,1)S(1)}, u32[]{:S(2)}, u32[]{:S(2)}) %all-to-all-start) | async-done | bytes 1277984 | tf_op jit(solution)/shard_map/all_to_all | solution.py:624
  62.2 7.2 middle.1
  72.1 2.3 reduce-window.6
  75.2 1.1 copy.62
  76.4 1.1 copy.63
  77.6 1.7 fusion.5.side_ref
  79.3 17.4 %pack_cotangent.1 = bf16[8,224,1152]{2,1,0:T(8,128)(2,1)S(1)} custom-call(bf16[2167,1024]{1,0:T(8,128)(2,1)} %x_ref.3, bf16[16,1024]{1,0:T(8,128)(2,1)S(1)} %pad.61.tail_ref, s32[2,2176]{1,0:T(2,128)S(1)} %pad.62.lp_ref, bf16[2,2176,128]{2,1,0:T(8,128)(2,1)S(1)} %fusion.5.side_ref), custom_call_target="tpu_custom_call" | custom-call | tf_op jit(solution)/shard_map/pack_cotangent/pallas_call | solution.py:235
  96.7 2.0 copy-done
  98.7 6.9 all-to-all-start.2
  105.6 6.5 all-gather.16.cloned.1.call-done
  112.4 1.4 copy.60
  113.8 1.3 pad.60.lp_ref
  115.5 13.4 %pack_rows.1 = bf16[8,224,1024]{2,1,0:T(8,128)(2,1)S(1)} custom-call(bf16[2496,1024]{1,0:T(8,128)(2,1)} %bitcast.73, s32[2,2496]{1,0:T(2,128)S(1)} %bitcast.66), custom_call_target="tpu_custom_call" | custom-call | tf_op jit(solution)/shard_map/pack_rows/pallas_call | solution.py:255
  128.9 1.8 copy-done.1
  130.7 66.4 %all-to-all-done.2 = bf16[8,224,1152]{2,1,0:T(8,128)(2,1)} async-done(((bf16[8,224,1152]{2,1,0:T(8,128)(2,1)}), bf16[8,224,1152]{2,1,0:T(8,128)(2,1)}, u32[]{:S(2)}, u32[]{:S(2)}) %all-to-all-start.2) | async-done | bytes 4128800 | tf_op jit(solution)/shard_map/all_to_all | solution.py:624
  197.1 4.7 all-to-all-start.1
  201.8 81.3 %all-to-all-done.1 = bf16[8,224,1024]{2,1,0:T(8,128)(2,1)} async-done(((bf16[8,224,1024]{2,1,0:T(8,128)(2,1)}), bf16[8,224,1024]{2,1,0:T(8,128)(2,1)}, u32[]{:S(2)}, u32[]{:S(2)}) %all-to-all-start.1) | async-done | bytes 3670048 | tf_op jit(solution)/shard_map/all_to_all | solution.py:624
  283.1 85.5 %expert.1 = (bf16[1792,1024]{1,0:T(8,128)(2,1)}, bf16[1792,4096]{1,0:T(8,128)(2,1)}, bf16[1792,4096]{1,0:T(8,128)(2,1)}, bf16[1792,1024]{1,0:T(8,128)(2,1)}, bf1...) custom-call(bf16[1792,1024]{1,0:T(8,128)(2,1)} %bitcast.13.x_ref.refs_1_, bf16[1792,1152]{1,0:T(8,128)(2,1)} %bitcast.17.g_ref, ...), custom_call_target="tpu_custom_call" | custom-call | flops 60129542144 | bytes 44040192 | tf_op jit(solution)/shard_map/expert/pallas_call | solution.py:522
  368.6 1.5 slice_reduce_fusion
  370.2 9.9 all_to_all.40
  380.2 4.5 all-to-all-start.3
  385.0 80.6 %all-to-all-done.3 = bf16[8,224,1024]{2,1,0:T(8,128)(2,1)} async-done(((bf16[8,224,1024]{2,1,0:T(8,128)(2,1)}), bf16[8,224,1024]{2,1,0:T(8,128)(2,1)}, u32[]{:S(2)}, u32[]{:S(2)}) %all-to-all-start.3) | async-done | bytes 3670048 | tf_op jit(solution)/shard_map/all_to_all | solution.py:624
  465.6 21.0 %unpack_rows.2 = bf16[12,208,1152]{2,1,0:T(8,128)(2,1)} custom-call(s32[12,208,2]{2,1,0:T(8,128)S(1)} %pad.60.lp_ref, bf16[1792,1024]{1,0:T(8,128)(2,1)} %bitcast.20.refs_0_, f32[1,1792]{1,0:T(1,128)S(1)} %reshape.105.refs_1_), custom_call_target="tpu_custom_call" | custom-call | tf_op jit(solution)/shard_map/unpack_rows/pallas_call | solution.py:297
  486.7 1.6 constant_dynamic-slice_fusion.2
  488.5 1.3 maximum_select_fusion.up_ref
  489.7 50.0 %reduce-scatter.7.cloned.1.call-done.rs_ref = bf16[3,208,1152]{2,1,0:T(8,128)(2,1)} async-done(((bf16[12,208,1152]{2,1,0:T(8,128)(2,1)}), bf16[3,208,1152]{2,1,0:T(8,128)(2,1)}) %reduce-scatter.7.cloned.1.call-update) | async-done | bytes 1437712 | tf_op jit(solution)/shard_map/reduce_scatter | solution.py:696
  539.7 1.3 copy-done.6
  541.0 1.3 copy-done.7
  542.3 11.3 %middle_back.1 = (f32[3,208,1024]{2,1,0:T(8,128)}, bf16[4,3,208,256]{3,2,1,0:T(8,128)(2,1)S(1)}, bf16[4,256,1024]{2,1,0:T(8,128)(2,1)}, f32[128,1024]{1,0:T(8,128)S(1)}, f32[1,1024]{1,0:T(1,128)S(1)}) custom-call(bf16[3,208,1152]{2,1,0:T(8,128)(2,1)} %reduce-scatter.7.cloned.1.call-done.rs_ref, f32[3,208,1024]{2,1,0:T(8,128)} %get-tuple-element.38.mid_ref, ...), custom_call_target="tpu_custom_call" | custom-call | tf_op jit(solution)/shard_map/middle_back/pallas_call | solution.py:402
  553.6 1.1 copy-done.14
  555.5 4.3 all-to-all-start.5
  559.9 20.9 %weight_grad.2 = bf16[4,1024,1024]{2,1,0:T(8,128)(2,1)} custom-call(bf16[1792,4096]{1,0:T(8,128)(2,1)} %get-tuple-element.42.refs_0_, bf16[1792,1024]{1,0:T(8,128)(2,1)} %bitcast.13.x_ref.refs_1_), custom_call_target="tpu_custom_call" | custom-call | flops 15032385536 | bytes 16777216 | tf_op jit(solution)/shard_map/weight_grad/pallas_call | solution.py:561
  580.8 1.4 copy-done.4
  582.2 1.3 copy-done.11
  583.5 33.9 %attend_back.1 = (bf16[12,208,1024]{2,1,0:T(8,128)(2,1)}, bf16[3,1024,256]{2,1,0:T(8,128)(2,1)}) custom-call(bf16[12,208,256]{2,1,0:T(8,128)(2,1)} %all-to-all-done.5.dmix_ref, bf16[3,12,208,256]{3,2,1,0:T(8,128)(2,1)} %get-tuple-element.51.qkv_ref, f32[12,208,128]{2,1,0:T(8,128)S(1)} %copy-done.11, bf16[12,208,1024]{2,1,0:T(8,128)(2,1)} %get-tuple-element.53.first_ref, ...), custom_call_target="tpu_custom_call" | custom-call | tf_op jit(solution)/shard_map/attend_back/pallas_call | solution.py:195
  617.4 88.0 %all_to_all.41 = bf16[8,224,1024]{2,1,0:T(8,128)(2,1)S(1)} all-to-all(bf16[8,224,1024]{2,1,0:T(8,128)(2,1)} %bitcast.74), channel_id=1, replica_groups=mesh['expert'=8,'tensor'=4] {'expert'}, dimensions={0} | all-to-all | bytes 7340032 | tf_op jit(solution)/shard_map/all_to_all | solution.py:624
  705.4 13.0 %unpack_rows.3 = bf16[12,208,1024]{2,1,0:T(8,128)(2,1)} custom-call(s32[12,208,2]{2,1,0:T(8,128)S(1)} %pad.60.lp_ref, bf16[1792,1024]{1,0:T(8,128)(2,1)S(1)} %bitcast.62), custom_call_target="tpu_custom_call" | custom-call | tf_op jit(solution)/shard_map/unpack_rows/pallas_call | solution.py:297
  718.5 2.0 copy-done.22
  720.5 19.6 %weight_grad.3 = bf16[4,1024,1024]{2,1,0:T(8,128)(2,1)} custom-call(bf16[1792,4096]{1,0:T(8,128)(2,1)} %get-tuple-element.63.refs_0_, bf16[1792,1024]{1,0:T(8,128)(2,1)S(1)} %copy-done.22), custom_call_target="tpu_custom_call" | custom-call | flops 15032385536 | bytes 16777216 | tf_op jit(solution)/shard_map/weight_grad/pallas_call | solution.py:561
  741.8 1.3 copy-done.15
  743.1 3.7 input_back.1
  747.9 20.4 %reduce-scatter.9.cloned.1.call-done = bf16[3,208,1024]{2,1,0:T(8,128)(2,1)} async-done(((bf16[12,208,1024]{2,1,0:T(8,128)(2,1)}), bf16[3,208,1024]{2,1,0:T(8,128)(2,1)}) %reduce-scatter.9.cloned.1.call-update) | async-done | bytes 1277968 | tf_op jit(solution)/shard_map/reduce_scatter | solution.py:715
  768.3 3.6 add_convert_fusion
  772.0 70.7 %reduce-scatter.17.cloned.1.call-done = bf16[1,1024,1024]{2,1,0:T(8,128)(2,1)} async-done(((bf16[4,1024,1024]{2,1,0:T(8,128)(2,1)}), bf16[1,1024,1024]{2,1,0:T(8,128)(2,1)}) %reduce-scatter.17.cloned.1.call-update) | async-done | bytes 2097168 | tf_op jit(solution)/shard_map/reduce_scatter | solution.py:693
  842.7 4.1 convert_element_type.135
  847.5 101.4 %all-reduce.18.cloned.1.call-done = (bf16[3,1024,256]{2,1,0:T(8,128)(2,1)}, bf16[256,1024]{1,0:T(8,128)(2,1)}) async-done(((bf16[3,1024,256]{2,1,0:T(8,128)(2,1)}, bf16[256,1024]{1,0:T(8,128)(2,1)}), (bf16[3,1024,256]{2,1,0:T(8,128)(2,1)}, bf16[256,1024]{1,0:T(8,128)(2,1)})) %all-reduce.18.cloned.1.call-update) | async-done | bytes 2097168 | tf_op jit(solution)/shard_map/psum | solution.py:719
  948.9 3.4 convert_element_type.132
  952.3 1.1 convert_element_type.133
  953.4 40.7 %psum.21 = f32[10,1024]{1,0:T(8,128)S(1)} all-reduce(f32[10,1024]{1,0:T(8,128)S(1)} %pad_maximum_fusion.1), channel_id=1, replica_groups=mesh['expert'=8,'tensor'=4] {'expert','tensor'}, use_global_device_ids=true, to_apply=%region_7.8 | all-reduce | flops 10240 | bytes 81920 | tf_op jit(solution)/shard_map/psum | solution.py:721
  995.3 29.2 %reduce-scatter.15.cloned.1.call-done = bf16[1,1024,1024]{2,1,0:T(8,128)(2,1)} async-done(((bf16[4,1024,1024]{2,1,0:T(8,128)(2,1)}), bf16[1,1024,1024]{2,1,0:T(8,128)(2,1)}) %reduce-scatter.15.cloned.1.call-update) | async-done | bytes 2097168 | tf_op jit(solution)/shard_map/reduce_scatter | solution.py:704
  1024.5 4.1 convert_bitcast_fusion
  1028.5 5.4 copy.65
  1033.9 31.7 %all-gather.22.cloned.1.call-done = bf16[12,208,1024]{2,1,0:T(8,128)(2,1)} async-done(((bf16[3,208,1024]{2,1,0:T(8,128)(2,1)}), bf16[12,208,1024]{2,1,0:T(8,128)(2,1)}) %all-gather.22.cloned.1.call-update) | async-done | bytes 5111824 | tf_op jit(solution)/shard_map/all_gather | solution.py:607
  1065.6 6.9 slice_convert_fusion
  1072.6 10.5 reshape.112
  1083.0 23.9 %all-gather.20.cloned.1.call-done = bf16[12,208,1024]{2,1,0:T(8,128)(2,1)} async-done(((bf16[3,208,1024]{2,1,0:T(8,128)(2,1)}), bf16[12,208,1024]{2,1,0:T(8,128)(2,1)}) %all-gather.20.cloned.1.call-update) | async-done | bytes 5111824 | tf_op jit(solution)/shard_map/all_gather | solution.py:607
  1106.9 4.8 slice.72
  1111.7 5.0 reshape.110
  (122 shorter events, 16.0 us)
Async XLA Ops:
  7.2 55.1 %all-gather.14.cloned.1.call-start = ((), (), s32[]{:S(2)}) async-start(), calls=%async_computation.20 | async-start | bytes 2621440 | tf_op jit(solution)/shard_map/all_gather | solution.py:607
  8.6 1.4 copy-start.3
  10.0 0.7 copy-start.19
  38.9 1.0 copy-start.10
  39.9 1.0 copy-start.12
  41.0 4.3 copy-start.25
  41.0 4.8 copy-start.26
  41.0 6.4 copy-start.27
  41.0 21.3 %all-to-all-start = ((bf16[12,208,256]{2,1,0:T(8,128)(2,1)}), bf16[12,208,256]{2,1,0:T(8,128)(2,1)S(1)}, u32[]{:S(2)}, u32[]{:S(2)}) async-start(bf16[12,208,256]{2,1,0:T(8,128)(2,1)} %copy-done.12), calls=%async_computation | async-start | bytes 2555904 | tf_op jit(solution)/shard_map/all_to_all | solution.py:624
  45.3 66.8 %all-gather.16.cloned.1.call-start = ((), (), s32[]{:S(2)}) async-start(), calls=%async_computation.21 | async-start | bytes 6389760 | tf_op jit(solution)/shard_map/all_gather | solution.py:607
  47.6 14.7 %copy-start.8 = (bf16[1024,128]{1,0:T(8,128)(2,1)}, bf16[1024,128]{1,0:T(8,128)(2,1)S(1)}, u32[]{:S(2)}) copy-start(bf16[1024,128]{1,0:T(8,128)(2,1)S(1)} %pad.56.router_ref) | copy-start | bytes 786436
  47.6 1.3 copy-start.23
  50.6 11.6 %copy-start.18 = (f32[1024]{0:T(1024)S(1)}, f32[1024]{0:T(1024)}, u32[]{:S(2)}) copy-start(f32[1024]{0:T(1024)} %param.15) | copy-start | bytes 12292
  62.2 7.2 copy-start.2
  69.4 1.1 copy-start.5
  70.5 0.7 copy-start.16
  71.2 6.3 slice-start
  71.2 130.6 %all-gather.12.cloned.1.call-start = ((), (), s32[]{:S(2)}) async-start(), calls=%async_computation.13 | async-start | bytes 10485760 | tf_op jit(solution)/shard_map/all_gather | solution.py:607
  96.7 2.0 copy-start
  98.7 98.4 %all-to-all-start.2 = ((bf16[8,224,1152]{2,1,0:T(8,128)(2,1)}), bf16[8,224,1152]{2,1,0:T(8,128)(2,1)}, u32[]{:S(2)}, u32[]{:S(2)}) async-start(bf16[8,224,1152]{2,1,0:T(8,128)(2,1)} %copy-done), calls=%async_computation.2 | async-start | bytes 8257536 | tf_op jit(solution)/shard_map/all_to_all | solution.py:624
  105.6 177.5 %all-gather.18.cloned.1.call-start = ((), (), s32[]{:S(2)}) async-start(), calls=%async_computation.22 | async-start | bytes 10485760 | tf_op jit(solution)/shard_map/all_gather | solution.py:607
  128.9 1.8 copy-start.1
  197.1 86.0 %all-to-all-start.1 = ((bf16[8,224,1024]{2,1,0:T(8,128)(2,1)}), bf16[8,224,1024]{2,1,0:T(8,128)(2,1)}, u32[]{:S(2)}, u32[]{:S(2)}) async-start(bf16[8,224,1024]{2,1,0:T(8,128)(2,1)} %copy-done.1), calls=%async_computation.1 | async-start | bytes 7340032 | tf_op jit(solution)/shard_map/all_to_all | solution.py:624
  380.2 85.5 %all-to-all-start.3 = ((bf16[8,224,1024]{2,1,0:T(8,128)(2,1)}), bf16[8,224,1024]{2,1,0:T(8,128)(2,1)}, u32[]{:S(2)}, u32[]{:S(2)}) async-start(bf16[8,224,1024]{2,1,0:T(8,128)(2,1)} %bitcast.75), calls=%async_computation.3 | async-start | bytes 7340032 | tf_op jit(solution)/shard_map/all_to_all | solution.py:624
  384.7 155.0 %reduce-scatter.7.cloned.1.call-start = ((), (), s32[]{:S(2)}) async-start(), calls=%async_computation.14 | async-start | bytes 7188480 | tf_op jit(solution)/shard_map/reduce_scatter | solution.py:696
  486.7 253.5 %reduce-scatter.13.cloned.1.call-start = ((), (), s32[]{:S(2)}) async-start(), calls=%async_computation.17 | async-start | bytes 2621440 | tf_op jit(solution)/shard_map/reduce_scatter | solution.py:720
  488.4 51.3 %copy-start.9 = (bf16[1024,128]{1,0:T(8,128)(2,1)S(1)}, bf16[1024,128]{1,0:T(8,128)(2,1)}, u32[]{:S(2)}) copy-start(bf16[1024,128]{1,0:T(8,128)(2,1)} %copy-done.8) | copy-start | bytes 786436
  488.4 51.3 %copy-start.17 = (f32[3,208,128]{2,1,0:T(8,128)S(1)}, f32[3,208,128]{2,1,0:T(8,128)}, u32[]{:S(2)}) copy-start(f32[3,208,128]{2,1,0:T(8,128)} %copy-done.16) | copy-start | bytes 958468
  539.7 1.3 copy-start.6
  541.0 1.3 copy-start.7
  553.6 1.1 copy-start.14
  554.7 0.8 copy-start.21
  555.5 25.2 %all-to-all-start.5 = ((bf16[12,208,256]{2,1,0:T(8,128)(2,1)}), bf16[12,208,256]{2,1,0:T(8,128)(2,1)}, u32[]{:S(2)}, u32[]{:S(2)}) async-start(bf16[12,208,256]{2,1,0:T(8,128)(2,1)} %bitcast.65), calls=%async_computation.6 | async-start | bytes 2555904 | tf_op jit(solution)/shard_map/all_to_all | solution.py:624
  559.9 181.9 %reduce-scatter.11.cloned.1.call-start = ((), (), s32[]{:S(2)}) async-start(), calls=%async_computation.16 | async-start | bytes 6389760 | tf_op jit(solution)/shard_map/reduce_scatter | solution.py:708
  580.8 1.4 copy-start.4
  582.2 1.3 copy-start.11
  617.4 151.0 %reduce-scatter.9.cloned.1.call-start = ((), (), s32[]{:S(2)}) async-start(), calls=%async_computation.15 | async-start | bytes 6389760 | tf_op jit(solution)/shard_map/reduce_scatter | solution.py:715
  718.4 124.3 %reduce-scatter.17.cloned.1.call-start = ((), (), s32[]{:S(2)}) async-start(), calls=%async_computation.19 | async-start | bytes 10485760 | tf_op jit(solution)/shard_map/reduce_scatter | solution.py:693
  718.5 2.0 copy-start.22
  740.1 208.8 %all-reduce.18.cloned.1.call-start = ((), (), s32[]{:S(2)}) async-start(), calls=%async_computation.25 | async-start | bytes 4194304 | tf_op jit(solution)/shard_map/psum | solution.py:719
  740.7 1.1 copy-start.20
  740.7 283.7 %reduce-scatter.15.cloned.1.call-start = ((), (), s32[]{:S(2)}) async-start(), calls=%async_computation.18 | async-start | bytes 10485760 | tf_op jit(solution)/shard_map/reduce_scatter | solution.py:704
  741.5 324.1 %all-gather.22.cloned.1.call-start = ((), (), s32[]{:S(2)}) async-start(), calls=%async_computation.24 | async-start | bytes 6389760 | tf_op jit(solution)/shard_map/all_gather | solution.py:607
  741.8 1.3 copy-start.15
  746.8 1.1 copy-start.13
  747.9 359.0 %all-gather.20.cloned.1.call-start = ((), (), s32[]{:S(2)}) async-start(), calls=%async_computation.23 | async-start | bytes 6389760 | tf_op jit(solution)/shard_map/all_gather | solution.py:607
  948.9 3.4 copy-start.24
Sparse Core Ops, SparseCore 0:
  9.6 25.3 all-gather.13
  71.3 40.7 all-gather.15
  113.7 58.2 all-gather.11
  173.4 58.2 all-gather.17
  486.8 52.8 reduce-scatter.6
  555.7 33.3 reduce-scatter.12
  617.5 51.8 reduce-scatter.10
  718.5 49.7 reduce-scatter.8
  770.9 71.7 reduce-scatter.16
  846.6 102.2 all-reduce.17
  952.2 72.2 reduce-scatter.14
  1025.9 39.6 all-gather.21
  1067.2 39.6 all-gather.19

commit v2 on v1

v2 whole, which is shorter than its diff:
```python
import functools

import jax
import jax.numpy as jnp
from jax import lax
from jax.experimental import pallas as pl
from jax.experimental.pallas import tpu as pltpu
from jax.sharding import PartitionSpec as P

HD = 64
SEQ = 197
LANES = 128
EPSILON = 1e-06
CHUNKS = 2
BF = jnp.bfloat16
F32 = jnp.float32


def up_to(value, unit):
    return -(-value // unit) * unit


def params(mib=48):
    return pltpu.CompilerParams(vmem_limit_bytes=mib * 1024 * 1024)


def dot(a, b, da=1, db=0):
    return lax.dot_general(a, b, (((da,), (db,)), ((), ())), preferred_element_type=F32)


def iota(rows, cols, dim):
    return lax.broadcasted_iota(jnp.int32, (rows, cols), dim)


def flag(mask):
    return jnp.where(mask, 1.0, 0.0)


def whole(shape, once=False):
    zeros = (0,) * len(shape)
    mode = pl.Buffered(1) if once else None
    return pl.BlockSpec(shape, lambda *_: zeros, pipeline_mode=mode)


def image(*shape):
    return pl.BlockSpec((1,) + shape, lambda i, *_: (i,) + (0,) * len(shape))


def fill(x_ref, tail_ref, rows_ref):
    full = x_ref.shape[0] // 16 * 16
    rows_ref[0:full, :] = x_ref[0:full, :]
    rows_ref[full : full + 16, :] = tail_ref[...]
    rest = rows_ref.shape[0] - full - 16
    if rest:
        rows_ref[full + 16 :, :] = jnp.zeros((rest, rows_ref.shape[1]), BF)


def norm_parts(field):
    centre = field - jnp.mean(field, -1, keepdims=True)
    spread = lax.rsqrt(jnp.mean(centre * centre, -1, keepdims=True) + EPSILON)
    return centre * spread, spread


def norm_field_back(upstream, gain, scaled, spread):
    weighted = upstream * gain
    return spread * (
        weighted
        - jnp.mean(weighted, -1, keepdims=True)
        - scaled * jnp.mean(weighted * scaled, -1, keepdims=True)
    )


def cost(flops, size):
    return pl.CostEstimate(flops=flops, bytes_accessed=size, transcendentals=0)


def halves(steps, tail, dtype):
    half = steps // 2
    shape = jax.ShapeDtypeStruct((half,) + tail, dtype)
    zeros = (0,) * len(tail)
    specs = [
        pl.BlockSpec((1,) + tail, lambda i, *_: (jnp.minimum(i, half - 1),) + zeros),
        pl.BlockSpec((1,) + tail, lambda i, *_: (jnp.maximum(i - half, 0),) + zeros),
    ]
    return specs, [shape, shape]


def store_half(low_ref, high_ref, value):
    early = pl.program_id(0) < pl.num_programs(0) // 2

    @pl.when(early)
    def _():
        low_ref[0] = value

    @pl.when(jnp.logical_not(early))
    def _():
        high_ref[0] = value


def head_masks():
    lane = iota(1, LANES, 1)
    return [(flag(lane // HD == h)).astype(BF) for h in range(2)]


def attend_kernel(images, order_ref, x_ref, tail_ref, gain_ref, w_ref, mixed_ref, first_ref, qkv_ref, log_ref, rows):
    @pl.when(pl.program_id(0) == 0)
    def _():
        fill(x_ref, tail_ref, rows)

    i = order_ref[pl.program_id(0)]
    height = first_ref.shape[1]
    window = height + 16
    start = jnp.minimum(i, images - 1) * SEQ
    aligned = start // 16 * 16
    r, c = iota(height, window, 0), iota(height, window, 1)
    limit = jnp.where(i < images, SEQ, 0)
    shift = flag((c == r + (start - aligned)) & (r < limit)).astype(BF)
    field = dot(shift, rows[pl.ds(pl.multiple_of(aligned, 16), window), :])
    scaled, _ = norm_parts(field)
    first = (scaled * gain_ref[...]).astype(BF)
    first_ref[0] = first
    for k in range(3):
        qkv_ref[k, 0] = dot(first, w_ref[k]).astype(BF)
    masks = head_masks()
    lane = iota(1, LANES, 1)
    key_lane = iota(1, height, 1)
    logs = jnp.zeros((height, LANES), F32)
    for pair in range(mixed_ref.shape[2] // LANES):
        cols = slice(pair * LANES, (pair + 1) * LANES)
        queries, keys, values = (qkv_ref[k, 0, :, cols] for k in range(3))
        total = jnp.zeros((height, LANES), F32)
        for h in range(2):
            scores = dot(queries * masks[h], keys, 1, 1) * HD ** (-0.5)
            scores = jnp.where(key_lane < SEQ, scores, -1e30)
            highest = jnp.max(scores, -1, keepdims=True)
            weights = jnp.exp(scores - highest)
            sums = jnp.sum(weights, -1, keepdims=True)
            probs = (weights * (1.0 / sums)).astype(BF)
            total += dot(probs, values * masks[h])
            logs = jnp.where(lane == pair * 2 + h, highest + jnp.log(sums), logs)
        mixed_ref[0, :, cols] = total.astype(BF)
    log_ref[0] = logs


def attend(order, block_in, tail, gain, head_in, images, image_slots, height):
    rows, width = block_in.shape
    cols = head_in.shape[2]
    spec = pltpu.PrefetchScalarGridSpec(
        num_scalar_prefetch=1,
        grid=(image_slots,),
        in_specs=[whole((rows, width), True), whole((16, width)), whole((1, width)), whole(head_in.shape, True)],
        out_specs=[
            image(height, cols),
            image(height, width),
            pl.BlockSpec((3, 1, height, cols), lambda i, *_: (0, i, 0, 0)),
            image(height, LANES),
        ],
        scratch_shapes=[pltpu.VMEM((rows // 16 * 16 + 48, width), BF)],
    )
    return pl.pallas_call(
        functools.partial(attend_kernel, images),
        grid_spec=spec,
        out_shape=[
            jax.ShapeDtypeStruct((image_slots, height, cols), BF),
            jax.ShapeDtypeStruct((image_slots, height, width), BF),
            jax.ShapeDtypeStruct((3, image_slots, height, cols), BF),
            jax.ShapeDtypeStruct((image_slots, height, LANES), F32),
        ],
        compiler_params=params(),
        cost_estimate=cost(16 * image_slots * height * width * cols, 16 * rows * width),
        name="attend",
    )(order, block_in, tail, gain, head_in)


def attend_back_kernel(
    dmix_ref, qkv_ref, log_ref, first_ref, wt_ref, gain_ref, low_ref, high_ref, hg_ref, ng_ref, acc, grads
):
    i = pl.program_id(0)
    height = first_ref.shape[1]
    masks = head_masks()
    lane = iota(1, LANES, 1)
    key_lane = iota(1, height, 1)
    scale = HD ** (-0.5)
    logs = log_ref[0]
    for pair in range(dmix_ref.shape[2] // LANES):
        cols = slice(pair * LANES, (pair + 1) * LANES)
        queries, keys, values = (qkv_ref[k, 0, :, cols] for k in range(3))
        out_grad = dmix_ref[0, :, cols]
        dq = jnp.zeros((height, LANES), F32)
        dk = jnp.zeros((height, LANES), F32)
        dv = jnp.zeros((height, LANES), F32)
        for h in range(2):
            q_h = queries * masks[h]
            o_h = out_grad * masks[h]
            log_h = jnp.sum(jnp.where(lane == pair * 2 + h, logs, 0.0), -1, keepdims=True)
            probs = jnp.exp(dot(q_h, keys, 1, 1) * scale - log_h)
            probs = jnp.where(key_lane < SEQ, probs, 0.0)
            prob_grad = dot(o_h, values, 1, 1)
            dv += dot(probs.astype(BF), o_h, 0, 0)
            delta = jnp.sum(probs * prob_grad, -1, keepdims=True)
            score_grad = (probs * (prob_grad - delta)).astype(BF)
            dq += dot(score_grad, keys * masks[h])
            dk += dot(score_grad, q_h, 0, 0)
        grads[0, :, cols] = (dq * scale).astype(BF)
        grads[1, :, cols] = (dk * scale).astype(BF)
        grads[2, :, cols] = dv.astype(BF)

    @pl.when(i == 0)
    def _():
        acc[...] = jnp.zeros_like(acc)

    first = first_ref[0]
    total = None
    for k in range(3):
        part = dot(grads[k], wt_ref[k])
        total = part if total is None else total + part
        acc[k] += dot(grads[k], first, 0, 0)
    store_half(low_ref, high_ref, total.astype(BF))

    @pl.when(i == pl.num_programs(0) - 1)
    def _():
        hg_ref[...] = acc[...].astype(BF)
        gain_grad = jnp.zeros_like(ng_ref)
        for k in range(3):
            gain_grad += jnp.sum(acc[k] * wt_ref[k].astype(F32), 0, keepdims=True)
        ng_ref[...] = gain_grad / gain_ref[...]


def attend_back(dmix, qkv, logs, first, head_in_t, gain):
    image_slots, height, cols = dmix.shape
    width = first.shape[2]
    specs, shapes = halves(image_slots, (height, width), BF)
    return pl.pallas_call(
        attend_back_kernel,
        grid=(image_slots,),
        in_specs=[
            image(height, cols),
            pl.BlockSpec((3, 1, height, cols), lambda i: (0, i, 0, 0)),
            image(height, LANES),
            image(height, width),
            whole(head_in_t.shape, True),
            whole((1, width)),
        ],
        out_specs=specs + [whole(head_in_t.shape), whole((1, width))],
        out_shape=shapes
        + [jax.ShapeDtypeStruct(head_in_t.shape, BF), jax.ShapeDtypeStruct((1, width), F32)],
        scratch_shapes=[pltpu.VMEM(head_in_t.shape, F32), pltpu.VMEM((3, height, cols), BF)],
        compiler_params=params(),
        cost_estimate=cost(24 * image_slots * height * width * cols, 20 * image_slots * height * width),
        name="attend_back",
    )(dmix, qkv, logs, first, head_in_t, gain)


def pack_first_kernel(slots, base, x_ref, tail_ref, lp_ref, side_ref, out_ref, rows):
    e = pl.program_id(0)

    @pl.when(e == 0)
    def _():
        fill(x_ref, tail_ref, rows)

    j = base + e * slots + iota(slots, rows.shape[0], 0)
    picks = [flag(lp_ref[c : c + 1, :] == j) for c in range(2)]
    width = x_ref.shape[1]
    out_ref[0, :, 0:width] = dot((picks[0] + picks[1]).astype(BF), rows[...]).astype(BF)
    out_ref[0, :, width:] = (
        dot(picks[0].astype(BF), side_ref[0]) + dot(picks[1].astype(BF), side_ref[1])
    ).astype(BF)


def pack_first(x, tail, lp, side, experts, slots, base):
    rows, width = x.shape
    padded = lp.shape[1]
    return pl.pallas_call(
        functools.partial(pack_first_kernel, slots, base),
        grid=(experts,),
        in_specs=[whole((rows, width), True), whole((16, width)), whole(lp.shape), whole(side.shape)],
        out_specs=image(slots, width + LANES),
        out_shape=jax.ShapeDtypeStruct((experts, slots, width + LANES), BF),
        scratch_shapes=[pltpu.VMEM((padded, width), BF)],
        compiler_params=params(),
        cost_estimate=cost(3 * experts * slots * padded * width, 2 * rows * width),
        name="pack_cotangent",
    )(x, tail, lp, side)


def pack_kernel(slots, base, count, *refs):
    lp_ref, out_ref = refs[count], refs[count + 1]
    total = None
    for p in range(count):
        j = base + pl.program_id(0) * slots + iota(slots, refs[p].shape[0], 0)
        picks = flag((lp_ref[p, 0:1, :] == j) | (lp_ref[p, 1:2, :] == j)).astype(BF)
        part = dot(picks, refs[p][...])
        total = part if total is None else total + part
    out_ref[0] = total.astype(BF)


def pack(pieces, lp, experts, slots, base):
    rows, width = pieces[0].shape
    count = len(pieces)
    return pl.pallas_call(
        functools.partial(pack_kernel, slots, base, count),
        grid=(experts,),
        in_specs=[whole((rows, width), True)] * count + [whole(lp.shape)],
        out_specs=image(slots, width),
        out_shape=jax.ShapeDtypeStruct((experts, slots, width), BF),
        compiler_params=params(),
        cost_estimate=cost(3 * experts * slots * rows * count * width, 2 * rows * count * width),
        name="pack_rows",
    )(*pieces, lp)


def unpack_kernel(count, slots, per, graded, lp_ref, *refs):
    row_refs, (low_ref, high_ref) = refs[:count], refs[count:]
    lp = lp_ref[0]
    height = lp.shape[0]
    rows, width = row_refs[0].shape
    total = jnp.zeros((height, width), F32)
    lanes = up_to(slots, LANES)
    extra = [jnp.zeros((height, lanes), F32) for _ in range(2)]
    for n in range(count):
        j = n * rows + iota(1, rows, 1)
        hits = (lp[:, 0:1] == j) | (lp[:, 1:2] == j)
        total += dot(flag(hits).astype(BF), row_refs[n][...])
        if graded:
            j = iota(1, lanes, 1)
            for e in range(rows // slots):
                spare = row_refs[n][(e + 1) * slots - 16 : (e + 1) * slots, 0 : 2 * lanes].astype(F32)
                spare = spare[per + 16 - slots : per + 17 - slots, :]
                values = spare[:, :lanes] + spare[:, lanes:]
                for c in range(2):
                    hit = lp[:, c : c + 1] - (n * rows + e * slots) == j
                    extra[c] += jnp.where(hit, values, 0.0)
    value = total.astype(BF)
    if graded:
        lane = iota(1, LANES, 1)
        tail = jnp.zeros((height, LANES), F32)
        for c in range(2):
            grad = jnp.sum(extra[c], -1, keepdims=True)
            high = grad.astype(BF).astype(F32)
            tail = jnp.where(lane == c, high, tail)
            tail = jnp.where(lane == 2 + c, grad - high, tail)
        value = jnp.concatenate([value, tail.astype(BF)], 1)
    store_half(low_ref, high_ref, value)


def unpack(lp, rows, slots, per, graded):
    image_slots, height, _ = lp.shape
    count = len(rows)
    width = rows[0].shape[1]
    specs, shapes = halves(image_slots, (height, width + (LANES if graded else 0)), BF)
    return pl.pallas_call(
        functools.partial(unpack_kernel, count, slots, per, graded),
        grid=(image_slots,),
        in_specs=[image(height, 2)] + [whole(item.shape, True) for item in rows],
        out_specs=specs,
        out_shape=shapes,
        compiler_params=params(),
        cost_estimate=cost(3 * image_slots * height * count * rows[0].size, 4 * count * rows[0].size),
        name="unpack_rows",
    )(lp, *rows)


def to_rows_kernel(own, height, count, start_ref, *refs):
    out_ref, rows = refs[count], refs[count + 1]
    b = pl.program_id(0)

    @pl.when(b == 0)
    def _():
        for p in range(count):
            at = pl.multiple_of(start_ref[p], 16)
            rows[pl.ds(at, own * height), :] = refs[p][...]

    tile = out_ref.shape[0]
    window = up_to(tile + 3 * (height - SEQ) + 16, 16)
    lift = height - SEQ
    first = b * tile
    start = (first + lift * (first // SEQ)) // 16 * 16
    start = jnp.minimum(start, rows.shape[0] - window)
    r = first + iota(tile, 1, 0)
    steps = sum(jnp.where(r >= (first // SEQ + n) * SEQ, 1, 0) for n in (1, 2))
    target = r + lift * (first // SEQ + steps) - start
    picks = flag(iota(tile, window, 1) == target).astype(BF)
    out_ref[...] = dot(picks, rows[pl.ds(pl.multiple_of(start, 16), window), :]).astype(out_ref.dtype)


def to_rows(starts, pieces, rows, dtype, height):
    each, width = pieces[0].shape
    count = len(pieces)
    spec = pltpu.PrefetchScalarGridSpec(
        num_scalar_prefetch=1,
        grid=(-(-rows // 208),),
        in_specs=[whole((each, width), True)] * count,
        out_specs=pl.BlockSpec((208, width), lambda i, *_: (i, 0)),
        scratch_shapes=[pltpu.VMEM((each * count, width), BF)],
    )
    return pl.pallas_call(
        functools.partial(to_rows_kernel, each // height, height, count),
        grid_spec=spec,
        out_shape=jax.ShapeDtypeStruct((rows, width), dtype),
        compiler_params=params(),
        cost_estimate=cost(2 * rows * 256 * width, 8 * rows * width),
        name="to_rows",
    )(starts, *pieces)


def middle_kernel(count, *refs):
    mixed_refs, wo_refs = refs[:count], refs[count : 2 * count]
    x_ref, gain_ref, router_ref, ids_ref, noise_ref, mid_ref, second_ref, gates_ref = refs[2 * count :]
    middle = x_ref[0].astype(F32)
    for mixed_ref, wo_ref in zip(mixed_refs, wo_refs):
        middle += dot(mixed_ref[0], wo_ref[...])
    mid_ref[0] = middle
    scaled, _ = norm_parts(middle)
    second = (scaled * gain_ref[...]).astype(BF)
    second_ref[0] = second
    logits = dot(second, router_ref[...])
    lane = iota(1, LANES, 1)
    chosen = [
        jnp.sum(jnp.where(lane == ids_ref[0, :, c : c + 1], logits, 0.0), -1, keepdims=True)
        + noise_ref[0, :, c : c + 1]
        for c in range(2)
    ]
    top = jnp.maximum(chosen[0], chosen[1])
    raw = [jnp.exp(item - top) for item in chosen]
    inverse = 1.0 / (raw[0] + raw[1])
    gates_ref[0] = jnp.where(lane == 0, raw[0] * inverse, 0.0) + jnp.where(lane == 1, raw[1] * inverse, 0.0)


def middle_of(mixed, head_out, x_own, gain, router, ids, noise):
    own, height, cols = mixed[0].shape
    parts = len(mixed)
    width = x_own.shape[2]
    return pl.pallas_call(
        functools.partial(middle_kernel, parts),
        grid=(own,),
        in_specs=[image(height, cols)] * parts
        + [whole((cols, width), True)] * parts
        + [
            image(height, width),
            whole((1, width)),
            whole(router.shape),
            image(height, 2),
            image(height, 2),
        ],
        out_specs=[image(height, width), image(height, width), image(height, LANES)],
        out_shape=[
            jax.ShapeDtypeStruct((own, height, width), F32),
            jax.ShapeDtypeStruct((own, height, width), BF),
            jax.ShapeDtypeStruct((own, height, LANES), F32),
        ],
        compiler_params=params(),
        cost_estimate=cost(4 * own * height * width * width, 24 * own * height * width),
        name="middle",
    )(*mixed, *head_out, x_own, gain, router, ids, noise)


def middle_back_kernel(count, *refs):
    rs_ref, mid_ref, second_ref, gates_ref, ids_ref, up_ref, gain_ref, router_ref = refs[:8]
    mixed_refs, wo_refs = refs[8 : 8 + count], refs[8 + count : 8 + 2 * count]
    mg_ref, hog_ref, rg_ref, ng_ref = refs[8 + 2 * count : 12 + 2 * count]
    dmix_refs, hog_acc = refs[12 + 2 * count : -1], refs[-1]
    i = pl.program_id(0)

    @pl.when(i == 0)
    def _():
        hog_acc[...] = jnp.zeros_like(hog_acc)
        rg_ref[...] = jnp.zeros_like(rg_ref)
        ng_ref[...] = jnp.zeros_like(ng_ref)

    width = up_ref.shape[2]
    lane = iota(1, LANES, 1)
    tail = rs_ref[0, :, width:]
    gates = gates_ref[0]
    gate, grad = [], []
    for c in range(2):
        gate.append(jnp.sum(jnp.where(lane == c, gates, 0.0), -1, keepdims=True))
        grad.append(jnp.sum(jnp.where((lane == c) | (lane == 2 + c), tail, 0.0), -1, keepdims=True))
    mean_term = gate[0] * grad[0] + gate[1] * grad[1]
    logit_grad = jnp.zeros((up_ref.shape[1], LANES), F32)
    for c in range(2):
        logit_grad = jnp.where(lane == ids_ref[0, :, c : c + 1], gate[c] * (grad[c] - mean_term), logit_grad)
    logit_grad = logit_grad.astype(BF)
    second_grad = rs_ref[0, :, 0:width] + dot(logit_grad, router_ref[...], 1, 1)
    rg_ref[...] += dot(logit_grad, second_ref[0], 0, 0)
    scaled, spread = norm_parts(mid_ref[0])
    ng_ref[...] += jnp.sum(second_grad * scaled, 0, keepdims=True)
    middle_grad = up_ref[0].astype(F32) + norm_field_back(second_grad, gain_ref[...], scaled, spread)
    mg_ref[0] = middle_grad
    rounded = middle_grad.astype(BF)
    for t in range(count):
        dmix_refs[t][0] = dot(rounded, wo_refs[t][...], 1, 1).astype(BF)
        hog_acc[t] += dot(mixed_refs[t][0], rounded, 0, 0)

    @pl.when(i == pl.num_programs(0) - 1)
    def _():
        hog_ref[...] = hog_acc[...].astype(BF)


def middle_back(rs, middle, second, gates, ids, up, mixed, head_out, gain, router):
    own, height, cols = mixed[0].shape
    parts = len(mixed)
    width = up.shape[2]
    return pl.pallas_call(
        functools.partial(middle_back_kernel, parts),
        grid=(own,),
        in_specs=[
            image(height, rs.shape[2]),
            image(height, width),
            image(height, width),
            image(height, LANES),
            image(height, 2),
            image(height, width),
            whole((1, width)),
            whole(router.shape),
        ]
        + [image(height, cols)] * parts
        + [whole((cols, width), True)] * parts,
        out_specs=[image(height, width), whole((parts, cols, width)), whole((LANES, width)), whole((1, width))]
        + [image(height, cols)] * parts,
        out_shape=[
            jax.ShapeDtypeStruct((own, height, width), F32),
            jax.ShapeDtypeStruct((parts, cols, width), BF),
            jax.ShapeDtypeStruct((LANES, width), F32),
            jax.ShapeDtypeStruct((1, width), F32),
        ]
        + [jax.ShapeDtypeStruct((own, height, cols), BF)] * parts,
        scratch_shapes=[pltpu.VMEM((parts, cols, width), F32)],
        compiler_params=params(),
        cost_estimate=cost(8 * own * height * width * width, 40 * own * height * width),
        name="middle_back",
    )(rs, middle, second, gates, ids, up, gain, router, *mixed, *head_out)


def input_back_kernel(fg_ref, x_ref, mg_ref, gain_ref, out_ref):
    scaled, spread = norm_parts(x_ref[0].astype(F32))
    out_ref[0] = (mg_ref[0] + norm_field_back(fg_ref[0], gain_ref[...], scaled, spread)).astype(BF)


def input_back(first_grad, x_own, middle_grad, gain):
    own, height, width = x_own.shape
    return pl.pallas_call(
        input_back_kernel,
        grid=(own,),
        in_specs=[image(height, width)] * 3 + [whole((1, width))],
        out_specs=image(height, width),
        out_shape=jax.ShapeDtypeStruct((own, height, width), BF),
        compiler_params=params(),
        cost_estimate=cost(20 * own * height * width, 16 * own * height * width),
        name="input_back",
    )(first_grad, x_own, middle_grad, gain)


def gelu_parts(v):
    x = jnp.abs(v) * 0.7071067811865476
    t = 1.0 / (1.0 + 0.3275911 * x)
    bell = jnp.exp(-x * x)
    poly = ((((1.061405429 * t - 1.453152027) * t + 1.421413741) * t - 0.284496736) * t + 0.254829592) * t
    below = 0.5 * poly * bell
    share = jnp.where(v < 0.0, below, 1.0 - below)
    return v * share, share + v * bell * 0.3989422804014327


def expert_kernel(count, slots, per, x_ref, g_ref, router_ref, *refs):
    w1_refs, w2_refs = refs[:count], refs[count : 2 * count]
    back_ref, act_ref, hg_ref, rg_ref, dx_ref = refs[2 * count :]
    width = x_ref.shape[1]
    rows = x_ref[...]
    lane = iota(1, LANES, 1)
    side = g_ref[:, width:].astype(F32)

    def column(*lanes):
        keep = lane == lanes[0]
        for other in lanes[1:]:
            keep = keep | (lane == other)
        return jnp.sum(jnp.where(keep, side, 0.0), -1, keepdims=True)

    logits = dot(rows, router_ref[...])
    lane_f = lane.astype(F32)
    mine = jnp.sum(jnp.where(lane_f == column(4), logits, 0.0), -1, keepdims=True)
    other = jnp.sum(jnp.where(lane_f == column(0), logits, 0.0), -1, keepdims=True)
    gate = 1.0 / (1.0 + jnp.exp(other - mine - column(1, 2, 3)))
    upstream = g_ref[:, 0:width].astype(F32)
    rows_grad = (gate * upstream).astype(BF)
    rg_ref[...] = rows_grad
    hidden_here = w1_refs[0].shape[1]
    step = min(512, hidden_here)
    for t in range(count):
        for at in range(0, hidden_here, step):
            cols = slice(at, at + step)
            place = slice(t * hidden_here + at, t * hidden_here + at + step)
            hidden = dot(rows, w1_refs[t][:, cols])
            active_grad = dot(rows_grad, w2_refs[t][cols, :], 1, 1)
            active, slope = gelu_parts(hidden)
            act_ref[:, place] = active.astype(BF)
            hg_ref[:, place] = (active_grad * slope).astype(BF)
    out = None
    grad = None
    for t in range(count):
        place = slice(t * hidden_here, (t + 1) * hidden_here)
        part = dot(act_ref[:, place], w2_refs[t][...])
        out = part if out is None else out + part
        part = dot(hg_ref[:, place], w1_refs[t][...], 1, 1)
        grad = part if grad is None else grad + part
    dx_ref[...] = grad.astype(BF)
    back_ref[...] = (gate * out).astype(BF)
    gate_grad = jnp.sum(upstream * out.astype(BF).astype(F32), -1, keepdims=True)
    lanes = up_to(slots, LANES)
    spread = iota(slots, lanes, 0) == iota(slots, lanes, 1)
    spare_row = iota(16, 1, 0) == per + 16 - slots
    for b in range(x_ref.shape[0] // slots):
        end = (b + 1) * slots
        line = jnp.sum(jnp.where(spread, gate_grad[end - slots : end], 0.0), 0, keepdims=True)
        high = line.astype(BF).astype(F32)
        line = jnp.concatenate([high, line - high, jnp.zeros((1, width - 2 * lanes), F32)], 1)
        dx_ref[end - 16 : end, :] = jnp.where(spare_row, line, grad[end - 16 : end]).astype(BF)


def expert(x, g, router, w1, w2, slots, per):
    rows, width = x.shape
    count = len(w1)
    total = count * w1[0].shape[1]
    blocks = rows // slots
    tile = slots * max(n for n in range(1, blocks + 1) if blocks % n == 0 and n * slots <= 448)

    def tiled(cols):
        return pl.BlockSpec((tile, cols), lambda i: (i, 0))

    flops = 8 * rows * width * total
    return pl.pallas_call(
        functools.partial(expert_kernel, count, slots, per),
        grid=(rows // tile,),
        in_specs=[tiled(width), tiled(g.shape[1]), whole(router.shape)]
        + [whole(item.shape, True) for item in w1]
        + [whole(item.shape, True) for item in w2],
        out_specs=[tiled(width), tiled(total), tiled(total), tiled(width), tiled(width)],
        out_shape=[
            jax.ShapeDtypeStruct((rows, width), BF),
            jax.ShapeDtypeStruct((rows, total), BF),
            jax.ShapeDtypeStruct((rows, total), BF),
            jax.ShapeDtypeStruct((rows, width), BF),
            jax.ShapeDtypeStruct((rows, width), BF),
        ],
        compiler_params=params(60),
        cost_estimate=pl.CostEstimate(flops=flops, bytes_accessed=rows * total * 6, transcendentals=rows * total * 2),
        name="expert",
    )(x, g, router, *w1, *w2)


def weight_kernel(count, *refs):
    ins, (low_ref, high_ref) = refs[:-2], refs[-2:]
    total = None
    for n in range(count):
        part = dot(ins[2 * n][...], ins[2 * n + 1][...], 0, 0)
        total = part if total is None else total + part
    store_half(low_ref, high_ref, total.astype(BF))


def weight_grad(columns, rows, parts):
    count = len(columns)
    total = columns[0].shape[1]
    width = rows[0].shape[1]
    here = total // parts
    step = min(512, here)
    specs, args = [], []
    for a, b in zip(columns, rows):
        specs += [pl.BlockSpec((a.shape[0], step), lambda i: (0, i)), whole(b.shape, True)]
        args += [a, b]
    steps = total // step
    out_specs, out_shape = halves(steps, (step, width), BF)
    low, high = pl.pallas_call(
        functools.partial(weight_kernel, count),
        grid=(steps,),
        in_specs=specs,
        out_specs=out_specs,
        out_shape=out_shape,
        compiler_params=params(),
        cost_estimate=pl.CostEstimate(
            flops=2 * sum(b.shape[0] for b in rows) * width * total, bytes_accessed=4 * total * width, transcendentals=0
        ),
        name="weight_grad",
    )(*args)
    return low.reshape(parts // 2, here, width), high.reshape(parts // 2, here, width)


def shards(
    block_in,
    norm_one,
    head_in,
    head_out,
    norm_two,
    router,
    expert_in,
    expert_out,
    expert_ids,
    route_noise,
    cotangent,
):
    rows_here, width = block_in.shape
    parts = lax.axis_size("tensor")
    groups = lax.axis_size("expert")
    me = lax.axis_index("tensor")
    images = rows_here // SEQ
    own = -(-images // parts)
    image_slots = own * parts
    height = up_to(SEQ, 16)
    experts = router.shape[1]
    capacity = (rows_here * 2 * 8 // (5 * experts) + 15) // 16 * 16
    share = -(-capacity // parts)
    per = -(-share // CHUNKS)
    slots = up_to(per + 1, 16)
    chunk_rows = experts * slots
    full = rows_here // 16 * 16

    paired = parts == 4
    order = (0, 2, 1, 3) if paired else tuple(range(parts))
    part_of = [me ^ k if paired else jnp.int32(k) for k in order]

    def cross(x, k):
        return lax.ppermute(x, "tensor", [(n, n ^ k) for n in range(parts)])

    def gathered(x):
        if not paired:
            every = lax.all_gather(x, "tensor", axis=0, tiled=False)
            return [every[p] for p in range(parts)]
        far, near = cross(x, 2), cross(x, 1)
        return [x, far, near, cross(far, 1)]

    def scattered(low, high):
        if not paired:
            both = jnp.concatenate([low, high], 0)
            return lax.psum_scatter(both, "tensor", scatter_dimension=0).astype(F32)
        both = (low.astype(F32) + cross(high, 1).astype(F32)).astype(BF)
        return both[0].astype(F32) + cross(both[1], 2).astype(F32)

    def swapped(pieces):
        if not paired:
            every = lax.all_to_all(jnp.stack(pieces), "tensor", split_axis=0, concat_axis=0, tiled=True)
            return [every[p] for p in range(parts)]
        return [cross(piece, k) if k else piece for piece, k in zip(pieces, order)]

    def over_experts(x):
        return lax.all_to_all(x, "expert", split_axis=0, concat_axis=0, tiled=True)

    def pinned(*items):
        return lax.optimization_barrier(items)

    def tail_of(x):
        return jnp.pad(x[full:], ((0, 16 - (rows_here - full)), (0, 0)))

    def to_images(x, value):
        x = x.reshape(images, SEQ, x.shape[-1])
        return jnp.pad(
            x, ((0, image_slots - images), (0, height - SEQ), (0, 0)), constant_values=value
        )

    def own_images(x):
        pieces = []
        for n in range(own):
            at = jnp.minimum(me * own + n, images - 1) * SEQ
            piece = lax.dynamic_slice(x, (at, 0), (SEQ, x.shape[1]))
            pieces.append(jnp.pad(piece, ((0, height - SEQ), (0, 0))))
        return jnp.stack(pieces)

    names = jnp.arange(experts, dtype=jnp.int32)
    member = [(expert_ids[:, c : c + 1] == names).astype(jnp.int32) for c in range(2)]
    both = member[0] + member[1]
    earlier = jnp.cumsum(both, 0) - both
    slot = jnp.stack([jnp.sum(earlier * item, -1) for item in member], 1)
    local = slot - me * share
    place = local // per * chunk_rows + expert_ids * slots + local % per
    place = jnp.where((local >= 0) & (local < share), place, -1)
    place_flat = jnp.pad(place.T, ((0, 0), (0, full + 16 - rows_here)), constant_values=-1)
    place_images = to_images(place, -1)
    place_images = jnp.concatenate(
        [lax.dynamic_slice_in_dim(place_images, part * own, own, 0) for part in part_of], 0
    )
    place_lanes = jnp.swapaxes(place_images.reshape(parts, own * height, 2), 1, 2)
    ids_own = lax.dynamic_slice_in_dim(to_images(expert_ids, -1), me * own, own, 0)
    noise_own = lax.dynamic_slice_in_dim(to_images(route_noise, 0.0), me * own, own, 0)
    image_order = jnp.concatenate([part * own + jnp.arange(own, dtype=jnp.int32) for part in part_of])
    row_starts = jnp.stack([part * (own * height) for part in part_of]).astype(jnp.int32)

    sides = []
    for c in range(2):
        gap = route_noise[:, c] - route_noise[:, 1 - c]
        high = gap.astype(BF)
        left = gap - high.astype(F32)
        mid = left.astype(BF)
        low = (left - mid.astype(F32)).astype(BF)
        columns = [expert_ids[:, 1 - c].astype(BF), high, mid, low, expert_ids[:, c].astype(BF)]
        sides.append(jnp.stack(columns, 1))
    side = jnp.pad(jnp.stack(sides), ((0, 0), (0, full + 16 - rows_here), (0, LANES - 5)))

    router_wide = jnp.pad(router, ((0, 0), (0, LANES - experts)))
    gain_one, gain_two = norm_one[None, :], norm_two[None, :]
    head_out_all = gathered(head_out)
    w1 = gathered(expert_in[0])

    tail = tail_of(cotangent)
    packed = [
        pack_first(cotangent, tail, place_flat, side, experts, slots, n * chunk_rows) for n in range(CHUNKS)
    ]
    block_rows, *packed = pinned(block_in, *packed)
    signals = [over_experts(item) for item in packed]

    mixed, first_in, qkv, logs = attend(
        image_order, block_rows, tail_of(block_in), gain_one, head_in, images, image_slots, height
    )
    mixed = swapped([mixed[p * own : (p + 1) * own] for p in range(parts)])
    *mixed, signals[0] = pinned(*mixed, signals[0])
    x_own = own_images(block_in)
    valid = (me * own + jnp.arange(own) < images)[:, None, None]
    up_own = jnp.where(valid, own_images(cotangent), 0)
    middle, second_in, gates = middle_of(
        mixed, head_out_all, x_own, gain_two, router_wide, ids_own, noise_own
    )
    *second_all, late_out, signals[-1] = pinned(*gathered(second_in), expert_out[0], signals[-1])
    w2 = gathered(late_out)
    second_all = [item.reshape(own * height, width) for item in second_all]

    outgoing = [pack(second_all, place_lanes, experts, slots, n * chunk_rows) for n in range(CHUNKS)]
    backs, actives, hidden_grads, rows_grads, arrived, returned = [], [], [], [], [], []
    x = over_experts(outgoing[0])
    for n in range(CHUNKS):
        coming = None
        if n + 1 < CHUNKS:
            x, ready = pinned(x, outgoing[n + 1])
            coming = over_experts(ready)
        x = x.reshape(groups * slots, width)
        signal = signals[n].reshape(groups * slots, width + LANES)
        back, active, hidden_grad, rows_grad, row_grad = expert(x, signal, router_wide, w1, w2, slots, per)
        arrived.append(x)
        actives.append(active)
        hidden_grads.append(hidden_grad)
        rows_grads.append(rows_grad)
        backs.append(back)
        if coming is not None:
            x, row_grad = pinned(coming, row_grad)
        returned.append(over_experts(row_grad.reshape(experts, slots, width)))

    out_low, out_high = weight_grad(actives, rows_grads, parts)
    in_low, in_high = weight_grad(hidden_grads, arrived, parts)
    *returned, in_low, in_high, out_low, out_high = pinned(*returned, in_low, in_high, out_low, out_high)
    out_grad = scattered(out_low, out_high)

    def whole_rows(items):
        return [item.reshape(chunk_rows, width) for item in items]

    def by_part(x):
        return x.reshape((parts // 2, own) + x.shape[1:])

    low, high = unpack(place_images, whole_rows(returned), slots, per, True)
    second_sum = scattered(by_part(low), by_part(high))
    combined = [over_experts(item.reshape(experts, slots, width)) for item in backs]
    second_sum, combined[0] = pinned(second_sum, combined[0])
    middle_grad, head_out_part, router_part, norm_two_part, *mixed_grad = middle_back(
        second_sum, middle, second_in, gates, ids_own, up_own, mixed, head_out_all, gain_two, router_wide
    )
    *mixed_grad, in_low, in_high = pinned(*swapped(mixed_grad), in_low, in_high)
    in_grad = scattered(in_low, in_high)
    first_low, first_high, head_in_part, norm_one_part = attend_back(
        jnp.concatenate(mixed_grad, 0), qkv, logs, first_in, jnp.swapaxes(head_in, 1, 2), gain_one
    )
    first_low, first_high, combined[-1] = pinned(first_low, first_high, combined[-1])
    first_grad = scattered(by_part(first_low), by_part(first_high))
    input_part = input_back(first_grad, x_own, middle_grad, gain_one)

    def finished(x, dtype):
        pieces = [item.reshape(own * height, width) for item in gathered(x)]
        return to_rows(row_starts, pieces, rows_here, dtype, height)

    low, high = unpack(place_images, whole_rows(combined), slots, per, False)
    block_own = (middle + scattered(by_part(low), by_part(high))).astype(BF)
    input_grad = finished(input_part, F32)
    block_out = finished(block_own, BF)

    cols = head_in.shape[2]
    half = parts // 2
    head_out_part = scattered(head_out_part[:half], head_out_part[half:]).astype(BF)
    small = jnp.concatenate([norm_one_part, norm_two_part, router_part[:experts]], 0).astype(BF)
    count = 4 * cols + 2 + experts
    total = up_to(count, 16 * groups)
    heads = jnp.concatenate(
        [head_in_part.reshape(3 * cols, width), head_out_part, jnp.pad(small, ((0, total - count), (0, 0)))], 0
    )
    heads = jnp.sum(over_experts(heads.reshape(groups, total // groups, width)).astype(F32), 0).astype(BF)
    heads = lax.all_gather(heads, "expert", axis=0, tiled=True)
    head_in_grad = jnp.swapaxes(heads[: 3 * cols].reshape(3, cols, width), 1, 2).astype(F32)
    head_out_grad = heads[3 * cols : 4 * cols].astype(F32)
    small = heads[4 * cols : count].astype(F32)
    if paired:
        small = small + cross(small, 1)
        small = small + cross(small, 2)
    else:
        small = lax.psum(small, "tensor")
    return (
        block_out,
        input_grad,
        small[0],
        head_in_grad,
        head_out_grad,
        small[1],
        small[2:].T,
        in_grad.T[None],
        out_grad[None],
    )


def solution(mesh):
    in_specs = (
        P("expert", None),
        P(),
        P(None, None, "tensor"),
        P("tensor", None),
        P(),
        P(),
        P("expert", None, "tensor"),
        P("expert", "tensor", None),
        P("expert", None),
        P("expert", None),
        P("expert", None),
    )
    out_specs = (
        P("expert", None),
        P("expert", None),
        P(),
        P(None, None, "tensor"),
        P("tensor", None),
        P(),
        P(),
        P("expert", None, "tensor"),
        P("expert", "tensor", None),
    )
    return jax.shard_map(shards, mesh=mesh, in_specs=in_specs, out_specs=out_specs, check_vma=False)
```

time: 1130 us -> 856 us (0.76)
  waiting for transfers between devices: 576 us -> 321 us
  blocking collectives: 139 us -> 0 us
  Pallas kernels: 275 us -> 326 us
  starting transfers between devices: 25.6 us -> 73 us
  other arithmetic: 29.3 us -> 55.2 us
    ppermute x0 -> x38, waiting for transfers between devices: none -> 241 us  [cross(): return lax.ppermute(x, 'tensor', [(n, n ^ k) for n in range(parts)])]
    reduce_scatter x6 -> x0, waiting for transfers between devices: 170 us -> none  [the longest x1 70.7 us: shards(): lax.psum_scatter(weight_grad(actives, rows_grads, parts), 'tensor', scatt...]
    all_to_all x5 -> x9, waiting for transfers between devices: 240 us -> 79.6 us  [over_experts(): return lax.all_to_all(x, 'expert', split_axis=0, concat_axis=0, tiled=True)]
    psum x1 -> x0, waiting for transfers between devices: 101 us -> none  [shards(): head_in_grad = lax.psum(head_in_part, 'expert').astype(F32)]
    all_to_all x2 -> x0, blocking collectives: 97.9 us -> none  [swap(): return lax.all_to_all(x, axis, split_axis=0, concat_axis=0, tiled=True)]
    all_gather x6 -> x1, waiting for transfers between devices: 62.1 us -> 0.01 us  [shards(): heads = lax.all_gather(heads, 'expert', axis=0, tiled=True)]
    pallas_call x9 -> x13, Pallas kernels: 220 us -> 266 us  [the longest x2 95.7 us: expert(): pl.pallas_call(functools.partial(expert_kernel, count, slots, per), grid=...]
    psum x1 -> x0, blocking collectives: 40.7 us -> none  [shards(): lax.psum(jnp.concatenate([norm_one_part, norm_two_part, router_part[:expe...]
  transfers between devices with their start and end apart: 18 -> 48, of which waited for: 12 -> 12; matrix products, arithmetic and copies ran while one was open for 5% -> 11% of each run, Pallas kernels for 13% -> 33%
where the time goes in v2:
time: 856 us; the launch traced here: 848 us
  Pallas kernels  326 us (38%)
  waiting for transfers between devices  321 us (38%)
  starting transfers between devices  73 us (9%)
  local copies, waits for them, and re-layouts  58.3 us (7%)
  other arithmetic  55.2 us (6%)
  between operations  15.1 us (2%)
    ppermute x38, waiting for transfers between devices, cross(): return lax.ppermute(x, 'tensor', [(n, n ^ k) for n in range(parts)])  241 us
    pallas_call x2, Pallas kernels, expert(): pl.pallas_call(functools.partial(expert_kernel, count, slots, per), grid=...  95.7 us
    all_to_all x9, waiting for transfers between devices, over_experts(): return lax.all_to_all(x, 'expert', split_axis=0, concat_axis=0, tiled=True)  79.6 us
    all_to_all x9, starting transfers between devices, over_experts(): return lax.all_to_all(x, 'expert', split_axis=0, concat_axis=0, tiled=True)  51.5 us
    pallas_call x2, Pallas kernels, weight_grad(): pl.pallas_call(functools.partial(weight_kernel, count), grid=(steps,), in...  46.3 us
    pallas_call x2, Pallas kernels, unpack(): pl.pallas_call(functools.partial(unpack_kernel, count, slots, per, graded...  35.6 us
    pallas_call x1, Pallas kernels, attend_back(): pl.pallas_call(attend_back_kernel, grid=(image_slots,), in_specs=[image(h...  33.2 us
    pallas_call x1, Pallas kernels, attend(): pl.pallas_call(functools.partial(attend_kernel, images), grid_spec=spec,...  28.7 us
  transfers between devices with their start and end apart: 48, of which 12 were waited for; matrix products, arithmetic and copies ran while one was open for 11% of the time, Pallas kernels for 33%

profile of v2, /device:TPU:0, one launch (start us, length us, event | category | flops | bytes accessed | tf_op | source)
XLA Modules:
  0.0 848.4 jit_solution(13028022376003901318)
XLA Ops:
  8.1 2.3 reduce-window.6
  13.4 11.5 %pack_cotangent.2 = bf16[8,112,1152]{2,1,0:T(8,128)(2,1)} custom-call(bf16[2167,1024]{1,0:T(8,128)(2,1)} %x_ref.3, bf16[16,1024]{1,0:T(8,128)(2,1)S(1)} %pad.56.tail_ref, s32[2,2176]{1,0:T(2,128)S(1)} %pad.58.lp_ref, bf16[2,2176,128]{2,1,0:T(8,128)(2,1)S(1)} %fusion.12.side_ref), custom_call_target="tpu_custom_call" | custom-call | flops 5989466112 | bytes 4438016 | tf_op jit(solution)/shard_map/pack_cotangent/pallas_call | solution.py:273
  24.9 11.5 %pack_cotangent.3 = bf16[8,112,1152]{2,1,0:T(8,128)(2,1)} custom-call(bf16[2167,1024]{1,0:T(8,128)(2,1)} %x_ref.3, bf16[16,1024]{1,0:T(8,128)(2,1)S(1)} %pad.56.tail_ref, s32[2,2176]{1,0:T(2,128)S(1)} %pad.58.lp_ref, bf16[2,2176,128]{2,1,0:T(8,128)(2,1)S(1)} %fusion.12.side_ref), custom_call_target="tpu_custom_call" | custom-call | flops 5989466112 | bytes 4438016 | tf_op jit(solution)/shard_map/pack_cotangent/pallas_call | solution.py:273
  36.4 7.4 all-to-all-start
  45.5 28.7 %attend.1 = (bf16[12,208,256]{2,1,0:T(8,128)(2,1)S(1)}, bf16[12,208,1024]{2,1,0:T(8,128)(2,1)}, bf16[3,12,208,256]{3,2,1,0:T(8,128)(2,1)}, f32[12,208,128]{2,1,0:T(8,128)S(1)}) custom-call(s32[12]{0:T(128)S(1)} %pad_add_fusion.2.order_ref, bf16[2167,1024]{1,0:T(8,128)(2,1)} %x_ref.4, bf16[16,1024]{1,0:T(8,128)(2,1)S(1)} %pad.60.tail_ref, ...), custom_call_target="tpu_custom_call" | custom-call | flops 10468982784 | bytes 35504128 | tf_op jit(solution)/shard_map/attend/pallas_call | solution.py:160
  75.2 16.2 %all-to-all-done = bf16[8,112,1152]{2,1,0:T(8,128)(2,1)} async-done(((bf16[8,112,1152]{2,1,0:T(8,128)(2,1)}), bf16[8,112,1152]{2,1,0:T(8,128)(2,1)}, u32[]{:S(2)}, u32[]{:S(2)}) %all-to-all-start) | async-done | bytes 2064416 | tf_op jit(solution)/shard_map/all_to_all | solution.py:742
  91.5 4.6 all-to-all-start.1
  100.7 2.5 constant_dynamic-slice_fusion.5
  108.6 3.1 collective-permute-done.2.refs_3_.refs_11_
  113.6 6.3 middle.1
  121.3 1.8 collective-permute-start.7
  123.1 28.6 %collective-permute-done.6 = bf16[3,208,1024]{2,1,0:T(8,128)(2,1)} collective-permute-done((bf16[3,208,1024]{2,1,0:T(8,128)(2,1)S(1)}, bf16[3,208,1024]{2,1,0:T(8,128)(2,1)}, u32[]{:S(2)}, u32[]{:S(2)}) %collective-permute-start.6) | collective-permute-done | bytes 1277984 | tf_op jit(solution)/shard_map/ppermute | solution.py:719
  153.4 1.6 collective-permute-done.8
  155.2 10.5 %pack_rows.2 = bf16[8,112,1024]{2,1,0:T(8,128)(2,1)} custom-call(bf16[624,1024]{1,0:T(8,128)(2,1)S(1)} %bitcast.151, bf16[624,1024]{1,0:T(8,128)(2,1)} %bitcast.16.refs_1_, bf16[624,1024]{1,0:T(8,128)(2,1)} %bitcast.17.refs_2_, bf16[624,1024]{1,0:T(8,128)(2,1)} %bitcast.18.refs_3_, s32[4,2,624]{2,1,0:T(2,128)S(1)} %bitcast.146), custom_call_target="tpu_custom_call" | custom-call | flops 6870269952 | bytes 5111808 | tf_op jit(solution)/shard_map/pack_rows/pallas_call | solution.py:300
  165.7 5.7 all-to-all-start.2
  171.4 29.1 %collective-permute-done.9.refs_1_ = bf16[1024,1024]{1,0:T(8,128)(2,1)} collective-permute-done((bf16[1024,1024]{1,0:T(8,128)(2,1)}, bf16[1024,1024]{1,0:T(8,128)(2,1)}, u32[]{:S(2)}, u32[]{:S(2)}) %collective-permute-start.9) | collective-permute-done | bytes 2097184 | tf_op jit(solution)/shard_map/ppermute | solution.py:719
  201.1 43.9 %collective-permute-done.12.refs_5_ = bf16[1024,1024]{1,0:T(8,128)(2,1)} collective-permute-done((bf16[1024,1024]{1,0:T(8,128)(2,1)}, bf16[1024,1024]{1,0:T(8,128)(2,1)}, u32[]{:S(2)}, u32[]{:S(2)}) %collective-permute-start.12) | collective-permute-done | bytes 2097184 | tf_op jit(solution)/shard_map/ppermute | solution.py:719
  246.3 10.6 %pack_rows.3 = bf16[8,112,1024]{2,1,0:T(8,128)(2,1)} custom-call(bf16[624,1024]{1,0:T(8,128)(2,1)S(1)} %bitcast.152, bf16[624,1024]{1,0:T(8,128)(2,1)} %bitcast.16.refs_1_, bf16[624,1024]{1,0:T(8,128)(2,1)} %bitcast.17.refs_2_, bf16[624,1024]{1,0:T(8,128)(2,1)} %bitcast.18.refs_3_, s32[4,2,624]{2,1,0:T(2,128)S(1)} %bitcast.147), custom_call_target="tpu_custom_call" | custom-call | flops 6870269952 | bytes 5111808 | tf_op jit(solution)/shard_map/pack_rows/pallas_call | solution.py:300
  256.9 5.7 all-to-all-start.3
  262.7 47.8 %expert.2 = (bf16[896,1024]{1,0:T(8,128)(2,1)}, bf16[896,4096]{1,0:T(8,128)(2,1)}, bf16[896,4096]{1,0:T(8,128)(2,1)}, bf16[896,1024]{1,0:T(8,128)(2,1)}, bf16[896,1024]{1,0:T(8,128)(2,1)}) custom-call(bf16[896,1024]{1,0:T(8,128)(2,1)} %bitcast.142, bf16[896,1152]{1,0:T(8,128)(2,1)} %bitcast.22.g_ref, bf16[1024,128]{1,0:T(8,128)(2,1)} %copy-done.11, ...), custom_call_target="tpu_custom_call" | custom-call | flops 30064771072 | bytes 22020096 | tf_op jit(solution)/shard_map/expert/pallas_call | solution.py:629
  310.5 6.0 all-to-all-start.4
  316.4 47.9 %expert.3 = (bf16[896,1024]{1,0:T(8,128)(2,1)}, bf16[896,4096]{1,0:T(8,128)(2,1)}, bf16[896,4096]{1,0:T(8,128)(2,1)}, bf16[896,1024]{1,0:T(8,128)(2,1)}, bf16[896,1024]{1,0:T(8,128)(2,1)}) custom-call(bf16[896,1024]{1,0:T(8,128)(2,1)} %bitcast.25.x_ref.refs_3_, bf16[896,1152]{1,0:T(8,128)(2,1)} %bitcast.26.g_ref, bf16[1024,128]{1,0:T(8,128)(2,1)} %copy-done.11, ...), custom_call_target="tpu_custom_call" | custom-call | flops 30064771072 | bytes 22020096 | tf_op jit(solution)/shard_map/expert/pallas_call | solution.py:629
  364.4 6.1 all-to-all-start.5
  370.5 23.5 %weight_grad.2 = (bf16[4,512,1024]{2,1,0:T(8,128)(2,1)}, bf16[4,512,1024]{2,1,0:T(8,128)(2,1)}) custom-call(bf16[896,4096]{1,0:T(8,128)(2,1)} %get-tuple-element.104.refs_0_, bf16[896,1024]{1,0:T(8,128)(2,1)S(1)} %bitcast.143, bf16[896,4096]{1,0:T(8,128)(2,1)} %get-tuple-element.105.refs_2_, bf16[896,1024]{1,0:T(8,128)(2,1)} %bitcast.25.x_ref.refs_3_), custom_call_target="tpu_custom_call" | custom-call | flops 15032385536 | bytes 16777216 | tf_op jit(solution)/shard_map/weight_grad/pallas_call | solution.py:670
  394.1 22.8 %weight_grad.3 = (bf16[4,512,1024]{2,1,0:T(8,128)(2,1)}, bf16[4,512,1024]{2,1,0:T(8,128)(2,1)}) custom-call(bf16[896,4096]{1,0:T(8,128)(2,1)} %get-tuple-element.108.refs_0_, bf16[896,1024]{1,0:T(8,128)(2,1)S(1)} %copy-done.30, bf16[896,4096]{1,0:T(8,128)(2,1)} %get-tuple-element.110.refs_2_, bf16[896,1024]{1,0:T(8,128)(2,1)S(1)} %copy-done.31), custom_call_target="tpu_custom_call" | custom-call | flops 15032385536 | bytes 16777216 | tf_op jit(solution)/shard_map/weight_grad/pallas_call | solution.py:670
  416.9 19.0 %unpack_rows.2 = (bf16[6,208,1152]{2,1,0:T(8,128)(2,1)}, bf16[6,208,1152]{2,1,0:T(8,128)(2,1)}) custom-call(s32[12,208,2]{2,1,0:T(8,128)S(1)} %pad_add_fusion.lp_ref, bf16[896,1024]{1,0:T(8,128)(2,1)} %bitcast.32.refs_0_, bf16[896,1024]{1,0:T(8,128)(2,1)} %bitcast.33.refs_1_), custom_call_target="tpu_custom_call" | custom-call | flops 13740539904 | bytes 7340032 | tf_op jit(solution)/shard_map/unpack_rows/pallas_call | solution.py:351
  435.9 6.0 all-to-all-start.6
  441.9 3.4 fusion
  447.0 1.6 constant_dynamic-slice_fusion.2
  450.4 34.8 %all-to-all-done.6 = bf16[8,112,1024]{2,1,0:T(8,128)(2,1)S(1)} async-done(((bf16[8,112,1024]{2,1,0:T(8,128)(2,1)}), bf16[8,112,1024]{2,1,0:T(8,128)(2,1)S(1)}, u32[]{:S(2)}, u32[]{:S(2)}) %all-to-all-start.6) | async-done | bytes 1835040 | tf_op jit(solution)/shard_map/all_to_all | solution.py:742
  485.2 4.3 all-to-all-start.7
  489.6 2.6 maximum_select_fusion.refs_5_
  492.2 3.8 convert_add_fusion.5.refs_0_
  496.0 11.6 %middle_back.1 = (f32[3,208,1024]{2,1,0:T(8,128)}, bf16[4,256,1024]{2,1,0:T(8,128)(2,1)}, f32[128,1024]{1,0:T(8,128)S(1)}, f32[1,1024]{1,0:T(1,128)S(1)}, bf16[3...) custom-call(f32[3,208,1152]{2,1,0:T(8,128)} %convert_add_fusion.5.re, ...), custom_call_target="tpu_custom_call" | custom-call | flops 5234491392 | bytes 25559040 | tf_op jit(solution)/shard_map/middle_back/pallas_call | solution.py:503
  510.5 2.6 copy.96
  514.0 2.4 slice.129
  516.8 2.3 collective-permute-done.17
  519.2 3.6 collective-permute-done.19
  524.1 33.2 %attend_back.1 = (bf16[6,208,1024]{2,1,0:T(8,128)(2,1)}, bf16[6,208,1024]{2,1,0:T(8,128)(2,1)}, bf16[3,256,1024]{2,1,0:T(8,128)(2,1)S(1)}, f32[1,1024]{1,0:T(1,128)S(1)}) custom-call(bf16[12,208,256]{2,1,0:T(8,128)(2,1)S(1)} %pad_maximum_fusion.2.dmix_ref, bf16[3,12,208,256]{3,2,1,0:T(8,128)(2,1)} %get-tuple-element.132.qkv_ref, ...), custom_call_target="tpu_custom_call" | custom-call | flops 15703474176 | bytes 51118080 | tf_op jit(solution)/shard_map/attend_back/pallas_call | solution.py:233
  558.5 1.9 add_convert_fusion.2
  561.8 16.5 %unpack_rows.3 = (bf16[6,208,1024]{2,1,0:T(8,128)(2,1)}, bf16[6,208,1024]{2,1,0:T(8,128)(2,1)}) custom-call(s32[12,208,2]{2,1,0:T(8,128)S(1)} %pad_add_fusion.lp_ref, bf16[896,1024]{1,0:T(8,128)(2,1)S(1)} %bitcast.141, bf16[896,1024]{1,0:T(8,128)(2,1)} %bitcast.45.refs_1_), custom_call_target="tpu_custom_call" | custom-call | flops 13740539904 | bytes 7340032 | tf_op jit(solution)/shard_map/unpack_rows/pallas_call | solution.py:351
  579.7 1.7 pad_maximum_fusion
  581.4 5.6 all-to-all-start.8
  587.1 6.4 copy.99
  594.0 3.9 fusion.2
  602.1 6.3 add_convert_fusion
  613.2 28.5 %all-to-all-done.8 = bf16[8,144,1024]{2,1,0:T(8,128)(2,1)S(1)} async-done(((bf16[8,144,1024]{2,1,0:T(8,128)(2,1)}), bf16[8,144,1024]{2,1,0:T(8,128)(2,1)S(1)}, u32[]{:S(2)}, u32[]{:S(2)}) %all-to-all-start.8) | async-done | bytes 2359328 | tf_op jit(solution)/shard_map/all_to_all | solution.py:742
  642.9 3.1 slice_bitcast_fusion
  646.1 2.0 collective-permute-start.37
  648.0 6.2 copy.98
  654.3 3.3 fusion.6
  658.0 4.3 add_convert_fusion.1
  662.3 2.0 copy-done.35
  665.8 1.7 collective-permute-start.35
  667.5 1.8 convert_add_fusion.6.fg_ref
  669.3 3.8 input_back.1
  674.0 57.4 %collective-permute-done.22 = bf16[3,208,1024]{2,1,0:T(8,128)(2,1)} collective-permute-done((bf16[3,208,1024]{2,1,0:T(8,128)(2,1)S(1)}, bf16[3,208,1024]{2,1,0:T(8,128)(2,1)}, u32[]{:S(2)}, u32[]{:S(2)}) %collective-permute-start.22) | collective-permute-done | bytes 1277984 | tf_op jit(solution)/shard_map/ppermute | solution.py:719
  732.0 71.2 %collective-permute-done.27 = bf16[3,208,1024]{2,1,0:T(8,128)(2,1)} collective-permute-done((bf16[3,208,1024]{2,1,0:T(8,128)(2,1)S(1)}, bf16[3,208,1024]{2,1,0:T(8,128)(2,1)}, u32[]{:S(2)}, u32[]{:S(2)}) %collective-permute-start.27) | collective-permute-done | bytes 1277984 | tf_op jit(solution)/shard_map/ppermute | solution.py:719
  803.3 5.3 fusion.3
  808.6 4.5 fusion.4
  813.1 9.9 %to_rows.2 = bf16[2167,1024]{1,0:T(8,128)(2,1)} custom-call(s32[4]{0:T(128)S(1)} %pad_add_fusion.1.start_ref, bf16[624,1024]{1,0:T(8,128)(2,1)S(1)} %bitcast.138, bf16[624,1024]{1,0:T(8,128)(2,1)} %bitcast.51.refs_1_, bf16[624,1024]{1,0:T(8,128)(2,1)} %bitcast.52.refs_2_, bf16[624,1024]{1,0:T(8,128)(2,1)} %bitcast.53.refs_3_), custom_call_target="tpu_custom_call" | custom-call | flops 1136132096 | bytes 17752064 | tf_op jit(solution)/shard_map/to_rows/pallas_call | solution.py:396
  824.3 10.8 %to_rows.3 = f32[2167,1024]{1,0:T(8,128)} custom-call(s32[4]{0:T(128)S(1)} %pad_add_fusion.1.start_ref, bf16[624,1024]{1,0:T(8,128)(2,1)S(1)} %bitcast.140, bf16[624,1024]{1,0:T(8,128)(2,1)} %bitcast.59.refs_1_, bf16[624,1024]{1,0:T(8,128)(2,1)} %bitcast.60.refs_2_, bf16[624,1024]{1,0:T(8,128)(2,1)} %bitcast.61.refs_3_), custom_call_target="tpu_custom_call" | custom-call | flops 1136132096 | bytes 17752064 | tf_op jit(solution)/shard_map/to_rows/pallas_call | solution.py:396
  835.2 1.8 collective-permute-start.33
  838.0 2.1 copy.97
  (239 shorter events, 54.0 us)
Async XLA Ops:
  36.4 8.9 %slice-start.1 = ((bf16[2167,1024]{1,0:T(8,128)(2,1)}), bf16[7,1024]{1,0:T(8,128)(2,1)S(1)}, s32[]{:S(2)}) async-start(bf16[2167,1024]{1,0:T(8,128)(2,1)} %x_ref.4), calls=%async_computation.11 | async-start | bytes 32768 | tf_op jit(solution)/shard_map/slice | solution.py:748
  36.4 9.0 %copy-start.3 = (bf16[3,1024,256]{2,1,0:T(8,128)(2,1)S(1)}, bf16[3,1024,256]{2,1,0:T(8,128)(2,1)}, u32[]{:S(2)}) copy-start(bf16[3,1024,256]{2,1,0:T(8,128)(2,1)} %w_ref.1) | copy-start | bytes 4718596
  36.4 9.0 %copy-start.13 = (f32[1024]{0:T(1024)S(1)}, f32[1024]{0:T(1024)}, u32[]{:S(2)}) copy-start(f32[1024]{0:T(1024)} %param.12) | copy-start | bytes 12292
  36.4 55.1 %all-to-all-start = ((bf16[8,112,1152]{2,1,0:T(8,128)(2,1)}), bf16[8,112,1152]{2,1,0:T(8,128)(2,1)}, u32[]{:S(2)}, u32[]{:S(2)}) async-start(bf16[8,112,1152]{2,1,0:T(8,128)(2,1)} %pack_cotangent.2), calls=%async_computation | async-start | bytes 4128768 | tf_op jit(solution)/shard_map/all_to_all | solution.py:742
  43.9 59.4 %collective-permute-start.3 = (bf16[256,1024]{1,0:T(8,128)(2,1)}, bf16[256,1024]{1,0:T(8,128)(2,1)}, u32[]{:S(2)}, u32[]{:S(2)}) collective-permute-start(bf16[256,1024]{1,0:T(8,128)(2,1)} %refs_12_.1), channel_id=1, source_target_pairs={{0,2},{1,3},{2,0},{3,1},{4,6},{5,7},{6,4},{7,5},{8,10},{9,11},{10,... | collective-permute-start | bytes 1572872 | tf_op jit(solution)/shard_map/ppermute | solution.py:719
  45.4 67.1 %collective-permute-start.4 = (bf16[256,1024]{1,0:T(8,128)(2,1)}, bf16[256,1024]{1,0:T(8,128)(2,1)}, u32[]{:S(2)}, u32[]{:S(2)}) collective-permute-start(bf16[256,1024]{1,0:T(8,128)(2,1)} %refs_12_.1), channel_id=1, source_target_pairs={{0,1},{1,0},{2,3},{3,2},{4,5},{5,4},{6,7},{7,6},{8,9},{9,8},{10,11... | collective-permute-start | bytes 1572872 | tf_op jit(solution)/shard_map/ppermute | solution.py:719
  91.5 61.9 %all-to-all-start.1 = ((bf16[8,112,1152]{2,1,0:T(8,128)(2,1)}), bf16[8,112,1152]{2,1,0:T(8,128)(2,1)}, u32[]{:S(2)}, u32[]{:S(2)}) async-start(bf16[8,112,1152]{2,1,0:T(8,128)(2,1)} %pack_cotangent.3), calls=%async_computation.1 | async-start | bytes 4128768 | tf_op jit(solution)/shard_map/all_to_all | solution.py:742
  97.0 11.6 %collective-permute-start = (bf16[3,208,256]{2,1,0:T(8,128)(2,1)}, bf16[3,208,256]{2,1,0:T(8,128)(2,1)S(1)}, u32[]{:S(2)}, u32[]{:S(2)}) collective-permute-start(bf16[3,208,256]{2,1,0:T(8,128)(2,1)} %get-tuple-element.169), channel_id=1, source_target_pairs={{0,2},{1,3},{2,0},{3,1},{4,6},{5,7},{6,4},{7,5},{8,10},{9,11},{10,... | collective-permute-start | bytes 958472 | tf_op jit(solution)/shard_map/ppermute | solution.py:719
  98.5 10.1 %collective-permute-start.1 = (bf16[3,208,256]{2,1,0:T(8,128)(2,1)}, bf16[3,208,256]{2,1,0:T(8,128)(2,1)S(1)}, u32[]{:S(2)}, u32[]{:S(2)}) collective-permute-start(bf16[3,208,256]{2,1,0:T(8,128)(2,1)} %get-tuple-element.168), channel_id=1, source_target_pairs={{0,1},{1,0},{2,3},{3,2},{4,5},{5,4},{6,7},{7,6},{8,9},{9,8},{10,11... | collective-permute-start | bytes 958472 | tf_op jit(solution)/shard_map/ppermute | solution.py:719
  98.5 13.2 %collective-permute-start.2 = (bf16[3,208,256]{2,1,0:T(8,128)(2,1)}, bf16[3,208,256]{2,1,0:T(8,128)(2,1)S(1)}, u32[]{:S(2)}, u32[]{:S(2)}) collective-permute-start(bf16[3,208,256]{2,1,0:T(8,128)(2,1)} %get-tuple-element.167), channel_id=1, source_target_pairs={{0,3},{1,2},{2,1},{3,0},{4,7},{5,6},{6,5},{7,4},{8,11},{9,10},{10,... | collective-permute-start | bytes 958472 | tf_op jit(solution)/shard_map/ppermute | solution.py:719
  103.2 9.2 %collective-permute-start.5 = (bf16[256,1024]{1,0:T(8,128)(2,1)}, bf16[256,1024]{1,0:T(8,128)(2,1)S(1)}, u32[]{:S(2)}, u32[]{:S(2)}) collective-permute-start(bf16[256,1024]{1,0:T(8,128)(2,1)} %collective-permute-done.3.refs_5_.refs_13_), channel_id=1, source_target_pairs={{0,1},{1,0},{2,3},{3,2},{4,5},{5,4},{6,7},{7,6},{8,9},{9,8},{10,11... | collective-permute-start | bytes 1572872 | tf_op jit(solution)/shard_map/ppermute | solution.py:719
  103.3 9.2 %copy-start.9 = (s32[3,208,2]{2,1,0:T(8,128)}, s32[3,208,2]{2,1,0:T(8,128)S(1)}, u32[]{:S(2)}) copy-start(s32[3,208,2]{2,1,0:T(8,128)S(1)} %pad_dynamic-slice_fusion.5.refs_11_.refs_4_) | copy-start | bytes 14980
  108.6 11.4 %copy-start.20 = (bf16[3,208,256]{2,1,0:T(8,128)(2,1)}, bf16[3,208,256]{2,1,0:T(8,128)(2,1)S(1)}, u32[]{:S(2)}) copy-start(bf16[3,208,256]{2,1,0:T(8,128)(2,1)S(1)} %collective-permute-done.refs_1_.refs_9_) | copy-start | bytes 958468
  108.6 11.4 %copy-start.22 = (bf16[3,208,256]{2,1,0:T(8,128)(2,1)}, bf16[3,208,256]{2,1,0:T(8,128)(2,1)S(1)}, u32[]{:S(2)}) copy-start(bf16[3,208,256]{2,1,0:T(8,128)(2,1)S(1)} %collective-permute-done.1.refs_2_.refs_10_) | copy-start | bytes 958468
  120.7 34.5 %copy-start.16 = (bf16[3,208,1024]{2,1,0:T(8,128)(2,1)}, bf16[3,208,1024]{2,1,0:T(8,128)(2,1)S(1)}, u32[]{:S(2)}) copy-start(bf16[3,208,1024]{2,1,0:T(8,128)(2,1)S(1)} %get-tuple-element.91.refs_2_) | copy-start | bytes 3833860
  120.7 30.9 %collective-permute-start.6 = (bf16[3,208,1024]{2,1,0:T(8,128)(2,1)S(1)}, bf16[3,208,1024]{2,1,0:T(8,128)(2,1)}, u32[]{:S(2)}, u32[]{:S(2)}) collective-permute-start(bf16[3,208,1024]{2,1,0:T(8,128)(2,1)S(1)} %get-tuple-element.91.refs_2_), channel_id=1, source_target_pairs={{0,2},{1,3},{2,0},{3,1},{4,6},{5,7},{6,4},{7,5},{8,10},{9,11},{10,... | collective-permute-start | bytes 3833864 | tf_op jit(solution)/shard_map/ppermute | solution.py:719
  121.3 32.1 %collective-permute-start.7 = (bf16[3,208,1024]{2,1,0:T(8,128)(2,1)S(1)}, bf16[3,208,1024]{2,1,0:T(8,128)(2,1)}, u32[]{:S(2)}, u32[]{:S(2)}) collective-permute-start(bf16[3,208,1024]{2,1,0:T(8,128)(2,1)S(1)} %get-tuple-element.91.refs_2_), channel_id=1, source_target_pairs={{0,1},{1,0},{2,3},{3,2},{4,5},{5,4},{6,7},{7,6},{8,9},{9,8},{10,11... | collective-permute-start | bytes 3833864 | tf_op jit(solution)/shard_map/ppermute | solution.py:719
  151.6 3.3 collective-permute-start.8
  151.8 48.8 %collective-permute-start.9 = (bf16[1024,1024]{1,0:T(8,128)(2,1)}, bf16[1024,1024]{1,0:T(8,128)(2,1)}, u32[]{:S(2)}, u32[]{:S(2)}) collective-permute-start(bf16[1024,1024]{1,0:T(8,128)(2,1)} %bitcast.23.refs_0_), channel_id=1, source_target_pairs={{0,2},{1,3},{2,0},{3,1},{4,6},{5,7},{6,4},{7,5},{8,10},{9,11},{10,... | collective-permute-start | bytes 6291464 | tf_op jit(solution)/shard_map/ppermute | solution.py:719
  155.0 90.0 %collective-permute-start.12 = (bf16[1024,1024]{1,0:T(8,128)(2,1)}, bf16[1024,1024]{1,0:T(8,128)(2,1)}, u32[]{:S(2)}, u32[]{:S(2)}) collective-permute-start(bf16[1024,1024]{1,0:T(8,128)(2,1)} %bitcast.178), channel_id=1, source_target_pairs={{0,2},{1,3},{2,0},{3,1},{4,6},{5,7},{6,4},{7,5},{8,10},{9,11},{10,... | collective-permute-start | bytes 6291464 | tf_op jit(solution)/shard_map/ppermute | solution.py:719
  165.7 91.2 %all-to-all-start.2 = ((bf16[8,112,1024]{2,1,0:T(8,128)(2,1)}), bf16[8,112,1024]{2,1,0:T(8,128)(2,1)S(1)}, u32[]{:S(2)}, u32[]{:S(2)}) async-start(bf16[8,112,1024]{2,1,0:T(8,128)(2,1)} %pack_rows.2), calls=%async_computation.2 | async-start | bytes 3670016 | tf_op jit(solution)/shard_map/all_to_all | solution.py:742
  171.4 91.2 %collective-permute-start.10 = (bf16[1024,1024]{1,0:T(8,128)(2,1)}, bf16[1024,1024]{1,0:T(8,128)(2,1)}, u32[]{:S(2)}, u32[]{:S(2)}) collective-permute-start(bf16[1024,1024]{1,0:T(8,128)(2,1)} %bitcast.23.refs_0_), channel_id=1, source_target_pairs={{0,1},{1,0},{2,3},{3,2},{4,5},{5,4},{6,7},{7,6},{8,9},{9,8},{10,11... | collective-permute-start | bytes 6291464 | tf_op jit(solution)/shard_map/ppermute | solution.py:719
  200.6 62.1 %collective-permute-start.11 = (bf16[1024,1024]{1,0:T(8,128)(2,1)}, bf16[1024,1024]{1,0:T(8,128)(2,1)}, u32[]{:S(2)}, u32[]{:S(2)}) collective-permute-start(bf16[1024,1024]{1,0:T(8,128)(2,1)} %collective-permute-done.9.refs_1_), channel_id=1, source_target_pairs={{0,1},{1,0},{2,3},{3,2},{4,5},{5,4},{6,7},{7,6},{8,9},{9,8},{10,11... | collective-permute-start | bytes 6291464 | tf_op jit(solution)/shard_map/ppermute | solution.py:719
  200.6 62.1 %collective-permute-start.13 = (bf16[1024,1024]{1,0:T(8,128)(2,1)}, bf16[1024,1024]{1,0:T(8,128)(2,1)}, u32[]{:S(2)}, u32[]{:S(2)}) collective-permute-start(bf16[1024,1024]{1,0:T(8,128)(2,1)} %bitcast.179), channel_id=1, source_target_pairs={{0,1},{1,0},{2,3},{3,2},{4,5},{5,4},{6,7},{7,6},{8,9},{9,8},{10,11... | collective-permute-start | bytes 6291464 | tf_op jit(solution)/shard_map/ppermute | solution.py:719
  245.0 17.7 %collective-permute-start.14 = (bf16[1024,1024]{1,0:T(8,128)(2,1)}, bf16[1024,1024]{1,0:T(8,128)(2,1)}, u32[]{:S(2)}, u32[]{:S(2)}) collective-permute-start(bf16[1024,1024]{1,0:T(8,128)(2,1)} %collective-permute-done.12.refs_5_), channel_id=1, source_target_pairs={{0,1},{1,0},{2,3},{3,2},{4,5},{5,4},{6,7},{7,6},{8,9},{9,8},{10,11... | collective-permute-start | bytes 6291464 | tf_op jit(solution)/shard_map/ppermute | solution.py:719
  256.9 53.6 %all-to-all-start.3 = ((bf16[8,112,1024]{2,1,0:T(8,128)(2,1)}), bf16[8,112,1024]{2,1,0:T(8,128)(2,1)}, u32[]{:S(2)}, u32[]{:S(2)}) async-start(bf16[8,112,1024]{2,1,0:T(8,128)(2,1)} %pack_rows.3), calls=%async_computation.3 | async-start | bytes 3670016 | tf_op jit(solution)/shard_map/all_to_all | solution.py:742
  310.5 53.9 %all-to-all-start.4 = ((bf16[8,112,1024]{2,1,0:T(8,128)(2,1)}), bf16[8,112,1024]{2,1,0:T(8,128)(2,1)}, u32[]{:S(2)}, u32[]{:S(2)}) async-start(bf16[8,112,1024]{2,1,0:T(8,128)(2,1)} %bitcast.169), calls=%async_computation.4 | async-start | bytes 3670016 | tf_op jit(solution)/shard_map/all_to_all | solution.py:742
  364.4 52.5 %all-to-all-start.5 = ((bf16[8,112,1024]{2,1,0:T(8,128)(2,1)}), bf16[8,112,1024]{2,1,0:T(8,128)(2,1)}, u32[]{:S(2)}, u32[]{:S(2)}) async-start(bf16[8,112,1024]{2,1,0:T(8,128)(2,1)} %bitcast.168), calls=%async_computation.5 | async-start | bytes 3670016 | tf_op jit(solution)/shard_map/all_to_all | solution.py:742
  370.5 23.5 %copy-start.30 = (bf16[896,1024]{1,0:T(8,128)(2,1)S(1)}, bf16[896,1024]{1,0:T(8,128)(2,1)}, u32[]{:S(2)}) copy-start(bf16[896,1024]{1,0:T(8,128)(2,1)} %get-tuple-element.109.refs_1_) | copy-start | bytes 5505028
  370.5 23.5 %copy-start.31 = (bf16[896,1024]{1,0:T(8,128)(2,1)S(1)}, bf16[896,1024]{1,0:T(8,128)(2,1)}, u32[]{:S(2)}) copy-start(bf16[896,1024]{1,0:T(8,128)(2,1)} %get-tuple-element.111.refs_3_) | copy-start | bytes 5505028
  435.9 6.0 collective-permute-start.15
  435.9 49.3 %all-to-all-start.6 = ((bf16[8,112,1024]{2,1,0:T(8,128)(2,1)}), bf16[8,112,1024]{2,1,0:T(8,128)(2,1)S(1)}, u32[]{:S(2)}, u32[]{:S(2)}) async-start(bf16[8,112,1024]{2,1,0:T(8,128)(2,1)} %bitcast.167), calls=%async_computation.6 | async-start | bytes 3670016 | tf_op jit(solution)/shard_map/all_to_all | solution.py:742
  446.7 45.5 %collective-permute-start.16 = (bf16[3,208,1152]{2,1,0:T(8,128)(2,1)}, bf16[3,208,1152]{2,1,0:T(8,128)(2,1)}, u32[]{:S(2)}, u32[]{:S(2)}) collective-permute-start(bf16[3,208,1152]{2,1,0:T(8,128)(2,1)} %slice_bitcast_fusion.4), channel_id=1, source_target_pairs={{0,2},{1,3},{2,0},{3,1},{4,6},{5,7},{6,4},{7,5},{8,10},{9,11},{10,... | collective-permute-start | bytes 4313096 | tf_op jit(solution)/shard_map/ppermute | solution.py:719
  485.2 73.3 %all-to-all-start.7 = ((bf16[8,112,1024]{2,1,0:T(8,128)(2,1)}), bf16[8,112,1024]{2,1,0:T(8,128)(2,1)}, u32[]{:S(2)}, u32[]{:S(2)}) async-start(bf16[8,112,1024]{2,1,0:T(8,128)(2,1)} %bitcast.166), calls=%async_computation.7 | async-start | bytes 3670016 | tf_op jit(solution)/shard_map/all_to_all | solution.py:742
  508.4 10.8 %collective-permute-start.17 = (bf16[3,208,256]{2,1,0:T(8,128)(2,1)}, bf16[3,208,256]{2,1,0:T(8,128)(2,1)}, u32[]{:S(2)}, u32[]{:S(2)}) collective-permute-start(bf16[3,208,256]{2,1,0:T(8,128)(2,1)} %get-tuple-element.123), channel_id=1, source_target_pairs={{0,2},{1,3},{2,0},{3,1},{4,6},{5,7},{6,4},{7,5},{8,10},{9,11},{10,... | collective-permute-start | bytes 958472 | tf_op jit(solution)/shard_map/ppermute | solution.py:719
  508.7 10.5 %collective-permute-start.18 = (bf16[3,208,256]{2,1,0:T(8,128)(2,1)}, bf16[3,208,256]{2,1,0:T(8,128)(2,1)}, u32[]{:S(2)}, u32[]{:S(2)}) collective-permute-start(bf16[3,208,256]{2,1,0:T(8,128)(2,1)} %get-tuple-element.124), channel_id=1, source_target_pairs={{0,1},{1,0},{2,3},{3,2},{4,5},{5,4},{6,7},{7,6},{8,9},{9,8},{10,11... | collective-permute-start | bytes 958472 | tf_op jit(solution)/shard_map/ppermute | solution.py:719
  509.2 13.6 %copy-start.8 = (bf16[3,208,256]{2,1,0:T(8,128)(2,1)S(1)}, bf16[3,208,256]{2,1,0:T(8,128)(2,1)}, u32[]{:S(2)}) copy-start(bf16[3,208,256]{2,1,0:T(8,128)(2,1)} %copy-done.7) | copy-start | bytes 958468
  509.2 13.6 %collective-permute-start.19 = (bf16[3,208,256]{2,1,0:T(8,128)(2,1)}, bf16[3,208,256]{2,1,0:T(8,128)(2,1)}, u32[]{:S(2)}, u32[]{:S(2)}) collective-permute-start(bf16[3,208,256]{2,1,0:T(8,128)(2,1)} %get-tuple-element.125), channel_id=1, source_target_pairs={{0,3},{1,2},{2,1},{3,0},{4,7},{5,6},{6,5},{7,4},{8,11},{9,10},{10,... | collective-permute-start | bytes 958472 | tf_op jit(solution)/shard_map/ppermute | solution.py:719
  513.1 88.9 %collective-permute-start.36 = (bf16[2,1024,1024]{2,1,0:T(8,128)(2,1)}, bf16[2,1024,1024]{2,1,0:T(8,128)(2,1)}, u32[]{:S(2)}, u32[]{:S(2)}) collective-permute-start(bf16[2,1024,1024]{2,1,0:T(8,128)(2,1)} %bitcast.174), channel_id=1, source_target_pairs={{0,1},{1,0},{2,3},{3,2},{4,5},{5,4},{6,7},{7,6},{8,9},{9,8},{10,11... | collective-permute-start | bytes 12582920 | tf_op jit(solution)/shard_map/ppermute | solution.py:719
  514.0 10.1 %copy-start.4 = (bf16[3,1024,256]{1,2,0:T(8,128)(2,1)S(1)}, bf16[3,1024,256]{1,2,0:T(8,128)(2,1)}, u32[]{:S(2)}) copy-start(bf16[3,1024,256]{1,2,0:T(8,128)(2,1)} %copy.96) | copy-start | bytes 4718596
  514.0 10.1 %copy-start.14 = (f32[1024]{0:T(1024)S(1)}, f32[1024]{0:T(1024)}, u32[]{:S(2)}) copy-start(f32[1024]{0:T(1024)} %param.12) | copy-start | bytes 12292
  514.0 10.1 %copy-start.33 = (f32[12,208,128]{2,1,0:T(8,128)S(1)}, f32[12,208,128]{2,1,0:T(8,128)}, u32[]{:S(2)}) copy-start(f32[12,208,128]{2,1,0:T(8,128)} %copy-done.32) | copy-start | bytes 3833860
  516.4 42.1 %collective-permute-start.30 = (bf16[2,256,1024]{2,1,0:T(8,128)(2,1)}, bf16[2,256,1024]{2,1,0:T(8,128)(2,1)}, u32[]{:S(2)}, u32[]{:S(2)}) collective-permute-start(bf16[2,256,1024]{2,1,0:T(8,128)(2,1)} %slice.129), channel_id=1, source_target_pairs={{0,1},{1,0},{2,3},{3,2},{4,5},{5,4},{6,7},{7,6},{8,9},{9,8},{10,11... | collective-permute-start | bytes 3145736 | tf_op jit(solution)/shard_map/ppermute | solution.py:719
  560.5 18.2 %collective-permute-start.31 = (bf16[256,1024]{1,0:T(8,128)(2,1)S(1)}, bf16[256,1024]{1,0:T(8,128)(2,1)S(1)}, u32[]{:S(2)}, u32[]{:S(2)}) collective-permute-start(bf16[256,1024]{1,0:T(8,128)(2,1)S(1)} %slice_bitcast_fusion.10), channel_id=1, source_target_pairs={{0,2},{1,3},{2,0},{3,1},{4,6},{5,7},{6,4},{7,5},{8,10},{9,11},{10,... | collective-permute-start | bytes 1572872 | tf_op jit(solution)/shard_map/ppermute | solution.py:719
  578.3 15.7 %collective-permute-start.20 = (bf16[2,3,208,1024]{3,2,1,0:T(8,128)(2,1)}, bf16[2,3,208,1024]{3,2,1,0:T(8,128)(2,1)}, u32[]{:S(2)}, u32[]{:S(2)}) collective-permute-start(bf16[2,3,208,1024]{3,2,1,0:T(8,128)(2,1)} %bitcast.177), channel_id=1, source_target_pairs={{0,1},{1,0},{2,3},{3,2},{4,5},{5,4},{6,7},{7,6},{8,9},{9,8},{10,11... | collective-permute-start | bytes 7667720 | tf_op jit(solution)/shard_map/ppermute | solution.py:719
  581.4 60.3 %all-to-all-start.8 = ((bf16[8,144,1024]{2,1,0:T(8,128)(2,1)}), bf16[8,144,1024]{2,1,0:T(8,128)(2,1)S(1)}, u32[]{:S(2)}, u32[]{:S(2)}) async-start(bf16[8,144,1024]{2,1,0:T(8,128)(2,1)} %bitcast.155), calls=%async_computation.8 | async-start | bytes 4718592 | tf_op jit(solution)/shard_map/all_to_all | solution.py:742
  587.1 236.0 %all-gather.2.cloned.1.call-start = ((), (), s32[]{:S(2)}) async-start(), calls=%async_computation.9 | async-start | bytes 2654208 | tf_op jit(solution)/shard_map/all_gather | solution.py:887
  593.5 64.2 %collective-permute-start.34 = (bf16[2,1024,1024]{1,2,0:T(8,128)(2,1)}, bf16[2,1024,1024]{1,2,0:T(8,128)(2,1)}, u32[]{:S(2)}, u32[]{:S(2)}) collective-permute-start(bf16[2,1024,1024]{1,2,0:T(8,128)(2,1)} %copy.99), channel_id=1, source_target_pairs={{0,1},{1,0},{2,3},{3,2},{4,5},{5,4},{6,7},{7,6},{8,9},{9,8},{10,11... | collective-permute-start | bytes 12582920 | tf_op jit(solution)/shard_map/ppermute | solution.py:719
  593.8 14.5 %collective-permute-start.25 = (bf16[2,3,208,1024]{3,2,1,0:T(8,128)(2,1)}, bf16[2,3,208,1024]{3,2,1,0:T(8,128)(2,1)S(1)}, u32[]{:S(2)}, u32[]{:S(2)}) collective-permute-start(bf16[2,3,208,1024]{3,2,1,0:T(8,128)(2,1)} %bitcast.176), channel_id=1, source_target_pairs={{0,1},{1,0},{2,3},{3,2},{4,5},{5,4},{6,7},{7,6},{8,9},{9,8},{10,11... | collective-permute-start | bytes 7667720 | tf_op jit(solution)/shard_map/ppermute | solution.py:719
  594.0 8.1 copy-start.43
  600.5 7.9 copy-start.44
  600.5 53.8 %collective-permute-start.21 = (bf16[3,208,1024]{2,1,0:T(8,128)(2,1)}, bf16[3,208,1024]{2,1,0:T(8,128)(2,1)}, u32[]{:S(2)}, u32[]{:S(2)}) collective-permute-start(bf16[3,208,1024]{2,1,0:T(8,128)(2,1)} %slice_bitcast_fusion.8), channel_id=1, source_target_pairs={{0,2},{1,3},{2,0},{3,1},{4,6},{5,7},{6,4},{7,5},{8,10},{9,11},{10,... | collective-permute-start | bytes 3833864 | tf_op jit(solution)/shard_map/ppermute | solution.py:719
  612.5 55.0 %collective-permute-start.26 = (bf16[3,208,1024]{2,1,0:T(8,128)(2,1)}, bf16[3,208,1024]{2,1,0:T(8,128)(2,1)}, u32[]{:S(2)}, u32[]{:S(2)}) collective-permute-start(bf16[3,208,1024]{2,1,0:T(8,128)(2,1)} %slice_bitcast_fusion.6), channel_id=1, source_target_pairs={{0,2},{1,3},{2,0},{3,1},{4,6},{5,7},{6,4},{7,5},{8,10},{9,11},{10,... | collective-permute-start | bytes 3833864 | tf_op jit(solution)/shard_map/ppermute | solution.py:719
  646.1 85.4 %collective-permute-start.37 = (bf16[1024,1024]{1,0:T(8,128)(2,1)}, bf16[1024,1024]{1,0:T(8,128)(2,1)}, u32[]{:S(2)}, u32[]{:S(2)}) collective-permute-start(bf16[1024,1024]{1,0:T(8,128)(2,1)} %slice_bitcast_fusion), channel_id=1, source_target_pairs={{0,2},{1,3},{2,0},{3,1},{4,6},{5,7},{6,4},{7,5},{8,10},{9,11},{10,... | collective-permute-start | bytes 6291464 | tf_op jit(solution)/shard_map/ppermute | solution.py:719
  657.6 73.9 %collective-permute-start.22 = (bf16[3,208,1024]{2,1,0:T(8,128)(2,1)S(1)}, bf16[3,208,1024]{2,1,0:T(8,128)(2,1)}, u32[]{:S(2)}, u32[]{:S(2)}) collective-permute-start(bf16[3,208,1024]{2,1,0:T(8,128)(2,1)S(1)} %fusion.6), channel_id=1, source_target_pairs={{0,2},{1,3},{2,0},{3,1},{4,6},{5,7},{6,4},{7,5},{8,10},{9,11},{10,... | collective-permute-start | bytes 3833864 | tf_op jit(solution)/shard_map/ppermute | solution.py:719
  665.8 142.8 %collective-permute-start.35 = (bf16[1024,1024]{0,1:T(8,128)(2,1)}, bf16[1024,1024]{0,1:T(8,128)(2,1)}, u32[]{:S(2)}, u32[]{:S(2)}) collective-permute-start(bf16[1024,1024]{0,1:T(8,128)(2,1)} %slice_bitcast_fusion.2), channel_id=1, source_target_pairs={{0,2},{1,3},{2,0},{3,1},{4,6},{5,7},{6,4},{7,5},{8,10},{9,11},{10,... | collective-permute-start | bytes 6291464 | tf_op jit(solution)/shard_map/ppermute | solution.py:719
  673.1 130.1 %collective-permute-start.27 = (bf16[3,208,1024]{2,1,0:T(8,128)(2,1)S(1)}, bf16[3,208,1024]{2,1,0:T(8,128)(2,1)}, u32[]{:S(2)}, u32[]{:S(2)}) collective-permute-start(bf16[3,208,1024]{2,1,0:T(8,128)(2,1)S(1)} %input_back.1), channel_id=1, source_target_pairs={{0,2},{1,3},{2,0},{3,1},{4,6},{5,7},{6,4},{7,5},{8,10},{9,11},{10,... | collective-permute-start | bytes 3833864 | tf_op jit(solution)/shard_map/ppermute | solution.py:719
  674.0 139.1 %collective-permute-start.23 = (bf16[3,208,1024]{2,1,0:T(8,128)(2,1)S(1)}, bf16[3,208,1024]{2,1,0:T(8,128)(2,1)}, u32[]{:S(2)}, u32[]{:S(2)}) collective-permute-start(bf16[3,208,1024]{2,1,0:T(8,128)(2,1)S(1)} %fusion.6), channel_id=1, source_target_pairs={{0,1},{1,0},{2,3},{3,2},{4,5},{5,4},{6,7},{7,6},{8,9},{9,8},{10,11... | collective-permute-start | bytes 3833864 | tf_op jit(solution)/shard_map/ppermute | solution.py:719
  731.4 81.7 %collective-permute-start.24 = (bf16[3,208,1024]{2,1,0:T(8,128)(2,1)}, bf16[3,208,1024]{2,1,0:T(8,128)(2,1)}, u32[]{:S(2)}, u32[]{:S(2)}) collective-permute-start(bf16[3,208,1024]{2,1,0:T(8,128)(2,1)} %collective-permute-done.22), channel_id=1, source_target_pairs={{0,1},{1,0},{2,3},{3,2},{4,5},{5,4},{6,7},{7,6},{8,9},{9,8},{10,11... | collective-permute-start | bytes 3833864 | tf_op jit(solution)/shard_map/ppermute | solution.py:719
  731.5 92.9 %collective-permute-start.28 = (bf16[3,208,1024]{2,1,0:T(8,128)(2,1)S(1)}, bf16[3,208,1024]{2,1,0:T(8,128)(2,1)}, u32[]{:S(2)}, u32[]{:S(2)}) collective-permute-start(bf16[3,208,1024]{2,1,0:T(8,128)(2,1)S(1)} %input_back.1), channel_id=1, source_target_pairs={{0,1},{1,0},{2,3},{3,2},{4,5},{5,4},{6,7},{7,6},{8,9},{9,8},{10,11... | collective-permute-start | bytes 3833864 | tf_op jit(solution)/shard_map/ppermute | solution.py:719
  803.2 21.1 %collective-permute-start.29 = (bf16[3,208,1024]{2,1,0:T(8,128)(2,1)}, bf16[3,208,1024]{2,1,0:T(8,128)(2,1)}, u32[]{:S(2)}, u32[]{:S(2)}) collective-permute-start(bf16[3,208,1024]{2,1,0:T(8,128)(2,1)} %collective-permute-done.27), channel_id=1, source_target_pairs={{0,1},{1,0},{2,3},{3,2},{4,5},{5,4},{6,7},{7,6},{8,9},{9,8},{10,11... | collective-permute-start | bytes 3833864 | tf_op jit(solution)/shard_map/ppermute | solution.py:719
  823.8 11.4 %collective-permute-start.32 = (f32[10,1024]{1,0:T(8,128)S(1)}, f32[10,1024]{1,0:T(8,128)S(1)}, u32[]{:S(2)}, u32[]{:S(2)}) collective-permute-start(f32[10,1024]{1,0:T(8,128)S(1)} %slice_convert_fusion.1), channel_id=1, source_target_pairs={{0,1},{1,0},{2,3},{3,2},{4,5},{5,4},{6,7},{7,6},{8,9},{9,8},{10,11... | collective-permute-start | bytes 122888 | tf_op jit(solution)/shard_map/ppermute | solution.py:719
  824.3 10.9 %copy-start.41 = (bf16[1152,1024]{1,0:T(8,128)(2,1)S(1)}, bf16[1152,1024]{1,0:T(8,128)(2,1)}, u32[]{:S(2)}) copy-start(bf16[1152,1024]{1,0:T(8,128)(2,1)} %all-gather.2.cloned.1.call-done) | copy-start | bytes 7077892
  835.2 4.9 collective-permute-start.33
  (35 other events, 115.0 us)
Sparse Core Ops, SparseCore 0:
  643.0 51.3 all-gather.1

commit v3 on v2

--- a/solution.py
+++ b/solution.py
@@ -725,12 +725,31 @@
         far, near = cross(x, 2), cross(x, 1)
         return [x, far, near, cross(far, 1)]
 
+    def near_hop(high):
+        return cross(high, 1) if paired else high
+
+    def near_sum(low, came):
+        if not paired:
+            return jnp.concatenate([low, came], 0)
+        return (low.astype(F32) + came.astype(F32)).astype(BF)
+
+    def far_hop(both):
+        if not paired:
+            return lax.psum_scatter(both, "tensor", scatter_dimension=0)
+        return cross(both[1], 2)
+
+    def far_sum(both, came):
+        return both[0].astype(F32) + came.astype(F32) if paired else came.astype(F32)
+
     def scattered(low, high):
-        if not paired:
-            both = jnp.concatenate([low, high], 0)
-            return lax.psum_scatter(both, "tensor", scatter_dimension=0).astype(F32)
-        both = (low.astype(F32) + cross(high, 1).astype(F32)).astype(BF)
-        return both[0].astype(F32) + cross(both[1], 2).astype(F32)
+        both = near_sum(low, near_hop(high))
+        return far_sum(both, far_hop(both))
+
+    def far_part(x):
+        return cross(x, 2) if paired else x
+
+    def gathered_from(x, far):
+        return [x, far, cross(x, 1), cross(far, 1)] if paired else gathered(x)
 
     def swapped(pieces):
         if not paired:
@@ -794,7 +813,7 @@
     router_wide = jnp.pad(router, ((0, 0), (0, LANES - experts)))
     gain_one, gain_two = norm_one[None, :], norm_two[None, :]
     head_out_all = gathered(head_out)
-    w1 = gathered(expert_in[0])
+    w1_far = far_part(expert_in[0])
 
     tail = tail_of(cotangent)
     packed = [
@@ -806,21 +825,25 @@
     mixed, first_in, qkv, logs = attend(
         image_order, block_rows, tail_of(block_in), gain_one, head_in, images, image_slots, height
     )
+    mixed, w1_far, late_out = pinned(mixed, w1_far, expert_out[0])
+    w1 = gathered_from(expert_in[0], w1_far)
+    w2_far = far_part(late_out)
     mixed = swapped([mixed[p * own : (p + 1) * own] for p in range(parts)])
-    *mixed, signals[0] = pinned(*mixed, signals[0])
     x_own = own_images(block_in)
     valid = (me * own + jnp.arange(own) < images)[:, None, None]
     up_own = jnp.where(valid, own_images(cotangent), 0)
     middle, second_in, gates = middle_of(
         mixed, head_out_all, x_own, gain_two, router_wide, ids_own, noise_own
     )
-    *second_all, late_out, signals[-1] = pinned(*gathered(second_in), expert_out[0], signals[-1])
-    w2 = gathered(late_out)
+    second_in, signals[0] = pinned(second_in, signals[0])
+    *second_all, signals[-1], w2_far = pinned(*gathered(second_in), signals[-1], w2_far)
+    w2 = gathered_from(expert_out[0], w2_far)
     second_all = [item.reshape(own * height, width) for item in second_all]
 
     outgoing = [pack(second_all, place_lanes, experts, slots, n * chunk_rows) for n in range(CHUNKS)]
     backs, actives, hidden_grads, rows_grads, arrived, returned = [], [], [], [], [], []
-    x = over_experts(outgoing[0])
+    x, *ready = pinned(over_experts(outgoing[0]), *w1, *w2)
+    w1, w2 = ready[:parts], ready[parts:]
     for n in range(CHUNKS):
         coming = None
         if n + 1 < CHUNKS:
@@ -840,8 +863,11 @@
 
     out_low, out_high = weight_grad(actives, rows_grads, parts)
     in_low, in_high = weight_grad(hidden_grads, arrived, parts)
-    *returned, in_low, in_high, out_low, out_high = pinned(*returned, in_low, in_high, out_low, out_high)
-    out_grad = scattered(out_low, out_high)
+    out_came, in_low, in_high = pinned(near_hop(out_high), in_low, in_high)
+    out_both = near_sum(out_low, out_came)
+    *returned, in_low, in_high, out_both = pinned(*returned, in_low, in_high, out_both)
+    out_far = far_hop(out_both)
+    in_came = near_hop(in_high)
 
     def whole_rows(items):
         return [item.reshape(chunk_rows, width) for item in items]
@@ -850,18 +876,22 @@
         return x.reshape((parts // 2, own) + x.shape[1:])
 
     low, high = unpack(place_images, whole_rows(returned), slots, per, True)
-    second_sum = scattered(by_part(low), by_part(high))
+    low, high, in_came = pinned(low, high, in_came)
+    in_both = near_sum(in_low, in_came)
+    second_sum, in_both = pinned(scattered(by_part(low), by_part(high)), in_both)
+    in_far = far_hop(in_both)
     combined = [over_experts(item.reshape(experts, slots, width)) for item in backs]
-    second_sum, combined[0] = pinned(second_sum, combined[0])
     middle_grad, head_out_part, router_part, norm_two_part, *mixed_grad = middle_back(
         second_sum, middle, second_in, gates, ids_own, up_own, mixed, head_out_all, gain_two, router_wide
     )
-    *mixed_grad, in_low, in_high = pinned(*swapped(mixed_grad), in_low, in_high)
-    in_grad = scattered(in_low, in_high)
+    *mixed_grad, combined[0], out_far = pinned(*mixed_grad, combined[0], out_far)
+    out_grad = far_sum(out_both, out_far)
+    mixed_grad = swapped(mixed_grad)
     first_low, first_high, head_in_part, norm_one_part = attend_back(
         jnp.concatenate(mixed_grad, 0), qkv, logs, first_in, jnp.swapaxes(head_in, 1, 2), gain_one
     )
-    first_low, first_high, combined[-1] = pinned(first_low, first_high, combined[-1])
+    first_low, first_high, combined[-1], in_far = pinned(first_low, first_high, combined[-1], in_far)
+    in_grad = far_sum(in_both, in_far)
     first_grad = scattered(by_part(first_low), by_part(first_high))
     input_part = input_back(first_grad, x_own, middle_grad, gain_one)
 

time: 856 us -> 834 us (0.974)
  waiting for transfers between devices: 321 us -> 306 us
    ppermute x38, waiting for transfers between devices: 241 us -> 232 us  [cross(): return lax.ppermute(x, 'tensor', [(n, n ^ k) for n in range(parts)])]
    unnamed x99 -> x125, local copies, waits for them, and re-layouts: 16.4 us -> 19.7 us
  transfers between devices with their start and end apart: 48 -> 48, of which waited for: 12 -> 21; matrix products, arithmetic and copies ran while one was open for 11% -> 10% of each run, Pallas kernels for 33% -> 35%
where the time goes in v3:
time: 834 us; the launch traced here: 826 us
  Pallas kernels  326 us (39%)
  waiting for transfers between devices  306 us (37%)
  starting transfers between devices  66.4 us (8%)
  local copies, waits for them, and re-layouts  59.7 us (7%)
  other arithmetic  52.9 us (6%)
  between operations  15.2 us (2%)
    ppermute x38, waiting for transfers between devices, cross(): return lax.ppermute(x, 'tensor', [(n, n ^ k) for n in range(parts)])  232 us
    pallas_call x2, Pallas kernels, expert(): pl.pallas_call(functools.partial(expert_kernel, count, slots, per), grid=...  95.7 us
    all_to_all x9, waiting for transfers between devices, over_experts(): return lax.all_to_all(x, 'expert', split_axis=0, concat_axis=0, tiled=True)  74.2 us
    all_to_all x9, starting transfers between devices, over_experts(): return lax.all_to_all(x, 'expert', split_axis=0, concat_axis=0, tiled=True)  49.7 us
    pallas_call x2, Pallas kernels, weight_grad(): pl.pallas_call(functools.partial(weight_kernel, count), grid=(steps,), in...  46.3 us
    pallas_call x2, Pallas kernels, unpack(): pl.pallas_call(functools.partial(unpack_kernel, count, slots, per, graded...  36 us
    pallas_call x1, Pallas kernels, attend_back(): pl.pallas_call(attend_back_kernel, grid=(image_slots,), in_specs=[image(h...  33.2 us
    pallas_call x1, Pallas kernels, attend(): pl.pallas_call(functools.partial(attend_kernel, images), grid_spec=spec,...  28.7 us
  transfers between devices with their start and end apart: 48, of which 21 were waited for; matrix products, arithmetic and copies ran while one was open for 10% of the time, Pallas kernels for 35%

profile of v3, /device:TPU:0, one launch (start us, length us, event | category | flops | bytes accessed | tf_op | source)
XLA Modules:
  0.0 826.4 jit_solution(1725140091682854290)
XLA Ops:
  8.1 2.3 reduce-window.6
  13.4 11.5 %pack_cotangent.2 = bf16[8,112,1152]{2,1,0:T(8,128)(2,1)} custom-call(bf16[2167,1024]{1,0:T(8,128)(2,1)} %x_ref.3, bf16[16,1024]{1,0:T(8,128)(2,1)S(1)} %pad.56.tail_ref, s32[2,2176]{1,0:T(2,128)S(1)} %pad.58.lp_ref, bf16[2,2176,128]{2,1,0:T(8,128)(2,1)S(1)} %fusion.13.side_ref), custom_call_target="tpu_custom_call" | custom-call | flops 5989466112 | bytes 4438016 | tf_op jit(solution)/shard_map/pack_cotangent/pallas_call | solution.py:273
  24.9 11.5 %pack_cotangent.3 = bf16[8,112,1152]{2,1,0:T(8,128)(2,1)} custom-call(bf16[2167,1024]{1,0:T(8,128)(2,1)} %x_ref.3, bf16[16,1024]{1,0:T(8,128)(2,1)S(1)} %pad.56.tail_ref, s32[2,2176]{1,0:T(2,128)S(1)} %pad.58.lp_ref, bf16[2,2176,128]{2,1,0:T(8,128)(2,1)S(1)} %fusion.13.side_ref), custom_call_target="tpu_custom_call" | custom-call | flops 5989466112 | bytes 4438016 | tf_op jit(solution)/shard_map/pack_cotangent/pallas_call | solution.py:273
  36.4 7.4 all-to-all-start
  46.0 28.7 %attend.1 = (bf16[12,208,256]{2,1,0:T(8,128)(2,1)S(1)}, bf16[12,208,1024]{2,1,0:T(8,128)(2,1)}, bf16[3,12,208,256]{3,2,1,0:T(8,128)(2,1)}, f32[12,208,128]{2,1,0:T(8,128)S(1)}) custom-call(s32[12]{0:T(128)S(1)} %pad_add_fusion.2.order_ref, bf16[2167,1024]{1,0:T(8,128)(2,1)} %x_ref.4, bf16[16,1024]{1,0:T(8,128)(2,1)S(1)} %pad.60.tail_ref, ...), custom_call_target="tpu_custom_call" | custom-call | flops 10468982784 | bytes 35504128 | tf_op jit(solution)/shard_map/attend/pallas_call | solution.py:160
  76.3 2.5 constant_dynamic-slice_fusion.5
  78.8 12.7 %all-to-all-done = bf16[8,112,1152]{2,1,0:T(8,128)(2,1)} async-done(((bf16[8,112,1152]{2,1,0:T(8,128)(2,1)}), bf16[8,112,1152]{2,1,0:T(8,128)(2,1)}, u32[]{:S(2)}, u32[]{:S(2)}) %all-to-all-start) | async-done | bytes 2064416 | tf_op jit(solution)/shard_map/all_to_all | solution.py:761
  91.5 4.5 all-to-all-start.1
  98.4 4.1 collective-permute-done.4.refs_5_.refs_13_
  108.4 5.6 collective-permute-done.1.refs_1_.refs_9_
  114.8 5.3 collective-permute-done.3.refs_3_.refs_11_
  122.8 6.3 middle.1
  131.9 28.9 %collective-permute-done.7 = bf16[3,208,1024]{2,1,0:T(8,128)(2,1)} collective-permute-done((bf16[3,208,1024]{2,1,0:T(8,128)(2,1)S(1)}, bf16[3,208,1024]{2,1,0:T(8,128)(2,1)}, u32[]{:S(2)}, u32[]{:S(2)}) %collective-permute-start.7) | collective-permute-done | bytes 1277984 | tf_op jit(solution)/shard_map/ppermute | solution.py:719
  162.1 43.4 %collective-permute-done.10.refs_5_ = bf16[1024,1024]{1,0:T(8,128)(2,1)} collective-permute-done((bf16[1024,1024]{1,0:T(8,128)(2,1)}, bf16[1024,1024]{1,0:T(8,128)(2,1)}, u32[]{:S(2)}, u32[]{:S(2)}) %collective-permute-start.10) | collective-permute-done | bytes 2097184 | tf_op jit(solution)/shard_map/ppermute | solution.py:719
  205.5 10.5 %pack_rows.2 = bf16[8,112,1024]{2,1,0:T(8,128)(2,1)} custom-call(bf16[624,1024]{1,0:T(8,128)(2,1)S(1)} %bitcast.150, bf16[624,1024]{1,0:T(8,128)(2,1)} %bitcast.17.refs_1_, bf16[624,1024]{1,0:T(8,128)(2,1)} %bitcast.18.refs_2_, bf16[624,1024]{1,0:T(8,128)(2,1)} %bitcast.19.refs_3_, s32[4,2,624]{2,1,0:T(2,128)S(1)} %bitcast.145), custom_call_target="tpu_custom_call" | custom-call | flops 6870269952 | bytes 5111808 | tf_op jit(solution)/shard_map/pack_rows/pallas_call | solution.py:300
  216.0 5.7 all-to-all-start.2
  224.1 10.6 %pack_rows.3 = bf16[8,112,1024]{2,1,0:T(8,128)(2,1)} custom-call(bf16[624,1024]{1,0:T(8,128)(2,1)S(1)} %bitcast.151, bf16[624,1024]{1,0:T(8,128)(2,1)} %bitcast.17.refs_1_, bf16[624,1024]{1,0:T(8,128)(2,1)} %bitcast.18.refs_2_, bf16[624,1024]{1,0:T(8,128)(2,1)} %bitcast.19.refs_3_, s32[4,2,624]{2,1,0:T(2,128)S(1)} %bitcast.146), custom_call_target="tpu_custom_call" | custom-call | flops 6870269952 | bytes 5111808 | tf_op jit(solution)/shard_map/pack_rows/pallas_call | solution.py:300
  238.0 26.4 %all-to-all-done.2 = bf16[8,112,1024]{2,1,0:T(8,128)(2,1)S(1)} async-done(((bf16[8,112,1024]{2,1,0:T(8,128)(2,1)}), bf16[8,112,1024]{2,1,0:T(8,128)(2,1)S(1)}, u32[]{:S(2)}, u32[]{:S(2)}) %all-to-all-start.2) | async-done | bytes 1835040 | tf_op jit(solution)/shard_map/all_to_all | solution.py:761
  264.4 4.3 all-to-all-start.3
  268.7 47.8 %expert.2 = (bf16[896,1024]{1,0:T(8,128)(2,1)}, bf16[896,4096]{1,0:T(8,128)(2,1)}, bf16[896,4096]{1,0:T(8,128)(2,1)}, bf16[896,1024]{1,0:T(8,128)(2,1)}, bf16[896,1024]{1,0:T(8,128)(2,1)}) custom-call(bf16[896,1024]{1,0:T(8,128)(2,1)} %bitcast.141, bf16[896,1152]{1,0:T(8,128)(2,1)} %bitcast.23.g_ref, bf16[1024,128]{1,0:T(8,128)(2,1)} %copy-done.9, ...), custom_call_target="tpu_custom_call" | custom-call | flops 30064771072 | bytes 22020096 | tf_op jit(solution)/shard_map/expert/pallas_call | solution.py:629
  316.5 5.9 all-to-all-start.4
  322.4 48.0 %expert.3 = (bf16[896,1024]{1,0:T(8,128)(2,1)}, bf16[896,4096]{1,0:T(8,128)(2,1)}, bf16[896,4096]{1,0:T(8,128)(2,1)}, bf16[896,1024]{1,0:T(8,128)(2,1)}, bf16[896,1024]{1,0:T(8,128)(2,1)}) custom-call(bf16[896,1024]{1,0:T(8,128)(2,1)} %bitcast.25.x_ref.refs_3_, bf16[896,1152]{1,0:T(8,128)(2,1)} %bitcast.26.g_ref, bf16[1024,128]{1,0:T(8,128)(2,1)} %copy-done.9, ...), custom_call_target="tpu_custom_call" | custom-call | flops 30064771072 | bytes 22020096 | tf_op jit(solution)/shard_map/expert/pallas_call | solution.py:629
  371.9 22.7 %weight_grad.2 = (bf16[4,512,1024]{2,1,0:T(8,128)(2,1)}, bf16[4,512,1024]{2,1,0:T(8,128)(2,1)}) custom-call(bf16[896,4096]{1,0:T(8,128)(2,1)} %get-tuple-element.128.refs_0_, bf16[896,1024]{1,0:T(8,128)(2,1)S(1)} %copy-done.33, bf16[896,4096]{1,0:T(8,128)(2,1)} %get-tuple-element.130.refs_2_, bf16[896,1024]{1,0:T(8,128)(2,1)S(1)} %copy-done.34), custom_call_target="tpu_custom_call" | custom-call | flops 15032385536 | bytes 16777216 | tf_op jit(solution)/shard_map/weight_grad/pallas_call | solution.py:670
  394.7 6.1 all-to-all-start.5
  400.8 23.5 %weight_grad.3 = (bf16[4,512,1024]{2,1,0:T(8,128)(2,1)}, bf16[4,512,1024]{2,1,0:T(8,128)(2,1)}) custom-call(bf16[896,4096]{1,0:T(8,128)(2,1)} %get-tuple-element.133.refs_0_, bf16[896,1024]{1,0:T(8,128)(2,1)S(1)} %bitcast.142, bf16[896,4096]{1,0:T(8,128)(2,1)} %get-tuple-element.134.refs_2_, bf16[896,1024]{1,0:T(8,128)(2,1)} %bitcast.25.x_ref.refs_3_), custom_call_target="tpu_custom_call" | custom-call | flops 15032385536 | bytes 16777216 | tf_op jit(solution)/shard_map/weight_grad/pallas_call | solution.py:670
  424.3 6.4 fusion
  430.7 13.3 %all-to-all-done.5 = bf16[8,112,1024]{2,1,0:T(8,128)(2,1)} async-done(((bf16[8,112,1024]{2,1,0:T(8,128)(2,1)}), bf16[8,112,1024]{2,1,0:T(8,128)(2,1)}, u32[]{:S(2)}, u32[]{:S(2)}) %all-to-all-start.5) | async-done | bytes 1835040 | tf_op jit(solution)/shard_map/all_to_all | solution.py:761
  444.0 6.2 copy.96
  450.2 19.0 %unpack_rows.2 = (bf16[6,208,1152]{2,1,0:T(8,128)(2,1)}, bf16[6,208,1152]{2,1,0:T(8,128)(2,1)}) custom-call(s32[12,208,2]{2,1,0:T(8,128)S(1)} %pad_add_fusion.lp_ref, bf16[896,1024]{1,0:T(8,128)(2,1)} %bitcast.32.refs_0_, bf16[896,1024]{1,0:T(8,128)(2,1)} %bitcast.33.refs_1_), custom_call_target="tpu_custom_call" | custom-call | flops 13740539904 | bytes 7340032 | tf_op jit(solution)/shard_map/unpack_rows/pallas_call | solution.py:351
  469.7 2.5 constant_dynamic-slice_fusion.2
  472.2 3.8 all-to-all-start.6
  476.1 3.4 fusion.1
  483.7 6.2 copy.97
  489.9 3.3 slice_bitcast_fusion.1
  494.0 6.3 add_convert_fusion
  500.4 15.1 %collective-permute-done.18 = bf16[3,208,1152]{2,1,0:T(8,128)(2,1)} collective-permute-done((bf16[3,208,1152]{2,1,0:T(8,128)(2,1)}, bf16[3,208,1152]{2,1,0:T(8,128)(2,1)}, u32[]{:S(2)}, u32[]{:S(2)}) %collective-permute-start.18) | collective-permute-done | bytes 1437728 | tf_op jit(solution)/shard_map/ppermute | solution.py:719
  515.4 3.3 convert_add_fusion.6.refs_0_
  518.8 11.5 %middle_back.1 = (f32[3,208,1024]{2,1,0:T(8,128)}, bf16[4,256,1024]{2,1,0:T(8,128)(2,1)}, f32[128,1024]{1,0:T(8,128)S(1)}, f32[1,1024]{1,0:T(1,128)S(1)}, bf16[3...) custom-call(f32[3,208,1152]{2,1,0:T(8,128)} %convert_add_fusion.6.re, ...), custom_call_target="tpu_custom_call" | custom-call | flops 5234491392 | bytes 25559040 | tf_op jit(solution)/shard_map/middle_back/pallas_call | solution.py:503
  534.0 2.3 slice.131
  536.2 2.6 copy.98
  538.8 6.2 all-to-all-start.7
  545.0 14.4 %collective-permute-done.19 = bf16[1024,1024]{1,0:T(8,128)(2,1)} collective-permute-done((bf16[1024,1024]{1,0:T(8,128)(2,1)}, bf16[1024,1024]{1,0:T(8,128)(2,1)}, u32[]{:S(2)}, u32[]{:S(2)}) %collective-permute-start.19) | collective-permute-done | bytes 2097184 | tf_op jit(solution)/shard_map/ppermute | solution.py:719
  561.5 3.1 slice_bitcast_fusion
  566.9 2.5 collective-permute-done.22
  569.4 6.9 collective-permute-done.20
  578.6 33.2 %attend_back.1 = (bf16[6,208,1024]{2,1,0:T(8,128)(2,1)}, bf16[6,208,1024]{2,1,0:T(8,128)(2,1)}, bf16[3,256,1024]{2,1,0:T(8,128)(2,1)S(1)}, f32[1,1024]{1,0:T(1,128)S(1)}) custom-call(bf16[12,208,256]{2,1,0:T(8,128)(2,1)S(1)} %pad_maximum_fusion.2.dmix_ref, bf16[3,12,208,256]{3,2,1,0:T(8,128)(2,1)} %get-tuple-element.163.qkv_ref, ...), custom_call_target="tpu_custom_call" | custom-call | flops 15703474176 | bytes 51118080 | tf_op jit(solution)/shard_map/attend_back/pallas_call | solution.py:233
  611.8 20.6 %collective-permute-done.35 = bf16[256,1024]{1,0:T(8,128)(2,1)S(1)} collective-permute-done((bf16[256,1024]{1,0:T(8,128)(2,1)S(1)}, bf16[256,1024]{1,0:T(8,128)(2,1)S(1)}, u32[]{:S(2)}, u32[]{:S(2)}) %collective-permute-start.35) | collective-permute-done | bytes 524320 | tf_op jit(solution)/shard_map/ppermute | solution.py:719
  634.3 5.7 all-to-all-start.8
  640.0 16.9 %unpack_rows.3 = (bf16[6,208,1024]{2,1,0:T(8,128)(2,1)}, bf16[6,208,1024]{2,1,0:T(8,128)(2,1)}) custom-call(s32[12,208,2]{2,1,0:T(8,128)S(1)} %pad_add_fusion.lp_ref, bf16[896,1024]{1,0:T(8,128)(2,1)S(1)} %bitcast.140, bf16[896,1024]{1,0:T(8,128)(2,1)} %bitcast.47.refs_1_), custom_call_target="tpu_custom_call" | custom-call | flops 13740539904 | bytes 7340032 | tf_op jit(solution)/shard_map/unpack_rows/pallas_call | solution.py:351
  657.5 7.5 collective-permute-done.24
  665.0 3.0 fusion.3
  672.4 21.8 %all-to-all-done.8 = bf16[8,144,1024]{2,1,0:T(8,128)(2,1)} async-done(((bf16[8,144,1024]{2,1,0:T(8,128)(2,1)}), bf16[8,144,1024]{2,1,0:T(8,128)(2,1)}, u32[]{:S(2)}, u32[]{:S(2)}) %all-to-all-start.8) | async-done | bytes 2359328 | tf_op jit(solution)/shard_map/all_to_all | solution.py:761
  694.2 2.9 reduce_sum.32
  697.6 2.5 collective-permute-done.25
  700.1 2.7 fusion.7
  702.9 25.4 %collective-permute-done.30 = bf16[3,208,1024]{2,1,0:T(8,128)(2,1)S(1)} collective-permute-done((bf16[3,208,1024]{2,1,0:T(8,128)(2,1)S(1)}, bf16[3,208,1024]{2,1,0:T(8,128)(2,1)S(1)}, u32[]{:S(2)}, u32[]{:S(2)}) %collective-permute-start.30) | collective-permute-done | bytes 1277984 | tf_op jit(solution)/shard_map/ppermute | solution.py:719
  728.8 3.5 input_back.1
  732.6 23.1 %collective-permute-done.26 = bf16[3,208,1024]{2,1,0:T(8,128)(2,1)} collective-permute-done((bf16[3,208,1024]{2,1,0:T(8,128)(2,1)S(1)}, bf16[3,208,1024]{2,1,0:T(8,128)(2,1)}, u32[]{:S(2)}, u32[]{:S(2)}) %collective-permute-start.26) | collective-permute-done | bytes 1277984 | tf_op jit(solution)/shard_map/ppermute | solution.py:719
  756.3 25.4 %collective-permute-done.31 = bf16[3,208,1024]{2,1,0:T(8,128)(2,1)} collective-permute-done((bf16[3,208,1024]{2,1,0:T(8,128)(2,1)S(1)}, bf16[3,208,1024]{2,1,0:T(8,128)(2,1)}, u32[]{:S(2)}, u32[]{:S(2)}) %collective-permute-start.31) | collective-permute-done | bytes 1277984 | tf_op jit(solution)/shard_map/ppermute | solution.py:719
  781.8 5.3 fusion.4
  787.1 4.5 fusion.5
  791.6 10.0 %to_rows.2 = bf16[2167,1024]{1,0:T(8,128)(2,1)} custom-call(s32[4]{0:T(128)S(1)} %pad_add_fusion.1.start_ref, bf16[624,1024]{1,0:T(8,128)(2,1)S(1)} %bitcast.137, bf16[624,1024]{1,0:T(8,128)(2,1)} %bitcast.53.refs_1_, bf16[624,1024]{1,0:T(8,128)(2,1)} %bitcast.54.refs_2_, bf16[624,1024]{1,0:T(8,128)(2,1)} %bitcast.55.refs_3_), custom_call_target="tpu_custom_call" | custom-call | flops 1136132096 | bytes 17752064 | tf_op jit(solution)/shard_map/to_rows/pallas_call | solution.py:396
  802.8 10.9 %to_rows.3 = f32[2167,1024]{1,0:T(8,128)} custom-call(s32[4]{0:T(128)S(1)} %pad_add_fusion.1.start_ref, bf16[624,1024]{1,0:T(8,128)(2,1)S(1)} %bitcast.139, bf16[624,1024]{1,0:T(8,128)(2,1)} %bitcast.61.refs_1_, bf16[624,1024]{1,0:T(8,128)(2,1)} %bitcast.62.refs_2_, bf16[624,1024]{1,0:T(8,128)(2,1)} %bitcast.63.refs_3_), custom_call_target="tpu_custom_call" | custom-call | flops 1136132096 | bytes 17752064 | tf_op jit(solution)/shard_map/to_rows/pallas_call | solution.py:396
  815.3 2.1 copy.99
  (265 shorter events, 59.8 us)
Async XLA Ops:
  36.4 55.1 %all-to-all-start = ((bf16[8,112,1152]{2,1,0:T(8,128)(2,1)}), bf16[8,112,1152]{2,1,0:T(8,128)(2,1)}, u32[]{:S(2)}, u32[]{:S(2)}) async-start(bf16[8,112,1152]{2,1,0:T(8,128)(2,1)} %pack_cotangent.2), calls=%async_computation | async-start | bytes 4128768 | tf_op jit(solution)/shard_map/all_to_all | solution.py:761
  43.9 58.6 %collective-permute-start = (bf16[1024,1024]{1,0:T(8,128)(2,1)}, bf16[1024,1024]{1,0:T(8,128)(2,1)}, u32[]{:S(2)}, u32[]{:S(2)}) collective-permute-start(bf16[1024,1024]{1,0:T(8,128)(2,1)} %bitcast.177), channel_id=1, source_target_pairs={{0,2},{1,3},{2,0},{3,1},{4,6},{5,7},{6,4},{7,5},{8,10},{9,11},{10,... | collective-permute-start | bytes 6291464 | tf_op jit(solution)/shard_map/ppermute | solution.py:719
  45.3 57.2 %collective-permute-start.4 = (bf16[256,1024]{1,0:T(8,128)(2,1)}, bf16[256,1024]{1,0:T(8,128)(2,1)}, u32[]{:S(2)}, u32[]{:S(2)}) collective-permute-start(bf16[256,1024]{1,0:T(8,128)(2,1)} %refs_12_.1), channel_id=1, source_target_pairs={{0,2},{1,3},{2,0},{3,1},{4,6},{5,7},{6,4},{7,5},{8,10},{9,11},{10,... | collective-permute-start | bytes 1572872 | tf_op jit(solution)/shard_map/ppermute | solution.py:719
  45.9 62.5 %collective-permute-start.5 = (bf16[256,1024]{1,0:T(8,128)(2,1)}, bf16[256,1024]{1,0:T(8,128)(2,1)}, u32[]{:S(2)}, u32[]{:S(2)}) collective-permute-start(bf16[256,1024]{1,0:T(8,128)(2,1)} %refs_12_.1), channel_id=1, source_target_pairs={{0,1},{1,0},{2,3},{3,2},{4,5},{5,4},{6,7},{7,6},{8,9},{9,8},{10,11... | collective-permute-start | bytes 1572872 | tf_op jit(solution)/shard_map/ppermute | solution.py:719
  91.5 70.6 %all-to-all-start.1 = ((bf16[8,112,1152]{2,1,0:T(8,128)(2,1)}), bf16[8,112,1152]{2,1,0:T(8,128)(2,1)}, u32[]{:S(2)}, u32[]{:S(2)}) async-start(bf16[8,112,1152]{2,1,0:T(8,128)(2,1)} %pack_cotangent.3), calls=%async_computation.1 | async-start | bytes 4128768 | tf_op jit(solution)/shard_map/all_to_all | solution.py:761
  96.1 24.8 %copy-start.7 = (s32[3,208,2]{2,1,0:T(8,128)}, s32[3,208,2]{2,1,0:T(8,128)S(1)}, u32[]{:S(2)}) copy-start(s32[3,208,2]{2,1,0:T(8,128)S(1)} %pad_dynamic-slice_fusion.5.refs_11_.refs_4_) | copy-start | bytes 14980
  102.5 5.9 collective-permute-start.6
  103.5 10.5 %collective-permute-start.1 = (bf16[3,208,256]{2,1,0:T(8,128)(2,1)}, bf16[3,208,256]{2,1,0:T(8,128)(2,1)S(1)}, u32[]{:S(2)}, u32[]{:S(2)}) collective-permute-start(bf16[3,208,256]{2,1,0:T(8,128)(2,1)} %get-tuple-element.199), channel_id=1, source_target_pairs={{0,2},{1,3},{2,0},{3,1},{4,6},{5,7},{6,4},{7,5},{8,10},{9,11},{10,... | collective-permute-start | bytes 958472 | tf_op jit(solution)/shard_map/ppermute | solution.py:719
  105.0 9.1 %collective-permute-start.2 = (bf16[3,208,256]{2,1,0:T(8,128)(2,1)}, bf16[3,208,256]{2,1,0:T(8,128)(2,1)S(1)}, u32[]{:S(2)}, u32[]{:S(2)}) collective-permute-start(bf16[3,208,256]{2,1,0:T(8,128)(2,1)} %get-tuple-element.198), channel_id=1, source_target_pairs={{0,1},{1,0},{2,3},{3,2},{4,5},{5,4},{6,7},{7,6},{8,9},{9,8},{10,11... | collective-permute-start | bytes 958472 | tf_op jit(solution)/shard_map/ppermute | solution.py:719
  105.2 14.9 %collective-permute-start.3 = (bf16[3,208,256]{2,1,0:T(8,128)(2,1)}, bf16[3,208,256]{2,1,0:T(8,128)(2,1)S(1)}, u32[]{:S(2)}, u32[]{:S(2)}) collective-permute-start(bf16[3,208,256]{2,1,0:T(8,128)(2,1)} %get-tuple-element.197), channel_id=1, source_target_pairs={{0,3},{1,2},{2,1},{3,0},{4,7},{5,6},{6,5},{7,4},{8,11},{9,10},{10,... | collective-permute-start | bytes 958472 | tf_op jit(solution)/shard_map/ppermute | solution.py:719
  108.4 20.7 %copy-start.16 = (bf16[256,1024]{1,0:T(8,128)(2,1)}, bf16[256,1024]{1,0:T(8,128)(2,1)S(1)}, u32[]{:S(2)}) copy-start(bf16[256,1024]{1,0:T(8,128)(2,1)S(1)} %collective-permute-done.6.refs_7_.refs_15_) | copy-start | bytes 1572868
  129.9 75.6 %copy-start.14 = (bf16[3,208,1024]{2,1,0:T(8,128)(2,1)}, bf16[3,208,1024]{2,1,0:T(8,128)(2,1)S(1)}, u32[]{:S(2)}) copy-start(bf16[3,208,1024]{2,1,0:T(8,128)(2,1)S(1)} %get-tuple-element.105.refs_2_) | copy-start | bytes 3833860
  129.9 31.0 %collective-permute-start.7 = (bf16[3,208,1024]{2,1,0:T(8,128)(2,1)S(1)}, bf16[3,208,1024]{2,1,0:T(8,128)(2,1)}, u32[]{:S(2)}, u32[]{:S(2)}) collective-permute-start(bf16[3,208,1024]{2,1,0:T(8,128)(2,1)S(1)} %get-tuple-element.105.refs_2_), channel_id=1, source_target_pairs={{0,2},{1,3},{2,0},{3,1},{4,6},{5,7},{6,4},{7,5},{8,10},{9,11},{10,... | collective-permute-start | bytes 3833864 | tf_op jit(solution)/shard_map/ppermute | solution.py:719
  131.3 74.1 %collective-permute-start.10 = (bf16[1024,1024]{1,0:T(8,128)(2,1)}, bf16[1024,1024]{1,0:T(8,128)(2,1)}, u32[]{:S(2)}, u32[]{:S(2)}) collective-permute-start(bf16[1024,1024]{1,0:T(8,128)(2,1)} %bitcast.11.refs_4_), channel_id=1, source_target_pairs={{0,2},{1,3},{2,0},{3,1},{4,6},{5,7},{6,4},{7,5},{8,10},{9,11},{10,... | collective-permute-start | bytes 6291464 | tf_op jit(solution)/shard_map/ppermute | solution.py:719
  131.9 73.6 %collective-permute-start.8 = (bf16[3,208,1024]{2,1,0:T(8,128)(2,1)S(1)}, bf16[3,208,1024]{2,1,0:T(8,128)(2,1)}, u32[]{:S(2)}, u32[]{:S(2)}) collective-permute-start(bf16[3,208,1024]{2,1,0:T(8,128)(2,1)S(1)} %get-tuple-element.105.refs_2_), channel_id=1, source_target_pairs={{0,1},{1,0},{2,3},{3,2},{4,5},{5,4},{6,7},{7,6},{8,9},{9,8},{10,11... | collective-permute-start | bytes 3833864 | tf_op jit(solution)/shard_map/ppermute | solution.py:719
  160.8 44.7 %collective-permute-start.9 = (bf16[3,208,1024]{2,1,0:T(8,128)(2,1)}, bf16[3,208,1024]{2,1,0:T(8,128)(2,1)}, u32[]{:S(2)}, u32[]{:S(2)}) collective-permute-start(bf16[3,208,1024]{2,1,0:T(8,128)(2,1)} %collective-permute-done.7), channel_id=1, source_target_pairs={{0,1},{1,0},{2,3},{3,2},{4,5},{5,4},{6,7},{7,6},{8,9},{9,8},{10,11... | collective-permute-start | bytes 3833864 | tf_op jit(solution)/shard_map/ppermute | solution.py:719
  216.0 48.3 %all-to-all-start.2 = ((bf16[8,112,1024]{2,1,0:T(8,128)(2,1)}), bf16[8,112,1024]{2,1,0:T(8,128)(2,1)S(1)}, u32[]{:S(2)}, u32[]{:S(2)}) async-start(bf16[8,112,1024]{2,1,0:T(8,128)(2,1)} %pack_rows.2), calls=%async_computation.2 | async-start | bytes 3670016 | tf_op jit(solution)/shard_map/all_to_all | solution.py:761
  221.8 12.9 %collective-permute-start.11 = (bf16[1024,1024]{1,0:T(8,128)(2,1)}, bf16[1024,1024]{1,0:T(8,128)(2,1)S(1)}, u32[]{:S(2)}, u32[]{:S(2)}) collective-permute-start(bf16[1024,1024]{1,0:T(8,128)(2,1)} %bitcast.178), channel_id=1, source_target_pairs={{0,1},{1,0},{2,3},{3,2},{4,5},{5,4},{6,7},{7,6},{8,9},{9,8},{10,11... | collective-permute-start | bytes 6291464 | tf_op jit(solution)/shard_map/ppermute | solution.py:719
  221.8 12.9 %collective-permute-start.13 = (bf16[1024,1024]{1,0:T(8,128)(2,1)}, bf16[1024,1024]{1,0:T(8,128)(2,1)S(1)}, u32[]{:S(2)}, u32[]{:S(2)}) collective-permute-start(bf16[1024,1024]{1,0:T(8,128)(2,1)} %bitcast.11.refs_4_), channel_id=1, source_target_pairs={{0,1},{1,0},{2,3},{3,2},{4,5},{5,4},{6,7},{7,6},{8,9},{9,8},{10,11... | collective-permute-start | bytes 6291464 | tf_op jit(solution)/shard_map/ppermute | solution.py:719
  222.3 12.9 %collective-permute-start.12 = (bf16[1024,1024]{1,0:T(8,128)(2,1)}, bf16[1024,1024]{1,0:T(8,128)(2,1)S(1)}, u32[]{:S(2)}, u32[]{:S(2)}) collective-permute-start(bf16[1024,1024]{1,0:T(8,128)(2,1)} %collective-permute-done.refs_1_), channel_id=1, source_target_pairs={{0,1},{1,0},{2,3},{3,2},{4,5},{5,4},{6,7},{7,6},{8,9},{9,8},{10,11... | collective-permute-start | bytes 6291464 | tf_op jit(solution)/shard_map/ppermute | solution.py:719
  222.3 15.7 %collective-permute-start.14 = (bf16[1024,1024]{1,0:T(8,128)(2,1)}, bf16[1024,1024]{1,0:T(8,128)(2,1)}, u32[]{:S(2)}, u32[]{:S(2)}) collective-permute-start(bf16[1024,1024]{1,0:T(8,128)(2,1)} %collective-permute-done.10.refs_5_), channel_id=1, source_target_pairs={{0,1},{1,0},{2,3},{3,2},{4,5},{5,4},{6,7},{7,6},{8,9},{9,8},{10,11... | collective-permute-start | bytes 6291464 | tf_op jit(solution)/shard_map/ppermute | solution.py:719
  264.4 52.1 %all-to-all-start.3 = ((bf16[8,112,1024]{2,1,0:T(8,128)(2,1)}), bf16[8,112,1024]{2,1,0:T(8,128)(2,1)}, u32[]{:S(2)}, u32[]{:S(2)}) async-start(bf16[8,112,1024]{2,1,0:T(8,128)(2,1)} %pack_rows.3), calls=%async_computation.3 | async-start | bytes 3670016 | tf_op jit(solution)/shard_map/all_to_all | solution.py:761
  316.5 78.1 %all-to-all-start.4 = ((bf16[8,112,1024]{2,1,0:T(8,128)(2,1)}), bf16[8,112,1024]{2,1,0:T(8,128)(2,1)}, u32[]{:S(2)}, u32[]{:S(2)}) async-start(bf16[8,112,1024]{2,1,0:T(8,128)(2,1)} %bitcast.168), calls=%async_computation.4 | async-start | bytes 3670016 | tf_op jit(solution)/shard_map/all_to_all | solution.py:761
  322.4 48.0 %copy-start.33 = (bf16[896,1024]{1,0:T(8,128)(2,1)S(1)}, bf16[896,1024]{1,0:T(8,128)(2,1)}, u32[]{:S(2)}) copy-start(bf16[896,1024]{1,0:T(8,128)(2,1)} %get-tuple-element.129.refs_1_) | copy-start | bytes 5505028
  394.6 29.7 %collective-permute-start.15 = (bf16[2,1024,1024]{2,1,0:T(8,128)(2,1)}, bf16[2,1024,1024]{2,1,0:T(8,128)(2,1)}, u32[]{:S(2)}, u32[]{:S(2)}) collective-permute-start(bf16[2,1024,1024]{2,1,0:T(8,128)(2,1)} %bitcast.173), channel_id=1, source_target_pairs={{0,1},{1,0},{2,3},{3,2},{4,5},{5,4},{6,7},{7,6},{8,9},{9,8},{10,11... | collective-permute-start | bytes 12582920 | tf_op jit(solution)/shard_map/ppermute | solution.py:719
  394.7 49.4 %all-to-all-start.5 = ((bf16[8,112,1024]{2,1,0:T(8,128)(2,1)}), bf16[8,112,1024]{2,1,0:T(8,128)(2,1)}, u32[]{:S(2)}, u32[]{:S(2)}) async-start(bf16[8,112,1024]{2,1,0:T(8,128)(2,1)} %bitcast.167), calls=%async_computation.5 | async-start | bytes 3670016 | tf_op jit(solution)/shard_map/all_to_all | solution.py:761
  400.8 23.5 %copy-start.47 = (bf16[4,512,1024]{2,1,0:T(8,128)(2,1)S(1)}, bf16[4,512,1024]{2,1,0:T(8,128)(2,1)}, u32[]{:S(2)}) copy-start(bf16[4,512,1024]{2,1,0:T(8,128)(2,1)} %get-tuple-element.139) | copy-start | bytes 12582916
  450.2 19.1 %collective-permute-start.16 = (bf16[2,1024,1024]{1,2,0:T(8,128)(2,1)}, bf16[2,1024,1024]{1,2,0:T(8,128)(2,1)}, u32[]{:S(2)}, u32[]{:S(2)}) collective-permute-start(bf16[2,1024,1024]{1,2,0:T(8,128)(2,1)} %copy.96), channel_id=1, source_target_pairs={{0,1},{1,0},{2,3},{3,2},{4,5},{5,4},{6,7},{7,6},{8,9},{9,8},{10,11... | collective-permute-start | bytes 12582920 | tf_op jit(solution)/shard_map/ppermute | solution.py:719
  469.3 6.8 collective-permute-start.17
  472.2 66.6 %all-to-all-start.6 = ((bf16[8,112,1024]{2,1,0:T(8,128)(2,1)}), bf16[8,112,1024]{2,1,0:T(8,128)(2,1)S(1)}, u32[]{:S(2)}, u32[]{:S(2)}) async-start(bf16[8,112,1024]{2,1,0:T(8,128)(2,1)} %bitcast.166), calls=%async_computation.6 | async-start | bytes 3670016 | tf_op jit(solution)/shard_map/all_to_all | solution.py:761
  480.8 34.7 %collective-permute-start.18 = (bf16[3,208,1152]{2,1,0:T(8,128)(2,1)}, bf16[3,208,1152]{2,1,0:T(8,128)(2,1)}, u32[]{:S(2)}, u32[]{:S(2)}) collective-permute-start(bf16[3,208,1152]{2,1,0:T(8,128)(2,1)} %slice_bitcast_fusion.2), channel_id=1, source_target_pairs={{0,2},{1,3},{2,0},{3,1},{4,6},{5,7},{6,4},{7,5},{8,10},{9,11},{10,... | collective-permute-start | bytes 4313096 | tf_op jit(solution)/shard_map/ppermute | solution.py:719
  493.1 22.3 %copy-start.40 = (bf16[2,3,208,1152]{3,2,1,0:T(8,128)(2,1)S(1)}, bf16[2,3,208,1152]{3,2,1,0:T(8,128)(2,1)}, u32[]{:S(2)}) copy-start(bf16[2,3,208,1152]{3,2,1,0:T(8,128)(2,1)} %copy-done.39) | copy-start | bytes 8626180
  493.1 66.2 %collective-permute-start.19 = (bf16[1024,1024]{1,0:T(8,128)(2,1)}, bf16[1024,1024]{1,0:T(8,128)(2,1)}, u32[]{:S(2)}, u32[]{:S(2)}) collective-permute-start(bf16[1024,1024]{1,0:T(8,128)(2,1)} %slice_bitcast_fusion.1), channel_id=1, source_target_pairs={{0,2},{1,3},{2,0},{3,1},{4,6},{5,7},{6,4},{7,5},{8,10},{9,11},{10,... | collective-permute-start | bytes 6291464 | tf_op jit(solution)/shard_map/ppermute | solution.py:719
  500.3 18.4 %copy-start.10 = (bf16[1024,128]{1,0:T(8,128)(2,1)S(1)}, bf16[1024,128]{1,0:T(8,128)(2,1)}, u32[]{:S(2)}) copy-start(bf16[1024,128]{1,0:T(8,128)(2,1)} %copy-done.9) | copy-start | bytes 786436
  500.3 18.4 %copy-start.17 = (bf16[256,1024]{1,0:T(8,128)(2,1)S(1)}, bf16[256,1024]{1,0:T(8,128)(2,1)}, u32[]{:S(2)}) copy-start(bf16[256,1024]{1,0:T(8,128)(2,1)} %copy-done.16) | copy-start | bytes 1572868
  500.3 18.4 %copy-start.19 = (bf16[3,208,256]{2,1,0:T(8,128)(2,1)S(1)}, bf16[3,208,256]{2,1,0:T(8,128)(2,1)}, u32[]{:S(2)}) copy-start(bf16[3,208,256]{2,1,0:T(8,128)(2,1)} %copy-done.18) | copy-start | bytes 958468
  500.3 18.4 %copy-start.22 = (bf16[3,208,256]{2,1,0:T(8,128)(2,1)S(1)}, bf16[3,208,256]{2,1,0:T(8,128)(2,1)}, u32[]{:S(2)}) copy-start(bf16[3,208,256]{2,1,0:T(8,128)(2,1)} %copy-done.20) | copy-start | bytes 958468
  500.4 18.4 %copy-start.25 = (bf16[3,208,256]{2,1,0:T(8,128)(2,1)S(1)}, bf16[3,208,256]{2,1,0:T(8,128)(2,1)}, u32[]{:S(2)}) copy-start(bf16[3,208,256]{2,1,0:T(8,128)(2,1)} %copy-done.23) | copy-start | bytes 958468
  500.4 18.4 %copy-start.32 = (f32[3,208,128]{2,1,0:T(8,128)S(1)}, f32[3,208,128]{2,1,0:T(8,128)}, u32[]{:S(2)}) copy-start(f32[3,208,128]{2,1,0:T(8,128)} %copy-done.31) | copy-start | bytes 958468
  536.2 40.3 %collective-permute-start.34 = (bf16[2,256,1024]{2,1,0:T(8,128)(2,1)}, bf16[2,256,1024]{2,1,0:T(8,128)(2,1)}, u32[]{:S(2)}, u32[]{:S(2)}) collective-permute-start(bf16[2,256,1024]{2,1,0:T(8,128)(2,1)} %slice.131), channel_id=1, source_target_pairs={{0,1},{1,0},{2,3},{3,2},{4,5},{5,4},{6,7},{7,6},{8,9},{9,8},{10,11... | collective-permute-start | bytes 3145736 | tf_op jit(solution)/shard_map/ppermute | solution.py:719
  538.8 22.1 %copy-start.27 = (bf16[3,208,256]{2,1,0:T(8,128)(2,1)S(1)}, bf16[3,208,256]{2,1,0:T(8,128)(2,1)}, u32[]{:S(2)}) copy-start(bf16[3,208,256]{2,1,0:T(8,128)(2,1)} %copy-done.26) | copy-start | bytes 958468
  538.8 95.4 %all-to-all-start.7 = ((bf16[8,112,1024]{2,1,0:T(8,128)(2,1)}), bf16[8,112,1024]{2,1,0:T(8,128)(2,1)}, u32[]{:S(2)}, u32[]{:S(2)}) async-start(bf16[8,112,1024]{2,1,0:T(8,128)(2,1)} %bitcast.165), calls=%async_computation.7 | async-start | bytes 3670016 | tf_op jit(solution)/shard_map/all_to_all | solution.py:761
  559.4 10.0 %collective-permute-start.22 = (bf16[3,208,256]{2,1,0:T(8,128)(2,1)}, bf16[3,208,256]{2,1,0:T(8,128)(2,1)S(1)}, u32[]{:S(2)}, u32[]{:S(2)}) collective-permute-start(bf16[3,208,256]{2,1,0:T(8,128)(2,1)} %copy-done.29), channel_id=1, source_target_pairs={{0,3},{1,2},{2,1},{3,0},{4,7},{5,6},{6,5},{7,4},{8,11},{9,10},{10,... | collective-permute-start | bytes 958472 | tf_op jit(solution)/shard_map/ppermute | solution.py:719
  559.6 9.8 %collective-permute-start.21 = (bf16[3,208,256]{2,1,0:T(8,128)(2,1)}, bf16[3,208,256]{2,1,0:T(8,128)(2,1)S(1)}, u32[]{:S(2)}, u32[]{:S(2)}) collective-permute-start(bf16[3,208,256]{2,1,0:T(8,128)(2,1)} %copy-done.28), channel_id=1, source_target_pairs={{0,1},{1,0},{2,3},{3,2},{4,5},{5,4},{6,7},{7,6},{8,9},{9,8},{10,11... | collective-permute-start | bytes 958472 | tf_op jit(solution)/shard_map/ppermute | solution.py:719
  561.0 15.3 %collective-permute-start.20 = (bf16[3,208,256]{2,1,0:T(8,128)(2,1)S(1)}, bf16[3,208,256]{2,1,0:T(8,128)(2,1)S(1)}, u32[]{:S(2)}, u32[]{:S(2)}) collective-permute-start(bf16[3,208,256]{2,1,0:T(8,128)(2,1)S(1)} %copy-done.27), channel_id=1, source_target_pairs={{0,2},{1,3},{2,0},{3,1},{4,6},{5,7},{6,4},{7,5},{8,10},{9,11},{10,... | collective-permute-start | bytes 958472 | tf_op jit(solution)/shard_map/ppermute | solution.py:719
  564.6 75.4 %collective-permute-start.23 = (bf16[1024,1024]{0,1:T(8,128)(2,1)}, bf16[1024,1024]{0,1:T(8,128)(2,1)}, u32[]{:S(2)}, u32[]{:S(2)}) collective-permute-start(bf16[1024,1024]{0,1:T(8,128)(2,1)} %slice_bitcast_fusion), channel_id=1, source_target_pairs={{0,2},{1,3},{2,0},{3,1},{4,6},{5,7},{6,4},{7,5},{8,10},{9,11},{10,... | collective-permute-start | bytes 6291464 | tf_op jit(solution)/shard_map/ppermute | solution.py:719
  578.4 54.1 %collective-permute-start.35 = (bf16[256,1024]{1,0:T(8,128)(2,1)S(1)}, bf16[256,1024]{1,0:T(8,128)(2,1)S(1)}, u32[]{:S(2)}, u32[]{:S(2)}) collective-permute-start(bf16[256,1024]{1,0:T(8,128)(2,1)S(1)} %slice_bitcast_fusion.8), channel_id=1, source_target_pairs={{0,2},{1,3},{2,0},{3,1},{4,6},{5,7},{6,4},{7,5},{8,10},{9,11},{10,... | collective-permute-start | bytes 1572872 | tf_op jit(solution)/shard_map/ppermute | solution.py:719
  634.3 59.9 %all-to-all-start.8 = ((bf16[8,144,1024]{2,1,0:T(8,128)(2,1)}), bf16[8,144,1024]{2,1,0:T(8,128)(2,1)}, u32[]{:S(2)}, u32[]{:S(2)}) async-start(bf16[8,144,1024]{2,1,0:T(8,128)(2,1)} %bitcast.154), calls=%async_computation.8 | async-start | bytes 4718592 | tf_op jit(solution)/shard_map/all_to_all | solution.py:761
  640.0 161.6 %all-gather.2.cloned.1.call-start = ((), (), s32[]{:S(2)}) async-start(), calls=%async_computation.9 | async-start | bytes 2654208 | tf_op jit(solution)/shard_map/all_gather | solution.py:917
  656.9 8.0 collective-permute-start.24
  656.9 12.2 %collective-permute-start.29 = (bf16[2,3,208,1024]{3,2,1,0:T(8,128)(2,1)S(1)}, bf16[2,3,208,1024]{3,2,1,0:T(8,128)(2,1)S(1)}, u32[]{:S(2)}, u32[]{:S(2)}) collective-permute-start(bf16[2,3,208,1024]{3,2,1,0:T(8,128)(2,1)S(1)} %bitcast.175), channel_id=1, source_target_pairs={{0,1},{1,0},{2,3},{3,2},{4,5},{5,4},{6,7},{7,6},{8,9},{9,8},{10,11... | collective-permute-start | bytes 7667720 | tf_op jit(solution)/shard_map/ppermute | solution.py:719
  669.1 31.0 %collective-permute-start.25 = (bf16[3,208,1024]{2,1,0:T(8,128)(2,1)}, bf16[3,208,1024]{2,1,0:T(8,128)(2,1)}, u32[]{:S(2)}, u32[]{:S(2)}) collective-permute-start(bf16[3,208,1024]{2,1,0:T(8,128)(2,1)} %slice_bitcast_fusion.6), channel_id=1, source_target_pairs={{0,2},{1,3},{2,0},{3,1},{4,6},{5,7},{6,4},{7,5},{8,10},{9,11},{10,... | collective-permute-start | bytes 3833864 | tf_op jit(solution)/shard_map/ppermute | solution.py:719
  672.4 24.8 %copy-start.41 = (bf16[2,3,208,1024]{3,2,1,0:T(8,128)(2,1)}, bf16[2,3,208,1024]{3,2,1,0:T(8,128)(2,1)S(1)}, u32[]{:S(2)}) copy-start(bf16[2,3,208,1024]{3,2,1,0:T(8,128)(2,1)S(1)} %fusion.2) | copy-start | bytes 7667716
  697.2 31.1 %collective-permute-start.30 = (bf16[3,208,1024]{2,1,0:T(8,128)(2,1)S(1)}, bf16[3,208,1024]{2,1,0:T(8,128)(2,1)S(1)}, u32[]{:S(2)}, u32[]{:S(2)}) collective-permute-start(bf16[3,208,1024]{2,1,0:T(8,128)(2,1)S(1)} %slice_bitcast_fusion.4), channel_id=1, source_target_pairs={{0,2},{1,3},{2,0},{3,1},{4,6},{5,7},{6,4},{7,5},{8,10},{9,11},{10,... | collective-permute-start | bytes 3833864 | tf_op jit(solution)/shard_map/ppermute | solution.py:719
  697.6 30.7 %copy-start.42 = (bf16[2,3,208,1024]{3,2,1,0:T(8,128)(2,1)S(1)}, bf16[2,3,208,1024]{3,2,1,0:T(8,128)(2,1)}, u32[]{:S(2)}) copy-start(bf16[2,3,208,1024]{3,2,1,0:T(8,128)(2,1)} %copy-done.41) | copy-start | bytes 7667716
  702.8 25.9 %copy-start = (bf16[3,208,1024]{2,1,0:T(8,128)(2,1)S(1)}, bf16[3,208,1024]{2,1,0:T(8,128)(2,1)}, u32[]{:S(2)}) copy-start(bf16[3,208,1024]{2,1,0:T(8,128)(2,1)} %pad_maximum_fusion.1.refs_8_.x_ref) | copy-start | bytes 3833860
  702.8 52.9 %collective-permute-start.26 = (bf16[3,208,1024]{2,1,0:T(8,128)(2,1)S(1)}, bf16[3,208,1024]{2,1,0:T(8,128)(2,1)}, u32[]{:S(2)}, u32[]{:S(2)}) collective-permute-start(bf16[3,208,1024]{2,1,0:T(8,128)(2,1)S(1)} %fusion.7), channel_id=1, source_target_pairs={{0,2},{1,3},{2,0},{3,1},{4,6},{5,7},{6,4},{7,5},{8,10},{9,11},{10,... | collective-permute-start | bytes 3833864 | tf_op jit(solution)/shard_map/ppermute | solution.py:719
  732.2 49.5 %collective-permute-start.31 = (bf16[3,208,1024]{2,1,0:T(8,128)(2,1)S(1)}, bf16[3,208,1024]{2,1,0:T(8,128)(2,1)}, u32[]{:S(2)}, u32[]{:S(2)}) collective-permute-start(bf16[3,208,1024]{2,1,0:T(8,128)(2,1)S(1)} %input_back.1), channel_id=1, source_target_pairs={{0,2},{1,3},{2,0},{3,1},{4,6},{5,7},{6,4},{7,5},{8,10},{9,11},{10,... | collective-permute-start | bytes 3833864 | tf_op jit(solution)/shard_map/ppermute | solution.py:719
  732.6 59.0 %collective-permute-start.27 = (bf16[3,208,1024]{2,1,0:T(8,128)(2,1)S(1)}, bf16[3,208,1024]{2,1,0:T(8,128)(2,1)}, u32[]{:S(2)}, u32[]{:S(2)}) collective-permute-start(bf16[3,208,1024]{2,1,0:T(8,128)(2,1)S(1)} %fusion.7), channel_id=1, source_target_pairs={{0,1},{1,0},{2,3},{3,2},{4,5},{5,4},{6,7},{7,6},{8,9},{9,8},{10,11... | collective-permute-start | bytes 3833864 | tf_op jit(solution)/shard_map/ppermute | solution.py:719
  755.8 35.8 %collective-permute-start.28 = (bf16[3,208,1024]{2,1,0:T(8,128)(2,1)}, bf16[3,208,1024]{2,1,0:T(8,128)(2,1)}, u32[]{:S(2)}, u32[]{:S(2)}) collective-permute-start(bf16[3,208,1024]{2,1,0:T(8,128)(2,1)} %collective-permute-done.26), channel_id=1, source_target_pairs={{0,1},{1,0},{2,3},{3,2},{4,5},{5,4},{6,7},{7,6},{8,9},{9,8},{10,11... | collective-permute-start | bytes 3833864 | tf_op jit(solution)/shard_map/ppermute | solution.py:719
  755.8 47.0 %collective-permute-start.32 = (bf16[3,208,1024]{2,1,0:T(8,128)(2,1)S(1)}, bf16[3,208,1024]{2,1,0:T(8,128)(2,1)}, u32[]{:S(2)}, u32[]{:S(2)}) collective-permute-start(bf16[3,208,1024]{2,1,0:T(8,128)(2,1)S(1)} %input_back.1), channel_id=1, source_target_pairs={{0,1},{1,0},{2,3},{3,2},{4,5},{5,4},{6,7},{7,6},{8,9},{9,8},{10,11... | collective-permute-start | bytes 3833864 | tf_op jit(solution)/shard_map/ppermute | solution.py:719
  781.7 21.1 %collective-permute-start.33 = (bf16[3,208,1024]{2,1,0:T(8,128)(2,1)}, bf16[3,208,1024]{2,1,0:T(8,128)(2,1)}, u32[]{:S(2)}, u32[]{:S(2)}) collective-permute-start(bf16[3,208,1024]{2,1,0:T(8,128)(2,1)} %collective-permute-done.31), channel_id=1, source_target_pairs={{0,1},{1,0},{2,3},{3,2},{4,5},{5,4},{6,7},{7,6},{8,9},{9,8},{10,11... | collective-permute-start | bytes 3833864 | tf_op jit(solution)/shard_map/ppermute | solution.py:719
  802.3 11.4 %collective-permute-start.36 = (f32[10,1024]{1,0:T(8,128)S(1)}, f32[10,1024]{1,0:T(8,128)S(1)}, u32[]{:S(2)}, u32[]{:S(2)}) collective-permute-start(f32[10,1024]{1,0:T(8,128)S(1)} %slice_convert_fusion.1), channel_id=1, source_target_pairs={{0,1},{1,0},{2,3},{3,2},{4,5},{5,4},{6,7},{7,6},{8,9},{9,8},{10,11... | collective-permute-start | bytes 122888 | tf_op jit(solution)/shard_map/ppermute | solution.py:719
  813.7 4.3 collective-permute-start.37
  (48 other events, 259.5 us)
Sparse Core Ops, SparseCore 0:
  697.2 50.1 all-gather.1

commit v4 on v2

v4 whole, which is shorter than its diff:
```python
import functools

import jax
import jax.numpy as jnp
from jax import lax
from jax.experimental import pallas as pl
from jax.experimental.pallas import tpu as pltpu
from jax.sharding import PartitionSpec as P

HD = 64
SEQ = 197
LANES = 128
EPSILON = 1e-06
CHUNKS = 2
BF = jnp.bfloat16
F32 = jnp.float32


def up_to(value, unit):
    return -(-value // unit) * unit


def params(mib=48):
    return pltpu.CompilerParams(vmem_limit_bytes=mib * 1024 * 1024)


def dot(a, b, da=1, db=0):
    return lax.dot_general(a, b, (((da,), (db,)), ((), ())), preferred_element_type=F32)


def iota(rows, cols, dim):
    return lax.broadcasted_iota(jnp.int32, (rows, cols), dim)


def flag(mask):
    return jnp.where(mask, 1.0, 0.0)


def whole(shape, once=False):
    zeros = (0,) * len(shape)
    mode = pl.Buffered(1) if once else None
    return pl.BlockSpec(shape, lambda *_: zeros, pipeline_mode=mode)


def image(*shape):
    return pl.BlockSpec((1,) + shape, lambda i, *_: (i,) + (0,) * len(shape))


def fill(x_ref, tail_ref, rows_ref):
    full = x_ref.shape[0] // 16 * 16
    rows_ref[0:full, :] = x_ref[0:full, :]
    rows_ref[full : full + 16, :] = tail_ref[...]
    rest = rows_ref.shape[0] - full - 16
    if rest:
        rows_ref[full + 16 :, :] = jnp.zeros((rest, rows_ref.shape[1]), BF)


def norm_parts(field):
    centre = field - jnp.mean(field, -1, keepdims=True)
    spread = lax.rsqrt(jnp.mean(centre * centre, -1, keepdims=True) + EPSILON)
    return centre * spread, spread


def norm_field_back(upstream, gain, scaled, spread):
    weighted = upstream * gain
    return spread * (
        weighted
        - jnp.mean(weighted, -1, keepdims=True)
        - scaled * jnp.mean(weighted * scaled, -1, keepdims=True)
    )


def cost(flops, size):
    return pl.CostEstimate(flops=flops, bytes_accessed=size, transcendentals=0)


def by_piece(count, steps, block, shape, dtype):
    def spec(p):
        def place(i, *_):
            return (jnp.clip(i - p * steps, 0, steps - 1), 0)

        return pl.BlockSpec(block, place)

    return [spec(p) for p in range(count)], [jax.ShapeDtypeStruct(shape, dtype)] * count


def store_piece(refs, steps, value):
    for p, ref in enumerate(refs):

        @pl.when(pl.program_id(0) // steps == p)
        def _():
            ref[...] = value


def rows_spec(tile, width):
    return pl.BlockSpec((tile, width), lambda i, *_: (i, 0))


def own_spec(tile, width):
    return pl.BlockSpec((tile, width), lambda i, at: (at[0] + i, 0))


def window_of(i, height, back=False):
    start = i * SEQ
    aligned = start // 16 * 16
    window = height + 16
    shape = (window, height) if back else (height, window)
    r, c = iota(*shape, 1 if back else 0), iota(*shape, 0 if back else 1)
    match = flag((c == r + (start - aligned)) & (r < SEQ)).astype(BF)
    return match, pl.ds(pl.multiple_of(aligned, 16), window)


def head_masks():
    lane = iota(1, LANES, 1)
    return [(flag(lane // HD == h)).astype(BF) for h in range(2)]


def attend_kernel(count, starts_ref, x_ref, tail_ref, gain_ref, w_ref, first_ref, qkv_ref, log_ref, *refs):
    piece_refs, rows, mixed = refs[:count], refs[count], refs[count + 1]
    i = pl.program_id(0)
    height = first_ref.shape[1]
    cols = mixed.shape[1]

    @pl.when(i == 0)
    def _():
        fill(x_ref, tail_ref, rows)
        mixed[...] = jnp.zeros_like(mixed)

    match, place = window_of(i, height)
    field = dot(match, rows[place, :])
    scaled, _ = norm_parts(field)
    first = (scaled * gain_ref[...]).astype(BF)
    first_ref[0] = first
    for k in range(3):
        qkv_ref[k, 0] = dot(first, w_ref[k]).astype(BF)
    masks = head_masks()
    lane = iota(1, LANES, 1)
    key_lane = iota(1, height, 1)
    logs = jnp.zeros((height, LANES), F32)
    back, _ = window_of(i, height, True)
    for pair in range(cols // LANES):
        part = slice(pair * LANES, (pair + 1) * LANES)
        queries, keys, values = (qkv_ref[k, 0, :, part] for k in range(3))
        total = jnp.zeros((height, LANES), F32)
        for h in range(2):
            scores = dot(queries * masks[h], keys, 1, 1) * HD ** (-0.5)
            scores = jnp.where(key_lane < SEQ, scores, -1e30)
            highest = jnp.max(scores, -1, keepdims=True)
            weights = jnp.exp(scores - highest)
            sums = jnp.sum(weights, -1, keepdims=True)
            probs = (weights * (1.0 / sums)).astype(BF)
            total += dot(probs, values * masks[h])
            logs = jnp.where(lane == pair * 2 + h, highest + jnp.log(sums), logs)
        mixed[place, part] = (mixed[place, part].astype(F32) + dot(back, total.astype(BF))).astype(BF)
    log_ref[0] = logs

    @pl.when(i == pl.num_programs(0) - 1)
    def _():
        for p in range(count):
            at = pl.multiple_of(starts_ref[p], 16)
            piece_refs[p][...] = mixed[pl.ds(at, piece_refs[p].shape[0]), :]


def attend(starts, block_in, tail, gain, head_in, images, height, each, count):
    rows, width = block_in.shape
    cols = head_in.shape[2]
    scratch_rows = max(rows // 16 * 16 + 48, each * count)
    spec = pltpu.PrefetchScalarGridSpec(
        num_scalar_prefetch=1,
        grid=(images,),
        in_specs=[whole((rows, width), True), whole((16, width)), whole((1, width)), whole(head_in.shape, True)],
        out_specs=[
            image(height, width),
            pl.BlockSpec((3, 1, height, cols), lambda i, *_: (0, i, 0, 0)),
            image(height, LANES),
        ]
        + [whole((each, cols))] * count,
        scratch_shapes=[pltpu.VMEM((scratch_rows, width), BF), pltpu.VMEM((scratch_rows, cols), BF)],
    )
    return pl.pallas_call(
        functools.partial(attend_kernel, count),
        grid_spec=spec,
        out_shape=[
            jax.ShapeDtypeStruct((images, height, width), BF),
            jax.ShapeDtypeStruct((3, images, height, cols), BF),
            jax.ShapeDtypeStruct((images, height, LANES), F32),
        ]
        + [jax.ShapeDtypeStruct((each, cols), BF)] * count,
        compiler_params=params(),
        cost_estimate=cost(16 * images * height * width * cols, 16 * rows * width),
        name="attend",
    )(starts, block_in, tail, gain, head_in)


def attend_back_kernel(count, starts_ref, qkv_ref, log_ref, first_ref, wt_ref, gain_ref, *refs):
    dmix_refs, piece_refs = refs[:count], refs[count : 2 * count]
    hg_ref, ng_ref, acc, grads, dmix, field = refs[2 * count :]
    i = pl.program_id(0)
    height = first_ref.shape[1]
    each = dmix_refs[0].shape[0]

    @pl.when(i == 0)
    def _():
        acc[...] = jnp.zeros_like(acc)
        field[...] = jnp.zeros_like(field)
        rest = dmix.shape[0] - each * count
        if rest:
            dmix[each * count :, :] = jnp.zeros((rest, dmix.shape[1]), BF)
        for p in range(count):
            dmix[pl.ds(pl.multiple_of(starts_ref[p], 16), each), :] = dmix_refs[p][...]

    match, place = window_of(i, height)
    back, _ = window_of(i, height, True)
    out_grads = dot(match, dmix[place, :]).astype(BF)
    masks = head_masks()
    lane = iota(1, LANES, 1)
    key_lane = iota(1, height, 1)
    scale = HD ** (-0.5)
    logs = log_ref[0]
    for pair in range(dmix.shape[1] // LANES):
        cols = slice(pair * LANES, (pair + 1) * LANES)
        queries, keys, values = (qkv_ref[k, 0, :, cols] for k in range(3))
        out_grad = out_grads[:, cols]
        dq = jnp.zeros((height, LANES), F32)
        dk = jnp.zeros((height, LANES), F32)
        dv = jnp.zeros((height, LANES), F32)
        for h in range(2):
            q_h = queries * masks[h]
            o_h = out_grad * masks[h]
            log_h = jnp.sum(jnp.where(lane == pair * 2 + h, logs, 0.0), -1, keepdims=True)
            probs = jnp.exp(dot(q_h, keys, 1, 1) * scale - log_h)
            probs = jnp.where(key_lane < SEQ, probs, 0.0)
            prob_grad = dot(o_h, values, 1, 1)
            dv += dot(probs.astype(BF), o_h, 0, 0)
            delta = jnp.sum(probs * prob_grad, -1, keepdims=True)
            score_grad = (probs * (prob_grad - delta)).astype(BF)
            dq += dot(score_grad, keys * masks[h])
            dk += dot(score_grad, q_h, 0, 0)
        grads[0, :, cols] = (dq * scale).astype(BF)
        grads[1, :, cols] = (dk * scale).astype(BF)
        grads[2, :, cols] = dv.astype(BF)

    first = first_ref[0]
    total = None
    for k in range(3):
        part = dot(grads[k], wt_ref[k])
        total = part if total is None else total + part
        acc[k] += dot(grads[k], first, 0, 0)
    field[place, :] = (field[place, :].astype(F32) + dot(back, total.astype(BF))).astype(BF)

    @pl.when(i == pl.num_programs(0) - 1)
    def _():
        for p in range(count):
            piece_refs[p][...] = field[pl.ds(pl.multiple_of(starts_ref[p], 16), each), :]
        hg_ref[...] = acc[...].astype(BF)
        gain_grad = jnp.zeros_like(ng_ref)
        for k in range(3):
            gain_grad += jnp.sum(acc[k] * wt_ref[k].astype(F32), 0, keepdims=True)
        ng_ref[...] = gain_grad / gain_ref[...]


def attend_back(starts, dmix, qkv, logs, first, head_in_t, gain):
    images, height, width = first.shape
    each, cols = dmix[0].shape
    count = len(dmix)
    scratch_rows = max(images * SEQ // 16 * 16 + 48, each * count)
    spec = pltpu.PrefetchScalarGridSpec(
        num_scalar_prefetch=1,
        grid=(images,),
        in_specs=[
            pl.BlockSpec((3, 1, height, cols), lambda i, *_: (0, i, 0, 0)),
            image(height, LANES),
            image(height, width),
            whole(head_in_t.shape, True),
            whole((1, width)),
        ]
        + [whole((each, cols), True)] * count,
        out_specs=[whole((each, width))] * count + [whole(head_in_t.shape), whole((1, width))],
        scratch_shapes=[
            pltpu.VMEM(head_in_t.shape, F32),
            pltpu.VMEM((3, height, cols), BF),
            pltpu.VMEM((scratch_rows, cols), BF),
            pltpu.VMEM((scratch_rows, width), BF),
        ],
    )
    return pl.pallas_call(
        functools.partial(attend_back_kernel, count),
        grid_spec=spec,
        out_shape=[jax.ShapeDtypeStruct((each, width), BF)] * count
        + [jax.ShapeDtypeStruct(head_in_t.shape, BF), jax.ShapeDtypeStruct((1, width), F32)],
        compiler_params=params(),
        cost_estimate=cost(24 * images * height * width * cols, 20 * images * height * width),
        name="attend_back",
    )(starts, qkv, logs, first, head_in_t, gain, *dmix)


def block_count(blocks, slots):
    return max(n for n in range(1, blocks + 1) if blocks % n == 0 and n * slots <= 448)


def pack_first_kernel(x_ref, tail_ref, lp_ref, side_ref, out_ref, rows):
    i, n = pl.program_id(0), pl.program_id(1)

    @pl.when((i == 0) & (n == 0))
    def _():
        fill(x_ref, tail_ref, rows)

    blocks, _, slots, _ = out_ref.shape
    tile = blocks * slots
    j = (n * pl.num_programs(0) + i) * tile + iota(tile, rows.shape[0], 0)
    picks = [flag(lp_ref[c : c + 1, :] == j) for c in range(2)]
    width = x_ref.shape[1]
    main = dot((picks[0] + picks[1]).astype(BF), rows[...]).astype(BF)
    out_ref[:, 0, :, 0:width] = main.reshape(blocks, slots, width)
    extra = dot(picks[0].astype(BF), side_ref[0]) + dot(picks[1].astype(BF), side_ref[1])
    out_ref[:, 0, :, width:] = extra.astype(BF).reshape(blocks, slots, LANES)


def pack_first(x, tail, lp, side, experts, slots):
    rows, width = x.shape
    padded = lp.shape[1]
    blocks = block_count(experts, slots)
    return pl.pallas_call(
        pack_first_kernel,
        grid=(experts // blocks, CHUNKS),
        in_specs=[whole((rows, width), True), whole((16, width)), whole(lp.shape), whole(side.shape)],
        out_specs=pl.BlockSpec((blocks, 1, slots, width + LANES), lambda i, n: (i, n, 0, 0)),
        out_shape=jax.ShapeDtypeStruct((experts, CHUNKS, slots, width + LANES), BF),
        scratch_shapes=[pltpu.VMEM((padded, width), BF)],
        compiler_params=params(),
        cost_estimate=cost(3 * CHUNKS * experts * slots * padded * width, 2 * rows * width),
        name="pack_cotangent",
    )(x, tail, lp, side)


def pack_kernel(base, count, part_ref, *refs):
    lp_ref, out_ref = refs[count], refs[count + 1]
    total = None
    tile = out_ref.shape[0]
    for p in range(count):
        j = base + pl.program_id(0) * tile + iota(tile, refs[p].shape[0], 0)
        lp = lp_ref[part_ref[p]]
        picks = flag((lp[0:1, :] == j) | (lp[1:2, :] == j)).astype(BF)
        part = dot(picks, refs[p][...])
        total = part if total is None else total + part
    out_ref[...] = total.astype(BF)


def pack(part_of, pieces, lp, experts, slots, base):
    rows, width = pieces[0].shape
    count = len(pieces)
    tile = slots * block_count(experts, slots)
    spec = pltpu.PrefetchScalarGridSpec(
        num_scalar_prefetch=1,
        grid=(experts * slots // tile,),
        in_specs=[whole((rows, width), True)] * count + [whole(lp.shape)],
        out_specs=rows_spec(tile, width),
    )
    return pl.pallas_call(
        functools.partial(pack_kernel, base, count),
        grid_spec=spec,
        out_shape=jax.ShapeDtypeStruct((experts * slots, width), BF),
        compiler_params=params(),
        cost_estimate=cost(3 * experts * slots * rows * count * width, 2 * rows * count * width),
        name="pack_rows",
    )(part_of, *pieces, lp)


def unpack_kernel(count, slots, per, graded, part_ref, lp_ref, *refs):
    row_refs, out_refs = refs[:count], refs[count:]
    lp = lp_ref[...]
    height = lp.shape[0]
    rows, width = row_refs[0].shape
    total = jnp.zeros((height, width), F32)
    lanes = up_to(slots, LANES)
    extra = [jnp.zeros((height, lanes), F32) for _ in range(2)]
    for n in range(count):
        j = n * rows + iota(1, rows, 1)
        hits = (lp[:, 0:1] == j) | (lp[:, 1:2] == j)
        total += dot(flag(hits).astype(BF), row_refs[n][...])
        if graded:
            j = iota(1, lanes, 1)
            for e in range(rows // slots):
                spare = row_refs[n][(e + 1) * slots - 16 : (e + 1) * slots, 0 : 2 * lanes].astype(F32)
                spare = spare[per + 16 - slots : per + 17 - slots, :]
                values = spare[:, :lanes] + spare[:, lanes:]
                for c in range(2):
                    hit = lp[:, c : c + 1] - (n * rows + e * slots) == j
                    extra[c] += jnp.where(hit, values, 0.0)
    value = total.astype(BF)
    if graded:
        lane = iota(1, LANES, 1)
        tail = jnp.zeros((height, LANES), F32)
        for c in range(2):
            grad = jnp.sum(extra[c], -1, keepdims=True)
            high = grad.astype(BF).astype(F32)
            tail = jnp.where(lane == c, high, tail)
            tail = jnp.where(lane == 2 + c, grad - high, tail)
        value = jnp.concatenate([value, tail.astype(BF)], 1)
    store_piece(out_refs, 1, value)


def unpack(part_of, lp, rows, slots, per, each, graded):
    parts = lp.shape[0] // each
    count = len(rows)
    width = rows[0].shape[1] + (LANES if graded else 0)
    out_specs, out_shape = by_piece(parts, 1, (each, width), (each, width), BF)
    spec = pltpu.PrefetchScalarGridSpec(
        num_scalar_prefetch=1,
        grid=(parts,),
        in_specs=[pl.BlockSpec((each, 2), lambda i, at: (at[i], 0))] + [whole(item.shape, True) for item in rows],
        out_specs=out_specs,
    )
    return pl.pallas_call(
        functools.partial(unpack_kernel, count, slots, per, graded),
        grid_spec=spec,
        out_shape=out_shape,
        compiler_params=params(),
        cost_estimate=cost(3 * lp.shape[0] * count * rows[0].size, 4 * count * rows[0].size),
        name="unpack_rows",
    )(part_of, lp, *rows)


def assemble_kernel(count, steps, part_ref, *refs):
    out_ref = refs[count]
    for p in range(count):

        @pl.when(pl.program_id(0) // steps == p)
        def _():
            out_ref[...] = refs[p][...].astype(out_ref.dtype)


def assemble(part_of, pieces, rows, dtype):
    each, width = pieces[0].shape
    count = len(pieces)
    tile = each // 2 if each % 32 == 0 else each
    steps = each // tile
    in_specs, _ = by_piece(count, steps, (tile, width), (each, width), BF)
    spec = pltpu.PrefetchScalarGridSpec(
        num_scalar_prefetch=1,
        grid=(count * steps,),
        in_specs=in_specs,
        out_specs=pl.BlockSpec((tile, width), lambda i, at: (at[i // steps] * steps + i % steps, 0)),
    )
    return pl.pallas_call(
        functools.partial(assemble_kernel, count, steps),
        grid_spec=spec,
        out_shape=jax.ShapeDtypeStruct((rows, width), dtype),
        compiler_params=params(),
        cost_estimate=cost(2 * rows * width, 8 * rows * width),
        name="assemble",
    )(part_of, *pieces)


def sum_turned_kernel(a_ref, b_ref, out_ref):
    out_ref[...] = (a_ref[...].astype(F32) + b_ref[...].astype(F32)).T


def sum_turned(a, b):
    rows, width = a.shape
    tile = min(256, rows)
    return pl.pallas_call(
        sum_turned_kernel,
        grid=(rows // tile,),
        in_specs=[rows_spec(tile, width)] * 2,
        out_specs=pl.BlockSpec((width, tile), lambda i: (0, i)),
        out_shape=jax.ShapeDtypeStruct((width, rows), F32),
        compiler_params=params(),
        cost_estimate=cost(rows * width, 8 * rows * width),
        name="sum_turned",
    )(a, b)


def middle_kernel(count, limit, at_ref, *refs):
    mixed_refs, wo_refs = refs[:count], refs[count : 2 * count]
    x_ref, gain_ref, router_ref, ids_ref, noise_ref, mid_ref, second_ref, gates_ref = refs[2 * count :]
    tile = x_ref.shape[0]
    valid = (at_ref[0] + pl.program_id(0)) * tile + iota(tile, 1, 0) < limit
    middle = jnp.where(valid, x_ref[...].astype(F32), 0.0)
    for mixed_ref, wo_ref in zip(mixed_refs, wo_refs):
        middle += dot(mixed_ref[...], wo_ref[...])
    mid_ref[...] = middle
    scaled, _ = norm_parts(middle)
    second = (scaled * gain_ref[...]).astype(BF)
    second_ref[...] = second
    logits = dot(second, router_ref[...])
    lane = iota(1, LANES, 1)
    chosen = [
        jnp.sum(jnp.where(lane == ids_ref[:, c : c + 1], logits, 0.0), -1, keepdims=True)
        + noise_ref[:, c : c + 1]
        for c in range(2)
    ]
    top = jnp.maximum(chosen[0], chosen[1])
    raw = [jnp.exp(item - top) for item in chosen]
    inverse = 1.0 / (raw[0] + raw[1])
    gates = jnp.where(lane == 0, raw[0] * inverse, 0.0) + jnp.where(lane == 1, raw[1] * inverse, 0.0)
    gates_ref[...] = jnp.where(valid, gates, 0.0)


def half_tile(each):
    return each // 2 if each % 32 == 0 else each


def middle_of(at, mixed, head_out, x, gain, router, ids, noise):
    each, cols = mixed[0].shape
    parts = len(mixed)
    rows, width = x.shape
    tile = half_tile(each)
    spec = pltpu.PrefetchScalarGridSpec(
        num_scalar_prefetch=1,
        grid=(each // tile,),
        in_specs=[rows_spec(tile, cols)] * parts
        + [whole((cols, width), True)] * parts
        + [
            own_spec(tile, width),
            whole((1, width)),
            whole(router.shape),
            own_spec(tile, 2),
            own_spec(tile, 2),
        ],
        out_specs=[rows_spec(tile, width), rows_spec(tile, width), rows_spec(tile, LANES)],
    )
    return pl.pallas_call(
        functools.partial(middle_kernel, parts, rows),
        grid_spec=spec,
        out_shape=[
            jax.ShapeDtypeStruct((each, width), F32),
            jax.ShapeDtypeStruct((each, width), BF),
            jax.ShapeDtypeStruct((each, LANES), F32),
        ],
        compiler_params=params(),
        cost_estimate=cost(4 * each * width * width, 24 * each * width),
        name="middle",
    )(at, *mixed, *head_out, x, gain, router, ids, noise)


def middle_back_kernel(count, limit, at_ref, *refs):
    keep_ref, far_ref, mid_ref, second_ref, gates_ref, ids_ref, up_ref, gain_ref, router_ref = refs[:9]
    mixed_refs, wo_refs = refs[9 : 9 + count], refs[9 + count : 9 + 2 * count]
    mg_ref, rg_ref, ng_ref = refs[9 + 2 * count : 12 + 2 * count]
    hog_refs, dmix_refs, hog_acc = refs[12 + 2 * count : 12 + 3 * count], refs[12 + 3 * count : -1], refs[-1]
    i = pl.program_id(0)

    @pl.when(i == 0)
    def _():
        hog_acc[...] = jnp.zeros_like(hog_acc)
        rg_ref[...] = jnp.zeros_like(rg_ref)
        ng_ref[...] = jnp.zeros_like(ng_ref)

    tile, width = up_ref.shape
    valid = (at_ref[0] + i) * tile + iota(tile, 1, 0) < limit
    lane = iota(1, LANES, 1)
    tail = keep_ref[:, width:].astype(F32) + far_ref[:, width:].astype(F32)
    gates = gates_ref[...]
    gate, grad = [], []
    for c in range(2):
        gate.append(jnp.sum(jnp.where(lane == c, gates, 0.0), -1, keepdims=True))
        grad.append(jnp.sum(jnp.where((lane == c) | (lane == 2 + c), tail, 0.0), -1, keepdims=True))
    mean_term = gate[0] * grad[0] + gate[1] * grad[1]
    logit_grad = jnp.zeros((tile, LANES), F32)
    for c in range(2):
        hit = (lane == ids_ref[:, c : c + 1]) & valid
        logit_grad = jnp.where(hit, gate[c] * (grad[c] - mean_term), logit_grad)
    logit_grad = logit_grad.astype(BF)
    routed = keep_ref[:, 0:width].astype(F32) + far_ref[:, 0:width].astype(F32)
    second_grad = routed + dot(logit_grad, router_ref[...], 1, 1)
    rg_ref[...] += dot(logit_grad, second_ref[...], 0, 0)
    scaled, spread = norm_parts(mid_ref[...])
    ng_ref[...] += jnp.sum(second_grad * scaled, 0, keepdims=True)
    upstream = jnp.where(valid, up_ref[...].astype(F32), 0.0)
    middle_grad = upstream + norm_field_back(second_grad, gain_ref[...], scaled, spread)
    mg_ref[...] = middle_grad
    rounded = middle_grad.astype(BF)
    for t in range(count):
        dmix_refs[t][...] = dot(rounded, wo_refs[t][...], 1, 1).astype(BF)
        hog_acc[t] += dot(mixed_refs[t][...], rounded, 0, 0)

    @pl.when(i == pl.num_programs(0) - 1)
    def _():
        for t in range(count):
            hog_refs[t][...] = hog_acc[t].astype(BF)


def middle_back(at, keep, far, middle, second, gates, ids, up, mixed, head_out, gain, router):
    each, cols = mixed[0].shape
    parts = len(mixed)
    rows, width = up.shape
    tile = half_tile(each)
    spec = pltpu.PrefetchScalarGridSpec(
        num_scalar_prefetch=1,
        grid=(each // tile,),
        in_specs=[
            rows_spec(tile, keep.shape[1]),
            rows_spec(tile, keep.shape[1]),
            rows_spec(tile, width),
            rows_spec(tile, width),
            rows_spec(tile, LANES),
            own_spec(tile, 2),
            own_spec(tile, width),
            whole((1, width)),
            whole(router.shape),
        ]
        + [rows_spec(tile, cols)] * parts
        + [whole((cols, width), True)] * parts,
        out_specs=[rows_spec(tile, width), whole((LANES, width)), whole((1, width))]
        + [whole((cols, width))] * parts
        + [rows_spec(tile, cols)] * parts,
        scratch_shapes=[pltpu.VMEM((parts, cols, width), F32)],
    )
    return pl.pallas_call(
        functools.partial(middle_back_kernel, parts, rows),
        grid_spec=spec,
        out_shape=[
            jax.ShapeDtypeStruct((each, width), F32),
            jax.ShapeDtypeStruct((LANES, width), F32),
            jax.ShapeDtypeStruct((1, width), F32),
        ]
        + [jax.ShapeDtypeStruct((cols, width), BF)] * parts
        + [jax.ShapeDtypeStruct((each, cols), BF)] * parts,
        compiler_params=params(),
        cost_estimate=cost(8 * each * width * width, 40 * each * width),
        name="middle_back",
    )(at, keep, far, middle, second, gates, ids, up, gain, router, *mixed, *head_out)


def input_back_kernel(limit, at_ref, keep_ref, far_ref, x_ref, mg_ref, gain_ref, out_ref):
    tile = x_ref.shape[0]
    valid = (at_ref[0] + pl.program_id(0)) * tile + iota(tile, 1, 0) < limit
    scaled, spread = norm_parts(jnp.where(valid, x_ref[...].astype(F32), 0.0))
    first_grad = keep_ref[...].astype(F32) + far_ref[...].astype(F32)
    out_ref[...] = (mg_ref[...] + norm_field_back(first_grad, gain_ref[...], scaled, spread)).astype(BF)


def input_back(at, keep, far, x, middle_grad, gain):
    each, width = middle_grad.shape
    tile = half_tile(each)
    spec = pltpu.PrefetchScalarGridSpec(
        num_scalar_prefetch=1,
        grid=(each // tile,),
        in_specs=[rows_spec(tile, width), rows_spec(tile, width), own_spec(tile, width), rows_spec(tile, width), whole((1, width))],
        out_specs=rows_spec(tile, width),
    )
    return pl.pallas_call(
        functools.partial(input_back_kernel, x.shape[0]),
        grid_spec=spec,
        out_shape=jax.ShapeDtypeStruct((each, width), BF),
        compiler_params=params(),
        cost_estimate=cost(20 * each * width, 16 * each * width),
        name="input_back",
    )(at, keep, far, x, middle_grad, gain)


def gelu_parts(v):
    x = jnp.abs(v) * 0.7071067811865476
    t = 1.0 / (1.0 + 0.3275911 * x)
    bell = jnp.exp(-x * x)
    poly = ((((1.061405429 * t - 1.453152027) * t + 1.421413741) * t - 0.284496736) * t + 0.254829592) * t
    below = 0.5 * poly * bell
    share = jnp.where(v < 0.0, below, 1.0 - below)
    return v * share, share + v * bell * 0.3989422804014327


def expert_kernel(count, slots, per, x_ref, g_ref, router_ref, *refs):
    w1_hbm, w2_hbm = refs[: 2 * count], refs[2 * count : 3 * count]
    back_ref, act_ref, hg_ref, rg_ref, dx_ref, w1, w2, sems = refs[3 * count :]
    rows, width = x_ref[...], x_ref.shape[1]
    half = width // 2
    copies = []
    for t in range(count):
        copies.append(
            [
                pltpu.make_async_copy(w1_hbm[2 * t], w1.at[t, pl.ds(0, half)], sems.at[3 * t]),
                pltpu.make_async_copy(w1_hbm[2 * t + 1], w1.at[t, pl.ds(half, half)], sems.at[3 * t + 1]),
                pltpu.make_async_copy(w2_hbm[t], w2.at[t], sems.at[3 * t + 2]),
            ]
        )

    @pl.when(pl.program_id(0) == 0)
    def _():
        for group in copies:
            for item in group:
                item.start()

    lane = iota(1, LANES, 1)
    signal = g_ref[:, 0].reshape(rows.shape[0], width + LANES)
    side = signal[:, width:].astype(F32)

    def column(*lanes):
        keep = lane == lanes[0]
        for other in lanes[1:]:
            keep = keep | (lane == other)
        return jnp.sum(jnp.where(keep, side, 0.0), -1, keepdims=True)

    logits = dot(rows, router_ref[...])
    lane_f = lane.astype(F32)
    mine = jnp.sum(jnp.where(lane_f == column(4), logits, 0.0), -1, keepdims=True)
    other = jnp.sum(jnp.where(lane_f == column(0), logits, 0.0), -1, keepdims=True)
    gate = 1.0 / (1.0 + jnp.exp(other - mine - column(1, 2, 3)))
    upstream = signal[:, 0:width].astype(F32)
    rows_grad = (gate * upstream).astype(BF)
    rg_ref[...] = rows_grad
    hidden_here = w1.shape[2]
    step = min(512, hidden_here)
    for t in range(count):

        @pl.when(pl.program_id(0) == 0)
        def _():
            for item in copies[t]:
                item.wait()

        for at in range(0, hidden_here, step):
            cols = slice(at, at + step)
            place = slice(t * hidden_here + at, t * hidden_here + at + step)
            hidden = dot(rows, w1[t, :, cols])
            active_grad = dot(rows_grad, w2[t, cols, :], 1, 1)
            active, slope = gelu_parts(hidden)
            act_ref[:, place] = active.astype(BF)
            hg_ref[:, place] = (active_grad * slope).astype(BF)
    out = None
    grad = None
    for t in range(count):
        place = slice(t * hidden_here, (t + 1) * hidden_here)
        part = dot(act_ref[:, place], w2[t])
        out = part if out is None else out + part
        part = dot(hg_ref[:, place], w1[t], 1, 1)
        grad = part if grad is None else grad + part
    dx_ref[...] = grad.astype(BF)
    back_ref[...] = (gate * out).astype(BF)
    gate_grad = jnp.sum(upstream * out.astype(BF).astype(F32), -1, keepdims=True)
    lanes = up_to(slots, LANES)
    spread = iota(slots, lanes, 0) == iota(slots, lanes, 1)
    spare_row = iota(16, 1, 0) == per + 16 - slots
    for b in range(x_ref.shape[0] // slots):
        end = (b + 1) * slots
        line = jnp.sum(jnp.where(spread, gate_grad[end - slots : end], 0.0), 0, keepdims=True)
        high = line.astype(BF).astype(F32)
        line = jnp.concatenate([high, line - high, jnp.zeros((1, width - 2 * lanes), F32)], 1)
        dx_ref[end - 16 : end, :] = jnp.where(spare_row, line, grad[end - 16 : end]).astype(BF)


def expert(x, g, chunk, router, w1, w2, slots, per):
    rows, width = x.shape
    count = len(w2)
    here = w2[0].shape[0]
    total = count * here
    blocks = block_count(rows // slots, slots)
    tile = slots * blocks

    def tiled(cols):
        return pl.BlockSpec((tile, cols), lambda i: (i, 0))

    flops = 8 * rows * width * total
    return pl.pallas_call(
        functools.partial(expert_kernel, count, slots, per),
        grid=(rows // tile,),
        in_specs=[
            tiled(width),
            pl.BlockSpec((blocks, 1, slots, g.shape[3]), lambda i: (i, chunk, 0, 0)),
            whole(router.shape),
        ]
        + [pl.BlockSpec(memory_space=pl.ANY)] * (3 * count),
        out_specs=[tiled(width), tiled(total), tiled(total), tiled(width), tiled(width)],
        out_shape=[
            jax.ShapeDtypeStruct((rows, width), BF),
            jax.ShapeDtypeStruct((rows, total), BF),
            jax.ShapeDtypeStruct((rows, total), BF),
            jax.ShapeDtypeStruct((rows, width), BF),
            jax.ShapeDtypeStruct((rows, width), BF),
        ],
        scratch_shapes=[
            pltpu.VMEM((count, width, here), BF),
            pltpu.VMEM((count, here, width), BF),
            pltpu.SemaphoreType.DMA((3 * count,)),
        ],
        compiler_params=params(60),
        cost_estimate=pl.CostEstimate(flops=flops, bytes_accessed=rows * total * 6, transcendentals=rows * total * 2),
        name="expert",
    )(x, g, router, *w1, *w2)


def weight_kernel(count, steps, *refs):
    ins, outs = refs[: 2 * count], refs[2 * count :]
    total = None
    for n in range(count):
        part = dot(ins[2 * n][...], ins[2 * n + 1][...], 0, 0)
        total = part if total is None else total + part
    store_piece(outs, steps, total.astype(BF))


def weight_grad(columns, rows, first, here):
    count = len(columns)
    width = rows[0].shape[1]
    step = min(512, here)
    steps = here // step
    offset = first * steps
    specs, args = [], []
    for a, b in zip(columns, rows):
        specs += [pl.BlockSpec((a.shape[0], step), lambda i: (0, i + offset)), whole(b.shape, True)]
        args += [a, b]
    out_specs, out_shape = by_piece(2, steps, (step, width), (here, width), BF)
    return pl.pallas_call(
        functools.partial(weight_kernel, count, steps),
        grid=(2 * steps,),
        in_specs=specs,
        out_specs=out_specs,
        out_shape=out_shape,
        compiler_params=params(),
        cost_estimate=cost(4 * sum(b.shape[0] for b in rows) * width * here, 8 * here * width),
        name="weight_grad",
    )(*args)


def shards(
    block_in,
    norm_one,
    head_in,
    head_out,
    norm_two,
    router,
    expert_in,
    expert_out,
    expert_ids,
    route_noise,
    cotangent,
):
    rows_here, width = block_in.shape
    parts = lax.axis_size("tensor")
    groups = lax.axis_size("expert")
    me = lax.axis_index("tensor")
    images = rows_here // SEQ
    height = up_to(SEQ, 16)
    each = up_to(-(-rows_here // parts), 16)
    experts = router.shape[1]
    capacity = (rows_here * 2 * 8 // (5 * experts) + 15) // 16 * 16
    share = -(-capacity // parts)
    per = -(-share // CHUNKS)
    slots = up_to(per + 1, 16)
    chunk_rows = experts * slots
    full = rows_here // 16 * 16
    here = expert_out.shape[1]

    paired = parts == 4
    order = (0, 2, 1, 3) if paired else tuple(range(parts))
    part_of = jnp.stack([me ^ k if paired else jnp.int32(k) for k in order]).astype(jnp.int32)
    starts = part_of * each
    own_block = (me * (each // half_tile(each)))[None].astype(jnp.int32)

    def cross(x, k):
        return lax.ppermute(x, "tensor", [(n, n ^ k) for n in range(parts)])

    def far_part(x):
        return cross(x, 2) if paired else x

    def gathered_from(x, far):
        if not paired:
            every = lax.all_gather(x, "tensor", axis=0, tiled=False)
            return [every[p] for p in range(parts)]
        return [x, far, cross(x, 1), cross(far, 1)]

    def gathered(x):
        return gathered_from(x, far_part(x))

    def near_hop(pieces):
        return [cross(piece, 1) for piece in pieces[2:]] if paired else pieces

    def near_sum(pieces, came):
        if not paired:
            return lax.psum_scatter(jnp.stack(pieces), "tensor", scatter_dimension=0), None
        kept, other = ((a.astype(F32) + b.astype(F32)).astype(BF) for a, b in zip(pieces, came))
        return kept, other

    def far_hop(kept, other):
        return cross(other, 2) if paired else jnp.zeros_like(kept)

    def scattered(pieces):
        kept, other = near_sum(pieces, near_hop(pieces))
        return kept, far_hop(kept, other)

    def swapped(pieces):
        if not paired:
            every = lax.all_to_all(jnp.stack(pieces), "tensor", split_axis=0, concat_axis=0, tiled=True)
            return [every[p] for p in range(parts)]
        return [cross(piece, k) if k else piece for piece, k in zip(pieces, order)]

    def over_experts(x):
        return lax.all_to_all(x, "expert", split_axis=0, concat_axis=0, tiled=True)

    def pinned(*items):
        return lax.optimization_barrier(items)

    def tail_of(x):
        return jnp.pad(x[full:], ((0, 16 - (rows_here - full)), (0, 0)))

    names = jnp.arange(experts, dtype=jnp.int32)
    member = [(expert_ids[:, c : c + 1] == names).astype(jnp.int32) for c in range(2)]
    both = member[0] + member[1]
    earlier = jnp.cumsum(both, 0) - both
    slot = jnp.stack([jnp.sum(earlier * item, -1) for item in member], 1)
    local = slot - me * share
    place = local // per * chunk_rows + expert_ids * slots + local % per
    place = jnp.where((local >= 0) & (local < share), place, -1)
    place = jnp.pad(place, ((0, each * parts - rows_here), (0, 0)), constant_values=-1)
    place_lanes = place.T
    place_parts = jnp.swapaxes(place_lanes.reshape(2, parts, each), 0, 1)

    sides = []
    for c in range(2):
        gap = route_noise[:, c] - route_noise[:, 1 - c]
        high = gap.astype(BF)
        left = gap - high.astype(F32)
        mid = left.astype(BF)
        low = (left - mid.astype(F32)).astype(BF)
        columns = [expert_ids[:, 1 - c].astype(BF), high, mid, low, expert_ids[:, c].astype(BF)]
        sides.append(jnp.stack(columns, 1))
    side = jnp.pad(jnp.stack(sides), ((0, 0), (0, each * parts - rows_here), (0, LANES - 5)))

    router_wide = jnp.pad(router, ((0, 0), (0, LANES - experts)))
    gain_one, gain_two = norm_one[None, :], norm_two[None, :]
    head_out_all = gathered(head_out)
    w1_own = [expert_in[0, : width // 2], expert_in[0, width // 2 :]]
    w1_far = [far_part(item) for item in w1_own]

    packed = pack_first(cotangent, tail_of(cotangent), place_lanes, side, experts, slots)
    block_rows, packed, w1_far[0] = pinned(block_in, packed, w1_far[0])
    signal = over_experts(packed)

    first_in, qkv, logs, *mixed = attend(
        starts, block_rows, tail_of(block_in), gain_one, head_in, images, height, each, parts
    )
    *mixed, w1_far[1] = pinned(*mixed, w1_far[1])
    mixed = swapped(mixed)
    middle, second_in, gates = middle_of(
        own_block, mixed, head_out_all, block_in, gain_two, router_wide, expert_ids, route_noise
    )
    *second_all, signal, late_out = pinned(*gathered(second_in), signal, expert_out[0])
    w1 = [gathered_from(a, b) for a, b in zip(w1_own, w1_far)]
    w1 = [w1[h][p] for p in range(parts) for h in range(2)]

    def packed_rows(n):
        return pack(part_of, second_all, place_parts, experts, slots, n * chunk_rows)

    def sent(x):
        return over_experts(x.reshape(experts, slots, width)).reshape(chunk_rows, width)

    x = sent(packed_rows(0))
    w2_far, *outgoing = pinned(far_part(late_out), *[packed_rows(n) for n in range(1, CHUNKS)])
    w2 = gathered_from(expert_out[0], w2_far)
    backs, actives, hidden_grads, rows_grads, arrived, returned = [], [], [], [], [], []
    for n in range(CHUNKS):
        coming = None
        if n + 1 < CHUNKS:
            x, ready = pinned(x, outgoing[n])
            coming = sent(ready)
        if n == 0:
            x, *ready = pinned(x, *w1, *w2)
            w1, w2 = ready[: 2 * parts], ready[2 * parts :]
        back, active, hidden_grad, rows_grad, row_grad = expert(
            x, signal, n, router_wide, w1, w2, slots, per
        )
        if returned:
            row_grad, returned[-1] = pinned(row_grad, returned[-1])
        arrived.append(x)
        actives.append(active)
        hidden_grads.append(hidden_grad)
        rows_grads.append(rows_grad)
        backs.append(back)
        if coming is not None:
            x, row_grad = pinned(coming, row_grad)
        returned.append(sent(row_grad))

    def weight_parts(columns, rows):
        pairs = [weight_grad(columns, rows, p, here) for p in range(parts - 2, -1, -2)]
        return [item for pair in pairs[::-1] for item in pair]

    out_parts = weight_parts(actives, rows_grads)
    out_kept, out_other = near_sum(out_parts, near_hop(out_parts))
    out_kept, *hidden_grads = pinned(out_kept, *hidden_grads)
    out_far = far_hop(out_kept, out_other)
    in_parts = weight_parts(hidden_grads, arrived)
    in_came = near_hop(in_parts)
    *returned, in_first = pinned(*returned, in_parts[0])
    in_parts[0] = in_first

    second_pieces = unpack(part_of, place, returned, slots, per, each, True)
    *second_pieces, out_far = pinned(*second_pieces, out_far)
    out_grad = out_kept.astype(F32) + out_far.astype(F32)
    second_kept, second_far = scattered(second_pieces)
    in_kept, in_other = near_sum(in_parts, in_came)
    second_far, in_kept = pinned(second_far, in_kept)
    if paired:
        second_far, in_other = pinned(second_far, in_other)
    in_far = far_hop(in_kept, in_other)
    combined = [sent(item) for item in backs]
    middle_grad, router_part, norm_two_part, *pieces = middle_back(
        own_block, second_kept, second_far, middle, second_in, gates, expert_ids, cotangent, mixed, head_out_all,
        gain_two, router_wide,
    )
    head_out_parts, mixed_grad = pieces[:parts], pieces[parts:]
    *mixed_grad, combined[0] = pinned(*mixed_grad, combined[0])
    mixed_grad = swapped(mixed_grad)
    head_out_kept, head_out_far = scattered(head_out_parts)
    *pieces, head_in_part, norm_one_part = attend_back(
        starts, mixed_grad, qkv, logs, first_in, jnp.swapaxes(head_in, 1, 2), gain_one
    )
    *pieces, combined[-1], in_far, head_out_far = pinned(*pieces, combined[-1], in_far, head_out_far)
    in_grad = sum_turned(in_kept, in_far)
    first_kept, first_far = scattered(pieces)
    block_pieces = unpack(part_of, place, combined, slots, per, each, False)
    first_far, *block_pieces = pinned(first_far, *block_pieces)
    input_part = input_back(own_block, first_kept, first_far, block_in, middle_grad, gain_one)
    block_kept, block_far = scattered(block_pieces)
    block_own = (middle + block_kept.astype(F32) + block_far.astype(F32)).astype(BF)

    cols = head_in.shape[2]
    head_out_part = (head_out_kept.astype(F32) + head_out_far.astype(F32)).astype(BF)
    small = jnp.concatenate([norm_one_part, norm_two_part, router_part[:experts]], 0).astype(BF)
    count = 4 * cols + 2 + experts
    total = up_to(count, 16 * groups)
    heads = jnp.concatenate(
        [head_in_part.reshape(3 * cols, width), head_out_part, jnp.pad(small, ((0, total - count), (0, 0)))], 0
    )
    heads = over_experts(heads.reshape(groups, total // groups, width))
    heads, block_own = pinned(heads, block_own)
    input_grad = assemble(part_of, gathered(input_part), rows_here, F32)
    block_out = assemble(part_of, gathered(block_own), rows_here, BF)
    heads = jnp.sum(heads.astype(F32), 0).astype(BF)
    heads = lax.all_gather(heads, "expert", axis=0, tiled=True)
    head_in_grad = jnp.swapaxes(heads[: 3 * cols].reshape(3, cols, width), 1, 2).astype(F32)
    head_out_grad = heads[3 * cols : 4 * cols].astype(F32)
    small = heads[4 * cols : count].astype(F32)
    if paired:
        small = small + cross(small, 1)
        small = small + cross(small, 2)
    else:
        small = lax.psum(small, "tensor")
    return (
        block_out,
        input_grad,
        small[0],
        head_in_grad,
        head_out_grad,
        small[1],
        small[2:].T,
        in_grad[None],
        out_grad[None],
    )


def solution(mesh):
    in_specs = (
        P("expert", None),
        P(),
        P(None, None, "tensor"),
        P("tensor", None),
        P(),
        P(),
        P("expert", None, "tensor"),
        P("expert", "tensor", None),
        P("expert", None),
        P("expert", None),
        P("expert", None),
    )
    out_specs = (
        P("expert", None),
        P("expert", None),
        P(),
        P(None, None, "tensor"),
        P("tensor", None),
        P(),
        P(),
        P("expert", None, "tensor"),
        P("expert", "tensor", None),
    )
    return jax.shard_map(shards, mesh=mesh, in_specs=in_specs, out_specs=out_specs, check_vma=False)
```

time: 856 us -> 736 us (0.86)
  waiting for transfers between devices: 321 us -> 243 us
  Pallas kernels: 326 us -> 307 us
  other arithmetic: 55.2 us -> 44.6 us
    all_to_all x9 -> x8, waiting for transfers between devices: 79.6 us -> 29.2 us  [over_experts(): return lax.all_to_all(x, 'expert', split_axis=0, concat_axis=0, tiled=True)]
    ppermute x38 -> x47, waiting for transfers between devices: 241 us -> 214 us  [cross(): return lax.ppermute(x, 'tensor', [(n, n ^ k) for n in range(parts)])]
    unnamed x99 -> x117, local copies, waits for them, and re-layouts: 16.4 us -> 40.5 us
    optimization_barrier x2 -> x0, local copies, waits for them, and re-layouts: 12.6 us -> none  [pinned(): return lax.optimization_barrier(items)]
    pallas_call x13 -> x15, Pallas kernels: 195 us -> 186 us  [the longest x4 50.7 us: weight_grad(): pl.pallas_call(functools.partial(weight_kernel, count, steps), grid=(2 *...]
    all_to_all x9 -> x8, starting transfers between devices: 51.5 us -> 44.5 us  [over_experts(): return lax.all_to_all(x, 'expert', split_axis=0, concat_axis=0, tiled=True)]
    convert_element_type x8 -> x12, other arithmetic: 24.7 us -> 28.4 us  [the longest x10 26 us: near_sum(): (a.astype(F32) + b.astype(F32)).astype(BF)]
    ppermute x38 -> x47, starting transfers between devices: 21.5 us -> 22.6 us  [cross(): return lax.ppermute(x, 'tensor', [(n, n ^ k) for n in range(parts)])]
  transfers between devices with their start and end apart: 48 -> 56, of which waited for: 12 -> 19; matrix products, arithmetic and copies ran while one was open for 11% -> 7% of each run, Pallas kernels for 33% -> 42%
where the time goes in v4:
time: 736 us; the launch traced here: 729 us
  Pallas kernels  307 us (42%)
  waiting for transfers between devices  243 us (33%)
  starting transfers between devices  67.1 us (9%)
  local copies, waits for them, and re-layouts  52.3 us (7%)
  other arithmetic  44.6 us (6%)
  between operations  15.1 us (2%)
    ppermute x47, waiting for transfers between devices, cross(): return lax.ppermute(x, 'tensor', [(n, n ^ k) for n in range(parts)])  214 us
    pallas_call x2, Pallas kernels, expert(): pl.pallas_call(functools.partial(expert_kernel, count, slots, per), grid=...  90.9 us
    pallas_call x4, Pallas kernels, weight_grad(): pl.pallas_call(functools.partial(weight_kernel, count, steps), grid=(2 *...  50.7 us
    all_to_all x8, starting transfers between devices, over_experts(): return lax.all_to_all(x, 'expert', split_axis=0, concat_axis=0, tiled=True)  44.5 us
    unnamed x117, local copies, waits for them, and re-layouts  40.5 us
    pallas_call x1, Pallas kernels, attend_back(): pl.pallas_call(functools.partial(attend_back_kernel, count), grid_spec=sp...  32.3 us
    pallas_call x2, Pallas kernels, unpack(): pl.pallas_call(functools.partial(unpack_kernel, count, slots, per, graded...  29.6 us
    pallas_call x1, Pallas kernels, attend(): pl.pallas_call(functools.partial(attend_kernel, count), grid_spec=spec, o...  29.4 us
  transfers between devices with their start and end apart: 56, of which 19 were waited for; matrix products, arithmetic and copies ran while one was open for 7% of the time, Pallas kernels for 42%

profile of v4, /device:TPU:0, one launch (start us, length us, event | category | flops | bytes accessed | tf_op | source)
XLA Modules:
  0.0 728.7 jit_solution(18202105403849288242)
XLA Ops:
  7.2 3.0 slice_bitcast_fusion
  10.2 2.9 collective-permute-start
  13.3 2.3 reduce-window.6
  21.3 16.2 %pack_cotangent.1 = bf16[8,2,112,1152]{3,2,1,0:T(8,128)(2,1)S(1)} custom-call(bf16[2167,1024]{1,0:T(8,128)(2,1)} %refs_6_.1, bf16[16,1024]{1,0:T(8,128)(2,1)S(1)} %pad.26.tail_ref, s32[2,2176]{1,0:T(2,128)S(1)} %copy.103.lp_ref, bf16[2,2176,128]{2,1,0:T(8,128)(2,1)S(1)} %fusion.5.side_ref), custom_call_target="tpu_custom_call" | custom-call | flops 11978932224 | bytes 4438016 | tf_op jit(solution)/shard_map/pack_cotangent/pallas_call | solution.py:323
  37.6 2.0 copy-done.2
  39.6 6.2 all-to-all-start
  48.0 12.8 %collective-permute-done.5.refs_5_.refs_14_ = bf16[256,1024]{1,0:T(8,128)(2,1)} collective-permute-done((bf16[256,1024]{1,0:T(8,128)(2,1)S(1)}, bf16[256,1024]{1,0:T(8,128)(2,1)}, u32[]{:S(2)}, u32[]{:S(2)}) %collective-permute-start.5) | collective-permute-done | bytes 524320 | tf_op jit(solution)/shard_map/ppermute | solution.py:849
  60.9 29.4 %attend.1 = (bf16[11,208,1024]{2,1,0:T(8,128)(2,1)}, bf16[3,11,208,256]{3,2,1,0:T(8,128)(2,1)}, f32[11,208,128]{2,1,0:T(8,128)S(1)}, bf16[544,256]{1,0:T(8,128)(...) custom-call(s32[4]{0:T(128)S(1)} %get-tuple-element.261.starts_ref, ...), custom_call_target="tpu_custom_call" | custom-call | flops 9596567552 | bytes 35504128 | tf_op jit(solution)/shard_map/attend/pallas_call | solution.py:180
  98.0 3.9 collective-permute-done.2.refs_1_.refs_10_
  101.9 5.2 collective-permute-done.4.refs_3_.refs_12_
  108.4 6.4 middle.1
  116.2 26.4 %collective-permute-done.8.refs_1_ = bf16[544,1024]{1,0:T(8,128)(2,1)S(1)} collective-permute-done((bf16[544,1024]{1,0:T(8,128)(2,1)}, bf16[544,1024]{1,0:T(8,128)(2,1)S(1)}, u32[]{:S(2)}, u32[]{:S(2)}) %collective-permute-start.8) | collective-permute-done | bytes 1114144 | tf_op jit(solution)/shard_map/ppermute | solution.py:849
  143.7 1.7 collective-permute-done.10.refs_3_
  151.1 7.5 %pack_rows.2 = bf16[896,1024]{1,0:T(8,128)(2,1)} custom-call(s32[4]{0:T(128)S(1)} %get-tuple-element.262.part_ref, bf16[544,1024]{1,0:T(8,128)(2,1)S(1)} %copy-done.26, bf16[544,1024]{1,0:T(8,128)(2,1)S(1)} %collective-permute-done.8.refs_1_, bf16[544,1024]{1,0:T(8,128)(2,1)S(1)} %copy-done.33, bf16[544,1024]{1,0:T(8,128)(2,1)S(1)} %copy-done.36, ...), custom_call_target="tpu_custom_call" | custom-call | flops 5989466112 | bytes 4456448 | tf_op jit(solution)/shard_map/pack_rows/pallas_call | solution.py:359
  158.7 5.7 all-to-all-start.1
  169.9 7.6 %pack_rows.3 = bf16[896,1024]{1,0:T(8,128)(2,1)} custom-call(s32[4]{0:T(128)S(1)} %get-tuple-element.262.part_ref, bf16[544,1024]{1,0:T(8,128)(2,1)S(1)} %copy-done.27, bf16[544,1024]{1,0:T(8,128)(2,1)S(1)} %copy-done.31, bf16[544,1024]{1,0:T(8,128)(2,1)S(1)} %copy-done.34, bf16[544,1024]{1,0:T(8,128)(2,1)S(1)} %copy-done.37, s32[4,2,544]{2,1,0:T(2,128)S(1)} %bitcast.60), custom_call_target="tpu_custom_call" | custom-call | flops 5989466112 | bytes 4456448 | tf_op jit(solution)/shard_map/pack_rows/pallas_call | solution.py:359
  177.4 17.0 %collective-permute-done.11.refs_9_ = bf16[1024,1024]{1,0:T(8,128)(2,1)} collective-permute-done((bf16[1024,1024]{1,0:T(8,128)(2,1)}, bf16[1024,1024]{1,0:T(8,128)(2,1)}, u32[]{:S(2)}, u32[]{:S(2)}) %collective-permute-start.11) | collective-permute-done | bytes 2097184 | tf_op jit(solution)/shard_map/ppermute | solution.py:849
  196.4 10.6 %all-to-all-done.1 = bf16[8,112,1024]{2,1,0:T(8,128)(2,1)S(1)} async-done(((bf16[8,112,1024]{2,1,0:T(8,128)(2,1)}), bf16[8,112,1024]{2,1,0:T(8,128)(2,1)S(1)}, u32[]{:S(2)}, u32[]{:S(2)}) %all-to-all-start.1) | async-done | bytes 1835040 | tf_op jit(solution)/shard_map/all_to_all | solution.py:886
  208.3 4.3 all-to-all-start.2
  212.7 45.4 %expert.2 = (bf16[896,1024]{1,0:T(8,128)(2,1)}, bf16[896,4096]{1,0:T(8,128)(2,1)}, bf16[896,4096]{1,0:T(8,128)(2,1)}, bf16[896,1024]{1,0:T(8,128)(2,1)}, bf16[896,1024]{1,0:T(8,128)(2,1)}) custom-call(bf16[896,1024]{1,0:T(8,128)(2,1)} %bitcast.56, bf16[8,2,112,1152]{3,2,1,0:T(8,128)(2,1)} %all-to-all-done.g_ref, bf16[1024,128]{1,0:T(8,128)(2,1)} %copy-done.14, ...), custom_call_target="tpu_custom_call" | custom-call | flops 30064771072 | bytes 22020096 | tf_op jit(solution)/shard_map/expert/pallas_call | solution.py:753
  258.1 5.9 all-to-all-start.3
  263.9 45.5 %expert.3 = (bf16[896,1024]{1,0:T(8,128)(2,1)}, bf16[896,4096]{1,0:T(8,128)(2,1)}, bf16[896,4096]{1,0:T(8,128)(2,1)}, bf16[896,1024]{1,0:T(8,128)(2,1)}, bf16[896,1024]{1,0:T(8,128)(2,1)}) custom-call(bf16[896,1024]{1,0:T(8,128)(2,1)} %bitcast.21.x_ref.refs_3_, bf16[8,2,112,1152]{3,2,1,0:T(8,128)(2,1)} %all-to-all-done.g_ref, bf16[1024,128]{1,0:T(8,128)(2,1)} %copy-done.14, ...), custom_call_target="tpu_custom_call" | custom-call | flops 30064771072 | bytes 22020096 | tf_op jit(solution)/shard_map/expert/pallas_call | solution.py:753
  312.4 12.3 %weight_grad.5 = (bf16[1024,1024]{1,0:T(8,128)(2,1)S(1)}, bf16[1024,1024]{1,0:T(8,128)(2,1)}) custom-call(bf16[896,4096]{1,0:T(8,128)(2,1)} %get-tuple-element.176.refs_0_, bf16[896,1024]{1,0:T(8,128)(2,1)S(1)} %copy-done.43, bf16[896,4096]{1,0:T(8,128)(2,1)} %get-tuple-element.178.refs_2_, bf16[896,1024]{1,0:T(8,128)(2,1)S(1)} %copy-done.45), custom_call_target="tpu_custom_call" | custom-call | flops 7516192768 | bytes 8388608 | tf_op jit(solution)/shard_map/weight_grad/pallas_call | solution.py:801
  325.3 6.0 all-to-all-start.4
  334.3 12.4 %weight_grad.4 = (bf16[1024,1024]{1,0:T(8,128)(2,1)S(1)}, bf16[1024,1024]{1,0:T(8,128)(2,1)}) custom-call(bf16[896,4096]{1,0:T(8,128)(2,1)} %get-tuple-element.176.refs_0_, bf16[896,1024]{1,0:T(8,128)(2,1)S(1)} %copy-done.44, bf16[896,4096]{1,0:T(8,128)(2,1)} %get-tuple-element.178.refs_2_, bf16[896,1024]{1,0:T(8,128)(2,1)S(1)} %copy-done.46), custom_call_target="tpu_custom_call" | custom-call | flops 7516192768 | bytes 8388608 | tf_op jit(solution)/shard_map/weight_grad/pallas_call | solution.py:801
  346.6 4.5 add_convert_fusion.2
  351.1 1.5 collective-permute-start.20
  352.6 4.0 add_convert_fusion.3
  356.6 13.0 %weight_grad.7 = (bf16[1024,1024]{1,0:T(8,128)(2,1)S(1)}, bf16[1024,1024]{1,0:T(8,128)(2,1)}) custom-call(bf16[896,4096]{1,0:T(8,128)(2,1)} %get-tuple-element.184.refs_0_, bf16[896,1024]{1,0:T(8,128)(2,1)S(1)} %bitcast.57, bf16[896,4096]{1,0:T(8,128)(2,1)} %get-tuple-element.185.refs_2_, bf16[896,1024]{1,0:T(8,128)(2,1)} %bitcast.21.x_ref.refs_3_), custom_call_target="tpu_custom_call" | custom-call | flops 7516192768 | bytes 8388608 | tf_op jit(solution)/shard_map/weight_grad/pallas_call | solution.py:801
  369.6 13.0 %weight_grad.6 = (bf16[1024,1024]{1,0:T(8,128)(2,1)S(1)}, bf16[1024,1024]{1,0:T(8,128)(2,1)}) custom-call(bf16[896,4096]{1,0:T(8,128)(2,1)} %get-tuple-element.184.refs_0_, bf16[896,1024]{1,0:T(8,128)(2,1)S(1)} %bitcast.58, bf16[896,4096]{1,0:T(8,128)(2,1)} %get-tuple-element.185.refs_2_, bf16[896,1024]{1,0:T(8,128)(2,1)} %bitcast.21.x_ref.refs_3_), custom_call_target="tpu_custom_call" | custom-call | flops 7516192768 | bytes 8388608 | tf_op jit(solution)/shard_map/weight_grad/pallas_call | solution.py:801
  383.9 6.0 all-to-all-start.5
  389.9 16.0 %unpack_rows.2 = (bf16[544,1152]{1,0:T(8,128)(2,1)S(1)}, bf16[544,1152]{1,0:T(8,128)(2,1)S(1)}, bf16[544,1152]{1,0:T(8,128)(2,1)}, bf16[544,1152]{1,0:T(8,128)(2,1)S(1)}) custom-call(s32[4]{0:T(128)S(1)} %get-tuple-element.262.part_ref, s32[2176,2]{1,0:T(8,128)S(1)} %get-tuple-element.266.lp_ref, bf16[896,1024]{1,0:T(8,128)(2,1)} %bitcast.23.refs_0_, ...), custom_call_target="tpu_custom_call" | custom-call | flops 11978932224 | bytes 7340032 | tf_op jit(solution)/shard_map/unpack_rows/pallas_call | solution.py:414
  406.7 2.2 collective-permute-done.22
  410.8 3.9 add_convert_fusion
  414.7 18.6 %all-to-all-done.5 = bf16[8,112,1024]{2,1,0:T(8,128)(2,1)} async-done(((bf16[8,112,1024]{2,1,0:T(8,128)(2,1)}), bf16[8,112,1024]{2,1,0:T(8,128)(2,1)}, u32[]{:S(2)}, u32[]{:S(2)}) %all-to-all-start.5) | async-done | bytes 1835040 | tf_op jit(solution)/shard_map/all_to_all | solution.py:886
  433.3 4.5 all-to-all-start.6
  437.8 3.3 add_convert_fusion.1.a_ref
  441.2 2.7 add_convert_fusion.5.refs_0_
  443.9 11.0 %middle_back.1 = (f32[544,1024]{1,0:T(8,128)}, f32[128,1024]{1,0:T(8,128)S(1)}, f32[1,1024]{1,0:T(1,128)S(1)}, bf16[256,1024]{1,0:T(8,128)(2,1)S(1)}, bf16[256,1...) custom-call(s32[1]{0:T(128)} %bitcast.12.at_ref, ...), custom_call_target="tpu_custom_call" | custom-call | flops 4563402752 | bytes 22282240 | tf_op jit(solution)/shard_map/middle_back/pallas_call | solution.py:610
  461.6 2.6 copy.104
  464.2 2.2 add_convert_fusion.12
  466.4 47.3 %collective-permute-done.26.refs_1_ = bf16[544,256]{1,0:T(8,128)(2,1)} collective-permute-done((bf16[544,256]{1,0:T(8,128)(2,1)}, bf16[544,256]{1,0:T(8,128)(2,1)}, u32[]{:S(2)}, u32[]{:S(2)}) %collective-permute-start.26) | collective-permute-done | bytes 278560 | tf_op jit(solution)/shard_map/ppermute | solution.py:849
  514.2 4.7 collective-permute-done.28.refs_3_
  519.8 32.3 %attend_back.1 = (bf16[544,1024]{1,0:T(8,128)(2,1)S(1)}, bf16[544,1024]{1,0:T(8,128)(2,1)S(1)}, bf16[544,1024]{1,0:T(8,128)(2,1)S(1)}, bf16[544,1024]{1,0:T(8,12...) custom-call(s32[4]{0:T(128)S(1)} %get-tuple-element.261.starts_ref, ...), custom_call_target="tpu_custom_call" | custom-call | flops 14394851328 | bytes 46858240 | tf_op jit(solution)/shard_map/attend_back/pallas_call | solution.py:286
  557.6 1.6 add_convert_fusion.11
  559.3 1.6 pad_maximum_fusion
  560.9 6.0 all-to-all-start.7
  566.9 2.0 add_convert_fusion.10
  569.5 13.6 %unpack_rows.3 = (bf16[544,1024]{1,0:T(8,128)(2,1)S(1)}, bf16[544,1024]{1,0:T(8,128)(2,1)S(1)}, bf16[544,1024]{1,0:T(8,128)(2,1)S(1)}, bf16[544,1024]{1,0:T(8,128)(2,1)S(1)}) custom-call(s32[4]{0:T(128)S(1)} %get-tuple-element.262.part_ref, s32[2176,2]{1,0:T(8,128)S(1)} %get-tuple-element.266.lp_ref, bf16[896,1024]{1,0:T(8,128)(2,1)} %bitcast.27.refs_0_, ...), custom_call_target="tpu_custom_call" | custom-call | flops 11978932224 | bytes 7340032 | tf_op jit(solution)/shard_map/unpack_rows/pallas_call | solution.py:414
  583.2 12.1 %collective-permute-done.34.far_ref = bf16[544,1024]{1,0:T(8,128)(2,1)S(1)} collective-permute-done((bf16[544,1024]{1,0:T(8,128)(2,1)S(1)}, bf16[544,1024]{1,0:T(8,128)(2,1)S(1)}, u32[]{:S(2)}, u32[]{:S(2)}) %collective-permute-start.34) | collective-permute-done | bytes 1114144 | tf_op jit(solution)/shard_map/ppermute | solution.py:849
  595.8 2.2 collective-permute-done.36
  599.6 25.5 %collective-permute-done.37 = bf16[544,1024]{1,0:T(8,128)(2,1)S(1)} collective-permute-done((bf16[544,1024]{1,0:T(8,128)(2,1)S(1)}, bf16[544,1024]{1,0:T(8,128)(2,1)S(1)}, u32[]{:S(2)}, u32[]{:S(2)}) %collective-permute-start.37) | collective-permute-done | bytes 1114144 | tf_op jit(solution)/shard_map/ppermute | solution.py:849
  626.0 2.9 reduce_sum.32
  629.0 3.0 collective-permute-done.41
  631.9 1.7 add_convert_fusion.6.keep_ref
  633.6 3.6 input_back.1.refs_0_
  637.7 1.5 collective-permute-start.38
  639.2 25.7 %collective-permute-done.42.refs_1_ = bf16[544,1024]{1,0:T(8,128)(2,1)} collective-permute-done((bf16[544,1024]{1,0:T(8,128)(2,1)}, bf16[544,1024]{1,0:T(8,128)(2,1)}, u32[]{:S(2)}, u32[]{:S(2)}) %collective-permute-start.42) | collective-permute-done | bytes 1114144 | tf_op jit(solution)/shard_map/ppermute | solution.py:849
  665.4 22.5 %collective-permute-done.38.refs_1_ = bf16[544,1024]{1,0:T(8,128)(2,1)} collective-permute-done((bf16[544,1024]{1,0:T(8,128)(2,1)S(1)}, bf16[544,1024]{1,0:T(8,128)(2,1)}, u32[]{:S(2)}, u32[]{:S(2)}) %collective-permute-start.38) | collective-permute-done | bytes 1114144 | tf_op jit(solution)/shard_map/ppermute | solution.py:849
  689.3 5.1 add_bitcast_fusion
  694.4 4.7 sum_turned.1
  699.1 8.7 %assemble.3 = f32[2167,1024]{1,0:T(8,128)} custom-call(s32[4]{0:T(128)S(1)} %get-tuple-element.262.part_ref, bf16[544,1024]{1,0:T(8,128)(2,1)} %input_back.1.refs_0_, bf16[544,1024]{1,0:T(8,128)(2,1)} %collective-permute-done.42.refs_1_, bf16[544,1024]{1,0:T(8,128)(2,1)} %collective-permute-done.43.refs_2_, bf16[544,1024]{1,0:T(8,128)(2,1)} %collective-permute-done.44.refs_3_), custom_call_target="tpu_custom_call" | custom-call | flops 4438016 | bytes 17752064 | tf_op jit(solution)/shard_map/assemble/pallas_call | solution.py:445
  707.9 8.1 %assemble.2 = bf16[2167,1024]{1,0:T(8,128)(2,1)} custom-call(s32[4]{0:T(128)S(1)} %get-tuple-element.262.part_ref, bf16[544,1024]{1,0:T(8,128)(2,1)S(1)} %add_convert_fusion.7.refs_0_, bf16[544,1024]{1,0:T(8,128)(2,1)} %collective-permute-done.38.refs_1_, bf16[544,1024]{1,0:T(8,128)(2,1)} %collective-permute-done.39.refs_2_, ...), custom_call_target="tpu_custom_call" | custom-call | flops 4438016 | bytes 17752064 | tf_op jit(solution)/shard_map/assemble/pallas_call | solution.py:445
  717.8 2.1 copy.110
  (250 shorter events, 67.2 us)
Async XLA Ops:
  10.2 29.4 %collective-permute-start = (bf16[512,1024]{1,0:T(8,128)(2,1)}, bf16[512,1024]{1,0:T(8,128)(2,1)}, u32[]{:S(2)}, u32[]{:S(2)}) collective-permute-start(bf16[512,1024]{1,0:T(8,128)(2,1)} %get-tuple-element.158.refs_0_), channel_id=1, source_target_pairs={{0,2},{1,3},{2,0},{3,1},{4,6},{5,7},{6,4},{7,5},{8,10},{9,11},{10,... | collective-permute-start | bytes 3145736 | tf_op jit(solution)/shard_map/ppermute | solution.py:849
  39.6 21.3 %copy-start.7 = (bf16[3,1024,256]{2,1,0:T(8,128)(2,1)S(1)}, bf16[3,1024,256]{2,1,0:T(8,128)(2,1)}, u32[]{:S(2)}) copy-start(bf16[3,1024,256]{2,1,0:T(8,128)(2,1)} %w_ref.1) | copy-start | bytes 4718596
  39.6 21.3 %copy-start.24 = (f32[1024]{0:T(1024)S(1)}, f32[1024]{0:T(1024)}, u32[]{:S(2)}) copy-start(f32[1024]{0:T(1024)} %param.12) | copy-start | bytes 12292
  39.6 106.9 %all-to-all-start = ((bf16[8,2,112,1152]{3,2,1,0:T(8,128)(2,1)}), bf16[8,2,112,1152]{3,2,1,0:T(8,128)(2,1)}, u32[]{:S(2)}, u32[]{:S(2)}) async-start(bf16[8,2,112,1152]{3,2,1,0:T(8,128)(2,1)} %copy-done.2), calls=%async_computation | async-start | bytes 8257536 | tf_op jit(solution)/shard_map/all_to_all | solution.py:886
  45.8 15.0 %collective-permute-start.5 = (bf16[256,1024]{1,0:T(8,128)(2,1)S(1)}, bf16[256,1024]{1,0:T(8,128)(2,1)}, u32[]{:S(2)}, u32[]{:S(2)}) collective-permute-start(bf16[256,1024]{1,0:T(8,128)(2,1)S(1)} %copy-done.16), channel_id=1, source_target_pairs={{0,2},{1,3},{2,0},{3,1},{4,6},{5,7},{6,4},{7,5},{8,10},{9,11},{10,... | collective-permute-start | bytes 1572872 | tf_op jit(solution)/shard_map/ppermute | solution.py:849
  46.4 45.7 %collective-permute-start.1 = (bf16[512,1024]{1,0:T(8,128)(2,1)}, bf16[512,1024]{1,0:T(8,128)(2,1)}, u32[]{:S(2)}, u32[]{:S(2)}) collective-permute-start(bf16[512,1024]{1,0:T(8,128)(2,1)} %get-tuple-element.159.refs_1_), channel_id=1, source_target_pairs={{0,2},{1,3},{2,0},{3,1},{4,6},{5,7},{6,4},{7,5},{8,10},{9,11},{10,... | collective-permute-start | bytes 3145736 | tf_op jit(solution)/shard_map/ppermute | solution.py:849
  47.9 50.0 %collective-permute-start.6 = (bf16[256,1024]{1,0:T(8,128)(2,1)S(1)}, bf16[256,1024]{1,0:T(8,128)(2,1)}, u32[]{:S(2)}, u32[]{:S(2)}) collective-permute-start(bf16[256,1024]{1,0:T(8,128)(2,1)S(1)} %copy-done.16), channel_id=1, source_target_pairs={{0,1},{1,0},{2,3},{3,2},{4,5},{5,4},{6,7},{7,6},{8,9},{9,8},{10,11... | collective-permute-start | bytes 1572872 | tf_op jit(solution)/shard_map/ppermute | solution.py:849
  60.9 37.1 %collective-permute-start.7 = (bf16[256,1024]{1,0:T(8,128)(2,1)}, bf16[256,1024]{1,0:T(8,128)(2,1)}, u32[]{:S(2)}, u32[]{:S(2)}) collective-permute-start(bf16[256,1024]{1,0:T(8,128)(2,1)} %collective-permute-done.5.refs_5_.refs_14_), channel_id=1, source_target_pairs={{0,1},{1,0},{2,3},{3,2},{4,5},{5,4},{6,7},{7,6},{8,9},{9,8},{10,11... | collective-permute-start | bytes 1572872 | tf_op jit(solution)/shard_map/ppermute | solution.py:849
  92.1 15.0 %copy-start.23 = (f32[1024]{0:T(1024)S(1)}, f32[1024]{0:T(1024)}, u32[]{:S(2)}) copy-start(f32[1024]{0:T(1024)} %param.15) | copy-start | bytes 12292
  92.1 15.0 %copy-start.21 = (bf16[544,256]{1,0:T(8,128)(2,1)S(1)}, bf16[544,256]{1,0:T(8,128)(2,1)}, u32[]{:S(2)}) copy-start(bf16[544,256]{1,0:T(8,128)(2,1)} %copy-done.20) | copy-start | bytes 835588
  92.1 9.8 %collective-permute-start.2 = (bf16[544,256]{1,0:T(8,128)(2,1)}, bf16[544,256]{1,0:T(8,128)(2,1)}, u32[]{:S(2)}, u32[]{:S(2)}) collective-permute-start(bf16[544,256]{1,0:T(8,128)(2,1)} %get-tuple-element.140), channel_id=1, source_target_pairs={{0,2},{1,3},{2,0},{3,1},{4,6},{5,7},{6,4},{7,5},{8,10},{9,11},{10,... | collective-permute-start | bytes 835592 | tf_op jit(solution)/shard_map/ppermute | solution.py:849
  92.7 9.2 %collective-permute-start.3 = (bf16[544,256]{1,0:T(8,128)(2,1)}, bf16[544,256]{1,0:T(8,128)(2,1)}, u32[]{:S(2)}, u32[]{:S(2)}) collective-permute-start(bf16[544,256]{1,0:T(8,128)(2,1)} %get-tuple-element.141), channel_id=1, source_target_pairs={{0,1},{1,0},{2,3},{3,2},{4,5},{5,4},{6,7},{7,6},{8,9},{9,8},{10,11... | collective-permute-start | bytes 835592 | tf_op jit(solution)/shard_map/ppermute | solution.py:849
  92.9 14.2 %collective-permute-start.4 = (bf16[544,256]{1,0:T(8,128)(2,1)}, bf16[544,256]{1,0:T(8,128)(2,1)}, u32[]{:S(2)}, u32[]{:S(2)}) collective-permute-start(bf16[544,256]{1,0:T(8,128)(2,1)} %get-tuple-element.142), channel_id=1, source_target_pairs={{0,3},{1,2},{2,1},{3,0},{4,7},{5,6},{6,5},{7,4},{8,11},{9,10},{10,... | collective-permute-start | bytes 835592 | tf_op jit(solution)/shard_map/ppermute | solution.py:849
  94.7 20.0 %copy-start = (s32[2167,2]{1,0:T(8,128)}, s32[2167,2]{1,0:T(8,128)S(1)}, u32[]{:S(2)}) copy-start(s32[2167,2]{1,0:T(8,128)S(1)} %copy.106.refs_11_.refs_5_) | copy-start | bytes 52012
  97.9 16.8 %copy-start.14 = (bf16[1024,128]{1,0:T(8,128)(2,1)}, bf16[1024,128]{1,0:T(8,128)(2,1)S(1)}, u32[]{:S(2)}) copy-start(bf16[1024,128]{1,0:T(8,128)(2,1)S(1)} %pad.31.refs_10_.router_ref.refs_8_) | copy-start | bytes 786436
  115.4 27.2 %collective-permute-start.8 = (bf16[544,1024]{1,0:T(8,128)(2,1)}, bf16[544,1024]{1,0:T(8,128)(2,1)S(1)}, u32[]{:S(2)}, u32[]{:S(2)}) collective-permute-start(bf16[544,1024]{1,0:T(8,128)(2,1)} %get-tuple-element.145.refs_0_.refs_3_), channel_id=1, source_target_pairs={{0,2},{1,3},{2,0},{3,1},{4,6},{5,7},{6,4},{7,5},{8,10},{9,11},{10,... | collective-permute-start | bytes 3342344 | tf_op jit(solution)/shard_map/ppermute | solution.py:849
  116.0 26.7 %collective-permute-start.9 = (bf16[544,1024]{1,0:T(8,128)(2,1)}, bf16[544,1024]{1,0:T(8,128)(2,1)S(1)}, u32[]{:S(2)}, u32[]{:S(2)}) collective-permute-start(bf16[544,1024]{1,0:T(8,128)(2,1)} %get-tuple-element.145.refs_0_.refs_3_), channel_id=1, source_target_pairs={{0,1},{1,0},{2,3},{3,2},{4,5},{5,4},{6,7},{7,6},{8,9},{9,8},{10,11... | collective-permute-start | bytes 3342344 | tf_op jit(solution)/shard_map/ppermute | solution.py:849
  142.6 16.0 %copy-start.30 = (bf16[544,1024]{1,0:T(8,128)(2,1)}, bf16[544,1024]{1,0:T(8,128)(2,1)S(1)}, u32[]{:S(2)}) copy-start(bf16[544,1024]{1,0:T(8,128)(2,1)S(1)} %collective-permute-done.8.refs_1_) | copy-start | bytes 3342340
  142.6 2.8 collective-permute-start.10
  146.4 48.0 %collective-permute-start.11 = (bf16[1024,1024]{1,0:T(8,128)(2,1)}, bf16[1024,1024]{1,0:T(8,128)(2,1)}, u32[]{:S(2)}, u32[]{:S(2)}) collective-permute-start(bf16[1024,1024]{1,0:T(8,128)(2,1)} %bitcast.84), channel_id=1, source_target_pairs={{0,2},{1,3},{2,0},{3,1},{4,6},{5,7},{6,4},{7,5},{8,10},{9,11},{10,... | collective-permute-start | bytes 6291464 | tf_op jit(solution)/shard_map/ppermute | solution.py:849
  158.7 48.3 %all-to-all-start.1 = ((bf16[8,112,1024]{2,1,0:T(8,128)(2,1)}), bf16[8,112,1024]{2,1,0:T(8,128)(2,1)S(1)}, u32[]{:S(2)}, u32[]{:S(2)}) async-start(bf16[8,112,1024]{2,1,0:T(8,128)(2,1)} %bitcast.77), calls=%async_computation.1 | async-start | bytes 3670016 | tf_op jit(solution)/shard_map/all_to_all | solution.py:886
  164.4 30.6 %collective-permute-start.12 = (bf16[512,1024]{1,0:T(8,128)(2,1)}, bf16[512,1024]{1,0:T(8,128)(2,1)S(1)}, u32[]{:S(2)}, u32[]{:S(2)}) collective-permute-start(bf16[512,1024]{1,0:T(8,128)(2,1)} %get-tuple-element.158.refs_0_), channel_id=1, source_target_pairs={{0,1},{1,0},{2,3},{3,2},{4,5},{5,4},{6,7},{7,6},{8,9},{9,8},{10,11... | collective-permute-start | bytes 3145736 | tf_op jit(solution)/shard_map/ppermute | solution.py:849
  164.4 48.3 %collective-permute-start.16 = (bf16[1024,1024]{1,0:T(8,128)(2,1)}, bf16[1024,1024]{1,0:T(8,128)(2,1)}, u32[]{:S(2)}, u32[]{:S(2)}) collective-permute-start(bf16[1024,1024]{1,0:T(8,128)(2,1)} %bitcast.85), channel_id=1, source_target_pairs={{0,1},{1,0},{2,3},{3,2},{4,5},{5,4},{6,7},{7,6},{8,9},{9,8},{10,11... | collective-permute-start | bytes 6291464 | tf_op jit(solution)/shard_map/ppermute | solution.py:849
  194.4 18.2 %collective-permute-start.17 = (bf16[1024,1024]{1,0:T(8,128)(2,1)}, bf16[1024,1024]{1,0:T(8,128)(2,1)}, u32[]{:S(2)}, u32[]{:S(2)}) collective-permute-start(bf16[1024,1024]{1,0:T(8,128)(2,1)} %collective-permute-done.11.refs_9_), channel_id=1, source_target_pairs={{0,1},{1,0},{2,3},{3,2},{4,5},{5,4},{6,7},{7,6},{8,9},{9,8},{10,11... | collective-permute-start | bytes 6291464 | tf_op jit(solution)/shard_map/ppermute | solution.py:849
  194.4 18.2 %collective-permute-start.13 = (bf16[512,1024]{1,0:T(8,128)(2,1)}, bf16[512,1024]{1,0:T(8,128)(2,1)}, u32[]{:S(2)}, u32[]{:S(2)}) collective-permute-start(bf16[512,1024]{1,0:T(8,128)(2,1)} %get-tuple-element.159.refs_1_), channel_id=1, source_target_pairs={{0,1},{1,0},{2,3},{3,2},{4,5},{5,4},{6,7},{7,6},{8,9},{9,8},{10,11... | collective-permute-start | bytes 3145736 | tf_op jit(solution)/shard_map/ppermute | solution.py:849
  194.9 17.7 %collective-permute-start.15 = (bf16[512,1024]{1,0:T(8,128)(2,1)}, bf16[512,1024]{1,0:T(8,128)(2,1)}, u32[]{:S(2)}, u32[]{:S(2)}) collective-permute-start(bf16[512,1024]{1,0:T(8,128)(2,1)} %collective-permute-done.1.refs_3_), channel_id=1, source_target_pairs={{0,1},{1,0},{2,3},{3,2},{4,5},{5,4},{6,7},{7,6},{8,9},{9,8},{10,11... | collective-permute-start | bytes 3145736 | tf_op jit(solution)/shard_map/ppermute | solution.py:849
  195.9 16.7 %collective-permute-start.14 = (bf16[512,1024]{1,0:T(8,128)(2,1)}, bf16[512,1024]{1,0:T(8,128)(2,1)}, u32[]{:S(2)}, u32[]{:S(2)}) collective-permute-start(bf16[512,1024]{1,0:T(8,128)(2,1)} %collective-permute-done.refs_2_), channel_id=1, source_target_pairs={{0,1},{1,0},{2,3},{3,2},{4,5},{5,4},{6,7},{7,6},{8,9},{9,8},{10,11... | collective-permute-start | bytes 3145736 | tf_op jit(solution)/shard_map/ppermute | solution.py:849
  208.3 49.8 %all-to-all-start.2 = ((bf16[8,112,1024]{2,1,0:T(8,128)(2,1)}), bf16[8,112,1024]{2,1,0:T(8,128)(2,1)}, u32[]{:S(2)}, u32[]{:S(2)}) async-start(bf16[8,112,1024]{2,1,0:T(8,128)(2,1)} %bitcast.75), calls=%async_computation.2 | async-start | bytes 3670016 | tf_op jit(solution)/shard_map/all_to_all | solution.py:886
  258.1 67.2 %all-to-all-start.3 = ((bf16[8,112,1024]{2,1,0:T(8,128)(2,1)}), bf16[8,112,1024]{2,1,0:T(8,128)(2,1)}, u32[]{:S(2)}, u32[]{:S(2)}) async-start(bf16[8,112,1024]{2,1,0:T(8,128)(2,1)} %bitcast.76), calls=%async_computation.3 | async-start | bytes 3670016 | tf_op jit(solution)/shard_map/all_to_all | solution.py:886
  324.7 21.9 %collective-permute-start.19 = (bf16[1024,1024]{1,0:T(8,128)(2,1)}, bf16[1024,1024]{1,0:T(8,128)(2,1)}, u32[]{:S(2)}, u32[]{:S(2)}) collective-permute-start(bf16[1024,1024]{1,0:T(8,128)(2,1)} %get-tuple-element.194), channel_id=1, source_target_pairs={{0,1},{1,0},{2,3},{3,2},{4,5},{5,4},{6,7},{7,6},{8,9},{9,8},{10,11... | collective-permute-start | bytes 6291464 | tf_op jit(solution)/shard_map/ppermute | solution.py:849
  324.8 27.9 %collective-permute-start.18 = (bf16[1024,1024]{1,0:T(8,128)(2,1)S(1)}, bf16[1024,1024]{1,0:T(8,128)(2,1)}, u32[]{:S(2)}, u32[]{:S(2)}) collective-permute-start(bf16[1024,1024]{1,0:T(8,128)(2,1)S(1)} %get-tuple-element.181), channel_id=1, source_target_pairs={{0,1},{1,0},{2,3},{3,2},{4,5},{5,4},{6,7},{7,6},{8,9},{9,8},{10,11... | collective-permute-start | bytes 6291464 | tf_op jit(solution)/shard_map/ppermute | solution.py:849
  325.3 58.7 %all-to-all-start.4 = ((bf16[8,112,1024]{2,1,0:T(8,128)(2,1)}), bf16[8,112,1024]{2,1,0:T(8,128)(2,1)}, u32[]{:S(2)}, u32[]{:S(2)}) async-start(bf16[8,112,1024]{2,1,0:T(8,128)(2,1)} %bitcast.74), calls=%async_computation.4 | async-start | bytes 3670016 | tf_op jit(solution)/shard_map/all_to_all | solution.py:886
  351.1 54.8 %collective-permute-start.20 = (bf16[1024,1024]{1,0:T(8,128)(2,1)}, bf16[1024,1024]{1,0:T(8,128)(2,1)}, u32[]{:S(2)}, u32[]{:S(2)}) collective-permute-start(bf16[1024,1024]{1,0:T(8,128)(2,1)} %add_convert_fusion.2), channel_id=1, source_target_pairs={{0,2},{1,3},{2,0},{3,1},{4,6},{5,7},{6,4},{7,5},{8,10},{9,11},{10,... | collective-permute-start | bytes 6291464 | tf_op jit(solution)/shard_map/ppermute | solution.py:849
  369.6 41.2 %collective-permute-start.25 = (bf16[1024,1024]{1,0:T(8,128)(2,1)}, bf16[1024,1024]{1,0:T(8,128)(2,1)}, u32[]{:S(2)}, u32[]{:S(2)}) collective-permute-start(bf16[1024,1024]{1,0:T(8,128)(2,1)} %get-tuple-element.203), channel_id=1, source_target_pairs={{0,1},{1,0},{2,3},{3,2},{4,5},{5,4},{6,7},{7,6},{8,9},{9,8},{10,11... | collective-permute-start | bytes 6291464 | tf_op jit(solution)/shard_map/ppermute | solution.py:849
  383.9 49.4 %all-to-all-start.5 = ((bf16[8,112,1024]{2,1,0:T(8,128)(2,1)}), bf16[8,112,1024]{2,1,0:T(8,128)(2,1)}, u32[]{:S(2)}, u32[]{:S(2)}) async-start(bf16[8,112,1024]{2,1,0:T(8,128)(2,1)} %bitcast.73), calls=%async_computation.5 | async-start | bytes 3670016 | tf_op jit(solution)/shard_map/all_to_all | solution.py:886
  406.0 3.0 collective-permute-start.22
  406.2 31.7 %collective-permute-start.24 = (bf16[1024,1024]{1,0:T(8,128)(2,1)S(1)}, bf16[1024,1024]{1,0:T(8,128)(2,1)}, u32[]{:S(2)}, u32[]{:S(2)}) collective-permute-start(bf16[1024,1024]{1,0:T(8,128)(2,1)S(1)} %get-tuple-element.200), channel_id=1, source_target_pairs={{0,1},{1,0},{2,3},{3,2},{4,5},{5,4},{6,7},{7,6},{8,9},{9,8},{10,11... | collective-permute-start | bytes 6291464 | tf_op jit(solution)/shard_map/ppermute | solution.py:849
  406.5 34.7 %collective-permute-start.21 = (bf16[544,1152]{1,0:T(8,128)(2,1)}, bf16[544,1152]{1,0:T(8,128)(2,1)}, u32[]{:S(2)}, u32[]{:S(2)}) collective-permute-start(bf16[544,1152]{1,0:T(8,128)(2,1)} %get-tuple-element.196), channel_id=1, source_target_pairs={{0,1},{1,0},{2,3},{3,2},{4,5},{5,4},{6,7},{7,6},{8,9},{9,8},{10,11... | collective-permute-start | bytes 3760136 | tf_op jit(solution)/shard_map/ppermute | solution.py:849
  410.3 33.6 %collective-permute-start.23 = (bf16[544,1152]{1,0:T(8,128)(2,1)}, bf16[544,1152]{1,0:T(8,128)(2,1)}, u32[]{:S(2)}, u32[]{:S(2)}) collective-permute-start(bf16[544,1152]{1,0:T(8,128)(2,1)} %add_convert_fusion.4), channel_id=1, source_target_pairs={{0,2},{1,3},{2,0},{3,1},{4,6},{5,7},{6,4},{7,5},{8,10},{9,11},{10,... | collective-permute-start | bytes 3760136 | tf_op jit(solution)/shard_map/ppermute | solution.py:849
  433.3 122.8 %all-to-all-start.6 = ((bf16[8,112,1024]{2,1,0:T(8,128)(2,1)}), bf16[8,112,1024]{2,1,0:T(8,128)(2,1)}, u32[]{:S(2)}, u32[]{:S(2)}) async-start(bf16[8,112,1024]{2,1,0:T(8,128)(2,1)} %bitcast.72), calls=%async_computation.6 | async-start | bytes 3670016 | tf_op jit(solution)/shard_map/all_to_all | solution.py:886
  458.9 5.2 collective-permute-start.31
  458.9 97.2 %collective-permute-start.30 = (bf16[1024,1024]{1,0:T(8,128)(2,1)}, bf16[1024,1024]{1,0:T(8,128)(2,1)}, u32[]{:S(2)}, u32[]{:S(2)}) collective-permute-start(bf16[1024,1024]{1,0:T(8,128)(2,1)} %add_convert_fusion), channel_id=1, source_target_pairs={{0,2},{1,3},{2,0},{3,1},{4,6},{5,7},{6,4},{7,5},{8,10},{9,11},{10,... | collective-permute-start | bytes 6291464 | tf_op jit(solution)/shard_map/ppermute | solution.py:849
  459.5 54.2 %collective-permute-start.26 = (bf16[544,256]{1,0:T(8,128)(2,1)}, bf16[544,256]{1,0:T(8,128)(2,1)}, u32[]{:S(2)}, u32[]{:S(2)}) collective-permute-start(bf16[544,256]{1,0:T(8,128)(2,1)} %get-tuple-element.213), channel_id=1, source_target_pairs={{0,2},{1,3},{2,0},{3,1},{4,6},{5,7},{6,4},{7,5},{8,10},{9,11},{10,... | collective-permute-start | bytes 835592 | tf_op jit(solution)/shard_map/ppermute | solution.py:849
  461.0 53.2 %collective-permute-start.27 = (bf16[544,256]{1,0:T(8,128)(2,1)}, bf16[544,256]{1,0:T(8,128)(2,1)}, u32[]{:S(2)}, u32[]{:S(2)}) collective-permute-start(bf16[544,256]{1,0:T(8,128)(2,1)} %get-tuple-element.214), channel_id=1, source_target_pairs={{0,1},{1,0},{2,3},{3,2},{4,5},{5,4},{6,7},{7,6},{8,9},{9,8},{10,11... | collective-permute-start | bytes 835592 | tf_op jit(solution)/shard_map/ppermute | solution.py:849
  461.0 57.9 %collective-permute-start.28 = (bf16[544,256]{1,0:T(8,128)(2,1)}, bf16[544,256]{1,0:T(8,128)(2,1)}, u32[]{:S(2)}, u32[]{:S(2)}) collective-permute-start(bf16[544,256]{1,0:T(8,128)(2,1)} %get-tuple-element.215), channel_id=1, source_target_pairs={{0,3},{1,2},{2,1},{3,0},{4,7},{5,6},{6,5},{7,4},{8,11},{9,10},{10,... | collective-permute-start | bytes 835592 | tf_op jit(solution)/shard_map/ppermute | solution.py:849
  464.2 93.4 %collective-permute-start.29 = (bf16[256,1024]{1,0:T(8,128)(2,1)}, bf16[256,1024]{1,0:T(8,128)(2,1)}, u32[]{:S(2)}, u32[]{:S(2)}) collective-permute-start(bf16[256,1024]{1,0:T(8,128)(2,1)} %copy-done.38), channel_id=1, source_target_pairs={{0,1},{1,0},{2,3},{3,2},{4,5},{5,4},{6,7},{7,6},{8,9},{9,8},{10,11... | collective-permute-start | bytes 1572872 | tf_op jit(solution)/shard_map/ppermute | solution.py:849
  513.7 42.5 %collective-permute-start.32 = (bf16[256,1024]{1,0:T(8,128)(2,1)}, bf16[256,1024]{1,0:T(8,128)(2,1)}, u32[]{:S(2)}, u32[]{:S(2)}) collective-permute-start(bf16[256,1024]{1,0:T(8,128)(2,1)} %add_convert_fusion.12), channel_id=1, source_target_pairs={{0,2},{1,3},{2,0},{3,1},{4,6},{5,7},{6,4},{7,5},{8,10},{9,11},{10,... | collective-permute-start | bytes 1572872 | tf_op jit(solution)/shard_map/ppermute | solution.py:849
  556.1 10.8 %collective-permute-start.33 = (bf16[544,1024]{1,0:T(8,128)(2,1)}, bf16[544,1024]{1,0:T(8,128)(2,1)}, u32[]{:S(2)}, u32[]{:S(2)}) collective-permute-start(bf16[544,1024]{1,0:T(8,128)(2,1)} %copy-done.29), channel_id=1, source_target_pairs={{0,1},{1,0},{2,3},{3,2},{4,5},{5,4},{6,7},{7,6},{8,9},{9,8},{10,11... | collective-permute-start | bytes 3342344 | tf_op jit(solution)/shard_map/ppermute | solution.py:849
  560.9 65.1 %all-to-all-start.7 = ((bf16[8,144,1024]{2,1,0:T(8,128)(2,1)}), bf16[8,144,1024]{2,1,0:T(8,128)(2,1)}, u32[]{:S(2)}, u32[]{:S(2)}) async-start(bf16[8,144,1024]{2,1,0:T(8,128)(2,1)} %bitcast.66), calls=%async_computation.7 | async-start | bytes 4718592 | tf_op jit(solution)/shard_map/all_to_all | solution.py:886
  566.9 121.1 %all-gather.2.cloned.1.call-start = ((), (), s32[]{:S(2)}) async-start(), calls=%async_computation.8 | async-start | bytes 2654208 | tf_op jit(solution)/shard_map/all_gather | solution.py:1027
  568.9 26.4 %collective-permute-start.34 = (bf16[544,1024]{1,0:T(8,128)(2,1)S(1)}, bf16[544,1024]{1,0:T(8,128)(2,1)S(1)}, u32[]{:S(2)}, u32[]{:S(2)}) collective-permute-start(bf16[544,1024]{1,0:T(8,128)(2,1)S(1)} %add_convert_fusion.10), channel_id=1, source_target_pairs={{0,2},{1,3},{2,0},{3,1},{4,6},{5,7},{6,4},{7,5},{8,10},{9,11},{10,... | collective-permute-start | bytes 3342344 | tf_op jit(solution)/shard_map/ppermute | solution.py:849
  583.1 42.0 %copy-start.48 = (f32[544,1024]{1,0:T(8,128)S(1)}, f32[544,1024]{1,0:T(8,128)}, u32[]{:S(2)}) copy-start(f32[544,1024]{1,0:T(8,128)} %get-tuple-element.205.refs_2_) | copy-start | bytes 6684676
  595.3 2.8 collective-permute-start.36
  595.3 4.3 collective-permute-start.35
  598.5 26.7 %collective-permute-start.37 = (bf16[544,1024]{1,0:T(8,128)(2,1)S(1)}, bf16[544,1024]{1,0:T(8,128)(2,1)S(1)}, u32[]{:S(2)}, u32[]{:S(2)}) collective-permute-start(bf16[544,1024]{1,0:T(8,128)(2,1)S(1)} %add_convert_fusion.8), channel_id=1, source_target_pairs={{0,2},{1,3},{2,0},{3,1},{4,6},{5,7},{6,4},{7,5},{8,10},{9,11},{10,... | collective-permute-start | bytes 3342344 | tf_op jit(solution)/shard_map/ppermute | solution.py:849
  628.9 3.0 collective-permute-start.41
  637.2 27.7 %collective-permute-start.42 = (bf16[544,1024]{1,0:T(8,128)(2,1)}, bf16[544,1024]{1,0:T(8,128)(2,1)}, u32[]{:S(2)}, u32[]{:S(2)}) collective-permute-start(bf16[544,1024]{1,0:T(8,128)(2,1)} %input_back.1.refs_0_), channel_id=1, source_target_pairs={{0,2},{1,3},{2,0},{3,1},{4,6},{5,7},{6,4},{7,5},{8,10},{9,11},{10,... | collective-permute-start | bytes 3342344 | tf_op jit(solution)/shard_map/ppermute | solution.py:849
  637.7 50.3 %collective-permute-start.38 = (bf16[544,1024]{1,0:T(8,128)(2,1)S(1)}, bf16[544,1024]{1,0:T(8,128)(2,1)}, u32[]{:S(2)}, u32[]{:S(2)}) collective-permute-start(bf16[544,1024]{1,0:T(8,128)(2,1)S(1)} %add_convert_fusion.7.refs_0_), channel_id=1, source_target_pairs={{0,2},{1,3},{2,0},{3,1},{4,6},{5,7},{6,4},{7,5},{8,10},{9,11},{10,... | collective-permute-start | bytes 3342344 | tf_op jit(solution)/shard_map/ppermute | solution.py:849
  639.2 59.9 %collective-permute-start.43 = (bf16[544,1024]{1,0:T(8,128)(2,1)}, bf16[544,1024]{1,0:T(8,128)(2,1)}, u32[]{:S(2)}, u32[]{:S(2)}) collective-permute-start(bf16[544,1024]{1,0:T(8,128)(2,1)} %input_back.1.refs_0_), channel_id=1, source_target_pairs={{0,1},{1,0},{2,3},{3,2},{4,5},{5,4},{6,7},{7,6},{8,9},{9,8},{10,11... | collective-permute-start | bytes 3342344 | tf_op jit(solution)/shard_map/ppermute | solution.py:849
  664.9 34.2 %collective-permute-start.44 = (bf16[544,1024]{1,0:T(8,128)(2,1)}, bf16[544,1024]{1,0:T(8,128)(2,1)}, u32[]{:S(2)}, u32[]{:S(2)}) collective-permute-start(bf16[544,1024]{1,0:T(8,128)(2,1)} %collective-permute-done.42.refs_1_), channel_id=1, source_target_pairs={{0,1},{1,0},{2,3},{3,2},{4,5},{5,4},{6,7},{7,6},{8,9},{9,8},{10,11... | collective-permute-start | bytes 3342344 | tf_op jit(solution)/shard_map/ppermute | solution.py:849
  664.9 42.9 %collective-permute-start.39 = (bf16[544,1024]{1,0:T(8,128)(2,1)S(1)}, bf16[544,1024]{1,0:T(8,128)(2,1)}, u32[]{:S(2)}, u32[]{:S(2)}) collective-permute-start(bf16[544,1024]{1,0:T(8,128)(2,1)S(1)} %add_convert_fusion.7.refs_0_), channel_id=1, source_target_pairs={{0,1},{1,0},{2,3},{3,2},{4,5},{5,4},{6,7},{7,6},{8,9},{9,8},{10,11... | collective-permute-start | bytes 3342344 | tf_op jit(solution)/shard_map/ppermute | solution.py:849
  688.0 19.9 %collective-permute-start.40 = (bf16[544,1024]{1,0:T(8,128)(2,1)}, bf16[544,1024]{1,0:T(8,128)(2,1)}, u32[]{:S(2)}, u32[]{:S(2)}) collective-permute-start(bf16[544,1024]{1,0:T(8,128)(2,1)} %collective-permute-done.38.refs_1_), channel_id=1, source_target_pairs={{0,1},{1,0},{2,3},{3,2},{4,5},{5,4},{6,7},{7,6},{8,9},{9,8},{10,11... | collective-permute-start | bytes 3342344 | tf_op jit(solution)/shard_map/ppermute | solution.py:849
  688.7 27.3 %collective-permute-start.45 = (f32[10,1024]{1,0:T(8,128)S(1)}, f32[10,1024]{1,0:T(8,128)S(1)}, u32[]{:S(2)}, u32[]{:S(2)}) collective-permute-start(f32[10,1024]{1,0:T(8,128)S(1)} %slice_convert_fusion.1), channel_id=1, source_target_pairs={{0,1},{1,0},{2,3},{3,2},{4,5},{5,4},{6,7},{7,6},{8,9},{9,8},{10,11... | collective-permute-start | bytes 122888 | tf_op jit(solution)/shard_map/ppermute | solution.py:849
  716.0 4.3 collective-permute-start.46
  (50 other events, 114.1 us)
Sparse Core Ops, SparseCore 0:
  629.0 52.2 all-gather.1

commit v5 on v4

--- a/solution.py
+++ b/solution.py
@@ -20,7 +20,7 @@
     return -(-value // unit) * unit
 
 
-def params(mib=48):
+def params(mib=60):
     return pltpu.CompilerParams(vmem_limit_bytes=mib * 1024 * 1024)
 
 
@@ -433,8 +433,7 @@
 def assemble(part_of, pieces, rows, dtype):
     each, width = pieces[0].shape
     count = len(pieces)
-    tile = each // 2 if each % 32 == 0 else each
-    steps = each // tile
+    tile, steps = each, 1
     in_specs, _ = by_piece(count, steps, (tile, width), (each, width), BF)
     spec = pltpu.PrefetchScalarGridSpec(
         num_scalar_prefetch=1,
@@ -701,24 +700,35 @@
     rg_ref[...] = rows_grad
     hidden_here = w1.shape[2]
     step = min(512, hidden_here)
-    for t in range(count):
-
+
+    def wait(groups):
         @pl.when(pl.program_id(0) == 0)
         def _():
-            for item in copies[t]:
-                item.wait()
-
+            for group in groups:
+                for item in group:
+                    item.wait()
+
+    def first_products(t):
+        parts = []
         for at in range(0, hidden_here, step):
             cols = slice(at, at + step)
+            parts.append((at, dot(rows, w1[t, :, cols]), dot(rows_grad, w2[t, cols, :], 1, 1)))
+        return parts
+
+    wait(copies[:1])
+    ready = first_products(0)
+    wait(copies[1:])
+    out = None
+    grad = None
+    for t in range(count):
+        parts = ready
+        if t + 1 < count:
+            ready = first_products(t + 1)
+        for at, hidden, active_grad in parts:
             place = slice(t * hidden_here + at, t * hidden_here + at + step)
-            hidden = dot(rows, w1[t, :, cols])
-            active_grad = dot(rows_grad, w2[t, cols, :], 1, 1)
             active, slope = gelu_parts(hidden)
             act_ref[:, place] = active.astype(BF)
             hg_ref[:, place] = (active_grad * slope).astype(BF)
-    out = None
-    grad = None
-    for t in range(count):
         place = slice(t * hidden_here, (t + 1) * hidden_here)
         part = dot(act_ref[:, place], w2[t])
         out = part if out is None else out + part
@@ -772,7 +782,7 @@
             pltpu.VMEM((count, here, width), BF),
             pltpu.SemaphoreType.DMA((3 * count,)),
         ],
-        compiler_params=params(60),
+        compiler_params=params(),
         cost_estimate=pl.CostEstimate(flops=flops, bytes_accessed=rows * total * 6, transcendentals=rows * total * 2),
         name="expert",
     )(x, g, router, *w1, *w2)
@@ -861,7 +871,7 @@
         return gathered_from(x, far_part(x))
 
     def near_hop(pieces):
-        return [cross(piece, 1) for piece in pieces[2:]] if paired else pieces
+        return pinned(*[cross(piece, 1) for piece in pieces[2:]]) if paired else pieces
 
     def near_sum(pieces, came):
         if not paired:
@@ -916,7 +926,7 @@
 
     router_wide = jnp.pad(router, ((0, 0), (0, LANES - experts)))
     gain_one, gain_two = norm_one[None, :], norm_two[None, :]
-    head_out_all = gathered(head_out)
+    head_out_far = far_part(head_out)
     w1_own = [expert_in[0, : width // 2], expert_in[0, width // 2 :]]
     w1_far = [far_part(item) for item in w1_own]
 
@@ -927,7 +937,8 @@
     first_in, qkv, logs, *mixed = attend(
         starts, block_rows, tail_of(block_in), gain_one, head_in, images, height, each, parts
     )
-    *mixed, w1_far[1] = pinned(*mixed, w1_far[1])
+    *mixed, w1_far[1], head_out_far = pinned(*mixed, w1_far[1], head_out_far)
+    head_out_all = gathered_from(head_out, head_out_far)
     mixed = swapped(mixed)
     middle, second_in, gates = middle_of(
         own_block, mixed, head_out_all, block_in, gain_two, router_wide, expert_ids, route_noise
@@ -958,7 +969,7 @@
             x, signal, n, router_wide, w1, w2, slots, per
         )
         if returned:
-            row_grad, returned[-1] = pinned(row_grad, returned[-1])
+            row_grad, active, returned[-1] = pinned(row_grad, active, returned[-1])
         arrived.append(x)
         actives.append(active)
         hidden_grads.append(hidden_grad)
@@ -974,22 +985,16 @@
 
     out_parts = weight_parts(actives, rows_grads)
     out_kept, out_other = near_sum(out_parts, near_hop(out_parts))
-    out_kept, *hidden_grads = pinned(out_kept, *hidden_grads)
     out_far = far_hop(out_kept, out_other)
+    *returned, out_kept = pinned(*returned, out_kept)
+
+    second_pieces = unpack(part_of, place, returned, slots, per, each, True)
+    second_kept, second_other = near_sum(second_pieces, near_hop(second_pieces))
+    second_kept, out_far, *hidden_grads = pinned(second_kept, out_far, *hidden_grads)
+    second_far = far_hop(second_kept, second_other)
     in_parts = weight_parts(hidden_grads, arrived)
     in_came = near_hop(in_parts)
-    *returned, in_first = pinned(*returned, in_parts[0])
-    in_parts[0] = in_first
-
-    second_pieces = unpack(part_of, place, returned, slots, per, each, True)
-    *second_pieces, out_far = pinned(*second_pieces, out_far)
-    out_grad = out_kept.astype(F32) + out_far.astype(F32)
-    second_kept, second_far = scattered(second_pieces)
-    in_kept, in_other = near_sum(in_parts, in_came)
-    second_far, in_kept = pinned(second_far, in_kept)
-    if paired:
-        second_far, in_other = pinned(second_far, in_other)
-    in_far = far_hop(in_kept, in_other)
+    second_far, *in_parts = pinned(second_far, *in_parts)
     combined = [sent(item) for item in backs]
     middle_grad, router_part, norm_two_part, *pieces = middle_back(
         own_block, second_kept, second_far, middle, second_in, gates, expert_ids, cotangent, mixed, head_out_all,
@@ -997,18 +1002,23 @@
     )
     head_out_parts, mixed_grad = pieces[:parts], pieces[parts:]
     *mixed_grad, combined[0] = pinned(*mixed_grad, combined[0])
-    mixed_grad = swapped(mixed_grad)
+    *mixed_grad, in_came = pinned(*swapped(mixed_grad), in_came)
+    in_kept, in_other = near_sum(in_parts, in_came)
+    in_far = far_hop(in_kept, in_other)
     head_out_kept, head_out_far = scattered(head_out_parts)
     *pieces, head_in_part, norm_one_part = attend_back(
         starts, mixed_grad, qkv, logs, first_in, jnp.swapaxes(head_in, 1, 2), gain_one
     )
     *pieces, combined[-1], in_far, head_out_far = pinned(*pieces, combined[-1], in_far, head_out_far)
-    in_grad = sum_turned(in_kept, in_far)
     first_kept, first_far = scattered(pieces)
     block_pieces = unpack(part_of, place, combined, slots, per, each, False)
-    first_far, *block_pieces = pinned(first_far, *block_pieces)
+    block_kept, block_other = near_sum(block_pieces, near_hop(block_pieces))
+    first_far, block_kept = pinned(first_far, block_kept)
+    block_far = far_hop(block_kept, block_other)
     input_part = input_back(own_block, first_kept, first_far, block_in, middle_grad, gain_one)
-    block_kept, block_far = scattered(block_pieces)
+    out_grad = out_kept.astype(F32) + out_far.astype(F32)
+    in_grad = sum_turned(in_kept, in_far)
+    input_far, out_grad, in_grad = pinned(far_part(input_part), out_grad, in_grad)
     block_own = (middle + block_kept.astype(F32) + block_far.astype(F32)).astype(BF)
 
     cols = head_in.shape[2]
@@ -1021,7 +1031,7 @@
     )
     heads = over_experts(heads.reshape(groups, total // groups, width))
     heads, block_own = pinned(heads, block_own)
-    input_grad = assemble(part_of, gathered(input_part), rows_here, F32)
+    input_grad = assemble(part_of, gathered_from(input_part, input_far), rows_here, F32)
     block_out = assemble(part_of, gathered(block_own), rows_here, BF)
     heads = jnp.sum(heads.astype(F32), 0).astype(BF)
     heads = lax.all_gather(heads, "expert", axis=0, tiled=True)

time: 736 us -> 709 us (0.963)
  waiting for transfers between devices: 243 us -> 219 us
  local copies, waits for them, and re-layouts: 52.3 us -> 28.8 us
  Pallas kernels: 307 us -> 327 us
    unnamed x117 -> x81, local copies, waits for them, and re-layouts: 40.5 us -> 13.3 us
    ppermute x47, waiting for transfers between devices: 214 us -> 194 us  [cross(): return lax.ppermute(x, 'tensor', [(n, n ^ k) for n in range(parts)])]
    convert_element_type x10 -> x11, other arithmetic: 26 us -> 23.8 us  [near_sum(): (a.astype(F32) + b.astype(F32)).astype(BF)]
  transfers between devices with their start and end apart: 56 -> 56, of which waited for: 19 -> 24; matrix products, arithmetic and copies ran while one was open for 7% -> 8% of each run, Pallas kernels for 42% -> 47%
where the time goes in v5:
time: 709 us; the launch traced here: 702 us
  Pallas kernels  327 us (46%)
  waiting for transfers between devices  219 us (31%)
  starting transfers between devices  67.3 us (9%)
  other arithmetic  43.7 us (6%)
  local copies, waits for them, and re-layouts  28.8 us (4%)
  between operations  14.9 us (2%)
    ppermute x47, waiting for transfers between devices, cross(): return lax.ppermute(x, 'tensor', [(n, n ^ k) for n in range(parts)])  194 us
    pallas_call x2, Pallas kernels, expert(): pl.pallas_call(functools.partial(expert_kernel, count, slots, per), grid=...  95.2 us
    pallas_call x4, Pallas kernels, weight_grad(): pl.pallas_call(functools.partial(weight_kernel, count, steps), grid=(2 *...  56 us
    all_to_all x8, starting transfers between devices, over_experts(): return lax.all_to_all(x, 'expert', split_axis=0, concat_axis=0, tiled=True)  40.9 us
    pallas_call x1, Pallas kernels, attend_back(): pl.pallas_call(functools.partial(attend_back_kernel, count), grid_spec=sp...  34.3 us
    pallas_call x2, Pallas kernels, unpack(): pl.pallas_call(functools.partial(unpack_kernel, count, slots, per, graded...  33.6 us
    pallas_call x1, Pallas kernels, attend(): pl.pallas_call(functools.partial(attend_kernel, count), grid_spec=spec, o...  30.3 us
    ppermute x47, starting transfers between devices, cross(): return lax.ppermute(x, 'tensor', [(n, n ^ k) for n in range(parts)])  26.4 us
  transfers between devices with their start and end apart: 56, of which 24 were waited for; matrix products, arithmetic and copies ran while one was open for 8% of the time, Pallas kernels for 47%

profile of v5, /device:TPU:0, one launch (start us, length us, event | category | flops | bytes accessed | tf_op | source)
XLA Modules:
  0.0 701.5 jit_solution(10093282205215038055)
XLA Ops:
  7.2 3.1 slice_bitcast_fusion
  10.2 2.9 collective-permute-start
  13.3 2.3 reduce-window.6
  23.3 17.3 %pack_cotangent.1 = bf16[8,2,112,1152]{3,2,1,0:T(8,128)(2,1)} custom-call(bf16[2167,1024]{1,0:T(8,128)(2,1)} %refs_6_.1, bf16[16,1024]{1,0:T(8,128)(2,1)} %pad.26.tail_ref, s32[2,2176]{1,0:T(2,128)} %copy.103.lp_ref, bf16[2,2176,128]{2,1,0:T(8,128)(2,1)} %fusion.5.side_ref), custom_call_target="tpu_custom_call" | custom-call | flops 11978932224 | bytes 4438016 | tf_op jit(solution)/shard_map/pack_cotangent/pallas_call | solution.py:323
  40.7 6.2 all-to-all-start
  50.3 30.3 %attend.1 = (bf16[11,208,1024]{2,1,0:T(8,128)(2,1)}, bf16[3,11,208,256]{3,2,1,0:T(8,128)(2,1)}, f32[11,208,128]{2,1,0:T(8,128)}, bf16[544,256]{1,0:T(8,128)(2,1)...) custom-call(s32[4]{0:T(128)} %get-tuple-element.291.starts_ref, ...), custom_call_target="tpu_custom_call" | custom-call | flops 9596567552 | bytes 35504128 | tf_op jit(solution)/shard_map/attend/pallas_call | solution.py:180
  80.6 1.9 collective-permute-done.2.refs_5_.refs_14_
  88.5 3.8 collective-permute-done.3.refs_1_.refs_10_
  92.3 5.1 collective-permute-done.5.refs_3_.refs_12_
  98.2 6.8 middle.1
  105.9 26.4 %collective-permute-done.8.refs_1_ = bf16[544,1024]{1,0:T(8,128)(2,1)S(1)} collective-permute-done((bf16[544,1024]{1,0:T(8,128)(2,1)}, bf16[544,1024]{1,0:T(8,128)(2,1)S(1)}, u32[]{:S(2)}, u32[]{:S(2)}) %collective-permute-start.8) | collective-permute-done | bytes 1114144 | tf_op jit(solution)/shard_map/ppermute | solution.py:859
  132.4 2.9 collective-permute-done.10.refs_3_
  135.3 3.1 all-to-all-done.g_ref
  139.9 9.9 %pack_rows.2 = bf16[896,1024]{1,0:T(8,128)(2,1)} custom-call(s32[4]{0:T(128)} %get-tuple-element.292.part_ref, bf16[544,1024]{1,0:T(8,128)(2,1)} %get-tuple-element.161.refs_0_.refs_3_, bf16[544,1024]{1,0:T(8,128)(2,1)} %copy-done.34, bf16[544,1024]{1,0:T(8,128)(2,1)} %copy-done.35, bf16[544,1024]{1,0:T(8,128)(2,1)} %collective-permute-done.10.refs_3_, ...), custom_call_target="tpu_custom_call" | custom-call | flops 5989466112 | bytes 4456448 | tf_op jit(solution)/shard_map/pack_rows/pallas_call | solution.py:359
  149.9 3.7 all-to-all-start.1
  154.1 9.9 %pack_rows.3 = bf16[896,1024]{1,0:T(8,128)(2,1)} custom-call(s32[4]{0:T(128)} %get-tuple-element.292.part_ref, bf16[544,1024]{1,0:T(8,128)(2,1)} %get-tuple-element.161.refs_0_.refs_3_, bf16[544,1024]{1,0:T(8,128)(2,1)} %copy-done.34, bf16[544,1024]{1,0:T(8,128)(2,1)} %copy-done.35, bf16[544,1024]{1,0:T(8,128)(2,1)} %collective-permute-done.10.refs_3_, ...), custom_call_target="tpu_custom_call" | custom-call | flops 5989466112 | bytes 4456448 | tf_op jit(solution)/shard_map/pack_rows/pallas_call | solution.py:359
  164.0 20.6 %collective-permute-done.11.refs_9_ = bf16[1024,1024]{1,0:T(8,128)(2,1)} collective-permute-done((bf16[1024,1024]{1,0:T(8,128)(2,1)}, bf16[1024,1024]{1,0:T(8,128)(2,1)}, u32[]{:S(2)}, u32[]{:S(2)}) %collective-permute-start.11) | collective-permute-done | bytes 2097184 | tf_op jit(solution)/shard_map/ppermute | solution.py:859
  185.7 10.4 %all-to-all-done.1 = bf16[8,112,1024]{2,1,0:T(8,128)(2,1)S(1)} async-done(((bf16[8,112,1024]{2,1,0:T(8,128)(2,1)}), bf16[8,112,1024]{2,1,0:T(8,128)(2,1)S(1)}, u32[]{:S(2)}, u32[]{:S(2)}) %all-to-all-start.1) | async-done | bytes 1835040 | tf_op jit(solution)/shard_map/all_to_all | solution.py:896
  197.4 4.3 all-to-all-start.2
  201.8 47.5 %expert.2 = (bf16[896,1024]{1,0:T(8,128)(2,1)}, bf16[896,4096]{1,0:T(8,128)(2,1)}, bf16[896,4096]{1,0:T(8,128)(2,1)}, bf16[896,1024]{1,0:T(8,128)(2,1)}, bf16[896,1024]{1,0:T(8,128)(2,1)}) custom-call(bf16[896,1024]{1,0:T(8,128)(2,1)} %bitcast.63, bf16[8,2,112,1152]{3,2,1,0:T(8,128)(2,1)} %all-to-all-done.g_ref, ...), custom_call_target="tpu_custom_call" | custom-call | flops 30064771072 | bytes 22020096 | tf_op jit(solution)/shard_map/expert/pallas_call | solution.py:763
  249.3 5.9 all-to-all-start.3
  255.2 47.7 %expert.3 = (bf16[896,1024]{1,0:T(8,128)(2,1)}, bf16[896,4096]{1,0:T(8,128)(2,1)}, bf16[896,4096]{1,0:T(8,128)(2,1)}, bf16[896,1024]{1,0:T(8,128)(2,1)}, bf16[896,1024]{1,0:T(8,128)(2,1)}) custom-call(bf16[896,1024]{1,0:T(8,128)(2,1)} %bitcast.21.x_ref.refs_3_, bf16[8,2,112,1152]{3,2,1,0:T(8,128)(2,1)} %all-to-all-done.g_ref, ...), custom_call_target="tpu_custom_call" | custom-call | flops 30064771072 | bytes 22020096 | tf_op jit(solution)/shard_map/expert/pallas_call | solution.py:763
  304.1 6.0 all-to-all-start.4
  310.1 14.0 %weight_grad.5 = (bf16[1024,1024]{1,0:T(8,128)(2,1)}, bf16[1024,1024]{1,0:T(8,128)(2,1)}) custom-call(bf16[896,4096]{1,0:T(8,128)(2,1)} %get-tuple-element.193.refs_0_, bf16[896,1024]{1,0:T(8,128)(2,1)} %get-tuple-element.194.refs_1_, bf16[896,4096]{1,0:T(8,128)(2,1)} %get-tuple-element.195.refs_2_, bf16[896,1024]{1,0:T(8,128)(2,1)} %get-tuple-element.196.refs_3_), custom_call_target="tpu_custom_call" | custom-call | flops 7516192768 | bytes 8388608 | tf_op jit(solution)/shard_map/weight_grad/pallas_call | solution.py:811
  324.6 14.0 %weight_grad.4 = (bf16[1024,1024]{1,0:T(8,128)(2,1)}, bf16[1024,1024]{1,0:T(8,128)(2,1)}) custom-call(bf16[896,4096]{1,0:T(8,128)(2,1)} %get-tuple-element.193.refs_0_, bf16[896,1024]{1,0:T(8,128)(2,1)} %get-tuple-element.194.refs_1_, bf16[896,4096]{1,0:T(8,128)(2,1)} %get-tuple-element.195.refs_2_, bf16[896,1024]{1,0:T(8,128)(2,1)} %get-tuple-element.196.refs_3_), custom_call_target="tpu_custom_call" | custom-call | flops 7516192768 | bytes 8388608 | tf_op jit(solution)/shard_map/weight_grad/pallas_call | solution.py:811
  339.9 3.4 add_convert_fusion.2
  344.9 2.3 add_convert_fusion.3
  347.1 4.4 all-to-all-done.4
  351.5 17.5 %unpack_rows.2 = (bf16[544,1152]{1,0:T(8,128)(2,1)}, bf16[544,1152]{1,0:T(8,128)(2,1)}, bf16[544,1152]{1,0:T(8,128)(2,1)}, bf16[544,1152]{1,0:T(8,128)(2,1)}) custom-call(s32[4]{0:T(128)} %get-tuple-element.292.part_ref, s32[2176,2]{1,0:T(8,128)} %copy-done.2, bf16[896,1024]{1,0:T(8,128)(2,1)} %bitcast.67, bf16[896,1024]{1,0:T(8,128)(2,1)} %bitcast.25.refs_1_), custom_call_target="tpu_custom_call" | custom-call | flops 11978932224 | bytes 7340032 | tf_op jit(solution)/shard_map/unpack_rows/pallas_call | solution.py:414
  369.6 4.3 all-to-all-start.5
  374.0 3.5 add_convert_fusion.5.refs_0_
  377.5 13.6 %collective-permute-done.22 = bf16[1024,1024]{1,0:T(8,128)(2,1)} collective-permute-done((bf16[1024,1024]{1,0:T(8,128)(2,1)S(1)}, bf16[1024,1024]{1,0:T(8,128)(2,1)}, u32[]{:S(2)}, u32[]{:S(2)}) %collective-permute-start.22) | collective-permute-done | bytes 2097184 | tf_op jit(solution)/shard_map/ppermute | solution.py:859
  391.1 14.0 %weight_grad.7 = (bf16[1024,1024]{1,0:T(8,128)(2,1)}, bf16[1024,1024]{1,0:T(8,128)(2,1)}) custom-call(bf16[896,4096]{1,0:T(8,128)(2,1)} %get-tuple-element.214.refs_0_, bf16[896,1024]{1,0:T(8,128)(2,1)} %bitcast.64, bf16[896,4096]{1,0:T(8,128)(2,1)} %get-tuple-element.215.refs_2_, bf16[896,1024]{1,0:T(8,128)(2,1)} %bitcast.21.x_ref.refs_3_), custom_call_target="tpu_custom_call" | custom-call | flops 7516192768 | bytes 8388608 | tf_op jit(solution)/shard_map/weight_grad/pallas_call | solution.py:811
  405.6 2.6 add_convert_fusion.4
  409.7 7.3 %all-to-all-done.5 = bf16[8,112,1024]{2,1,0:T(8,128)(2,1)} async-done(((bf16[8,112,1024]{2,1,0:T(8,128)(2,1)}), bf16[8,112,1024]{2,1,0:T(8,128)(2,1)}, u32[]{:S(2)}, u32[]{:S(2)}) %all-to-all-start.5) | async-done | bytes 1835040 | tf_op jit(solution)/shard_map/all_to_all | solution.py:896
  417.0 4.5 all-to-all-start.6
  421.5 14.0 %weight_grad.6 = (bf16[1024,1024]{1,0:T(8,128)(2,1)}, bf16[1024,1024]{1,0:T(8,128)(2,1)}) custom-call(bf16[896,4096]{1,0:T(8,128)(2,1)} %get-tuple-element.214.refs_0_, bf16[896,1024]{1,0:T(8,128)(2,1)} %bitcast.65, bf16[896,4096]{1,0:T(8,128)(2,1)} %get-tuple-element.215.refs_2_, bf16[896,1024]{1,0:T(8,128)(2,1)} %bitcast.21.x_ref.refs_3_), custom_call_target="tpu_custom_call" | custom-call | flops 7516192768 | bytes 8388608 | tf_op jit(solution)/shard_map/weight_grad/pallas_call | solution.py:811
  435.5 2.4 collective-permute-done.23.refs_1_
  439.0 12.1 %middle_back.1 = (f32[544,1024]{1,0:T(8,128)}, f32[128,1024]{1,0:T(8,128)}, f32[1,1024]{1,0:T(1,128)}, bf16[256,1024]{1,0:T(8,128)(2,1)}, bf16[256,1024]{1,0:T(8...) custom-call(s32[1]{0:T(128)} %bitcast.12.at_ref, ...), custom_call_target="tpu_custom_call" | custom-call | flops 4563402752 | bytes 22282240 | tf_op jit(solution)/shard_map/middle_back/pallas_call | solution.py:609
  453.8 7.1 %collective-permute-done.24.refs_1_ = bf16[544,256]{1,0:T(8,128)(2,1)S(1)} collective-permute-done((bf16[544,256]{1,0:T(8,128)(2,1)}, bf16[544,256]{1,0:T(8,128)(2,1)S(1)}, u32[]{:S(2)}, u32[]{:S(2)}) %collective-permute-start.24) | collective-permute-done | bytes 278560 | tf_op jit(solution)/shard_map/ppermute | solution.py:859
  461.0 3.4 collective-permute-done.26.refs_3_
  464.4 4.5 add_convert_fusion.1
  469.7 2.6 copy.104
  475.4 34.3 %attend_back.1 = (bf16[544,1024]{1,0:T(8,128)(2,1)}, bf16[544,1024]{1,0:T(8,128)(2,1)}, bf16[544,1024]{1,0:T(8,128)(2,1)}, bf16[544,1024]{1,0:T(8,128)(2,1)}, bf...) custom-call(s32[4]{0:T(128)} %get-tuple-element.291.starts_ref, bf16[3,11,208,256]{3,2,1,0:T(8,128)(2,1)} %get-tuple-element.147.qkv_ref, ...), custom_call_target="tpu_custom_call" | custom-call | flops 14394851328 | bytes 46858240 | tf_op jit(solution)/shard_map/attend_back/pallas_call | solution.py:286
  510.5 18.3 %collective-permute-done.32 = bf16[256,1024]{1,0:T(8,128)(2,1)S(1)} collective-permute-done((bf16[256,1024]{1,0:T(8,128)(2,1)}, bf16[256,1024]{1,0:T(8,128)(2,1)S(1)}, u32[]{:S(2)}, u32[]{:S(2)}) %collective-permute-start.32) | collective-permute-done | bytes 524320 | tf_op jit(solution)/shard_map/ppermute | solution.py:859
  530.1 1.6 pad_maximum_fusion
  531.7 6.0 all-to-all-start.7
  537.7 16.1 %unpack_rows.3 = (bf16[544,1024]{1,0:T(8,128)(2,1)}, bf16[544,1024]{1,0:T(8,128)(2,1)}, bf16[544,1024]{1,0:T(8,128)(2,1)}, bf16[544,1024]{1,0:T(8,128)(2,1)}) custom-call(s32[4]{0:T(128)} %get-tuple-element.292.part_ref, s32[2176,2]{1,0:T(8,128)} %copy-done.2, bf16[896,1024]{1,0:T(8,128)(2,1)} %bitcast.27.refs_0_, bf16[896,1024]{1,0:T(8,128)(2,1)} %bitcast.30.refs_1_), custom_call_target="tpu_custom_call" | custom-call | flops 11978932224 | bytes 7340032 | tf_op jit(solution)/shard_map/unpack_rows/pallas_call | solution.py:414
  554.9 1.9 collective-permute-done.36
  556.8 3.2 collective-permute-done.37
  563.0 1.7 collective-permute-start.38
  565.1 24.4 %collective-permute-done.35.far_ref = bf16[544,1024]{1,0:T(8,128)(2,1)S(1)} collective-permute-done((bf16[544,1024]{1,0:T(8,128)(2,1)S(1)}, bf16[544,1024]{1,0:T(8,128)(2,1)S(1)}, u32[]{:S(2)}, u32[]{:S(2)}) %collective-permute-start.35) | collective-permute-done | bytes 1114144 | tf_op jit(solution)/shard_map/ppermute | solution.py:859
  590.5 22.1 %collective-permute-done.38 = bf16[544,1024]{1,0:T(8,128)(2,1)S(1)} collective-permute-done((bf16[544,1024]{1,0:T(8,128)(2,1)S(1)}, bf16[544,1024]{1,0:T(8,128)(2,1)S(1)}, u32[]{:S(2)}, u32[]{:S(2)}) %collective-permute-start.38) | collective-permute-done | bytes 1114144 | tf_op jit(solution)/shard_map/ppermute | solution.py:859
  614.4 3.0 add_convert_fusion.6.keep_ref
  617.4 4.4 input_back.1.refs_0_
  623.9 4.5 convert_add_fusion
  628.4 2.3 add_convert_fusion.a_ref
  630.7 5.3 sum_turned.1
  636.0 13.7 %collective-permute-done.42.refs_1_ = bf16[544,1024]{1,0:T(8,128)(2,1)} collective-permute-done((bf16[544,1024]{1,0:T(8,128)(2,1)}, bf16[544,1024]{1,0:T(8,128)(2,1)}, u32[]{:S(2)}, u32[]{:S(2)}) %collective-permute-start.42) | collective-permute-done | bytes 1114144 | tf_op jit(solution)/shard_map/ppermute | solution.py:859
  650.2 21.6 %collective-permute-done.39.refs_1_ = bf16[544,1024]{1,0:T(8,128)(2,1)} collective-permute-done((bf16[544,1024]{1,0:T(8,128)(2,1)S(1)}, bf16[544,1024]{1,0:T(8,128)(2,1)}, u32[]{:S(2)}, u32[]{:S(2)}) %collective-permute-start.39) | collective-permute-done | bytes 1114144 | tf_op jit(solution)/shard_map/ppermute | solution.py:859
  673.1 6.7 assemble.3
  680.8 5.4 assemble.2
  687.5 2.1 slice_convert_fusion
  691.1 2.1 copy.110
  (215 shorter events, 56.4 us)
Async XLA Ops:
  10.2 30.4 %collective-permute-start = (bf16[512,1024]{1,0:T(8,128)(2,1)}, bf16[512,1024]{1,0:T(8,128)(2,1)}, u32[]{:S(2)}, u32[]{:S(2)}) collective-permute-start(bf16[512,1024]{1,0:T(8,128)(2,1)} %get-tuple-element.174.refs_0_), channel_id=1, source_target_pairs={{0,2},{1,3},{2,0},{3,1},{4,6},{5,7},{6,4},{7,5},{8,10},{9,11},{10,... | collective-permute-start | bytes 3145736 | tf_op jit(solution)/shard_map/ppermute | solution.py:859
  19.4 119.5 %copy-start.2 = (s32[2176,2]{1,0:T(8,128)}, s32[2176,2]{1,0:T(8,128)S(1)}, u32[]{:S(2)}) copy-start(s32[2176,2]{1,0:T(8,128)S(1)} %get-tuple-element.296.lp_ref) | copy-start | bytes 52228
  40.7 97.7 %all-to-all-start = ((bf16[8,2,112,1152]{3,2,1,0:T(8,128)(2,1)}), bf16[8,2,112,1152]{3,2,1,0:T(8,128)(2,1)}, u32[]{:S(2)}, u32[]{:S(2)}) async-start(bf16[8,2,112,1152]{3,2,1,0:T(8,128)(2,1)} %pack_cotangent.1), calls=%async_computation | async-start | bytes 8257536 | tf_op jit(solution)/shard_map/all_to_all | solution.py:896
  46.9 35.6 %collective-permute-start.1 = (bf16[512,1024]{1,0:T(8,128)(2,1)S(1)}, bf16[512,1024]{1,0:T(8,128)(2,1)}, u32[]{:S(2)}, u32[]{:S(2)}) collective-permute-start(bf16[512,1024]{1,0:T(8,128)(2,1)S(1)} %copy-done.21), channel_id=1, source_target_pairs={{0,2},{1,3},{2,0},{3,1},{4,6},{5,7},{6,4},{7,5},{8,10},{9,11},{10,... | collective-permute-start | bytes 3145736 | tf_op jit(solution)/shard_map/ppermute | solution.py:859
  47.5 35.0 %collective-permute-start.2 = (bf16[256,1024]{1,0:T(8,128)(2,1)S(1)}, bf16[256,1024]{1,0:T(8,128)(2,1)S(1)}, u32[]{:S(2)}, u32[]{:S(2)}) collective-permute-start(bf16[256,1024]{1,0:T(8,128)(2,1)S(1)} %copy-done.23), channel_id=1, source_target_pairs={{0,2},{1,3},{2,0},{3,1},{4,6},{5,7},{6,4},{7,5},{8,10},{9,11},{10,... | collective-permute-start | bytes 1572872 | tf_op jit(solution)/shard_map/ppermute | solution.py:859
  49.0 39.5 %collective-permute-start.6 = (bf16[256,1024]{1,0:T(8,128)(2,1)S(1)}, bf16[256,1024]{1,0:T(8,128)(2,1)}, u32[]{:S(2)}, u32[]{:S(2)}) collective-permute-start(bf16[256,1024]{1,0:T(8,128)(2,1)S(1)} %copy-done.23), channel_id=1, source_target_pairs={{0,1},{1,0},{2,3},{3,2},{4,5},{5,4},{6,7},{7,6},{8,9},{9,8},{10,11... | collective-permute-start | bytes 1572872 | tf_op jit(solution)/shard_map/ppermute | solution.py:859
  82.5 14.9 %collective-permute-start.7 = (bf16[256,1024]{1,0:T(8,128)(2,1)S(1)}, bf16[256,1024]{1,0:T(8,128)(2,1)S(1)}, u32[]{:S(2)}, u32[]{:S(2)}) collective-permute-start(bf16[256,1024]{1,0:T(8,128)(2,1)S(1)} %collective-permute-done.2.refs_5_.refs_14_), channel_id=1, source_target_pairs={{0,1},{1,0},{2,3},{3,2},{4,5},{5,4},{6,7},{7,6},{8,9},{9,8},{10,11... | collective-permute-start | bytes 1572872 | tf_op jit(solution)/shard_map/ppermute | solution.py:859
  82.5 9.7 %collective-permute-start.3 = (bf16[544,256]{1,0:T(8,128)(2,1)}, bf16[544,256]{1,0:T(8,128)(2,1)S(1)}, u32[]{:S(2)}, u32[]{:S(2)}) collective-permute-start(bf16[544,256]{1,0:T(8,128)(2,1)} %get-tuple-element.155), channel_id=1, source_target_pairs={{0,2},{1,3},{2,0},{3,1},{4,6},{5,7},{6,4},{7,5},{8,10},{9,11},{10,... | collective-permute-start | bytes 835592 | tf_op jit(solution)/shard_map/ppermute | solution.py:859
  83.1 9.1 %collective-permute-start.4 = (bf16[544,256]{1,0:T(8,128)(2,1)}, bf16[544,256]{1,0:T(8,128)(2,1)}, u32[]{:S(2)}, u32[]{:S(2)}) collective-permute-start(bf16[544,256]{1,0:T(8,128)(2,1)} %get-tuple-element.156), channel_id=1, source_target_pairs={{0,1},{1,0},{2,3},{3,2},{4,5},{5,4},{6,7},{7,6},{8,9},{9,8},{10,11... | collective-permute-start | bytes 835592 | tf_op jit(solution)/shard_map/ppermute | solution.py:859
  83.3 14.1 %collective-permute-start.5 = (bf16[544,256]{1,0:T(8,128)(2,1)}, bf16[544,256]{1,0:T(8,128)(2,1)}, u32[]{:S(2)}, u32[]{:S(2)}) collective-permute-start(bf16[544,256]{1,0:T(8,128)(2,1)} %get-tuple-element.157), channel_id=1, source_target_pairs={{0,3},{1,2},{2,1},{3,0},{4,7},{5,6},{6,5},{7,4},{8,11},{9,10},{10,... | collective-permute-start | bytes 835592 | tf_op jit(solution)/shard_map/ppermute | solution.py:859
  105.0 27.3 %collective-permute-start.8 = (bf16[544,1024]{1,0:T(8,128)(2,1)}, bf16[544,1024]{1,0:T(8,128)(2,1)S(1)}, u32[]{:S(2)}, u32[]{:S(2)}) collective-permute-start(bf16[544,1024]{1,0:T(8,128)(2,1)} %get-tuple-element.161.refs_0_.refs_3_), channel_id=1, source_target_pairs={{0,2},{1,3},{2,0},{3,1},{4,6},{5,7},{6,4},{7,5},{8,10},{9,11},{10,... | collective-permute-start | bytes 3342344 | tf_op jit(solution)/shard_map/ppermute | solution.py:859
  105.7 26.7 %collective-permute-start.9 = (bf16[544,1024]{1,0:T(8,128)(2,1)}, bf16[544,1024]{1,0:T(8,128)(2,1)S(1)}, u32[]{:S(2)}, u32[]{:S(2)}) collective-permute-start(bf16[544,1024]{1,0:T(8,128)(2,1)} %get-tuple-element.161.refs_0_.refs_3_), channel_id=1, source_target_pairs={{0,1},{1,0},{2,3},{3,2},{4,5},{5,4},{6,7},{7,6},{8,9},{9,8},{10,11... | collective-permute-start | bytes 3342344 | tf_op jit(solution)/shard_map/ppermute | solution.py:859
  132.4 2.9 collective-permute-start.10
  138.4 46.2 %collective-permute-start.11 = (bf16[1024,1024]{1,0:T(8,128)(2,1)}, bf16[1024,1024]{1,0:T(8,128)(2,1)}, u32[]{:S(2)}, u32[]{:S(2)}) collective-permute-start(bf16[1024,1024]{1,0:T(8,128)(2,1)} %bitcast.85), channel_id=1, source_target_pairs={{0,2},{1,3},{2,0},{3,1},{4,6},{5,7},{6,4},{7,5},{8,10},{9,11},{10,... | collective-permute-start | bytes 6291464 | tf_op jit(solution)/shard_map/ppermute | solution.py:859
  149.9 46.2 %all-to-all-start.1 = ((bf16[8,112,1024]{2,1,0:T(8,128)(2,1)}), bf16[8,112,1024]{2,1,0:T(8,128)(2,1)S(1)}, u32[]{:S(2)}, u32[]{:S(2)}) async-start(bf16[8,112,1024]{2,1,0:T(8,128)(2,1)} %bitcast.70), calls=%async_computation.1 | async-start | bytes 3670016 | tf_op jit(solution)/shard_map/all_to_all | solution.py:896
  153.5 31.1 %copy-start.22 = (bf16[512,1024]{1,0:T(8,128)(2,1)S(1)}, bf16[512,1024]{1,0:T(8,128)(2,1)}, u32[]{:S(2)}) copy-start(bf16[512,1024]{1,0:T(8,128)(2,1)} %get-tuple-element.175.refs_1_) | copy-start | bytes 3145732
  153.5 31.6 %collective-permute-start.12 = (bf16[512,1024]{1,0:T(8,128)(2,1)}, bf16[512,1024]{1,0:T(8,128)(2,1)}, u32[]{:S(2)}, u32[]{:S(2)}) collective-permute-start(bf16[512,1024]{1,0:T(8,128)(2,1)} %get-tuple-element.174.refs_0_), channel_id=1, source_target_pairs={{0,1},{1,0},{2,3},{3,2},{4,5},{5,4},{6,7},{7,6},{8,9},{9,8},{10,11... | collective-permute-start | bytes 3145736 | tf_op jit(solution)/shard_map/ppermute | solution.py:859
  153.6 48.1 %collective-permute-start.16 = (bf16[1024,1024]{1,0:T(8,128)(2,1)}, bf16[1024,1024]{1,0:T(8,128)(2,1)}, u32[]{:S(2)}, u32[]{:S(2)}) collective-permute-start(bf16[1024,1024]{1,0:T(8,128)(2,1)} %bitcast.86), channel_id=1, source_target_pairs={{0,1},{1,0},{2,3},{3,2},{4,5},{5,4},{6,7},{7,6},{8,9},{9,8},{10,11... | collective-permute-start | bytes 6291464 | tf_op jit(solution)/shard_map/ppermute | solution.py:859
  184.6 17.1 %collective-permute-start.17 = (bf16[1024,1024]{1,0:T(8,128)(2,1)}, bf16[1024,1024]{1,0:T(8,128)(2,1)}, u32[]{:S(2)}, u32[]{:S(2)}) collective-permute-start(bf16[1024,1024]{1,0:T(8,128)(2,1)} %collective-permute-done.11.refs_9_), channel_id=1, source_target_pairs={{0,1},{1,0},{2,3},{3,2},{4,5},{5,4},{6,7},{7,6},{8,9},{9,8},{10,11... | collective-permute-start | bytes 6291464 | tf_op jit(solution)/shard_map/ppermute | solution.py:859
  184.7 17.0 %collective-permute-start.13 = (bf16[512,1024]{1,0:T(8,128)(2,1)S(1)}, bf16[512,1024]{1,0:T(8,128)(2,1)}, u32[]{:S(2)}, u32[]{:S(2)}) collective-permute-start(bf16[512,1024]{1,0:T(8,128)(2,1)S(1)} %copy-done.22), channel_id=1, source_target_pairs={{0,1},{1,0},{2,3},{3,2},{4,5},{5,4},{6,7},{7,6},{8,9},{9,8},{10,11... | collective-permute-start | bytes 3145736 | tf_op jit(solution)/shard_map/ppermute | solution.py:859
  185.2 16.5 %collective-permute-start.15 = (bf16[512,1024]{1,0:T(8,128)(2,1)}, bf16[512,1024]{1,0:T(8,128)(2,1)}, u32[]{:S(2)}, u32[]{:S(2)}) collective-permute-start(bf16[512,1024]{1,0:T(8,128)(2,1)} %collective-permute-done.1.refs_3_), channel_id=1, source_target_pairs={{0,1},{1,0},{2,3},{3,2},{4,5},{5,4},{6,7},{7,6},{8,9},{9,8},{10,11... | collective-permute-start | bytes 3145736 | tf_op jit(solution)/shard_map/ppermute | solution.py:859
  185.2 16.6 %collective-permute-start.14 = (bf16[512,1024]{1,0:T(8,128)(2,1)}, bf16[512,1024]{1,0:T(8,128)(2,1)}, u32[]{:S(2)}, u32[]{:S(2)}) collective-permute-start(bf16[512,1024]{1,0:T(8,128)(2,1)} %collective-permute-done.refs_2_), channel_id=1, source_target_pairs={{0,1},{1,0},{2,3},{3,2},{4,5},{5,4},{6,7},{7,6},{8,9},{9,8},{10,11... | collective-permute-start | bytes 3145736 | tf_op jit(solution)/shard_map/ppermute | solution.py:859
  197.4 51.9 %all-to-all-start.2 = ((bf16[8,112,1024]{2,1,0:T(8,128)(2,1)}), bf16[8,112,1024]{2,1,0:T(8,128)(2,1)}, u32[]{:S(2)}, u32[]{:S(2)}) async-start(bf16[8,112,1024]{2,1,0:T(8,128)(2,1)} %bitcast.69), calls=%async_computation.2 | async-start | bytes 3670016 | tf_op jit(solution)/shard_map/all_to_all | solution.py:896
  249.3 53.6 %all-to-all-start.3 = ((bf16[8,112,1024]{2,1,0:T(8,128)(2,1)}), bf16[8,112,1024]{2,1,0:T(8,128)(2,1)S(1)}, u32[]{:S(2)}, u32[]{:S(2)}) async-start(bf16[8,112,1024]{2,1,0:T(8,128)(2,1)} %bitcast.71), calls=%async_computation.3 | async-start | bytes 3670016 | tf_op jit(solution)/shard_map/all_to_all | solution.py:896
  304.1 47.4 %all-to-all-start.4 = ((bf16[8,112,1024]{2,1,0:T(8,128)(2,1)}), bf16[8,112,1024]{2,1,0:T(8,128)(2,1)}, u32[]{:S(2)}, u32[]{:S(2)}) async-start(bf16[8,112,1024]{2,1,0:T(8,128)(2,1)} %bitcast.68), calls=%async_computation.4 | async-start | bytes 3670016 | tf_op jit(solution)/shard_map/all_to_all | solution.py:896
  324.1 14.5 %collective-permute-start.18 = (bf16[1024,1024]{1,0:T(8,128)(2,1)}, bf16[1024,1024]{1,0:T(8,128)(2,1)S(1)}, u32[]{:S(2)}, u32[]{:S(2)}) collective-permute-start(bf16[1024,1024]{1,0:T(8,128)(2,1)} %get-tuple-element.198), channel_id=1, source_target_pairs={{0,1},{1,0},{2,3},{3,2},{4,5},{5,4},{6,7},{7,6},{8,9},{9,8},{10,11... | collective-permute-start | bytes 6291464 | tf_op jit(solution)/shard_map/ppermute | solution.py:859
  324.1 14.5 %collective-permute-start.19 = (bf16[1024,1024]{1,0:T(8,128)(2,1)}, bf16[1024,1024]{1,0:T(8,128)(2,1)}, u32[]{:S(2)}, u32[]{:S(2)}) collective-permute-start(bf16[1024,1024]{1,0:T(8,128)(2,1)} %get-tuple-element.199), channel_id=1, source_target_pairs={{0,1},{1,0},{2,3},{3,2},{4,5},{5,4},{6,7},{7,6},{8,9},{9,8},{10,11... | collective-permute-start | bytes 6291464 | tf_op jit(solution)/shard_map/ppermute | solution.py:859
  343.3 47.8 %collective-permute-start.22 = (bf16[1024,1024]{1,0:T(8,128)(2,1)S(1)}, bf16[1024,1024]{1,0:T(8,128)(2,1)}, u32[]{:S(2)}, u32[]{:S(2)}) collective-permute-start(bf16[1024,1024]{1,0:T(8,128)(2,1)S(1)} %add_convert_fusion.2), channel_id=1, source_target_pairs={{0,2},{1,3},{2,0},{3,1},{4,6},{5,7},{6,4},{7,5},{8,10},{9,11},{10,... | collective-permute-start | bytes 6291464 | tf_op jit(solution)/shard_map/ppermute | solution.py:859
  369.0 4.8 collective-permute-start.20
  369.0 5.0 collective-permute-start.21
  369.6 47.4 %all-to-all-start.5 = ((bf16[8,112,1024]{2,1,0:T(8,128)(2,1)}), bf16[8,112,1024]{2,1,0:T(8,128)(2,1)}, u32[]{:S(2)}, u32[]{:S(2)}) async-start(bf16[8,112,1024]{2,1,0:T(8,128)(2,1)} %bitcast.66), calls=%async_computation.5 | async-start | bytes 3670016 | tf_op jit(solution)/shard_map/all_to_all | solution.py:896
  405.1 48.2 %collective-permute-start.27 = (bf16[1024,1024]{1,0:T(8,128)(2,1)}, bf16[1024,1024]{1,0:T(8,128)(2,1)S(1)}, u32[]{:S(2)}, u32[]{:S(2)}) collective-permute-start(bf16[1024,1024]{1,0:T(8,128)(2,1)} %get-tuple-element.218), channel_id=1, source_target_pairs={{0,1},{1,0},{2,3},{3,2},{4,5},{5,4},{6,7},{7,6},{8,9},{9,8},{10,11... | collective-permute-start | bytes 6291464 | tf_op jit(solution)/shard_map/ppermute | solution.py:859
  405.1 48.2 %collective-permute-start.28 = (bf16[1024,1024]{1,0:T(8,128)(2,1)}, bf16[1024,1024]{1,0:T(8,128)(2,1)}, u32[]{:S(2)}, u32[]{:S(2)}) collective-permute-start(bf16[1024,1024]{1,0:T(8,128)(2,1)} %get-tuple-element.219), channel_id=1, source_target_pairs={{0,1},{1,0},{2,3},{3,2},{4,5},{5,4},{6,7},{7,6},{8,9},{9,8},{10,11... | collective-permute-start | bytes 6291464 | tf_op jit(solution)/shard_map/ppermute | solution.py:859
  408.2 29.7 %collective-permute-start.23 = (bf16[544,1152]{1,0:T(8,128)(2,1)}, bf16[544,1152]{1,0:T(8,128)(2,1)S(1)}, u32[]{:S(2)}, u32[]{:S(2)}) collective-permute-start(bf16[544,1152]{1,0:T(8,128)(2,1)} %add_convert_fusion.4), channel_id=1, source_target_pairs={{0,2},{1,3},{2,0},{3,1},{4,6},{5,7},{6,4},{7,5},{8,10},{9,11},{10,... | collective-permute-start | bytes 3760136 | tf_op jit(solution)/shard_map/ppermute | solution.py:859
  417.0 93.5 %all-to-all-start.6 = ((bf16[8,112,1024]{2,1,0:T(8,128)(2,1)}), bf16[8,112,1024]{2,1,0:T(8,128)(2,1)}, u32[]{:S(2)}, u32[]{:S(2)}) async-start(bf16[8,112,1024]{2,1,0:T(8,128)(2,1)} %bitcast.62), calls=%async_computation.6 | async-start | bytes 3670016 | tf_op jit(solution)/shard_map/all_to_all | solution.py:896
  451.1 9.9 %collective-permute-start.24 = (bf16[544,256]{1,0:T(8,128)(2,1)}, bf16[544,256]{1,0:T(8,128)(2,1)S(1)}, u32[]{:S(2)}, u32[]{:S(2)}) collective-permute-start(bf16[544,256]{1,0:T(8,128)(2,1)} %get-tuple-element.229), channel_id=1, source_target_pairs={{0,2},{1,3},{2,0},{3,1},{4,6},{5,7},{6,4},{7,5},{8,10},{9,11},{10,... | collective-permute-start | bytes 835592 | tf_op jit(solution)/shard_map/ppermute | solution.py:859
  452.7 8.3 %collective-permute-start.25 = (bf16[544,256]{1,0:T(8,128)(2,1)}, bf16[544,256]{1,0:T(8,128)(2,1)S(1)}, u32[]{:S(2)}, u32[]{:S(2)}) collective-permute-start(bf16[544,256]{1,0:T(8,128)(2,1)} %get-tuple-element.230), channel_id=1, source_target_pairs={{0,1},{1,0},{2,3},{3,2},{4,5},{5,4},{6,7},{7,6},{8,9},{9,8},{10,11... | collective-permute-start | bytes 835592 | tf_op jit(solution)/shard_map/ppermute | solution.py:859
  452.7 11.7 %collective-permute-start.26 = (bf16[544,256]{1,0:T(8,128)(2,1)}, bf16[544,256]{1,0:T(8,128)(2,1)}, u32[]{:S(2)}, u32[]{:S(2)}) collective-permute-start(bf16[544,256]{1,0:T(8,128)(2,1)} %get-tuple-element.231), channel_id=1, source_target_pairs={{0,3},{1,2},{2,1},{3,0},{4,7},{5,6},{6,5},{7,4},{8,11},{9,10},{10,... | collective-permute-start | bytes 835592 | tf_op jit(solution)/shard_map/ppermute | solution.py:859
  453.3 15.6 %copy-start.5 = (bf16[1024,1024]{1,0:T(8,128)(2,1)}, bf16[1024,1024]{1,0:T(8,128)(2,1)S(1)}, u32[]{:S(2)}) copy-start(bf16[1024,1024]{1,0:T(8,128)(2,1)S(1)} %collective-permute-done.27) | copy-start | bytes 6291460
  453.3 19.7 %collective-permute-start.29 = (bf16[256,1024]{1,0:T(8,128)(2,1)}, bf16[256,1024]{1,0:T(8,128)(2,1)}, u32[]{:S(2)}, u32[]{:S(2)}) collective-permute-start(bf16[256,1024]{1,0:T(8,128)(2,1)} %get-tuple-element.240), channel_id=1, source_target_pairs={{0,1},{1,0},{2,3},{3,2},{4,5},{5,4},{6,7},{7,6},{8,9},{9,8},{10,11... | collective-permute-start | bytes 1572872 | tf_op jit(solution)/shard_map/ppermute | solution.py:859
  453.3 19.7 %collective-permute-start.30 = (bf16[256,1024]{1,0:T(8,128)(2,1)}, bf16[256,1024]{1,0:T(8,128)(2,1)S(1)}, u32[]{:S(2)}, u32[]{:S(2)}) collective-permute-start(bf16[256,1024]{1,0:T(8,128)(2,1)} %get-tuple-element.241), channel_id=1, source_target_pairs={{0,1},{1,0},{2,3},{3,2},{4,5},{5,4},{6,7},{7,6},{8,9},{9,8},{10,11... | collective-permute-start | bytes 1572872 | tf_op jit(solution)/shard_map/ppermute | solution.py:859
  468.9 59.8 %collective-permute-start.31 = (bf16[1024,1024]{1,0:T(8,128)(2,1)}, bf16[1024,1024]{1,0:T(8,128)(2,1)}, u32[]{:S(2)}, u32[]{:S(2)}) collective-permute-start(bf16[1024,1024]{1,0:T(8,128)(2,1)} %add_convert_fusion.1), channel_id=1, source_target_pairs={{0,2},{1,3},{2,0},{3,1},{4,6},{5,7},{6,4},{7,5},{8,10},{9,11},{10,... | collective-permute-start | bytes 6291464 | tf_op jit(solution)/shard_map/ppermute | solution.py:859
  474.1 54.6 %collective-permute-start.32 = (bf16[256,1024]{1,0:T(8,128)(2,1)}, bf16[256,1024]{1,0:T(8,128)(2,1)S(1)}, u32[]{:S(2)}, u32[]{:S(2)}) collective-permute-start(bf16[256,1024]{1,0:T(8,128)(2,1)} %add_convert_fusion.12), channel_id=1, source_target_pairs={{0,2},{1,3},{2,0},{3,1},{4,6},{5,7},{6,4},{7,5},{8,10},{9,11},{10,... | collective-permute-start | bytes 1572872 | tf_op jit(solution)/shard_map/ppermute | solution.py:859
  475.4 53.4 %copy-start.27 = (bf16[256,1024]{1,0:T(8,128)(2,1)S(1)}, bf16[256,1024]{1,0:T(8,128)(2,1)}, u32[]{:S(2)}) copy-start(bf16[256,1024]{1,0:T(8,128)(2,1)} %get-tuple-element.239) | copy-start | bytes 1572868
  509.6 20.4 %copy-start.13 = (bf16[3,256,1024]{2,1,0:T(8,128)(2,1)S(1)}, bf16[3,256,1024]{2,1,0:T(8,128)(2,1)}, u32[]{:S(2)}) copy-start(bf16[3,256,1024]{2,1,0:T(8,128)(2,1)} %get-tuple-element.238) | copy-start | bytes 4718596
  531.7 81.5 %all-to-all-start.7 = ((bf16[8,144,1024]{2,1,0:T(8,128)(2,1)}), bf16[8,144,1024]{2,1,0:T(8,128)(2,1)S(1)}, u32[]{:S(2)}, u32[]{:S(2)}) async-start(bf16[8,144,1024]{2,1,0:T(8,128)(2,1)} %bitcast.54), calls=%async_computation.7 | async-start | bytes 4718592 | tf_op jit(solution)/shard_map/all_to_all | solution.py:896
  537.7 23.9 %copy-start.18 = (bf16[544,1024]{1,0:T(8,128)(2,1)S(1)}, bf16[544,1024]{1,0:T(8,128)(2,1)}, u32[]{:S(2)}) copy-start(bf16[544,1024]{1,0:T(8,128)(2,1)} %get-tuple-element.256) | copy-start | bytes 3342340
  537.7 134.2 %all-gather.2.cloned.1.call-start = ((), (), s32[]{:S(2)}) async-start(), calls=%async_computation.8 | async-start | bytes 2654208 | tf_op jit(solution)/shard_map/all_gather | solution.py:1037
  553.8 3.0 collective-permute-start.36
  553.9 6.1 collective-permute-start.37
  554.4 5.8 collective-permute-start.33
  554.4 7.2 %collective-permute-start.34 = (bf16[544,1024]{1,0:T(8,128)(2,1)}, bf16[544,1024]{1,0:T(8,128)(2,1)S(1)}, u32[]{:S(2)}, u32[]{:S(2)}) collective-permute-start(bf16[544,1024]{1,0:T(8,128)(2,1)} %get-tuple-element.258), channel_id=1, source_target_pairs={{0,1},{1,0},{2,3},{3,2},{4,5},{5,4},{6,7},{7,6},{8,9},{9,8},{10,11... | collective-permute-start | bytes 3342344 | tf_op jit(solution)/shard_map/ppermute | solution.py:859
  562.0 27.5 %collective-permute-start.35 = (bf16[544,1024]{1,0:T(8,128)(2,1)S(1)}, bf16[544,1024]{1,0:T(8,128)(2,1)S(1)}, u32[]{:S(2)}, u32[]{:S(2)}) collective-permute-start(bf16[544,1024]{1,0:T(8,128)(2,1)S(1)} %add_convert_fusion.10), channel_id=1, source_target_pairs={{0,2},{1,3},{2,0},{3,1},{4,6},{5,7},{6,4},{7,5},{8,10},{9,11},{10,... | collective-permute-start | bytes 3342344 | tf_op jit(solution)/shard_map/ppermute | solution.py:859
  563.0 49.6 %copy-start.4 = (f32[544,1024]{1,0:T(8,128)S(1)}, f32[544,1024]{1,0:T(8,128)}, u32[]{:S(2)}) copy-start(f32[544,1024]{1,0:T(8,128)} %get-tuple-element.221.refs_2_) | copy-start | bytes 6684676
  563.0 49.6 %collective-permute-start.38 = (bf16[544,1024]{1,0:T(8,128)(2,1)S(1)}, bf16[544,1024]{1,0:T(8,128)(2,1)S(1)}, u32[]{:S(2)}, u32[]{:S(2)}) collective-permute-start(bf16[544,1024]{1,0:T(8,128)(2,1)S(1)} %add_convert_fusion.8), channel_id=1, source_target_pairs={{0,2},{1,3},{2,0},{3,1},{4,6},{5,7},{6,4},{7,5},{8,10},{9,11},{10,... | collective-permute-start | bytes 3342344 | tf_op jit(solution)/shard_map/ppermute | solution.py:859
  613.2 36.5 %copy-start.1 = (bf16[544,1024]{1,0:T(8,128)(2,1)}, bf16[544,1024]{1,0:T(8,128)(2,1)S(1)}, u32[]{:S(2)}) copy-start(bf16[544,1024]{1,0:T(8,128)(2,1)S(1)} %add_convert_fusion.7.refs_0_) | copy-start | bytes 3342340
  621.8 27.9 %collective-permute-start.42 = (bf16[544,1024]{1,0:T(8,128)(2,1)}, bf16[544,1024]{1,0:T(8,128)(2,1)}, u32[]{:S(2)}, u32[]{:S(2)}) collective-permute-start(bf16[544,1024]{1,0:T(8,128)(2,1)} %input_back.1.refs_0_), channel_id=1, source_target_pairs={{0,2},{1,3},{2,0},{3,1},{4,6},{5,7},{6,4},{7,5},{8,10},{9,11},{10,... | collective-permute-start | bytes 3342344 | tf_op jit(solution)/shard_map/ppermute | solution.py:859
  622.3 49.5 %collective-permute-start.39 = (bf16[544,1024]{1,0:T(8,128)(2,1)S(1)}, bf16[544,1024]{1,0:T(8,128)(2,1)}, u32[]{:S(2)}, u32[]{:S(2)}) collective-permute-start(bf16[544,1024]{1,0:T(8,128)(2,1)S(1)} %add_convert_fusion.7.refs_0_), channel_id=1, source_target_pairs={{0,2},{1,3},{2,0},{3,1},{4,6},{5,7},{6,4},{7,5},{8,10},{9,11},{10,... | collective-permute-start | bytes 3342344 | tf_op jit(solution)/shard_map/ppermute | solution.py:859
  636.0 37.2 %collective-permute-start.43 = (bf16[544,1024]{1,0:T(8,128)(2,1)S(1)}, bf16[544,1024]{1,0:T(8,128)(2,1)}, u32[]{:S(2)}, u32[]{:S(2)}) collective-permute-start(bf16[544,1024]{1,0:T(8,128)(2,1)S(1)} %copy-done.3), channel_id=1, source_target_pairs={{0,1},{1,0},{2,3},{3,2},{4,5},{5,4},{6,7},{7,6},{8,9},{9,8},{10,11... | collective-permute-start | bytes 3342344 | tf_op jit(solution)/shard_map/ppermute | solution.py:859
  649.7 23.4 %collective-permute-start.44 = (bf16[544,1024]{1,0:T(8,128)(2,1)}, bf16[544,1024]{1,0:T(8,128)(2,1)}, u32[]{:S(2)}, u32[]{:S(2)}) collective-permute-start(bf16[544,1024]{1,0:T(8,128)(2,1)} %collective-permute-done.42.refs_1_), channel_id=1, source_target_pairs={{0,1},{1,0},{2,3},{3,2},{4,5},{5,4},{6,7},{7,6},{8,9},{9,8},{10,11... | collective-permute-start | bytes 3342344 | tf_op jit(solution)/shard_map/ppermute | solution.py:859
  649.7 30.1 %collective-permute-start.40 = (bf16[544,1024]{1,0:T(8,128)(2,1)S(1)}, bf16[544,1024]{1,0:T(8,128)(2,1)S(1)}, u32[]{:S(2)}, u32[]{:S(2)}) collective-permute-start(bf16[544,1024]{1,0:T(8,128)(2,1)S(1)} %add_convert_fusion.7.refs_0_), channel_id=1, source_target_pairs={{0,1},{1,0},{2,3},{3,2},{4,5},{5,4},{6,7},{7,6},{8,9},{9,8},{10,11... | collective-permute-start | bytes 3342344 | tf_op jit(solution)/shard_map/ppermute | solution.py:859
  671.9 8.0 %collective-permute-start.41 = (bf16[544,1024]{1,0:T(8,128)(2,1)}, bf16[544,1024]{1,0:T(8,128)(2,1)}, u32[]{:S(2)}, u32[]{:S(2)}) collective-permute-start(bf16[544,1024]{1,0:T(8,128)(2,1)} %collective-permute-done.39.refs_1_), channel_id=1, source_target_pairs={{0,1},{1,0},{2,3},{3,2},{4,5},{5,4},{6,7},{7,6},{8,9},{9,8},{10,11... | collective-permute-start | bytes 3342344 | tf_op jit(solution)/shard_map/ppermute | solution.py:859
  672.6 13.6 %collective-permute-start.45 = (f32[10,1024]{1,0:T(8,128)S(1)}, f32[10,1024]{1,0:T(8,128)S(1)}, u32[]{:S(2)}, u32[]{:S(2)}) collective-permute-start(f32[10,1024]{1,0:T(8,128)S(1)} %slice_convert_fusion.1), channel_id=1, source_target_pairs={{0,1},{1,0},{2,3},{3,2},{4,5},{5,4},{6,7},{7,6},{8,9},{9,8},{10,11... | collective-permute-start | bytes 122888 | tf_op jit(solution)/shard_map/ppermute | solution.py:859
  687.0 6.2 collective-permute-start.46
  (32 other events, 164.5 us)
Sparse Core Ops, SparseCore 0:
  614.5 52.5 all-gather.1

commit v6 on v5

--- a/solution.py
+++ b/solution.py
@@ -533,11 +533,19 @@
     )(at, *mixed, *head_out, x, gain, router, ids, noise)
 
 
-def middle_back_kernel(count, limit, at_ref, *refs):
-    keep_ref, far_ref, mid_ref, second_ref, gates_ref, ids_ref, up_ref, gain_ref, router_ref = refs[:9]
-    mixed_refs, wo_refs = refs[9 : 9 + count], refs[9 + count : 9 + 2 * count]
-    mg_ref, rg_ref, ng_ref = refs[9 + 2 * count : 12 + 2 * count]
-    hog_refs, dmix_refs, hog_acc = refs[12 + 2 * count : 12 + 3 * count], refs[12 + 3 * count : -1], refs[-1]
+def of_tiles(refs):
+    value = refs[0][...].astype(F32)
+    for n, ref in enumerate(refs[1:]):
+        value = jnp.where(pl.program_id(0) > n, ref[...].astype(F32), value)
+    return value
+
+
+def middle_back_kernel(count, limit, tiles, at_ref, *refs):
+    far_refs, refs = refs[:tiles], refs[tiles:]
+    keep_ref, mid_ref, second_ref, gates_ref, ids_ref, up_ref, gain_ref, router_ref = refs[:8]
+    mixed_refs, wo_refs = refs[8 : 8 + count], refs[8 + count : 8 + 2 * count]
+    mg_ref, rg_ref, ng_ref = refs[8 + 2 * count : 11 + 2 * count]
+    hog_refs, dmix_refs, hog_acc = refs[11 + 2 * count : 11 + 3 * count], refs[11 + 3 * count : -1], refs[-1]
     i = pl.program_id(0)
 
     @pl.when(i == 0)
@@ -549,7 +557,8 @@
     tile, width = up_ref.shape
     valid = (at_ref[0] + i) * tile + iota(tile, 1, 0) < limit
     lane = iota(1, LANES, 1)
-    tail = keep_ref[:, width:].astype(F32) + far_ref[:, width:].astype(F32)
+    both = keep_ref[...].astype(F32) + of_tiles(far_refs)
+    tail = both[:, width:]
     gates = gates_ref[...]
     gate, grad = [], []
     for c in range(2):
@@ -561,8 +570,7 @@
         hit = (lane == ids_ref[:, c : c + 1]) & valid
         logit_grad = jnp.where(hit, gate[c] * (grad[c] - mean_term), logit_grad)
     logit_grad = logit_grad.astype(BF)
-    routed = keep_ref[:, 0:width].astype(F32) + far_ref[:, 0:width].astype(F32)
-    second_grad = routed + dot(logit_grad, router_ref[...], 1, 1)
+    second_grad = both[:, 0:width] + dot(logit_grad, router_ref[...], 1, 1)
     rg_ref[...] += dot(logit_grad, second_ref[...], 0, 0)
     scaled, spread = norm_parts(mid_ref[...])
     ng_ref[...] += jnp.sum(second_grad * scaled, 0, keepdims=True)
@@ -588,8 +596,8 @@
     spec = pltpu.PrefetchScalarGridSpec(
         num_scalar_prefetch=1,
         grid=(each // tile,),
-        in_specs=[
-            rows_spec(tile, keep.shape[1]),
+        in_specs=[whole((tile, keep.shape[1]))] * len(far)
+        + [
             rows_spec(tile, keep.shape[1]),
             rows_spec(tile, width),
             rows_spec(tile, width),
@@ -607,7 +615,7 @@
         scratch_shapes=[pltpu.VMEM((parts, cols, width), F32)],
     )
     return pl.pallas_call(
-        functools.partial(middle_back_kernel, parts, rows),
+        functools.partial(middle_back_kernel, parts, rows, len(far)),
         grid_spec=spec,
         out_shape=[
             jax.ShapeDtypeStruct((each, width), F32),
@@ -619,14 +627,15 @@
         compiler_params=params(),
         cost_estimate=cost(8 * each * width * width, 40 * each * width),
         name="middle_back",
-    )(at, keep, far, middle, second, gates, ids, up, gain, router, *mixed, *head_out)
-
-
-def input_back_kernel(limit, at_ref, keep_ref, far_ref, x_ref, mg_ref, gain_ref, out_ref):
+    )(at, *far, keep, middle, second, gates, ids, up, gain, router, *mixed, *head_out)
+
+
+def input_back_kernel(limit, tiles, at_ref, *refs):
+    far_refs, (keep_ref, x_ref, mg_ref, gain_ref, out_ref) = refs[:tiles], refs[tiles:]
     tile = x_ref.shape[0]
     valid = (at_ref[0] + pl.program_id(0)) * tile + iota(tile, 1, 0) < limit
     scaled, spread = norm_parts(jnp.where(valid, x_ref[...].astype(F32), 0.0))
-    first_grad = keep_ref[...].astype(F32) + far_ref[...].astype(F32)
+    first_grad = keep_ref[...].astype(F32) + of_tiles(far_refs)
     out_ref[...] = (mg_ref[...] + norm_field_back(first_grad, gain_ref[...], scaled, spread)).astype(BF)
 
 
@@ -636,17 +645,18 @@
     spec = pltpu.PrefetchScalarGridSpec(
         num_scalar_prefetch=1,
         grid=(each // tile,),
-        in_specs=[rows_spec(tile, width), rows_spec(tile, width), own_spec(tile, width), rows_spec(tile, width), whole((1, width))],
+        in_specs=[whole((tile, width))] * len(far)
+        + [rows_spec(tile, width), own_spec(tile, width), rows_spec(tile, width), whole((1, width))],
         out_specs=rows_spec(tile, width),
     )
     return pl.pallas_call(
-        functools.partial(input_back_kernel, x.shape[0]),
+        functools.partial(input_back_kernel, x.shape[0], len(far)),
         grid_spec=spec,
         out_shape=jax.ShapeDtypeStruct((each, width), BF),
         compiler_params=params(),
         cost_estimate=cost(20 * each * width, 16 * each * width),
         name="input_back",
-    )(at, keep, far, x, middle_grad, gain)
+    )(at, *far, keep, x, middle_grad, gain)
 
 
 def gelu_parts(v):
@@ -882,6 +892,12 @@
     def far_hop(kept, other):
         return cross(other, 2) if paired else jnp.zeros_like(kept)
 
+    def far_tiles(kept, other):
+        tile = half_tile(each)
+        source = other if paired else jnp.zeros_like(kept)
+        tiles = [source[at : at + tile] for at in range(0, each, tile)]
+        return [cross(item, 2) for item in tiles] if paired else tiles
+
     def scattered(pieces):
         kept, other = near_sum(pieces, near_hop(pieces))
         return kept, far_hop(kept, other)
@@ -943,7 +959,7 @@
     middle, second_in, gates = middle_of(
         own_block, mixed, head_out_all, block_in, gain_two, router_wide, expert_ids, route_noise
     )
-    *second_all, signal, late_out = pinned(*gathered(second_in), signal, expert_out[0])
+    *second_all, late_out = pinned(*gathered(second_in), expert_out[0])
     w1 = [gathered_from(a, b) for a, b in zip(w1_own, w1_far)]
     w1 = [w1[h][p] for p in range(parts) for h in range(2)]
 
@@ -954,7 +970,9 @@
         return over_experts(x.reshape(experts, slots, width)).reshape(chunk_rows, width)
 
     x = sent(packed_rows(0))
-    w2_far, *outgoing = pinned(far_part(late_out), *[packed_rows(n) for n in range(1, CHUNKS)])
+    w2_far, head_in_t, signal, *outgoing = pinned(
+        far_part(late_out), jnp.swapaxes(head_in, 1, 2), signal, *[packed_rows(n) for n in range(1, CHUNKS)]
+    )
     w2 = gathered_from(expert_out[0], w2_far)
     backs, actives, hidden_grads, rows_grads, arrived, returned = [], [], [], [], [], []
     for n in range(CHUNKS):
@@ -990,11 +1008,17 @@
 
     second_pieces = unpack(part_of, place, returned, slots, per, each, True)
     second_kept, second_other = near_sum(second_pieces, near_hop(second_pieces))
-    second_kept, out_far, *hidden_grads = pinned(second_kept, out_far, *hidden_grads)
-    second_far = far_hop(second_kept, second_other)
-    in_parts = weight_parts(hidden_grads, arrived)
-    in_came = near_hop(in_parts)
-    second_far, *in_parts = pinned(second_far, *in_parts)
+    if paired:
+        second_other, *hidden_grads = pinned(second_other, *hidden_grads)
+    second_far = far_tiles(second_kept, second_other)
+    in_parts = []
+    for p in range(parts - 2, -1, -2):
+        *hidden_grads, pair = pinned(*hidden_grads, weight_grad(hidden_grads, arrived, p, here))
+        in_parts = list(pair) + in_parts
+        if p == parts - 2:
+            in_came = near_hop([None] * p + list(pair)) if paired else ()
+            second_far[0], pair = pinned(second_far[0], pair)
+    second_far[-1], out_far, *in_parts = pinned(second_far[-1], out_far, *in_parts)
     combined = [sent(item) for item in backs]
     middle_grad, router_part, norm_two_part, *pieces = middle_back(
         own_block, second_kept, second_far, middle, second_in, gates, expert_ids, cotangent, mixed, head_out_all,
@@ -1002,23 +1026,30 @@
     )
     head_out_parts, mixed_grad = pieces[:parts], pieces[parts:]
     *mixed_grad, combined[0] = pinned(*mixed_grad, combined[0])
-    *mixed_grad, in_came = pinned(*swapped(mixed_grad), in_came)
+    mixed_grad = swapped(mixed_grad)
+    head_out_kept, head_out_far = scattered(head_out_parts)
     in_kept, in_other = near_sum(in_parts, in_came)
+    if paired:
+        in_other = pinned(in_other, head_out_far, *mixed_grad)[0]
     in_far = far_hop(in_kept, in_other)
-    head_out_kept, head_out_far = scattered(head_out_parts)
     *pieces, head_in_part, norm_one_part = attend_back(
-        starts, mixed_grad, qkv, logs, first_in, jnp.swapaxes(head_in, 1, 2), gain_one
-    )
-    *pieces, combined[-1], in_far, head_out_far = pinned(*pieces, combined[-1], in_far, head_out_far)
-    first_kept, first_far = scattered(pieces)
+        starts, mixed_grad, qkv, logs, first_in, head_in_t, gain_one
+    )
+    *pieces, combined[-1] = pinned(*pieces, combined[-1])
+    first_kept, first_other = near_sum(pieces, near_hop(pieces))
+    if paired:
+        first_other, first_kept, *combined = pinned(first_other, first_kept, *combined)
+    first_far = far_tiles(first_kept, first_other)
     block_pieces = unpack(part_of, place, combined, slots, per, each, False)
+    first_far[0], *block_pieces = pinned(first_far[0], *block_pieces)
     block_kept, block_other = near_sum(block_pieces, near_hop(block_pieces))
-    first_far, block_kept = pinned(first_far, block_kept)
+    if paired:
+        first_far[-1], block_other = pinned(first_far[-1], block_other)
     block_far = far_hop(block_kept, block_other)
     input_part = input_back(own_block, first_kept, first_far, block_in, middle_grad, gain_one)
     out_grad = out_kept.astype(F32) + out_far.astype(F32)
     in_grad = sum_turned(in_kept, in_far)
-    input_far, out_grad, in_grad = pinned(far_part(input_part), out_grad, in_grad)
+    input_far, out_grad, in_grad, block_far = pinned(far_part(input_part), out_grad, in_grad, block_far)
     block_own = (middle + block_kept.astype(F32) + block_far.astype(F32)).astype(BF)
 
     cols = head_in.shape[2]

time: 709 us -> 780 us (1.10)
  waiting for transfers between devices: 219 us -> 264 us
  Pallas kernels: 327 us -> 339 us
    all_gather x1, waiting for transfers between devices: 0.01 us -> 27.8 us  [shards(): heads = lax.all_gather(heads, 'expert', axis=0, tiled=True)]
    ppermute x47 -> x49, waiting for transfers between devices: 194 us -> 216 us  [cross(): return lax.ppermute(x, 'tensor', [(n, n ^ k) for n in range(parts)])]
    pallas_call x2, Pallas kernels: 95.2 us -> 107 us  [expert(): pl.pallas_call(functools.partial(expert_kernel, count, slots, per), grid=...]
    ppermute x47 -> x49, starting transfers between devices: 26.4 us -> 29 us  [cross(): return lax.ppermute(x, 'tensor', [(n, n ^ k) for n in range(parts)])]
    convert_element_type x11 -> x10, other arithmetic: 23.8 us -> 24.9 us  [near_sum(): (a.astype(F32) + b.astype(F32)).astype(BF)]
  transfers between devices with their start and end apart: 56 -> 58, of which waited for: 24 -> 18; matrix products, arithmetic and copies ran while one was open for 8% -> 9% of each run, Pallas kernels for 47% -> 44%
where the time goes in v6:
time: 780 us; the launch traced here: 773 us
  Pallas kernels  339 us (43%)
  waiting for transfers between devices  264 us (34%)
  starting transfers between devices  72.6 us (9%)
  other arithmetic  49.3 us (6%)
  local copies, waits for them, and re-layouts  32.2 us (4%)
  between operations  15.2 us (2%)
    ppermute x49, waiting for transfers between devices, cross(): return lax.ppermute(x, 'tensor', [(n, n ^ k) for n in range(parts)])  216 us
    pallas_call x2, Pallas kernels, expert(): pl.pallas_call(functools.partial(expert_kernel, count, slots, per), grid=...  107 us
    pallas_call x4, Pallas kernels, weight_grad(): pl.pallas_call(functools.partial(weight_kernel, count, steps), grid=(2 *...  56.1 us
    all_to_all x8, starting transfers between devices, over_experts(): return lax.all_to_all(x, 'expert', split_axis=0, concat_axis=0, tiled=True)  43.3 us
    pallas_call x1, Pallas kernels, attend_back(): pl.pallas_call(functools.partial(attend_back_kernel, count), grid_spec=sp...  34.3 us
    pallas_call x2, Pallas kernels, unpack(): pl.pallas_call(functools.partial(unpack_kernel, count, slots, per, graded...  33.3 us
    pallas_call x1, Pallas kernels, attend(): pl.pallas_call(functools.partial(attend_kernel, count), grid_spec=spec, o...  30.4 us
    ppermute x49, starting transfers between devices, cross(): return lax.ppermute(x, 'tensor', [(n, n ^ k) for n in range(parts)])  29 us
  transfers between devices with their start and end apart: 58, of which 18 were waited for; matrix products, arithmetic and copies ran while one was open for 9% of the time, Pallas kernels for 44%

profile of v6, /device:TPU:0, one launch (start us, length us, event | category | flops | bytes accessed | tf_op | source)
XLA Modules:
  0.0 772.6 jit_solution(8985933121399182062)
XLA Ops:
  7.2 3.1 slice_bitcast_fusion
  10.3 2.9 collective-permute-start
  13.4 2.3 reduce-window.6
  23.5 2.6 fusion.5.side_ref
  26.0 17.3 %pack_cotangent.1 = bf16[8,2,112,1152]{3,2,1,0:T(8,128)(2,1)} custom-call(bf16[2167,1024]{1,0:T(8,128)(2,1)} %refs_7_.1, bf16[16,1024]{1,0:T(8,128)(2,1)} %pad.26.tail_ref, s32[2,2176]{1,0:T(2,128)} %copy.103.lp_ref, bf16[2,2176,128]{2,1,0:T(8,128)(2,1)} %fusion.5.side_ref), custom_call_target="tpu_custom_call" | custom-call | flops 11978932224 | bytes 4438016 | tf_op jit(solution)/shard_map/pack_cotangent/pallas_call | solution.py:323
  43.4 6.3 all-to-all-start
  53.1 30.4 %attend.1 = (bf16[11,208,1024]{2,1,0:T(8,128)(2,1)}, bf16[3,11,208,256]{3,2,1,0:T(8,128)(2,1)}, f32[11,208,128]{2,1,0:T(8,128)}, bf16[544,256]{1,0:T(8,128)(2,1)...) custom-call(s32[4]{0:T(128)} %get-tuple-element.313.starts_ref, ...), custom_call_target="tpu_custom_call" | custom-call | flops 9596567552 | bytes 35504128 | tf_op jit(solution)/shard_map/attend/pallas_call | solution.py:180
  83.5 2.0 collective-permute-done.2.refs_5_.refs_15_
  91.3 3.8 collective-permute-done.3.refs_1_.refs_11_
  95.1 5.3 collective-permute-done.5.refs_3_.refs_13_
  101.2 6.8 middle.1
  108.9 26.4 %collective-permute-done.8.refs_1_ = bf16[544,1024]{1,0:T(8,128)(2,1)S(1)} collective-permute-done((bf16[544,1024]{1,0:T(8,128)(2,1)}, bf16[544,1024]{1,0:T(8,128)(2,1)S(1)}, u32[]{:S(2)}, u32[]{:S(2)}) %collective-permute-start.8) | collective-permute-done | bytes 1114144 | tf_op jit(solution)/shard_map/ppermute | solution.py:869
  135.3 2.7 collective-permute-done.10.refs_3_
  140.6 9.9 %pack_rows.3 = bf16[896,1024]{1,0:T(8,128)(2,1)} custom-call(s32[4]{0:T(128)} %get-tuple-element.314.part_ref, bf16[544,1024]{1,0:T(8,128)(2,1)} %get-tuple-element.173.refs_0_.refs_4_, bf16[544,1024]{1,0:T(8,128)(2,1)} %copy-done.26, bf16[544,1024]{1,0:T(8,128)(2,1)} %copy-done.27, bf16[544,1024]{1,0:T(8,128)(2,1)} %copy-done.28, s32[4,2,544]{2,1,0:T(2,128)} %bitcast.74), custom_call_target="tpu_custom_call" | custom-call | flops 5989466112 | bytes 4456448 | tf_op jit(solution)/shard_map/pack_rows/pallas_call | solution.py:359
  150.5 5.6 all-to-all-start.1
  156.6 1.7 copy.107
  158.3 9.9 %pack_rows.2 = bf16[896,1024]{1,0:T(8,128)(2,1)} custom-call(s32[4]{0:T(128)} %get-tuple-element.314.part_ref, bf16[544,1024]{1,0:T(8,128)(2,1)} %get-tuple-element.173.refs_0_.refs_4_, bf16[544,1024]{1,0:T(8,128)(2,1)} %copy-done.26, bf16[544,1024]{1,0:T(8,128)(2,1)} %copy-done.27, bf16[544,1024]{1,0:T(8,128)(2,1)} %copy-done.28, s32[4,2,544]{2,1,0:T(2,128)} %bitcast.75), custom_call_target="tpu_custom_call" | custom-call | flops 5989466112 | bytes 4456448 | tf_op jit(solution)/shard_map/pack_rows/pallas_call | solution.py:359
  168.3 18.8 %collective-permute-done.11.refs_9_ = bf16[1024,1024]{1,0:T(8,128)(2,1)} collective-permute-done((bf16[1024,1024]{1,0:T(8,128)(2,1)}, bf16[1024,1024]{1,0:T(8,128)(2,1)}, u32[]{:S(2)}, u32[]{:S(2)}) %collective-permute-start.11) | collective-permute-done | bytes 2097184 | tf_op jit(solution)/shard_map/ppermute | solution.py:869
  188.1 10.7 %all-to-all-done.1 = bf16[8,112,1024]{2,1,0:T(8,128)(2,1)S(1)} async-done(((bf16[8,112,1024]{2,1,0:T(8,128)(2,1)}), bf16[8,112,1024]{2,1,0:T(8,128)(2,1)S(1)}, u32[]{:S(2)}, u32[]{:S(2)}) %all-to-all-start.1) | async-done | bytes 1835040 | tf_op jit(solution)/shard_map/all_to_all | solution.py:912
  200.0 4.3 all-to-all-start.2
  205.4 59.1 %expert.2 = (bf16[896,1024]{1,0:T(8,128)(2,1)}, bf16[896,4096]{1,0:T(8,128)(2,1)}, bf16[896,4096]{1,0:T(8,128)(2,1)}, bf16[896,1024]{1,0:T(8,128)(2,1)}, bf16[896,1024]{1,0:T(8,128)(2,1)}) custom-call(bf16[896,1024]{1,0:T(8,128)(2,1)} %bitcast.63, bf16[8,2,112,1152]{3,2,1,0:T(8,128)(2,1)} %all-to-all-done.g_ref, ...), custom_call_target="tpu_custom_call" | custom-call | flops 30064771072 | bytes 22020096 | tf_op jit(solution)/shard_map/expert/pallas_call | solution.py:773
  264.5 5.9 all-to-all-start.3
  270.4 47.6 %expert.3 = (bf16[896,1024]{1,0:T(8,128)(2,1)}, bf16[896,4096]{1,0:T(8,128)(2,1)}, bf16[896,4096]{1,0:T(8,128)(2,1)}, bf16[896,1024]{1,0:T(8,128)(2,1)}, bf16[896,1024]{1,0:T(8,128)(2,1)}) custom-call(bf16[896,1024]{1,0:T(8,128)(2,1)} %bitcast.21.x_ref.refs_3_, bf16[8,2,112,1152]{3,2,1,0:T(8,128)(2,1)} %all-to-all-done.g_ref, ...), custom_call_target="tpu_custom_call" | custom-call | flops 30064771072 | bytes 22020096 | tf_op jit(solution)/shard_map/expert/pallas_call | solution.py:773
  319.2 6.0 all-to-all-start.4
  325.2 14.0 %weight_grad.5 = (bf16[1024,1024]{1,0:T(8,128)(2,1)}, bf16[1024,1024]{1,0:T(8,128)(2,1)}) custom-call(bf16[896,4096]{1,0:T(8,128)(2,1)} %get-tuple-element.205.refs_0_, bf16[896,1024]{1,0:T(8,128)(2,1)} %get-tuple-element.206.refs_1_, bf16[896,4096]{1,0:T(8,128)(2,1)} %get-tuple-element.207.refs_2_, bf16[896,1024]{1,0:T(8,128)(2,1)} %get-tuple-element.208.refs_3_), custom_call_target="tpu_custom_call" | custom-call | flops 7516192768 | bytes 8388608 | tf_op jit(solution)/shard_map/weight_grad/pallas_call | solution.py:821
  339.7 14.0 %weight_grad.4 = (bf16[1024,1024]{1,0:T(8,128)(2,1)}, bf16[1024,1024]{1,0:T(8,128)(2,1)}) custom-call(bf16[896,4096]{1,0:T(8,128)(2,1)} %get-tuple-element.205.refs_0_, bf16[896,1024]{1,0:T(8,128)(2,1)} %get-tuple-element.206.refs_1_, bf16[896,4096]{1,0:T(8,128)(2,1)} %get-tuple-element.207.refs_2_, bf16[896,1024]{1,0:T(8,128)(2,1)} %get-tuple-element.208.refs_3_), custom_call_target="tpu_custom_call" | custom-call | flops 7516192768 | bytes 8388608 | tf_op jit(solution)/shard_map/weight_grad/pallas_call | solution.py:821
  353.7 3.9 add_convert_fusion.3
  357.6 9.1 %all-to-all-done.4 = bf16[8,112,1024]{2,1,0:T(8,128)(2,1)} async-done(((bf16[8,112,1024]{2,1,0:T(8,128)(2,1)}), bf16[8,112,1024]{2,1,0:T(8,128)(2,1)}, u32[]{:S(2)}, u32[]{:S(2)}) %all-to-all-start.4) | async-done | bytes 1835040 | tf_op jit(solution)/shard_map/all_to_all | solution.py:912
  366.6 4.3 all-to-all-start.5
  371.0 17.5 %unpack_rows.2 = (bf16[544,1152]{1,0:T(8,128)(2,1)}, bf16[544,1152]{1,0:T(8,128)(2,1)}, bf16[544,1152]{1,0:T(8,128)(2,1)}, bf16[544,1152]{1,0:T(8,128)(2,1)}) custom-call(s32[4]{0:T(128)} %get-tuple-element.314.part_ref, s32[2176,2]{1,0:T(8,128)} %copy-done.1, bf16[896,1024]{1,0:T(8,128)(2,1)} %bitcast.66, bf16[896,1024]{1,0:T(8,128)(2,1)} %bitcast.25.refs_1_), custom_call_target="tpu_custom_call" | custom-call | flops 11978932224 | bytes 7340032 | tf_op jit(solution)/shard_map/unpack_rows/pallas_call | solution.py:414
  389.0 3.3 add_convert_fusion.2
  392.3 1.6 collective-permute-start.24
  398.0 14.0 %weight_grad.6 = (bf16[1024,1024]{1,0:T(8,128)(2,1)}, bf16[1024,1024]{1,0:T(8,128)(2,1)}) custom-call(bf16[896,4096]{1,0:T(8,128)(2,1)} %get-tuple-element.231.refs_0_, bf16[896,1024]{1,0:T(8,128)(2,1)} %bitcast.64, bf16[896,4096]{1,0:T(8,128)(2,1)} %get-tuple-element.232.refs_2_, bf16[896,1024]{1,0:T(8,128)(2,1)} %bitcast.21.x_ref.refs_3_), custom_call_target="tpu_custom_call" | custom-call | flops 7516192768 | bytes 8388608 | tf_op jit(solution)/shard_map/weight_grad/pallas_call | solution.py:821
  412.9 5.1 all-to-all-start.7
  418.0 14.1 %weight_grad.7 = (bf16[1024,1024]{1,0:T(8,128)(2,1)}, bf16[1024,1024]{1,0:T(8,128)(2,1)}) custom-call(bf16[896,4096]{1,0:T(8,128)(2,1)} %get-tuple-element.231.refs_0_, bf16[896,1024]{1,0:T(8,128)(2,1)} %bitcast.65, bf16[896,4096]{1,0:T(8,128)(2,1)} %get-tuple-element.232.refs_2_, bf16[896,1024]{1,0:T(8,128)(2,1)} %bitcast.21.x_ref.refs_3_), custom_call_target="tpu_custom_call" | custom-call | flops 7516192768 | bytes 8388608 | tf_op jit(solution)/shard_map/weight_grad/pallas_call | solution.py:821
  432.1 2.6 add_convert_fusion.4.refs_2_
  434.7 32.2 %collective-permute-done.22.refs_0_ = bf16[272,1152]{1,0:T(8,128)(2,1)} collective-permute-done((bf16[272,1152]{1,0:T(8,128)(2,1)}, bf16[272,1152]{1,0:T(8,128)(2,1)}, u32[]{:S(2)}, u32[]{:S(2)}) %collective-permute-start.22) | collective-permute-done | bytes 626720 | tf_op jit(solution)/shard_map/ppermute | solution.py:869
  466.9 12.4 %middle_back.1 = (f32[544,1024]{1,0:T(8,128)}, f32[128,1024]{1,0:T(8,128)}, f32[1,1024]{1,0:T(1,128)}, bf16[256,1024]{1,0:T(8,128)(2,1)}, bf16[256,1024]{1,0:T(8...) custom-call(s32[1]{0:T(128)} %bitcast.11.at_ref, ...), custom_call_target="tpu_custom_call" | custom-call | flops 4563402752 | bytes 22282240 | tf_op jit(solution)/shard_map/middle_back/pallas_call | solution.py:617
  483.5 1.6 collective-permute-start.30
  485.0 4.6 collective-permute-done.25.refs_1_
  489.6 5.1 collective-permute-done.27.refs_3_
  495.4 34.3 %attend_back.1 = (bf16[544,1024]{1,0:T(8,128)(2,1)}, bf16[544,1024]{1,0:T(8,128)(2,1)}, bf16[544,1024]{1,0:T(8,128)(2,1)}, bf16[544,1024]{1,0:T(8,128)(2,1)}, bf...) custom-call(s32[4]{0:T(128)} %get-tuple-element.313.starts_ref, bf16[3,11,208,256]{3,2,1,0:T(8,128)(2,1)} %get-tuple-element.158.qkv_ref, ...), custom_call_target="tpu_custom_call" | custom-call | flops 14394851328 | bytes 46858240 | tf_op jit(solution)/shard_map/attend_back/pallas_call | solution.py:286
  533.9 1.6 pad_maximum_fusion
  535.5 5.9 all-to-all-start.6
  541.7 2.0 add_convert_fusion.10
  543.8 2.7 add_convert_fusion.9.refs_2_
  548.9 15.8 %unpack_rows.3 = (bf16[544,1024]{1,0:T(8,128)(2,1)}, bf16[544,1024]{1,0:T(8,128)(2,1)}, bf16[544,1024]{1,0:T(8,128)(2,1)}, bf16[544,1024]{1,0:T(8,128)(2,1)}) custom-call(s32[4]{0:T(128)} %get-tuple-element.314.part_ref, s32[2176,2]{1,0:T(8,128)} %copy-done.1, bf16[896,1024]{1,0:T(8,128)(2,1)} %bitcast.27.refs_0_, bf16[896,1024]{1,0:T(8,128)(2,1)} %bitcast.31.refs_1_), custom_call_target="tpu_custom_call" | custom-call | flops 11978932224 | bytes 7340032 | tf_op jit(solution)/shard_map/unpack_rows/pallas_call | solution.py:414
  565.2 4.5 add_convert_fusion
  572.2 57.3 %collective-permute-done.36.refs_1_ = bf16[272,1024]{1,0:T(8,128)(2,1)S(1)} collective-permute-done((bf16[272,1024]{1,0:T(8,128)(2,1)}, bf16[272,1024]{1,0:T(8,128)(2,1)S(1)}, u32[]{:S(2)}, u32[]{:S(2)}) %collective-permute-start.36) | collective-permute-done | bytes 557088 | tf_op jit(solution)/shard_map/ppermute | solution.py:869
  630.3 4.6 input_back.1.refs_0_
  635.4 1.5 collective-permute-start.41
  636.9 5.1 convert_add_fusion
  642.1 3.9 add_convert_fusion.1.a_ref
  645.9 5.2 sum_turned.1
  651.1 11.6 %collective-permute-done.37.refs_1_ = bf16[544,1024]{1,0:T(8,128)(2,1)} collective-permute-done((bf16[544,1024]{1,0:T(8,128)(2,1)}, bf16[544,1024]{1,0:T(8,128)(2,1)}, u32[]{:S(2)}, u32[]{:S(2)}) %collective-permute-start.37) | collective-permute-done | bytes 1114144 | tf_op jit(solution)/shard_map/ppermute | solution.py:869
  662.7 22.1 %collective-permute-done.41 = bf16[544,1024]{1,0:T(8,128)(2,1)} collective-permute-done((bf16[544,1024]{1,0:T(8,128)(2,1)S(1)}, bf16[544,1024]{1,0:T(8,128)(2,1)}, u32[]{:S(2)}, u32[]{:S(2)}) %collective-permute-start.41) | collective-permute-done | bytes 1114144 | tf_op jit(solution)/shard_map/ppermute | solution.py:869
  684.8 3.4 add_convert_fusion.6.refs_0_
  690.5 23.7 %collective-permute-done.42.refs_1_ = bf16[544,1024]{1,0:T(8,128)(2,1)S(1)} collective-permute-done((bf16[544,1024]{1,0:T(8,128)(2,1)S(1)}, bf16[544,1024]{1,0:T(8,128)(2,1)S(1)}, u32[]{:S(2)}, u32[]{:S(2)}) %collective-permute-start.42) | collective-permute-done | bytes 1114144 | tf_op jit(solution)/shard_map/ppermute | solution.py:869
  714.3 27.8 %all-gather.2.cloned.1.call-done = bf16[1152,1024]{1,0:T(8,128)(2,1)} async-done(((bf16[144,1024]{1,0:T(8,128)(2,1)}), bf16[1152,1024]{1,0:T(8,128)(2,1)}) %all-gather.2.cloned.1.call-update) | async-done | bytes 2359312 | tf_op jit(solution)/shard_map/all_gather | solution.py:1068
  742.9 6.8 assemble.3
  750.7 5.4 assemble.2
  758.4 2.1 slice_convert_fusion
  760.5 1.5 slice.100
  762.0 2.1 copy.110
  (210 shorter events, 56.1 us)
Async XLA Ops:
  10.3 33.1 %collective-permute-start = (bf16[512,1024]{1,0:T(8,128)(2,1)}, bf16[512,1024]{1,0:T(8,128)(2,1)}, u32[]{:S(2)}, u32[]{:S(2)}) collective-permute-start(bf16[512,1024]{1,0:T(8,128)(2,1)} %get-tuple-element.186.refs_0_), channel_id=1, source_target_pairs={{0,2},{1,3},{2,0},{3,1},{4,6},{5,7},{6,4},{7,5},{8,10},{9,11},{10,... | collective-permute-start | bytes 3145736 | tf_op jit(solution)/shard_map/ppermute | solution.py:869
  21.9 117.7 %copy-start.1 = (s32[2176,2]{1,0:T(8,128)}, s32[2176,2]{1,0:T(8,128)S(1)}, u32[]{:S(2)}) copy-start(s32[2176,2]{1,0:T(8,128)S(1)} %get-tuple-element.322.lp_ref) | copy-start | bytes 52228
  43.4 107.1 %all-to-all-start = ((bf16[8,2,112,1152]{3,2,1,0:T(8,128)(2,1)}), bf16[8,2,112,1152]{3,2,1,0:T(8,128)(2,1)}, u32[]{:S(2)}, u32[]{:S(2)}) async-start(bf16[8,2,112,1152]{3,2,1,0:T(8,128)(2,1)} %pack_cotangent.1), calls=%async_computation | async-start | bytes 8257536 | tf_op jit(solution)/shard_map/all_to_all | solution.py:912
  49.7 35.7 %collective-permute-start.1 = (bf16[512,1024]{1,0:T(8,128)(2,1)S(1)}, bf16[512,1024]{1,0:T(8,128)(2,1)}, u32[]{:S(2)}, u32[]{:S(2)}) collective-permute-start(bf16[512,1024]{1,0:T(8,128)(2,1)S(1)} %copy-done.14), channel_id=1, source_target_pairs={{0,2},{1,3},{2,0},{3,1},{4,6},{5,7},{6,4},{7,5},{8,10},{9,11},{10,... | collective-permute-start | bytes 3145736 | tf_op jit(solution)/shard_map/ppermute | solution.py:869
  50.3 41.0 %collective-permute-start.6 = (bf16[256,1024]{1,0:T(8,128)(2,1)S(1)}, bf16[256,1024]{1,0:T(8,128)(2,1)S(1)}, u32[]{:S(2)}, u32[]{:S(2)}) collective-permute-start(bf16[256,1024]{1,0:T(8,128)(2,1)S(1)} %copy-done.17), channel_id=1, source_target_pairs={{0,1},{1,0},{2,3},{3,2},{4,5},{5,4},{6,7},{7,6},{8,9},{9,8},{10,11... | collective-permute-start | bytes 1572872 | tf_op jit(solution)/shard_map/ppermute | solution.py:869
  50.3 35.1 %collective-permute-start.2 = (bf16[256,1024]{1,0:T(8,128)(2,1)S(1)}, bf16[256,1024]{1,0:T(8,128)(2,1)}, u32[]{:S(2)}, u32[]{:S(2)}) collective-permute-start(bf16[256,1024]{1,0:T(8,128)(2,1)S(1)} %copy-done.17), channel_id=1, source_target_pairs={{0,2},{1,3},{2,0},{3,1},{4,6},{5,7},{6,4},{7,5},{8,10},{9,11},{10,... | collective-permute-start | bytes 1572872 | tf_op jit(solution)/shard_map/ppermute | solution.py:869
  85.4 15.0 %collective-permute-start.7 = (bf16[256,1024]{1,0:T(8,128)(2,1)}, bf16[256,1024]{1,0:T(8,128)(2,1)S(1)}, u32[]{:S(2)}, u32[]{:S(2)}) collective-permute-start(bf16[256,1024]{1,0:T(8,128)(2,1)} %collective-permute-done.2.refs_5_.refs_15_), channel_id=1, source_target_pairs={{0,1},{1,0},{2,3},{3,2},{4,5},{5,4},{6,7},{7,6},{8,9},{9,8},{10,11... | collective-permute-start | bytes 1572872 | tf_op jit(solution)/shard_map/ppermute | solution.py:869
  85.4 9.7 %collective-permute-start.3 = (bf16[544,256]{1,0:T(8,128)(2,1)}, bf16[544,256]{1,0:T(8,128)(2,1)S(1)}, u32[]{:S(2)}, u32[]{:S(2)}) collective-permute-start(bf16[544,256]{1,0:T(8,128)(2,1)} %get-tuple-element.166), channel_id=1, source_target_pairs={{0,2},{1,3},{2,0},{3,1},{4,6},{5,7},{6,4},{7,5},{8,10},{9,11},{10,... | collective-permute-start | bytes 835592 | tf_op jit(solution)/shard_map/ppermute | solution.py:869
  86.0 9.1 %collective-permute-start.4 = (bf16[544,256]{1,0:T(8,128)(2,1)}, bf16[544,256]{1,0:T(8,128)(2,1)}, u32[]{:S(2)}, u32[]{:S(2)}) collective-permute-start(bf16[544,256]{1,0:T(8,128)(2,1)} %get-tuple-element.167), channel_id=1, source_target_pairs={{0,1},{1,0},{2,3},{3,2},{4,5},{5,4},{6,7},{7,6},{8,9},{9,8},{10,11... | collective-permute-start | bytes 835592 | tf_op jit(solution)/shard_map/ppermute | solution.py:869
  86.2 14.2 %collective-permute-start.5 = (bf16[544,256]{1,0:T(8,128)(2,1)}, bf16[544,256]{1,0:T(8,128)(2,1)}, u32[]{:S(2)}, u32[]{:S(2)}) collective-permute-start(bf16[544,256]{1,0:T(8,128)(2,1)} %get-tuple-element.168), channel_id=1, source_target_pairs={{0,3},{1,2},{2,1},{3,0},{4,7},{5,6},{6,5},{7,4},{8,11},{9,10},{10,... | collective-permute-start | bytes 835592 | tf_op jit(solution)/shard_map/ppermute | solution.py:869
  108.0 27.2 %collective-permute-start.8 = (bf16[544,1024]{1,0:T(8,128)(2,1)}, bf16[544,1024]{1,0:T(8,128)(2,1)S(1)}, u32[]{:S(2)}, u32[]{:S(2)}) collective-permute-start(bf16[544,1024]{1,0:T(8,128)(2,1)} %get-tuple-element.173.refs_0_.refs_4_), channel_id=1, source_target_pairs={{0,2},{1,3},{2,0},{3,1},{4,6},{5,7},{6,4},{7,5},{8,10},{9,11},{10,... | collective-permute-start | bytes 3342344 | tf_op jit(solution)/shard_map/ppermute | solution.py:869
  108.6 26.7 %collective-permute-start.9 = (bf16[544,1024]{1,0:T(8,128)(2,1)}, bf16[544,1024]{1,0:T(8,128)(2,1)S(1)}, u32[]{:S(2)}, u32[]{:S(2)}) collective-permute-start(bf16[544,1024]{1,0:T(8,128)(2,1)} %get-tuple-element.173.refs_0_.refs_4_), channel_id=1, source_target_pairs={{0,1},{1,0},{2,3},{3,2},{4,5},{5,4},{6,7},{7,6},{8,9},{9,8},{10,11... | collective-permute-start | bytes 3342344 | tf_op jit(solution)/shard_map/ppermute | solution.py:869
  135.3 2.8 collective-permute-start.10
  139.0 48.0 %collective-permute-start.11 = (bf16[1024,1024]{1,0:T(8,128)(2,1)}, bf16[1024,1024]{1,0:T(8,128)(2,1)}, u32[]{:S(2)}, u32[]{:S(2)}) collective-permute-start(bf16[1024,1024]{1,0:T(8,128)(2,1)} %bitcast.84), channel_id=1, source_target_pairs={{0,2},{1,3},{2,0},{3,1},{4,6},{5,7},{6,4},{7,5},{8,10},{9,11},{10,... | collective-permute-start | bytes 6291464 | tf_op jit(solution)/shard_map/ppermute | solution.py:869
  150.5 48.2 %all-to-all-start.1 = ((bf16[8,112,1024]{2,1,0:T(8,128)(2,1)}), bf16[8,112,1024]{2,1,0:T(8,128)(2,1)S(1)}, u32[]{:S(2)}, u32[]{:S(2)}) async-start(bf16[8,112,1024]{2,1,0:T(8,128)(2,1)} %bitcast.69), calls=%async_computation.1 | async-start | bytes 3670016 | tf_op jit(solution)/shard_map/all_to_all | solution.py:912
  156.1 31.5 %collective-permute-start.13 = (bf16[512,1024]{1,0:T(8,128)(2,1)}, bf16[512,1024]{1,0:T(8,128)(2,1)}, u32[]{:S(2)}, u32[]{:S(2)}) collective-permute-start(bf16[512,1024]{1,0:T(8,128)(2,1)} %get-tuple-element.187.refs_1_), channel_id=1, source_target_pairs={{0,1},{1,0},{2,3},{3,2},{4,5},{5,4},{6,7},{7,6},{8,9},{9,8},{10,11... | collective-permute-start | bytes 3145736 | tf_op jit(solution)/shard_map/ppermute | solution.py:869
  156.1 48.3 %collective-permute-start.16 = (bf16[1024,1024]{1,0:T(8,128)(2,1)}, bf16[1024,1024]{1,0:T(8,128)(2,1)}, u32[]{:S(2)}, u32[]{:S(2)}) collective-permute-start(bf16[1024,1024]{1,0:T(8,128)(2,1)} %bitcast.85), channel_id=1, source_target_pairs={{0,1},{1,0},{2,3},{3,2},{4,5},{5,4},{6,7},{7,6},{8,9},{9,8},{10,11... | collective-permute-start | bytes 6291464 | tf_op jit(solution)/shard_map/ppermute | solution.py:869
  187.0 17.4 %collective-permute-start.17 = (bf16[1024,1024]{1,0:T(8,128)(2,1)}, bf16[1024,1024]{1,0:T(8,128)(2,1)}, u32[]{:S(2)}, u32[]{:S(2)}) collective-permute-start(bf16[1024,1024]{1,0:T(8,128)(2,1)} %collective-permute-done.11.refs_9_), channel_id=1, source_target_pairs={{0,1},{1,0},{2,3},{3,2},{4,5},{5,4},{6,7},{7,6},{8,9},{9,8},{10,11... | collective-permute-start | bytes 6291464 | tf_op jit(solution)/shard_map/ppermute | solution.py:869
  187.0 17.3 %collective-permute-start.12 = (bf16[512,1024]{1,0:T(8,128)(2,1)}, bf16[512,1024]{1,0:T(8,128)(2,1)S(1)}, u32[]{:S(2)}, u32[]{:S(2)}) collective-permute-start(bf16[512,1024]{1,0:T(8,128)(2,1)} %get-tuple-element.186.refs_0_), channel_id=1, source_target_pairs={{0,1},{1,0},{2,3},{3,2},{4,5},{5,4},{6,7},{7,6},{8,9},{9,8},{10,11... | collective-permute-start | bytes 3145736 | tf_op jit(solution)/shard_map/ppermute | solution.py:869
  187.5 16.9 %collective-permute-start.14 = (bf16[512,1024]{1,0:T(8,128)(2,1)}, bf16[512,1024]{1,0:T(8,128)(2,1)}, u32[]{:S(2)}, u32[]{:S(2)}) collective-permute-start(bf16[512,1024]{1,0:T(8,128)(2,1)} %collective-permute-done.refs_2_), channel_id=1, source_target_pairs={{0,1},{1,0},{2,3},{3,2},{4,5},{5,4},{6,7},{7,6},{8,9},{9,8},{10,11... | collective-permute-start | bytes 3145736 | tf_op jit(solution)/shard_map/ppermute | solution.py:869
  187.5 16.9 %collective-permute-start.15 = (bf16[512,1024]{1,0:T(8,128)(2,1)}, bf16[512,1024]{1,0:T(8,128)(2,1)}, u32[]{:S(2)}, u32[]{:S(2)}) collective-permute-start(bf16[512,1024]{1,0:T(8,128)(2,1)} %collective-permute-done.1.refs_3_), channel_id=1, source_target_pairs={{0,1},{1,0},{2,3},{3,2},{4,5},{5,4},{6,7},{7,6},{8,9},{9,8},{10,11... | collective-permute-start | bytes 3145736 | tf_op jit(solution)/shard_map/ppermute | solution.py:869
  200.0 64.4 %all-to-all-start.2 = ((bf16[8,112,1024]{2,1,0:T(8,128)(2,1)}), bf16[8,112,1024]{2,1,0:T(8,128)(2,1)}, u32[]{:S(2)}, u32[]{:S(2)}) async-start(bf16[8,112,1024]{2,1,0:T(8,128)(2,1)} %bitcast.67), calls=%async_computation.2 | async-start | bytes 3670016 | tf_op jit(solution)/shard_map/all_to_all | solution.py:912
  264.5 53.5 %all-to-all-start.3 = ((bf16[8,112,1024]{2,1,0:T(8,128)(2,1)}), bf16[8,112,1024]{2,1,0:T(8,128)(2,1)S(1)}, u32[]{:S(2)}, u32[]{:S(2)}) async-start(bf16[8,112,1024]{2,1,0:T(8,128)(2,1)} %bitcast.70), calls=%async_computation.3 | async-start | bytes 3670016 | tf_op jit(solution)/shard_map/all_to_all | solution.py:912
  319.2 47.4 %all-to-all-start.4 = ((bf16[8,112,1024]{2,1,0:T(8,128)(2,1)}), bf16[8,112,1024]{2,1,0:T(8,128)(2,1)}, u32[]{:S(2)}, u32[]{:S(2)}) async-start(bf16[8,112,1024]{2,1,0:T(8,128)(2,1)} %bitcast.68), calls=%async_computation.4 | async-start | bytes 3670016 | tf_op jit(solution)/shard_map/all_to_all | solution.py:912
  339.2 14.5 %collective-permute-start.18 = (bf16[1024,1024]{1,0:T(8,128)(2,1)}, bf16[1024,1024]{1,0:T(8,128)(2,1)S(1)}, u32[]{:S(2)}, u32[]{:S(2)}) collective-permute-start(bf16[1024,1024]{1,0:T(8,128)(2,1)} %get-tuple-element.210), channel_id=1, source_target_pairs={{0,1},{1,0},{2,3},{3,2},{4,5},{5,4},{6,7},{7,6},{8,9},{9,8},{10,11... | collective-permute-start | bytes 6291464 | tf_op jit(solution)/shard_map/ppermute | solution.py:869
  339.2 14.5 %collective-permute-start.19 = (bf16[1024,1024]{1,0:T(8,128)(2,1)}, bf16[1024,1024]{1,0:T(8,128)(2,1)}, u32[]{:S(2)}, u32[]{:S(2)}) collective-permute-start(bf16[1024,1024]{1,0:T(8,128)(2,1)} %get-tuple-element.211), channel_id=1, source_target_pairs={{0,1},{1,0},{2,3},{3,2},{4,5},{5,4},{6,7},{7,6},{8,9},{9,8},{10,11... | collective-permute-start | bytes 6291464 | tf_op jit(solution)/shard_map/ppermute | solution.py:869
  366.6 46.3 %all-to-all-start.5 = ((bf16[8,112,1024]{2,1,0:T(8,128)(2,1)}), bf16[8,112,1024]{2,1,0:T(8,128)(2,1)}, u32[]{:S(2)}, u32[]{:S(2)}) async-start(bf16[8,112,1024]{2,1,0:T(8,128)(2,1)} %bitcast.26), calls=%async_computation.5 | async-start | bytes 3670016 | tf_op jit(solution)/shard_map/all_to_all | solution.py:912
  388.5 5.4 collective-permute-start.20
  388.5 5.4 collective-permute-start.21
  392.3 74.6 %collective-permute-start.24 = (bf16[1024,1024]{1,0:T(8,128)(2,1)S(1)}, bf16[1024,1024]{1,0:T(8,128)(2,1)}, u32[]{:S(2)}, u32[]{:S(2)}) collective-permute-start(bf16[1024,1024]{1,0:T(8,128)(2,1)S(1)} %add_convert_fusion.2), channel_id=1, source_target_pairs={{0,2},{1,3},{2,0},{3,1},{4,6},{5,7},{6,4},{7,5},{8,10},{9,11},{10,... | collective-permute-start | bytes 6291464 | tf_op jit(solution)/shard_map/ppermute | solution.py:869
  396.0 70.9 %collective-permute-start.23 = (bf16[272,1152]{1,0:T(8,128)(2,1)}, bf16[272,1152]{1,0:T(8,128)(2,1)}, u32[]{:S(2)}, u32[]{:S(2)}) collective-permute-start(bf16[272,1152]{1,0:T(8,128)(2,1)} %get-tuple-element.317), channel_id=1, source_target_pairs={{0,2},{1,3},{2,0},{3,1},{4,6},{5,7},{6,4},{7,5},{8,10},{9,11},{10,... | collective-permute-start | bytes 1880072 | tf_op jit(solution)/shard_map/ppermute | solution.py:869
  396.5 70.4 %collective-permute-start.22 = (bf16[272,1152]{1,0:T(8,128)(2,1)}, bf16[272,1152]{1,0:T(8,128)(2,1)}, u32[]{:S(2)}, u32[]{:S(2)}) collective-permute-start(bf16[272,1152]{1,0:T(8,128)(2,1)} %get-tuple-element.318), channel_id=1, source_target_pairs={{0,2},{1,3},{2,0},{3,1},{4,6},{5,7},{6,4},{7,5},{8,10},{9,11},{10,... | collective-permute-start | bytes 1880072 | tf_op jit(solution)/shard_map/ppermute | solution.py:869
  412.9 116.8 %all-to-all-start.7 = ((bf16[8,112,1024]{2,1,0:T(8,128)(2,1)}), bf16[8,112,1024]{2,1,0:T(8,128)(2,1)}, u32[]{:S(2)}, u32[]{:S(2)}) async-start(bf16[8,112,1024]{2,1,0:T(8,128)(2,1)} %bitcast.62), calls=%async_computation.7 | async-start | bytes 3670016 | tf_op jit(solution)/shard_map/all_to_all | solution.py:912
  418.0 14.1 %copy-start.7 = (bf16[544,1152]{1,0:T(8,128)(2,1)S(1)}, bf16[544,1152]{1,0:T(8,128)(2,1)}, u32[]{:S(2)}) copy-start(bf16[544,1152]{1,0:T(8,128)(2,1)} %get-tuple-element.238) | copy-start | bytes 3760132
  479.3 2.7 collective-permute-start.28
  479.4 2.9 collective-permute-start.29
  479.9 9.7 %collective-permute-start.25 = (bf16[544,256]{1,0:T(8,128)(2,1)}, bf16[544,256]{1,0:T(8,128)(2,1)S(1)}, u32[]{:S(2)}, u32[]{:S(2)}) collective-permute-start(bf16[544,256]{1,0:T(8,128)(2,1)} %get-tuple-element.248), channel_id=1, source_target_pairs={{0,2},{1,3},{2,0},{3,1},{4,6},{5,7},{6,4},{7,5},{8,10},{9,11},{10,... | collective-permute-start | bytes 835592 | tf_op jit(solution)/shard_map/ppermute | solution.py:869
  481.4 8.2 %collective-permute-start.26 = (bf16[544,256]{1,0:T(8,128)(2,1)}, bf16[544,256]{1,0:T(8,128)(2,1)S(1)}, u32[]{:S(2)}, u32[]{:S(2)}) collective-permute-start(bf16[544,256]{1,0:T(8,128)(2,1)} %get-tuple-element.249), channel_id=1, source_target_pairs={{0,1},{1,0},{2,3},{3,2},{4,5},{5,4},{6,7},{7,6},{8,9},{9,8},{10,11... | collective-permute-start | bytes 835592 | tf_op jit(solution)/shard_map/ppermute | solution.py:869
  481.4 13.3 %collective-permute-start.27 = (bf16[544,256]{1,0:T(8,128)(2,1)}, bf16[544,256]{1,0:T(8,128)(2,1)S(1)}, u32[]{:S(2)}, u32[]{:S(2)}) collective-permute-start(bf16[544,256]{1,0:T(8,128)(2,1)} %get-tuple-element.250), channel_id=1, source_target_pairs={{0,3},{1,2},{2,1},{3,0},{4,7},{5,6},{6,5},{7,4},{8,11},{9,10},{10,... | collective-permute-start | bytes 835592 | tf_op jit(solution)/shard_map/ppermute | solution.py:869
  483.5 49.1 %collective-permute-start.30 = (bf16[256,1024]{1,0:T(8,128)(2,1)S(1)}, bf16[256,1024]{1,0:T(8,128)(2,1)}, u32[]{:S(2)}, u32[]{:S(2)}) collective-permute-start(bf16[256,1024]{1,0:T(8,128)(2,1)S(1)} %add_convert_fusion.12), channel_id=1, source_target_pairs={{0,2},{1,3},{2,0},{3,1},{4,6},{5,7},{6,4},{7,5},{8,10},{9,11},{10,... | collective-permute-start | bytes 1572872 | tf_op jit(solution)/shard_map/ppermute | solution.py:869
  495.4 35.6 %copy-start.25 = (f32[1,1024]{1,0:T(1,128)S(1)}, f32[1,1024]{1,0:T(1,128)}, u32[]{:S(2)}) copy-start(f32[1,1024]{1,0:T(1,128)} %get-tuple-element.259) | copy-start | bytes 12292
  495.4 37.1 %copy-start.20 = (bf16[256,1024]{1,0:T(8,128)(2,1)S(1)}, bf16[256,1024]{1,0:T(8,128)(2,1)}, u32[]{:S(2)}) copy-start(bf16[256,1024]{1,0:T(8,128)(2,1)} %get-tuple-element.252) | copy-start | bytes 1572868
  529.7 12.0 %collective-permute-start.31 = (bf16[544,1024]{1,0:T(8,128)(2,1)}, bf16[544,1024]{1,0:T(8,128)(2,1)}, u32[]{:S(2)}, u32[]{:S(2)}) collective-permute-start(bf16[544,1024]{1,0:T(8,128)(2,1)} %get-tuple-element.267), channel_id=1, source_target_pairs={{0,1},{1,0},{2,3},{3,2},{4,5},{5,4},{6,7},{7,6},{8,9},{9,8},{10,11... | collective-permute-start | bytes 3342344 | tf_op jit(solution)/shard_map/ppermute | solution.py:869
  530.4 11.3 %collective-permute-start.32 = (bf16[544,1024]{1,0:T(8,128)(2,1)}, bf16[544,1024]{1,0:T(8,128)(2,1)}, u32[]{:S(2)}, u32[]{:S(2)}) collective-permute-start(bf16[544,1024]{1,0:T(8,128)(2,1)} %get-tuple-element.268), channel_id=1, source_target_pairs={{0,1},{1,0},{2,3},{3,2},{4,5},{5,4},{6,7},{7,6},{8,9},{9,8},{10,11... | collective-permute-start | bytes 3342344 | tf_op jit(solution)/shard_map/ppermute | solution.py:869
  530.5 34.7 %collective-permute-start.38 = (bf16[1024,1024]{1,0:T(8,128)(2,1)}, bf16[1024,1024]{1,0:T(8,128)(2,1)}, u32[]{:S(2)}, u32[]{:S(2)}) collective-permute-start(bf16[1024,1024]{1,0:T(8,128)(2,1)} %get-tuple-element.226), channel_id=1, source_target_pairs={{0,1},{1,0},{2,3},{3,2},{4,5},{5,4},{6,7},{7,6},{8,9},{9,8},{10,11... | collective-permute-start | bytes 6291464 | tf_op jit(solution)/shard_map/ppermute | solution.py:869
  531.0 34.3 %collective-permute-start.39 = (bf16[1024,1024]{1,0:T(8,128)(2,1)}, bf16[1024,1024]{1,0:T(8,128)(2,1)}, u32[]{:S(2)}, u32[]{:S(2)}) collective-permute-start(bf16[1024,1024]{1,0:T(8,128)(2,1)} %get-tuple-element.227), channel_id=1, source_target_pairs={{0,1},{1,0},{2,3},{3,2},{4,5},{5,4},{6,7},{7,6},{8,9},{9,8},{10,11... | collective-permute-start | bytes 6291464 | tf_op jit(solution)/shard_map/ppermute | solution.py:869
  535.5 152.7 %all-to-all-start.6 = ((bf16[8,144,1024]{2,1,0:T(8,128)(2,1)}), bf16[8,144,1024]{2,1,0:T(8,128)(2,1)S(1)}, u32[]{:S(2)}, u32[]{:S(2)}) async-start(bf16[8,144,1024]{2,1,0:T(8,128)(2,1)} %bitcast.54), calls=%async_computation.6 | async-start | bytes 4718592 | tf_op jit(solution)/shard_map/all_to_all | solution.py:912
  541.4 200.7 %all-gather.2.cloned.1.call-start = ((), (), s32[]{:S(2)}) async-start(), calls=%async_computation.8 | async-start | bytes 2654208 | tf_op jit(solution)/shard_map/all_gather | solution.py:1068
  547.4 17.3 %collective-permute-start.33 = (bf16[272,1024]{1,0:T(8,128)(2,1)S(1)}, bf16[272,1024]{1,0:T(8,128)(2,1)S(1)}, u32[]{:S(2)}, u32[]{:S(2)}) collective-permute-start(bf16[272,1024]{1,0:T(8,128)(2,1)S(1)} %get-tuple-element.320), channel_id=1, source_target_pairs={{0,2},{1,3},{2,0},{3,1},{4,6},{5,7},{6,4},{7,5},{8,10},{9,11},{10,... | collective-permute-start | bytes 1671176 | tf_op jit(solution)/shard_map/ppermute | solution.py:869
  564.7 7.1 collective-permute-start.34
  564.7 7.0 collective-permute-start.35
  569.8 76.2 %collective-permute-start.40 = (bf16[1024,1024]{1,0:T(8,128)(2,1)}, bf16[1024,1024]{1,0:T(8,128)(2,1)}, u32[]{:S(2)}, u32[]{:S(2)}) collective-permute-start(bf16[1024,1024]{1,0:T(8,128)(2,1)} %add_convert_fusion), channel_id=1, source_target_pairs={{0,2},{1,3},{2,0},{3,1},{4,6},{5,7},{6,4},{7,5},{8,10},{9,11},{10,... | collective-permute-start | bytes 6291464 | tf_op jit(solution)/shard_map/ppermute | solution.py:869
  570.3 59.2 %collective-permute-start.36 = (bf16[272,1024]{1,0:T(8,128)(2,1)}, bf16[272,1024]{1,0:T(8,128)(2,1)S(1)}, u32[]{:S(2)}, u32[]{:S(2)}) collective-permute-start(bf16[272,1024]{1,0:T(8,128)(2,1)} %get-tuple-element.319), channel_id=1, source_target_pairs={{0,2},{1,3},{2,0},{3,1},{4,6},{5,7},{6,4},{7,5},{8,10},{9,11},{10,... | collective-permute-start | bytes 1671176 | tf_op jit(solution)/shard_map/ppermute | solution.py:869
  634.9 27.8 %collective-permute-start.37 = (bf16[544,1024]{1,0:T(8,128)(2,1)}, bf16[544,1024]{1,0:T(8,128)(2,1)}, u32[]{:S(2)}, u32[]{:S(2)}) collective-permute-start(bf16[544,1024]{1,0:T(8,128)(2,1)} %input_back.1.refs_0_), channel_id=1, source_target_pairs={{0,2},{1,3},{2,0},{3,1},{4,6},{5,7},{6,4},{7,5},{8,10},{9,11},{10,... | collective-permute-start | bytes 3342344 | tf_op jit(solution)/shard_map/ppermute | solution.py:869
  635.4 49.4 %collective-permute-start.41 = (bf16[544,1024]{1,0:T(8,128)(2,1)S(1)}, bf16[544,1024]{1,0:T(8,128)(2,1)}, u32[]{:S(2)}, u32[]{:S(2)}) collective-permute-start(bf16[544,1024]{1,0:T(8,128)(2,1)S(1)} %add_convert_fusion.7), channel_id=1, source_target_pairs={{0,2},{1,3},{2,0},{3,1},{4,6},{5,7},{6,4},{7,5},{8,10},{9,11},{10,... | collective-permute-start | bytes 3342344 | tf_op jit(solution)/shard_map/ppermute | solution.py:869
  688.2 61.5 %copy-start = (bf16[544,1024]{1,0:T(8,128)(2,1)}, bf16[544,1024]{1,0:T(8,128)(2,1)S(1)}, u32[]{:S(2)}) copy-start(bf16[544,1024]{1,0:T(8,128)(2,1)S(1)} %add_convert_fusion.6.refs_0_) | copy-start | bytes 3342340
  689.4 24.8 %collective-permute-start.42 = (bf16[544,1024]{1,0:T(8,128)(2,1)S(1)}, bf16[544,1024]{1,0:T(8,128)(2,1)S(1)}, u32[]{:S(2)}, u32[]{:S(2)}) collective-permute-start(bf16[544,1024]{1,0:T(8,128)(2,1)S(1)} %add_convert_fusion.6.refs_0_), channel_id=1, source_target_pairs={{0,2},{1,3},{2,0},{3,1},{4,6},{5,7},{6,4},{7,5},{8,10},{9,11},{10,... | collective-permute-start | bytes 3342344 | tf_op jit(solution)/shard_map/ppermute | solution.py:869
  690.0 52.9 %collective-permute-start.45 = (bf16[544,1024]{1,0:T(8,128)(2,1)}, bf16[544,1024]{1,0:T(8,128)(2,1)}, u32[]{:S(2)}, u32[]{:S(2)}) collective-permute-start(bf16[544,1024]{1,0:T(8,128)(2,1)} %input_back.1.refs_0_), channel_id=1, source_target_pairs={{0,1},{1,0},{2,3},{3,2},{4,5},{5,4},{6,7},{7,6},{8,9},{9,8},{10,11... | collective-permute-start | bytes 3342344 | tf_op jit(solution)/shard_map/ppermute | solution.py:869
  690.0 52.9 %collective-permute-start.46 = (bf16[544,1024]{1,0:T(8,128)(2,1)}, bf16[544,1024]{1,0:T(8,128)(2,1)}, u32[]{:S(2)}, u32[]{:S(2)}) collective-permute-start(bf16[544,1024]{1,0:T(8,128)(2,1)} %collective-permute-done.37.refs_1_), channel_id=1, source_target_pairs={{0,1},{1,0},{2,3},{3,2},{4,5},{5,4},{6,7},{7,6},{8,9},{9,8},{10,11... | collective-permute-start | bytes 3342344 | tf_op jit(solution)/shard_map/ppermute | solution.py:869
  690.5 59.1 %collective-permute-start.43 = (bf16[544,1024]{1,0:T(8,128)(2,1)S(1)}, bf16[544,1024]{1,0:T(8,128)(2,1)S(1)}, u32[]{:S(2)}, u32[]{:S(2)}) collective-permute-start(bf16[544,1024]{1,0:T(8,128)(2,1)S(1)} %add_convert_fusion.6.refs_0_), channel_id=1, source_target_pairs={{0,1},{1,0},{2,3},{3,2},{4,5},{5,4},{6,7},{7,6},{8,9},{9,8},{10,11... | collective-permute-start | bytes 3342344 | tf_op jit(solution)/shard_map/ppermute | solution.py:869
  714.3 35.4 %copy-start.10 = (bf16[544,1024]{1,0:T(8,128)(2,1)}, bf16[544,1024]{1,0:T(8,128)(2,1)S(1)}, u32[]{:S(2)}) copy-start(bf16[544,1024]{1,0:T(8,128)(2,1)S(1)} %collective-permute-done.42.refs_1_) | copy-start | bytes 3342340
  714.3 35.4 %collective-permute-start.44 = (bf16[544,1024]{1,0:T(8,128)(2,1)S(1)}, bf16[544,1024]{1,0:T(8,128)(2,1)}, u32[]{:S(2)}, u32[]{:S(2)}) collective-permute-start(bf16[544,1024]{1,0:T(8,128)(2,1)S(1)} %collective-permute-done.42.refs_1_), channel_id=1, source_target_pairs={{0,1},{1,0},{2,3},{3,2},{4,5},{5,4},{6,7},{7,6},{8,9},{9,8},{10,11... | collective-permute-start | bytes 3342344 | tf_op jit(solution)/shard_map/ppermute | solution.py:869
  742.9 13.2 %collective-permute-start.47 = (f32[10,1024]{1,0:T(8,128)S(1)}, f32[10,1024]{1,0:T(8,128)S(1)}, u32[]{:S(2)}, u32[]{:S(2)}) collective-permute-start(f32[10,1024]{1,0:T(8,128)S(1)} %slice_convert_fusion.1), channel_id=1, source_target_pairs={{0,1},{1,0},{2,3},{3,2},{4,5},{5,4},{6,7},{7,6},{8,9},{9,8},{10,11... | collective-permute-start | bytes 122888 | tf_op jit(solution)/shard_map/ppermute | solution.py:869
  756.9 7.2 collective-permute-start.48
  (29 other events, 122.9 us)
Sparse Core Ops, SparseCore 0:
  689.5 52.5 all-gather.1

commit v7 on v6

--- a/solution.py
+++ b/solution.py
@@ -451,23 +451,32 @@
     )(part_of, *pieces)
 
 
-def sum_turned_kernel(a_ref, b_ref, out_ref):
-    out_ref[...] = (a_ref[...].astype(F32) + b_ref[...].astype(F32)).T
-
-
-def sum_turned(a, b):
-    rows, width = a.shape
-    tile = min(256, rows)
+def of_tiles(refs):
+    value = refs[0][...].astype(F32)
+    for n, ref in enumerate(refs[1:]):
+        value = jnp.where(pl.program_id(0) > n, ref[...].astype(F32), value)
+    return value
+
+
+def sum_far_kernel(turned, *refs):
+    far_refs, keep_ref, out_ref = refs[:-2], refs[-2], refs[-1]
+    total = keep_ref[...].astype(F32) + of_tiles(far_refs)
+    out_ref[...] = total.T if turned else total
+
+
+def sum_far(keep, far, turned):
+    rows, width = keep.shape
+    tile = rows // len(far)
     return pl.pallas_call(
-        sum_turned_kernel,
-        grid=(rows // tile,),
-        in_specs=[rows_spec(tile, width)] * 2,
-        out_specs=pl.BlockSpec((width, tile), lambda i: (0, i)),
-        out_shape=jax.ShapeDtypeStruct((width, rows), F32),
+        functools.partial(sum_far_kernel, turned),
+        grid=(len(far),),
+        in_specs=[whole((tile, width))] * len(far) + [rows_spec(tile, width)],
+        out_specs=pl.BlockSpec((width, tile), lambda i: (0, i)) if turned else rows_spec(tile, width),
+        out_shape=jax.ShapeDtypeStruct((width, rows) if turned else (rows, width), F32),
         compiler_params=params(),
         cost_estimate=cost(rows * width, 8 * rows * width),
-        name="sum_turned",
-    )(a, b)
+        name="sum_far",
+    )(*far, keep)
 
 
 def middle_kernel(count, limit, at_ref, *refs):
@@ -531,13 +540,6 @@
         cost_estimate=cost(4 * each * width * width, 24 * each * width),
         name="middle",
     )(at, *mixed, *head_out, x, gain, router, ids, noise)
-
-
-def of_tiles(refs):
-    value = refs[0][...].astype(F32)
-    for n, ref in enumerate(refs[1:]):
-        value = jnp.where(pl.program_id(0) > n, ref[...].astype(F32), value)
-    return value
 
 
 def middle_back_kernel(count, limit, tiles, at_ref, *refs):
@@ -892,11 +894,13 @@
     def far_hop(kept, other):
         return cross(other, 2) if paired else jnp.zeros_like(kept)
 
-    def far_tiles(kept, other):
-        tile = half_tile(each)
-        source = other if paired else jnp.zeros_like(kept)
-        tiles = [source[at : at + tile] for at in range(0, each, tile)]
-        return [cross(item, 2) for item in tiles] if paired else tiles
+    def far_tile(kept, other, n, tile):
+        if not paired:
+            return jnp.zeros_like(kept[n * tile : (n + 1) * tile])
+        return cross(other[n * tile : (n + 1) * tile], 2)
+
+    def after(x, *items):
+        return x if x is None else pinned(x, *items)[0]
 
     def scattered(pieces):
         kept, other = near_sum(pieces, near_hop(pieces))
@@ -1003,52 +1007,61 @@
 
     out_parts = weight_parts(actives, rows_grads)
     out_kept, out_other = near_sum(out_parts, near_hop(out_parts))
-    out_far = far_hop(out_kept, out_other)
-    *returned, out_kept = pinned(*returned, out_kept)
+    quarter = here // 4
+    tile = half_tile(each)
+    tiles = each // tile
+    out_far = [far_tile(out_kept, out_other, n, quarter) for n in range(2)]
+    *returned, out_kept, out_far[0] = pinned(*returned, out_kept, out_far[0])
 
     second_pieces = unpack(part_of, place, returned, slots, per, each, True)
+    *second_pieces, out_far[1] = pinned(*second_pieces, out_far[1])
+    out_far += [far_tile(out_kept, out_other, n, quarter) for n in range(2, 4)]
     second_kept, second_other = near_sum(second_pieces, near_hop(second_pieces))
-    if paired:
-        second_other, *hidden_grads = pinned(second_other, *hidden_grads)
-    second_far = far_tiles(second_kept, second_other)
+    second_kept, out_far[2] = pinned(second_kept, out_far[2])
+    second_other = after(second_other, second_kept)
+    *hidden_grads, second_kept = pinned(*hidden_grads, second_kept)
+    second_far = [far_tile(second_kept, second_other, n, tile) for n in range(tiles)]
     in_parts = []
     for p in range(parts - 2, -1, -2):
         *hidden_grads, pair = pinned(*hidden_grads, weight_grad(hidden_grads, arrived, p, here))
         in_parts = list(pair) + in_parts
         if p == parts - 2:
             in_came = near_hop([None] * p + list(pair)) if paired else ()
-            second_far[0], pair = pinned(second_far[0], pair)
-    second_far[-1], out_far, *in_parts = pinned(second_far[-1], out_far, *in_parts)
+            second_far[0], out_far[3], pair = pinned(second_far[0], out_far[3], pair)
+    in_kept, in_other = near_sum(in_parts, in_came)
+    second_far[-1], in_kept = pinned(second_far[-1], in_kept)
+    in_other = after(in_other, in_kept)
+    in_far = [far_tile(in_kept, in_other, 0, quarter)]
     combined = [sent(item) for item in backs]
     middle_grad, router_part, norm_two_part, *pieces = middle_back(
         own_block, second_kept, second_far, middle, second_in, gates, expert_ids, cotangent, mixed, head_out_all,
         gain_two, router_wide,
     )
     head_out_parts, mixed_grad = pieces[:parts], pieces[parts:]
-    *mixed_grad, combined[0] = pinned(*mixed_grad, combined[0])
+    *mixed_grad, combined[0], in_far[0] = pinned(*mixed_grad, combined[0], in_far[0])
     mixed_grad = swapped(mixed_grad)
     head_out_kept, head_out_far = scattered(head_out_parts)
-    in_kept, in_other = near_sum(in_parts, in_came)
-    if paired:
-        in_other = pinned(in_other, head_out_far, *mixed_grad)[0]
-    in_far = far_hop(in_kept, in_other)
+    in_other = after(in_other, *mixed_grad)
+    in_far += [far_tile(in_kept, in_other, n, quarter) for n in (1, 2)]
     *pieces, head_in_part, norm_one_part = attend_back(
         starts, mixed_grad, qkv, logs, first_in, head_in_t, gain_one
     )
-    *pieces, combined[-1] = pinned(*pieces, combined[-1])
+    *pieces, combined[-1], in_far[1], in_far[2], head_out_far = pinned(
+        *pieces, combined[-1], in_far[1], in_far[2], head_out_far
+    )
     first_kept, first_other = near_sum(pieces, near_hop(pieces))
-    if paired:
-        first_other, first_kept, *combined = pinned(first_other, first_kept, *combined)
-    first_far = far_tiles(first_kept, first_other)
+    first_kept, head_in_part, head_out_far, *combined = pinned(first_kept, head_in_part, head_out_far, *combined)
+    first_other = after(first_other, first_kept)
+    first_far = [far_tile(first_kept, first_other, n, tile) for n in range(tiles)]
     block_pieces = unpack(part_of, place, combined, slots, per, each, False)
-    first_far[0], *block_pieces = pinned(first_far[0], *block_pieces)
+    first_far, block_pieces = pinned(first_far, block_pieces)
+    in_far.append(far_tile(in_kept, after(in_other, block_pieces[0]), 3, quarter))
     block_kept, block_other = near_sum(block_pieces, near_hop(block_pieces))
-    if paired:
-        first_far[-1], block_other = pinned(first_far[-1], block_other)
-    block_far = far_hop(block_kept, block_other)
     input_part = input_back(own_block, first_kept, first_far, block_in, middle_grad, gain_one)
-    out_grad = out_kept.astype(F32) + out_far.astype(F32)
-    in_grad = sum_turned(in_kept, in_far)
+    input_part, block_kept, in_far[3] = pinned(input_part, block_kept, in_far[3])
+    block_far = far_hop(block_kept, after(block_other, block_kept))
+    out_grad = sum_far(out_kept, out_far, False)
+    in_grad = sum_far(in_kept, in_far, True)
     input_far, out_grad, in_grad, block_far = pinned(far_part(input_part), out_grad, in_grad, block_far)
     block_own = (middle + block_kept.astype(F32) + block_far.astype(F32)).astype(BF)
 
@@ -1061,7 +1074,7 @@
         [head_in_part.reshape(3 * cols, width), head_out_part, jnp.pad(small, ((0, total - count), (0, 0)))], 0
     )
     heads = over_experts(heads.reshape(groups, total // groups, width))
-    heads, block_own = pinned(heads, block_own)
+    heads, input_part = pinned(heads, input_part)
     input_grad = assemble(part_of, gathered_from(input_part, input_far), rows_here, F32)
     block_out = assemble(part_of, gathered(block_own), rows_here, BF)
     heads = jnp.sum(heads.astype(F32), 0).astype(BF)

time: 780 us -> 749 us (0.960)
  waiting for transfers between devices: 264 us -> 217 us
    all_gather x1, waiting for transfers between devices: 27.8 us -> 0.01 us  [shards(): heads = lax.all_gather(heads, 'expert', axis=0, tiled=True)]
    ppermute x49 -> x55, waiting for transfers between devices: 216 us -> 189 us  [cross(): return lax.ppermute(x, 'tensor', [(n, n ^ k) for n in range(parts)])]
    convert_element_type x10 -> x11, other arithmetic: 24.9 us -> 30.1 us  [near_sum(): (a.astype(F32) + b.astype(F32)).astype(BF)]
    ppermute x49 -> x55, starting transfers between devices: 29 us -> 34 us  [cross(): return lax.ppermute(x, 'tensor', [(n, n ^ k) for n in range(parts)])]
  transfers between devices with their start and end apart: 58 -> 64, of which waited for: 18 -> 23; matrix products, arithmetic and copies ran while one was open for 9% -> 9% of each run, Pallas kernels for 44% -> 45%
where the time goes in v7:
time: 749 us; the launch traced here: 742 us
  Pallas kernels  345 us (46%)
  waiting for transfers between devices  217 us (29%)
  starting transfers between devices  78.4 us (10%)
  other arithmetic  48.6 us (6%)
  local copies, waits for them, and re-layouts  37.3 us (5%)
  between operations  14.9 us (2%)
    ppermute x55, waiting for transfers between devices, cross(): return lax.ppermute(x, 'tensor', [(n, n ^ k) for n in range(parts)])  189 us
    pallas_call x2, Pallas kernels, expert(): pl.pallas_call(functools.partial(expert_kernel, count, slots, per), grid=...  107 us
    pallas_call x4, Pallas kernels, weight_grad(): pl.pallas_call(functools.partial(weight_kernel, count, steps), grid=(2 *...  56.5 us
    all_to_all x8, starting transfers between devices, over_experts(): return lax.all_to_all(x, 'expert', split_axis=0, concat_axis=0, tiled=True)  44.3 us
    pallas_call x1, Pallas kernels, attend_back(): pl.pallas_call(functools.partial(attend_back_kernel, count), grid_spec=sp...  34.3 us
    ppermute x55, starting transfers between devices, cross(): return lax.ppermute(x, 'tensor', [(n, n ^ k) for n in range(parts)])  34 us
    pallas_call x2, Pallas kernels, unpack(): pl.pallas_call(functools.partial(unpack_kernel, count, slots, per, graded...  33.5 us
    pallas_call x1, Pallas kernels, attend(): pl.pallas_call(functools.partial(attend_kernel, count), grid_spec=spec, o...  30.4 us
  transfers between devices with their start and end apart: 64, of which 23 were waited for; matrix products, arithmetic and copies ran while one was open for 9% of the time, Pallas kernels for 45%

profile of v7, /device:TPU:0, one launch (start us, length us, event | category | flops | bytes accessed | tf_op | source)
XLA Modules:
  0.0 741.9 jit_solution(4877218242215089912)
XLA Ops:
  7.2 3.1 slice_bitcast_fusion
  10.3 2.9 collective-permute-start
  13.4 2.3 reduce-window.6
  23.5 2.6 fusion.5.side_ref
  26.1 17.3 %pack_cotangent.1 = bf16[8,2,112,1152]{3,2,1,0:T(8,128)(2,1)} custom-call(bf16[2167,1024]{1,0:T(8,128)(2,1)} %refs_7_.1, bf16[16,1024]{1,0:T(8,128)(2,1)} %pad.26.tail_ref, s32[2,2176]{1,0:T(2,128)} %copy.103.lp_ref, bf16[2,2176,128]{2,1,0:T(8,128)(2,1)} %fusion.5.side_ref), custom_call_target="tpu_custom_call" | custom-call | flops 11978932224 | bytes 4438016 | tf_op jit(solution)/shard_map/pack_cotangent/pallas_call | solution.py:323
  43.5 6.4 all-to-all-start
  53.2 30.4 %attend.1 = (bf16[11,208,1024]{2,1,0:T(8,128)(2,1)}, bf16[3,11,208,256]{3,2,1,0:T(8,128)(2,1)}, f32[11,208,128]{2,1,0:T(8,128)}, bf16[544,256]{1,0:T(8,128)(2,1)...) custom-call(s32[4]{0:T(128)} %get-tuple-element.351.starts_ref, ...), custom_call_target="tpu_custom_call" | custom-call | flops 9596567552 | bytes 35504128 | tf_op jit(solution)/shard_map/attend/pallas_call | solution.py:180
  83.6 2.0 collective-permute-done.2.refs_5_.refs_15_
  91.5 3.8 collective-permute-done.3.refs_1_.refs_11_
  95.3 5.3 collective-permute-done.5.refs_3_.refs_13_
  101.5 6.8 middle.1
  109.1 26.4 %collective-permute-done.8.refs_1_ = bf16[544,1024]{1,0:T(8,128)(2,1)S(1)} collective-permute-done((bf16[544,1024]{1,0:T(8,128)(2,1)}, bf16[544,1024]{1,0:T(8,128)(2,1)S(1)}, u32[]{:S(2)}, u32[]{:S(2)}) %collective-permute-start.8) | collective-permute-done | bytes 1114144 | tf_op jit(solution)/shard_map/ppermute | solution.py:871
  135.5 2.7 collective-permute-done.10.refs_3_
  140.8 9.9 %pack_rows.3 = bf16[896,1024]{1,0:T(8,128)(2,1)} custom-call(s32[4]{0:T(128)} %get-tuple-element.352.part_ref, bf16[544,1024]{1,0:T(8,128)(2,1)} %get-tuple-element.193.refs_0_.refs_4_, bf16[544,1024]{1,0:T(8,128)(2,1)} %copy-done.33, bf16[544,1024]{1,0:T(8,128)(2,1)} %copy-done.34, bf16[544,1024]{1,0:T(8,128)(2,1)} %copy-done.35, s32[4,2,544]{2,1,0:T(2,128)} %bitcast.75), custom_call_target="tpu_custom_call" | custom-call | flops 5989466112 | bytes 4456448 | tf_op jit(solution)/shard_map/pack_rows/pallas_call | solution.py:359
  150.8 5.6 all-to-all-start.1
  158.6 9.9 %pack_rows.2 = bf16[896,1024]{1,0:T(8,128)(2,1)} custom-call(s32[4]{0:T(128)} %get-tuple-element.352.part_ref, bf16[544,1024]{1,0:T(8,128)(2,1)} %get-tuple-element.193.refs_0_.refs_4_, bf16[544,1024]{1,0:T(8,128)(2,1)} %copy-done.33, bf16[544,1024]{1,0:T(8,128)(2,1)} %copy-done.34, bf16[544,1024]{1,0:T(8,128)(2,1)} %copy-done.35, s32[4,2,544]{2,1,0:T(2,128)} %bitcast.76), custom_call_target="tpu_custom_call" | custom-call | flops 5989466112 | bytes 4456448 | tf_op jit(solution)/shard_map/pack_rows/pallas_call | solution.py:359
  168.6 18.7 %collective-permute-done.11.refs_9_ = bf16[1024,1024]{1,0:T(8,128)(2,1)} collective-permute-done((bf16[1024,1024]{1,0:T(8,128)(2,1)}, bf16[1024,1024]{1,0:T(8,128)(2,1)}, u32[]{:S(2)}, u32[]{:S(2)}) %collective-permute-start.11) | collective-permute-done | bytes 2097184 | tf_op jit(solution)/shard_map/ppermute | solution.py:871
  188.3 10.7 %all-to-all-done.1 = bf16[8,112,1024]{2,1,0:T(8,128)(2,1)S(1)} async-done(((bf16[8,112,1024]{2,1,0:T(8,128)(2,1)}), bf16[8,112,1024]{2,1,0:T(8,128)(2,1)S(1)}, u32[]{:S(2)}, u32[]{:S(2)}) %all-to-all-start.1) | async-done | bytes 1835040 | tf_op jit(solution)/shard_map/all_to_all | solution.py:916
  200.2 4.3 all-to-all-start.2
  205.6 59.1 %expert.2 = (bf16[896,1024]{1,0:T(8,128)(2,1)}, bf16[896,4096]{1,0:T(8,128)(2,1)}, bf16[896,4096]{1,0:T(8,128)(2,1)}, bf16[896,1024]{1,0:T(8,128)(2,1)}, bf16[896,1024]{1,0:T(8,128)(2,1)}) custom-call(bf16[896,1024]{1,0:T(8,128)(2,1)} %bitcast.63, bf16[8,2,112,1152]{3,2,1,0:T(8,128)(2,1)} %all-to-all-done.g_ref, ...), custom_call_target="tpu_custom_call" | custom-call | flops 30064771072 | bytes 22020096 | tf_op jit(solution)/shard_map/expert/pallas_call | solution.py:775
  264.7 5.9 all-to-all-start.3
  270.6 47.7 %expert.3 = (bf16[896,1024]{1,0:T(8,128)(2,1)}, bf16[896,4096]{1,0:T(8,128)(2,1)}, bf16[896,4096]{1,0:T(8,128)(2,1)}, bf16[896,1024]{1,0:T(8,128)(2,1)}, bf16[896,1024]{1,0:T(8,128)(2,1)}) custom-call(bf16[896,1024]{1,0:T(8,128)(2,1)} %bitcast.21.x_ref.refs_3_, bf16[8,2,112,1152]{3,2,1,0:T(8,128)(2,1)} %all-to-all-done.g_ref, ...), custom_call_target="tpu_custom_call" | custom-call | flops 30064771072 | bytes 22020096 | tf_op jit(solution)/shard_map/expert/pallas_call | solution.py:775
  318.3 14.6 %weight_grad.5 = (bf16[1024,1024]{1,0:T(8,128)(2,1)}, bf16[1024,1024]{1,0:T(8,128)(2,1)}) custom-call(bf16[896,4096]{1,0:T(8,128)(2,1)} %get-tuple-element.225.refs_0_, bf16[896,1024]{1,0:T(8,128)(2,1)} %get-tuple-element.226.refs_1_, bf16[896,4096]{1,0:T(8,128)(2,1)} %get-tuple-element.227.refs_2_, bf16[896,1024]{1,0:T(8,128)(2,1)} %get-tuple-element.228.refs_3_), custom_call_target="tpu_custom_call" | custom-call | flops 7516192768 | bytes 8388608 | tf_op jit(solution)/shard_map/weight_grad/pallas_call | solution.py:823
  333.4 6.0 all-to-all-start.4
  339.3 14.0 %weight_grad.4 = (bf16[1024,1024]{1,0:T(8,128)(2,1)}, bf16[1024,1024]{1,0:T(8,128)(2,1)}) custom-call(bf16[896,4096]{1,0:T(8,128)(2,1)} %get-tuple-element.225.refs_0_, bf16[896,1024]{1,0:T(8,128)(2,1)} %get-tuple-element.226.refs_1_, bf16[896,4096]{1,0:T(8,128)(2,1)} %get-tuple-element.227.refs_2_, bf16[896,1024]{1,0:T(8,128)(2,1)} %get-tuple-element.228.refs_3_), custom_call_target="tpu_custom_call" | custom-call | flops 7516192768 | bytes 8388608 | tf_op jit(solution)/shard_map/weight_grad/pallas_call | solution.py:823
  353.4 3.2 add_convert_fusion.2
  359.8 2.3 add_convert_fusion.3.refs_4_
  362.1 10.6 %collective-permute-done.20.refs_0_ = bf16[256,1024]{1,0:T(8,128)(2,1)} collective-permute-done((bf16[256,1024]{1,0:T(8,128)(2,1)S(1)}, bf16[256,1024]{1,0:T(8,128)(2,1)}, u32[]{:S(2)}, u32[]{:S(2)}) %collective-permute-start.20) | collective-permute-done | bytes 524320 | tf_op jit(solution)/shard_map/ppermute | solution.py:871
  372.7 9.7 %all-to-all-done.4 = bf16[8,112,1024]{2,1,0:T(8,128)(2,1)} async-done(((bf16[8,112,1024]{2,1,0:T(8,128)(2,1)}), bf16[8,112,1024]{2,1,0:T(8,128)(2,1)}, u32[]{:S(2)}, u32[]{:S(2)}) %all-to-all-start.4) | async-done | bytes 1835040 | tf_op jit(solution)/shard_map/all_to_all | solution.py:916
  382.3 17.5 %unpack_rows.2 = (bf16[544,1152]{1,0:T(8,128)(2,1)}, bf16[544,1152]{1,0:T(8,128)(2,1)}, bf16[544,1152]{1,0:T(8,128)(2,1)}, bf16[544,1152]{1,0:T(8,128)(2,1)}) custom-call(s32[4]{0:T(128)} %get-tuple-element.352.part_ref, s32[2176,2]{1,0:T(8,128)} %copy-done.2, bf16[896,1024]{1,0:T(8,128)(2,1)} %bitcast.67, bf16[896,1024]{1,0:T(8,128)(2,1)} %bitcast.25.refs_1_), custom_call_target="tpu_custom_call" | custom-call | flops 11978932224 | bytes 7340032 | tf_op jit(solution)/shard_map/unpack_rows/pallas_call | solution.py:414
  400.7 3.6 all-to-all-start.5
  405.9 3.5 add_convert_fusion.4.refs_2_
  409.3 8.9 %collective-permute-done.24.refs_2_ = bf16[256,1024]{1,0:T(8,128)(2,1)S(1)} collective-permute-done((bf16[256,1024]{1,0:T(8,128)(2,1)}, bf16[256,1024]{1,0:T(8,128)(2,1)S(1)}, u32[]{:S(2)}, u32[]{:S(2)}) %collective-permute-start.24) | collective-permute-done | bytes 524320 | tf_op jit(solution)/shard_map/ppermute | solution.py:871
  419.0 13.9 %weight_grad.6 = (bf16[1024,1024]{1,0:T(8,128)(2,1)}, bf16[1024,1024]{1,0:T(8,128)(2,1)}) custom-call(bf16[896,4096]{1,0:T(8,128)(2,1)} %get-tuple-element.258.refs_0_, bf16[896,1024]{1,0:T(8,128)(2,1)} %bitcast.64, bf16[896,4096]{1,0:T(8,128)(2,1)} %get-tuple-element.259.refs_2_, bf16[896,1024]{1,0:T(8,128)(2,1)} %bitcast.21.x_ref.refs_3_), custom_call_target="tpu_custom_call" | custom-call | flops 7516192768 | bytes 8388608 | tf_op jit(solution)/shard_map/weight_grad/pallas_call | solution.py:823
  434.9 2.0 add_convert_fusion.5
  440.1 14.0 %weight_grad.7 = (bf16[1024,1024]{1,0:T(8,128)(2,1)}, bf16[1024,1024]{1,0:T(8,128)(2,1)}) custom-call(bf16[896,4096]{1,0:T(8,128)(2,1)} %get-tuple-element.258.refs_0_, bf16[896,1024]{1,0:T(8,128)(2,1)} %bitcast.65, bf16[896,4096]{1,0:T(8,128)(2,1)} %get-tuple-element.259.refs_2_, bf16[896,1024]{1,0:T(8,128)(2,1)} %bitcast.21.x_ref.refs_3_), custom_call_target="tpu_custom_call" | custom-call | flops 7516192768 | bytes 8388608 | tf_op jit(solution)/shard_map/weight_grad/pallas_call | solution.py:823
  454.1 20.4 %collective-permute-done.25.refs_0_ = bf16[272,1152]{1,0:T(8,128)(2,1)} collective-permute-done((bf16[272,1152]{1,0:T(8,128)(2,1)}, bf16[272,1152]{1,0:T(8,128)(2,1)}, u32[]{:S(2)}, u32[]{:S(2)}) %collective-permute-start.25) | collective-permute-done | bytes 626720 | tf_op jit(solution)/shard_map/ppermute | solution.py:871
  474.5 5.2 add_convert_fusion.1.refs_4_
  481.0 6.0 all-to-all-start.6
  487.1 3.2 add_convert_fusion
  491.9 12.4 %middle_back.1 = (f32[544,1024]{1,0:T(8,128)}, f32[128,1024]{1,0:T(8,128)}, f32[1,1024]{1,0:T(1,128)}, bf16[256,1024]{1,0:T(8,128)(2,1)}, bf16[256,1024]{1,0:T(8...) custom-call(s32[1]{0:T(128)} %bitcast.4.at_ref, ...), custom_call_target="tpu_custom_call" | custom-call | flops 4563402752 | bytes 22282240 | tf_op jit(solution)/shard_map/middle_back/pallas_call | solution.py:619
  509.1 5.5 collective-permute-done.31.refs_1_
  514.6 4.3 collective-permute-done.33.refs_3_
  522.0 34.3 %attend_back.1 = (bf16[544,1024]{1,0:T(8,128)(2,1)}, bf16[544,1024]{1,0:T(8,128)(2,1)}, bf16[544,1024]{1,0:T(8,128)(2,1)}, bf16[544,1024]{1,0:T(8,128)(2,1)}, bf...) custom-call(s32[4]{0:T(128)} %get-tuple-element.351.starts_ref, bf16[3,11,208,256]{3,2,1,0:T(8,128)(2,1)} %get-tuple-element.187.qkv_ref, ...), custom_call_target="tpu_custom_call" | custom-call | flops 14394851328 | bytes 46858240 | tf_op jit(solution)/shard_map/attend_back/pallas_call | solution.py:286
  561.7 2.7 add_convert_fusion.9.refs_2_
  567.5 6.4 all-to-all-start.7
  578.6 16.0 %unpack_rows.3 = (bf16[544,1024]{1,0:T(8,128)(2,1)}, bf16[544,1024]{1,0:T(8,128)(2,1)}, bf16[544,1024]{1,0:T(8,128)(2,1)}, bf16[544,1024]{1,0:T(8,128)(2,1)}) custom-call(s32[4]{0:T(128)} %get-tuple-element.352.part_ref, s32[2176,2]{1,0:T(8,128)} %copy-done.2, bf16[896,1024]{1,0:T(8,128)(2,1)} %bitcast.62, bf16[896,1024]{1,0:T(8,128)(2,1)} %bitcast.29.refs_1_), custom_call_target="tpu_custom_call" | custom-call | flops 11978932224 | bytes 7340032 | tf_op jit(solution)/shard_map/unpack_rows/pallas_call | solution.py:414
  594.6 8.7 %collective-permute-done.41.refs_0_ = bf16[272,1024]{1,0:T(8,128)(2,1)S(1)} collective-permute-done((bf16[272,1024]{1,0:T(8,128)(2,1)S(1)}, bf16[272,1024]{1,0:T(8,128)(2,1)S(1)}, u32[]{:S(2)}, u32[]{:S(2)}) %collective-permute-start.41) | collective-permute-done | bytes 557088 | tf_op jit(solution)/shard_map/ppermute | solution.py:871
  607.1 4.6 input_back.1.refs_0_
  612.7 2.0 add_convert_fusion.8
  614.7 6.0 collective-permute-done.45.refs_3_
  620.7 7.6 %all-to-all-done.7 = bf16[8,144,1024]{2,1,0:T(8,128)(2,1)S(1)} async-done(((bf16[8,144,1024]{2,1,0:T(8,128)(2,1)}), bf16[8,144,1024]{2,1,0:T(8,128)(2,1)S(1)}, u32[]{:S(2)}, u32[]{:S(2)}) %all-to-all-start.7) | async-done | bytes 2359328 | tf_op jit(solution)/shard_map/all_to_all | solution.py:916
  629.6 3.1 add_convert_fusion.7
  634.7 5.4 sum_far.2
  640.1 5.5 sum_far.3
  645.6 14.8 %collective-permute-done.47 = bf16[544,1024]{1,0:T(8,128)(2,1)S(1)} collective-permute-done((bf16[544,1024]{1,0:T(8,128)(2,1)}, bf16[544,1024]{1,0:T(8,128)(2,1)S(1)}, u32[]{:S(2)}, u32[]{:S(2)}) %collective-permute-start.47) | collective-permute-done | bytes 1114144 | tf_op jit(solution)/shard_map/ppermute | solution.py:871
  661.4 21.2 %collective-permute-done.46.refs_1_ = bf16[544,1024]{1,0:T(8,128)(2,1)} collective-permute-done((bf16[544,1024]{1,0:T(8,128)(2,1)S(1)}, bf16[544,1024]{1,0:T(8,128)(2,1)}, u32[]{:S(2)}, u32[]{:S(2)}) %collective-permute-start.46) | collective-permute-done | bytes 1114144 | tf_op jit(solution)/shard_map/ppermute | solution.py:871
  682.6 2.5 add_convert_fusion.6.refs_0_
  685.7 24.2 %collective-permute-done.48.refs_1_ = bf16[544,1024]{1,0:T(8,128)(2,1)S(1)} collective-permute-done((bf16[544,1024]{1,0:T(8,128)(2,1)S(1)}, bf16[544,1024]{1,0:T(8,128)(2,1)S(1)}, u32[]{:S(2)}, u32[]{:S(2)}) %collective-permute-start.48) | collective-permute-done | bytes 1114144 | tf_op jit(solution)/shard_map/ppermute | solution.py:871
  711.8 2.6 collective-permute-done.50.refs_3_
  714.4 5.4 assemble.2
  719.9 6.7 assemble.3
  727.9 2.1 slice_convert_fusion
  731.5 2.1 copy.110
  (237 shorter events, 78.1 us)
Async XLA Ops:
  10.3 33.1 %collective-permute-start = (bf16[512,1024]{1,0:T(8,128)(2,1)}, bf16[512,1024]{1,0:T(8,128)(2,1)}, u32[]{:S(2)}, u32[]{:S(2)}) collective-permute-start(bf16[512,1024]{1,0:T(8,128)(2,1)} %get-tuple-element.206.refs_0_), channel_id=1, source_target_pairs={{0,2},{1,3},{2,0},{3,1},{4,6},{5,7},{6,4},{7,5},{8,10},{9,11},{10,... | collective-permute-start | bytes 3145736 | tf_op jit(solution)/shard_map/ppermute | solution.py:871
  43.5 107.3 %all-to-all-start = ((bf16[8,2,112,1152]{3,2,1,0:T(8,128)(2,1)}), bf16[8,2,112,1152]{3,2,1,0:T(8,128)(2,1)}, u32[]{:S(2)}, u32[]{:S(2)}) async-start(bf16[8,2,112,1152]{3,2,1,0:T(8,128)(2,1)} %pack_cotangent.1), calls=%async_computation | async-start | bytes 8257536 | tf_op jit(solution)/shard_map/all_to_all | solution.py:916
  49.9 35.7 %collective-permute-start.1 = (bf16[512,1024]{1,0:T(8,128)(2,1)S(1)}, bf16[512,1024]{1,0:T(8,128)(2,1)}, u32[]{:S(2)}, u32[]{:S(2)}) collective-permute-start(bf16[512,1024]{1,0:T(8,128)(2,1)S(1)} %copy-done.16), channel_id=1, source_target_pairs={{0,2},{1,3},{2,0},{3,1},{4,6},{5,7},{6,4},{7,5},{8,10},{9,11},{10,... | collective-permute-start | bytes 3145736 | tf_op jit(solution)/shard_map/ppermute | solution.py:871
  50.5 41.0 %collective-permute-start.6 = (bf16[256,1024]{1,0:T(8,128)(2,1)S(1)}, bf16[256,1024]{1,0:T(8,128)(2,1)S(1)}, u32[]{:S(2)}, u32[]{:S(2)}) collective-permute-start(bf16[256,1024]{1,0:T(8,128)(2,1)S(1)} %copy-done.19), channel_id=1, source_target_pairs={{0,1},{1,0},{2,3},{3,2},{4,5},{5,4},{6,7},{7,6},{8,9},{9,8},{10,11... | collective-permute-start | bytes 1572872 | tf_op jit(solution)/shard_map/ppermute | solution.py:871
  50.5 35.1 %collective-permute-start.2 = (bf16[256,1024]{1,0:T(8,128)(2,1)S(1)}, bf16[256,1024]{1,0:T(8,128)(2,1)}, u32[]{:S(2)}, u32[]{:S(2)}) collective-permute-start(bf16[256,1024]{1,0:T(8,128)(2,1)S(1)} %copy-done.19), channel_id=1, source_target_pairs={{0,2},{1,3},{2,0},{3,1},{4,6},{5,7},{6,4},{7,5},{8,10},{9,11},{10,... | collective-permute-start | bytes 1572872 | tf_op jit(solution)/shard_map/ppermute | solution.py:871
  85.6 15.0 %collective-permute-start.7 = (bf16[256,1024]{1,0:T(8,128)(2,1)}, bf16[256,1024]{1,0:T(8,128)(2,1)S(1)}, u32[]{:S(2)}, u32[]{:S(2)}) collective-permute-start(bf16[256,1024]{1,0:T(8,128)(2,1)} %collective-permute-done.2.refs_5_.refs_15_), channel_id=1, source_target_pairs={{0,1},{1,0},{2,3},{3,2},{4,5},{5,4},{6,7},{7,6},{8,9},{9,8},{10,11... | collective-permute-start | bytes 1572872 | tf_op jit(solution)/shard_map/ppermute | solution.py:871
  85.6 9.7 %collective-permute-start.3 = (bf16[544,256]{1,0:T(8,128)(2,1)}, bf16[544,256]{1,0:T(8,128)(2,1)S(1)}, u32[]{:S(2)}, u32[]{:S(2)}) collective-permute-start(bf16[544,256]{1,0:T(8,128)(2,1)} %get-tuple-element.182), channel_id=1, source_target_pairs={{0,2},{1,3},{2,0},{3,1},{4,6},{5,7},{6,4},{7,5},{8,10},{9,11},{10,... | collective-permute-start | bytes 835592 | tf_op jit(solution)/shard_map/ppermute | solution.py:871
  86.2 9.1 %collective-permute-start.4 = (bf16[544,256]{1,0:T(8,128)(2,1)}, bf16[544,256]{1,0:T(8,128)(2,1)}, u32[]{:S(2)}, u32[]{:S(2)}) collective-permute-start(bf16[544,256]{1,0:T(8,128)(2,1)} %get-tuple-element.183), channel_id=1, source_target_pairs={{0,1},{1,0},{2,3},{3,2},{4,5},{5,4},{6,7},{7,6},{8,9},{9,8},{10,11... | collective-permute-start | bytes 835592 | tf_op jit(solution)/shard_map/ppermute | solution.py:871
  86.4 14.2 %collective-permute-start.5 = (bf16[544,256]{1,0:T(8,128)(2,1)}, bf16[544,256]{1,0:T(8,128)(2,1)}, u32[]{:S(2)}, u32[]{:S(2)}) collective-permute-start(bf16[544,256]{1,0:T(8,128)(2,1)} %get-tuple-element.184), channel_id=1, source_target_pairs={{0,3},{1,2},{2,1},{3,0},{4,7},{5,6},{6,5},{7,4},{8,11},{9,10},{10,... | collective-permute-start | bytes 835592 | tf_op jit(solution)/shard_map/ppermute | solution.py:871
  108.3 27.2 %collective-permute-start.8 = (bf16[544,1024]{1,0:T(8,128)(2,1)}, bf16[544,1024]{1,0:T(8,128)(2,1)S(1)}, u32[]{:S(2)}, u32[]{:S(2)}) collective-permute-start(bf16[544,1024]{1,0:T(8,128)(2,1)} %get-tuple-element.193.refs_0_.refs_4_), channel_id=1, source_target_pairs={{0,2},{1,3},{2,0},{3,1},{4,6},{5,7},{6,4},{7,5},{8,10},{9,11},{10,... | collective-permute-start | bytes 3342344 | tf_op jit(solution)/shard_map/ppermute | solution.py:871
  108.9 26.7 %collective-permute-start.9 = (bf16[544,1024]{1,0:T(8,128)(2,1)}, bf16[544,1024]{1,0:T(8,128)(2,1)S(1)}, u32[]{:S(2)}, u32[]{:S(2)}) collective-permute-start(bf16[544,1024]{1,0:T(8,128)(2,1)} %get-tuple-element.193.refs_0_.refs_4_), channel_id=1, source_target_pairs={{0,1},{1,0},{2,3},{3,2},{4,5},{5,4},{6,7},{7,6},{8,9},{9,8},{10,11... | collective-permute-start | bytes 3342344 | tf_op jit(solution)/shard_map/ppermute | solution.py:871
  135.5 2.8 collective-permute-start.10
  139.3 48.0 %collective-permute-start.11 = (bf16[1024,1024]{1,0:T(8,128)(2,1)}, bf16[1024,1024]{1,0:T(8,128)(2,1)}, u32[]{:S(2)}, u32[]{:S(2)}) collective-permute-start(bf16[1024,1024]{1,0:T(8,128)(2,1)} %bitcast.85), channel_id=1, source_target_pairs={{0,2},{1,3},{2,0},{3,1},{4,6},{5,7},{6,4},{7,5},{8,10},{9,11},{10,... | collective-permute-start | bytes 6291464 | tf_op jit(solution)/shard_map/ppermute | solution.py:871
  150.8 48.2 %all-to-all-start.1 = ((bf16[8,112,1024]{2,1,0:T(8,128)(2,1)}), bf16[8,112,1024]{2,1,0:T(8,128)(2,1)S(1)}, u32[]{:S(2)}, u32[]{:S(2)}) async-start(bf16[8,112,1024]{2,1,0:T(8,128)(2,1)} %bitcast.70), calls=%async_computation.1 | async-start | bytes 3670016 | tf_op jit(solution)/shard_map/all_to_all | solution.py:916
  156.3 31.5 %collective-permute-start.13 = (bf16[512,1024]{1,0:T(8,128)(2,1)}, bf16[512,1024]{1,0:T(8,128)(2,1)}, u32[]{:S(2)}, u32[]{:S(2)}) collective-permute-start(bf16[512,1024]{1,0:T(8,128)(2,1)} %get-tuple-element.207.refs_1_), channel_id=1, source_target_pairs={{0,1},{1,0},{2,3},{3,2},{4,5},{5,4},{6,7},{7,6},{8,9},{9,8},{10,11... | collective-permute-start | bytes 3145736 | tf_op jit(solution)/shard_map/ppermute | solution.py:871
  156.4 48.2 %collective-permute-start.16 = (bf16[1024,1024]{1,0:T(8,128)(2,1)}, bf16[1024,1024]{1,0:T(8,128)(2,1)}, u32[]{:S(2)}, u32[]{:S(2)}) collective-permute-start(bf16[1024,1024]{1,0:T(8,128)(2,1)} %bitcast.86), channel_id=1, source_target_pairs={{0,1},{1,0},{2,3},{3,2},{4,5},{5,4},{6,7},{7,6},{8,9},{9,8},{10,11... | collective-permute-start | bytes 6291464 | tf_op jit(solution)/shard_map/ppermute | solution.py:871
  187.3 17.3 %collective-permute-start.17 = (bf16[1024,1024]{1,0:T(8,128)(2,1)}, bf16[1024,1024]{1,0:T(8,128)(2,1)}, u32[]{:S(2)}, u32[]{:S(2)}) collective-permute-start(bf16[1024,1024]{1,0:T(8,128)(2,1)} %collective-permute-done.11.refs_9_), channel_id=1, source_target_pairs={{0,1},{1,0},{2,3},{3,2},{4,5},{5,4},{6,7},{7,6},{8,9},{9,8},{10,11... | collective-permute-start | bytes 6291464 | tf_op jit(solution)/shard_map/ppermute | solution.py:871
  187.3 17.3 %collective-permute-start.12 = (bf16[512,1024]{1,0:T(8,128)(2,1)}, bf16[512,1024]{1,0:T(8,128)(2,1)S(1)}, u32[]{:S(2)}, u32[]{:S(2)}) collective-permute-start(bf16[512,1024]{1,0:T(8,128)(2,1)} %get-tuple-element.206.refs_0_), channel_id=1, source_target_pairs={{0,1},{1,0},{2,3},{3,2},{4,5},{5,4},{6,7},{7,6},{8,9},{9,8},{10,11... | collective-permute-start | bytes 3145736 | tf_op jit(solution)/shard_map/ppermute | solution.py:871
  187.8 16.8 %collective-permute-start.14 = (bf16[512,1024]{1,0:T(8,128)(2,1)}, bf16[512,1024]{1,0:T(8,128)(2,1)}, u32[]{:S(2)}, u32[]{:S(2)}) collective-permute-start(bf16[512,1024]{1,0:T(8,128)(2,1)} %collective-permute-done.refs_2_), channel_id=1, source_target_pairs={{0,1},{1,0},{2,3},{3,2},{4,5},{5,4},{6,7},{7,6},{8,9},{9,8},{10,11... | collective-permute-start | bytes 3145736 | tf_op jit(solution)/shard_map/ppermute | solution.py:871
  187.8 16.8 %collective-permute-start.15 = (bf16[512,1024]{1,0:T(8,128)(2,1)}, bf16[512,1024]{1,0:T(8,128)(2,1)}, u32[]{:S(2)}, u32[]{:S(2)}) collective-permute-start(bf16[512,1024]{1,0:T(8,128)(2,1)} %collective-permute-done.1.refs_3_), channel_id=1, source_target_pairs={{0,1},{1,0},{2,3},{3,2},{4,5},{5,4},{6,7},{7,6},{8,9},{9,8},{10,11... | collective-permute-start | bytes 3145736 | tf_op jit(solution)/shard_map/ppermute | solution.py:871
  200.2 64.4 %all-to-all-start.2 = ((bf16[8,112,1024]{2,1,0:T(8,128)(2,1)}), bf16[8,112,1024]{2,1,0:T(8,128)(2,1)}, u32[]{:S(2)}, u32[]{:S(2)}) async-start(bf16[8,112,1024]{2,1,0:T(8,128)(2,1)} %bitcast.69), calls=%async_computation.2 | async-start | bytes 3670016 | tf_op jit(solution)/shard_map/all_to_all | solution.py:916
  264.7 53.6 %all-to-all-start.3 = ((bf16[8,112,1024]{2,1,0:T(8,128)(2,1)}), bf16[8,112,1024]{2,1,0:T(8,128)(2,1)S(1)}, u32[]{:S(2)}, u32[]{:S(2)}) async-start(bf16[8,112,1024]{2,1,0:T(8,128)(2,1)} %bitcast.71), calls=%async_computation.3 | async-start | bytes 3670016 | tf_op jit(solution)/shard_map/all_to_all | solution.py:916
  332.8 20.5 %collective-permute-start.18 = (bf16[1024,1024]{1,0:T(8,128)(2,1)}, bf16[1024,1024]{1,0:T(8,128)(2,1)S(1)}, u32[]{:S(2)}, u32[]{:S(2)}) collective-permute-start(bf16[1024,1024]{1,0:T(8,128)(2,1)} %get-tuple-element.230), channel_id=1, source_target_pairs={{0,1},{1,0},{2,3},{3,2},{4,5},{5,4},{6,7},{7,6},{8,9},{9,8},{10,11... | collective-permute-start | bytes 6291464 | tf_op jit(solution)/shard_map/ppermute | solution.py:871
  332.9 20.5 %collective-permute-start.19 = (bf16[1024,1024]{1,0:T(8,128)(2,1)}, bf16[1024,1024]{1,0:T(8,128)(2,1)}, u32[]{:S(2)}, u32[]{:S(2)}) collective-permute-start(bf16[1024,1024]{1,0:T(8,128)(2,1)} %get-tuple-element.231), channel_id=1, source_target_pairs={{0,1},{1,0},{2,3},{3,2},{4,5},{5,4},{6,7},{7,6},{8,9},{9,8},{10,11... | collective-permute-start | bytes 6291464 | tf_op jit(solution)/shard_map/ppermute | solution.py:871
  333.4 49.0 %all-to-all-start.4 = ((bf16[8,112,1024]{2,1,0:T(8,128)(2,1)}), bf16[8,112,1024]{2,1,0:T(8,128)(2,1)}, u32[]{:S(2)}, u32[]{:S(2)}) async-start(bf16[8,112,1024]{2,1,0:T(8,128)(2,1)} %bitcast.68), calls=%async_computation.4 | async-start | bytes 3670016 | tf_op jit(solution)/shard_map/all_to_all | solution.py:916
  357.7 14.9 %collective-permute-start.20 = (bf16[256,1024]{1,0:T(8,128)(2,1)S(1)}, bf16[256,1024]{1,0:T(8,128)(2,1)}, u32[]{:S(2)}, u32[]{:S(2)}) collective-permute-start(bf16[256,1024]{1,0:T(8,128)(2,1)S(1)} %get-tuple-element.358), channel_id=1, source_target_pairs={{0,2},{1,3},{2,0},{3,1},{4,6},{5,7},{6,4},{7,5},{8,10},{9,11},{10,... | collective-permute-start | bytes 1572872 | tf_op jit(solution)/shard_map/ppermute | solution.py:871
  359.2 40.6 %collective-permute-start.21 = (bf16[256,1024]{1,0:T(8,128)(2,1)S(1)}, bf16[256,1024]{1,0:T(8,128)(2,1)S(1)}, u32[]{:S(2)}, u32[]{:S(2)}) collective-permute-start(bf16[256,1024]{1,0:T(8,128)(2,1)S(1)} %get-tuple-element.357), channel_id=1, source_target_pairs={{0,2},{1,3},{2,0},{3,1},{4,6},{5,7},{6,4},{7,5},{8,10},{9,11},{10,... | collective-permute-start | bytes 1572872 | tf_op jit(solution)/shard_map/ppermute | solution.py:871
  399.8 6.0 collective-permute-start.22
  399.9 5.9 collective-permute-start.23
  400.7 79.1 %all-to-all-start.5 = ((bf16[8,112,1024]{2,1,0:T(8,128)(2,1)}), bf16[8,112,1024]{2,1,0:T(8,128)(2,1)S(1)}, u32[]{:S(2)}, u32[]{:S(2)}) async-start(bf16[8,112,1024]{2,1,0:T(8,128)(2,1)} %bitcast.66), calls=%async_computation.5 | async-start | bytes 3670016 | tf_op jit(solution)/shard_map/all_to_all | solution.py:916
  404.3 13.9 %collective-permute-start.24 = (bf16[256,1024]{1,0:T(8,128)(2,1)}, bf16[256,1024]{1,0:T(8,128)(2,1)S(1)}, u32[]{:S(2)}, u32[]{:S(2)}) collective-permute-start(bf16[256,1024]{1,0:T(8,128)(2,1)} %get-tuple-element.356), channel_id=1, source_target_pairs={{0,2},{1,3},{2,0},{3,1},{4,6},{5,7},{6,4},{7,5},{8,10},{9,11},{10,... | collective-permute-start | bytes 1572872 | tf_op jit(solution)/shard_map/ppermute | solution.py:871
  432.9 41.6 %collective-permute-start.28 = (bf16[1024,1024]{1,0:T(8,128)(2,1)}, bf16[1024,1024]{1,0:T(8,128)(2,1)}, u32[]{:S(2)}, u32[]{:S(2)}) collective-permute-start(bf16[1024,1024]{1,0:T(8,128)(2,1)} %get-tuple-element.255), channel_id=1, source_target_pairs={{0,1},{1,0},{2,3},{3,2},{4,5},{5,4},{6,7},{7,6},{8,9},{9,8},{10,11... | collective-permute-start | bytes 6291464 | tf_op jit(solution)/shard_map/ppermute | solution.py:871
  432.9 41.6 %collective-permute-start.29 = (bf16[1024,1024]{1,0:T(8,128)(2,1)}, bf16[1024,1024]{1,0:T(8,128)(2,1)S(1)}, u32[]{:S(2)}, u32[]{:S(2)}) collective-permute-start(bf16[1024,1024]{1,0:T(8,128)(2,1)} %get-tuple-element.256), channel_id=1, source_target_pairs={{0,1},{1,0},{2,3},{3,2},{4,5},{5,4},{6,7},{7,6},{8,9},{9,8},{10,11... | collective-permute-start | bytes 6291464 | tf_op jit(solution)/shard_map/ppermute | solution.py:871
  433.4 20.6 %collective-permute-start.26 = (bf16[256,1024]{1,0:T(8,128)(2,1)}, bf16[256,1024]{1,0:T(8,128)(2,1)}, u32[]{:S(2)}, u32[]{:S(2)}) collective-permute-start(bf16[256,1024]{1,0:T(8,128)(2,1)} %get-tuple-element.355), channel_id=1, source_target_pairs={{0,2},{1,3},{2,0},{3,1},{4,6},{5,7},{6,4},{7,5},{8,10},{9,11},{10,... | collective-permute-start | bytes 1572872 | tf_op jit(solution)/shard_map/ppermute | solution.py:871
  438.0 41.7 %collective-permute-start.27 = (bf16[272,1152]{1,0:T(8,128)(2,1)}, bf16[272,1152]{1,0:T(8,128)(2,1)}, u32[]{:S(2)}, u32[]{:S(2)}) collective-permute-start(bf16[272,1152]{1,0:T(8,128)(2,1)} %get-tuple-element.361), channel_id=1, source_target_pairs={{0,2},{1,3},{2,0},{3,1},{4,6},{5,7},{6,4},{7,5},{8,10},{9,11},{10,... | collective-permute-start | bytes 1880072 | tf_op jit(solution)/shard_map/ppermute | solution.py:871
  438.6 35.9 %collective-permute-start.25 = (bf16[272,1152]{1,0:T(8,128)(2,1)}, bf16[272,1152]{1,0:T(8,128)(2,1)}, u32[]{:S(2)}, u32[]{:S(2)}) collective-permute-start(bf16[272,1152]{1,0:T(8,128)(2,1)} %get-tuple-element.362), channel_id=1, source_target_pairs={{0,2},{1,3},{2,0},{3,1},{4,6},{5,7},{6,4},{7,5},{8,10},{9,11},{10,... | collective-permute-start | bytes 1880072 | tf_op jit(solution)/shard_map/ppermute | solution.py:871
  481.0 75.2 %all-to-all-start.6 = ((bf16[8,112,1024]{2,1,0:T(8,128)(2,1)}), bf16[8,112,1024]{2,1,0:T(8,128)(2,1)}, u32[]{:S(2)}, u32[]{:S(2)}) async-start(bf16[8,112,1024]{2,1,0:T(8,128)(2,1)} %bitcast.28), calls=%async_computation.6 | async-start | bytes 3670016 | tf_op jit(solution)/shard_map/all_to_all | solution.py:916
  490.3 14.5 %collective-permute-start.30 = (bf16[256,1024]{1,0:T(8,128)(2,1)S(1)}, bf16[256,1024]{1,0:T(8,128)(2,1)S(1)}, u32[]{:S(2)}, u32[]{:S(2)}) collective-permute-start(bf16[256,1024]{1,0:T(8,128)(2,1)S(1)} %slice.114), channel_id=1, source_target_pairs={{0,2},{1,3},{2,0},{3,1},{4,6},{5,7},{6,4},{7,5},{8,10},{9,11},{10,... | collective-permute-start | bytes 1572872 | tf_op jit(solution)/shard_map/ppermute | solution.py:871
  504.3 2.7 collective-permute-start.36
  504.3 2.9 collective-permute-start.37
  504.9 9.7 %collective-permute-start.31 = (bf16[544,256]{1,0:T(8,128)(2,1)}, bf16[544,256]{1,0:T(8,128)(2,1)S(1)}, u32[]{:S(2)}, u32[]{:S(2)}) collective-permute-start(bf16[544,256]{1,0:T(8,128)(2,1)} %get-tuple-element.277), channel_id=1, source_target_pairs={{0,2},{1,3},{2,0},{3,1},{4,6},{5,7},{6,4},{7,5},{8,10},{9,11},{10,... | collective-permute-start | bytes 835592 | tf_op jit(solution)/shard_map/ppermute | solution.py:871
  505.4 9.2 %collective-permute-start.32 = (bf16[544,256]{1,0:T(8,128)(2,1)}, bf16[544,256]{1,0:T(8,128)(2,1)}, u32[]{:S(2)}, u32[]{:S(2)}) collective-permute-start(bf16[544,256]{1,0:T(8,128)(2,1)} %get-tuple-element.278), channel_id=1, source_target_pairs={{0,1},{1,0},{2,3},{3,2},{4,5},{5,4},{6,7},{7,6},{8,9},{9,8},{10,11... | collective-permute-start | bytes 835592 | tf_op jit(solution)/shard_map/ppermute | solution.py:871
  505.4 13.5 %collective-permute-start.33 = (bf16[544,256]{1,0:T(8,128)(2,1)}, bf16[544,256]{1,0:T(8,128)(2,1)}, u32[]{:S(2)}, u32[]{:S(2)}) collective-permute-start(bf16[544,256]{1,0:T(8,128)(2,1)} %get-tuple-element.279), channel_id=1, source_target_pairs={{0,3},{1,2},{2,1},{3,0},{4,7},{5,6},{6,5},{7,4},{8,11},{9,10},{10,... | collective-permute-start | bytes 835592 | tf_op jit(solution)/shard_map/ppermute | solution.py:871
  508.4 47.8 %collective-permute-start.38 = (bf16[256,1024]{1,0:T(8,128)(2,1)S(1)}, bf16[256,1024]{1,0:T(8,128)(2,1)}, u32[]{:S(2)}, u32[]{:S(2)}) collective-permute-start(bf16[256,1024]{1,0:T(8,128)(2,1)S(1)} %add_convert_fusion.13), channel_id=1, source_target_pairs={{0,2},{1,3},{2,0},{3,1},{4,6},{5,7},{6,4},{7,5},{8,10},{9,11},{10,... | collective-permute-start | bytes 1572872 | tf_op jit(solution)/shard_map/ppermute | solution.py:871
  519.9 36.3 %collective-permute-start.35 = (bf16[256,1024]{1,0:T(8,128)(2,1)}, bf16[256,1024]{1,0:T(8,128)(2,1)S(1)}, u32[]{:S(2)}, u32[]{:S(2)}) collective-permute-start(bf16[256,1024]{1,0:T(8,128)(2,1)} %get-tuple-element.353), channel_id=1, source_target_pairs={{0,2},{1,3},{2,0},{3,1},{4,6},{5,7},{6,4},{7,5},{8,10},{9,11},{10,... | collective-permute-start | bytes 1572872 | tf_op jit(solution)/shard_map/ppermute | solution.py:871
  521.2 35.0 %collective-permute-start.34 = (bf16[256,1024]{1,0:T(8,128)(2,1)}, bf16[256,1024]{1,0:T(8,128)(2,1)S(1)}, u32[]{:S(2)}, u32[]{:S(2)}) collective-permute-start(bf16[256,1024]{1,0:T(8,128)(2,1)} %get-tuple-element.354), channel_id=1, source_target_pairs={{0,2},{1,3},{2,0},{3,1},{4,6},{5,7},{6,4},{7,5},{8,10},{9,11},{10,... | collective-permute-start | bytes 1572872 | tf_op jit(solution)/shard_map/ppermute | solution.py:871
  556.3 4.5 collective-permute-start.39
  557.4 4.3 collective-permute-start.40
  567.5 60.8 %all-to-all-start.7 = ((bf16[8,144,1024]{2,1,0:T(8,128)(2,1)}), bf16[8,144,1024]{2,1,0:T(8,128)(2,1)S(1)}, u32[]{:S(2)}, u32[]{:S(2)}) async-start(bf16[8,144,1024]{2,1,0:T(8,128)(2,1)} %bitcast.54), calls=%async_computation.7 | async-start | bytes 4718592 | tf_op jit(solution)/shard_map/all_to_all | solution.py:916
  574.0 136.5 %all-gather.2.cloned.1.call-start = ((), (), s32[]{:S(2)}) async-start(), calls=%async_computation.8 | async-start | bytes 2654208 | tf_op jit(solution)/shard_map/all_gather | solution.py:1081
  576.6 18.0 %collective-permute-start.42 = (bf16[272,1024]{1,0:T(8,128)(2,1)}, bf16[272,1024]{1,0:T(8,128)(2,1)S(1)}, u32[]{:S(2)}, u32[]{:S(2)}) collective-permute-start(bf16[272,1024]{1,0:T(8,128)(2,1)} %get-tuple-element.363), channel_id=1, source_target_pairs={{0,2},{1,3},{2,0},{3,1},{4,6},{5,7},{6,4},{7,5},{8,10},{9,11},{10,... | collective-permute-start | bytes 1671176 | tf_op jit(solution)/shard_map/ppermute | solution.py:871
  577.1 26.2 %collective-permute-start.41 = (bf16[272,1024]{1,0:T(8,128)(2,1)S(1)}, bf16[272,1024]{1,0:T(8,128)(2,1)S(1)}, u32[]{:S(2)}, u32[]{:S(2)}) collective-permute-start(bf16[272,1024]{1,0:T(8,128)(2,1)S(1)} %get-tuple-element.364), channel_id=1, source_target_pairs={{0,2},{1,3},{2,0},{3,1},{4,6},{5,7},{6,4},{7,5},{8,10},{9,11},{10,... | collective-permute-start | bytes 1671176 | tf_op jit(solution)/shard_map/ppermute | solution.py:871
  604.2 7.5 %collective-permute-start.43 = (bf16[544,1024]{1,0:T(8,128)(2,1)}, bf16[544,1024]{1,0:T(8,128)(2,1)S(1)}, u32[]{:S(2)}, u32[]{:S(2)}) collective-permute-start(bf16[544,1024]{1,0:T(8,128)(2,1)} %get-tuple-element.312), channel_id=1, source_target_pairs={{0,1},{1,0},{2,3},{3,2},{4,5},{5,4},{6,7},{7,6},{8,9},{9,8},{10,11... | collective-permute-start | bytes 3342344 | tf_op jit(solution)/shard_map/ppermute | solution.py:871
  604.2 8.5 %collective-permute-start.44 = (bf16[544,1024]{1,0:T(8,128)(2,1)}, bf16[544,1024]{1,0:T(8,128)(2,1)}, u32[]{:S(2)}, u32[]{:S(2)}) collective-permute-start(bf16[544,1024]{1,0:T(8,128)(2,1)} %get-tuple-element.313), channel_id=1, source_target_pairs={{0,1},{1,0},{2,3},{3,2},{4,5},{5,4},{6,7},{7,6},{8,9},{9,8},{10,11... | collective-permute-start | bytes 3342344 | tf_op jit(solution)/shard_map/ppermute | solution.py:871
  606.6 14.1 %collective-permute-start.45 = (bf16[256,1024]{1,0:T(8,128)(2,1)}, bf16[256,1024]{1,0:T(8,128)(2,1)}, u32[]{:S(2)}, u32[]{:S(2)}) collective-permute-start(bf16[256,1024]{1,0:T(8,128)(2,1)} %slice.119), channel_id=1, source_target_pairs={{0,2},{1,3},{2,0},{3,1},{4,6},{5,7},{6,4},{7,5},{8,10},{9,11},{10,... | collective-permute-start | bytes 1572872 | tf_op jit(solution)/shard_map/ppermute | solution.py:871
  632.7 27.7 %collective-permute-start.47 = (bf16[544,1024]{1,0:T(8,128)(2,1)}, bf16[544,1024]{1,0:T(8,128)(2,1)S(1)}, u32[]{:S(2)}, u32[]{:S(2)}) collective-permute-start(bf16[544,1024]{1,0:T(8,128)(2,1)} %add_convert_fusion.7), channel_id=1, source_target_pairs={{0,2},{1,3},{2,0},{3,1},{4,6},{5,7},{6,4},{7,5},{8,10},{9,11},{10,... | collective-permute-start | bytes 3342344 | tf_op jit(solution)/shard_map/ppermute | solution.py:871
  633.2 49.4 %collective-permute-start.46 = (bf16[544,1024]{1,0:T(8,128)(2,1)S(1)}, bf16[544,1024]{1,0:T(8,128)(2,1)}, u32[]{:S(2)}, u32[]{:S(2)}) collective-permute-start(bf16[544,1024]{1,0:T(8,128)(2,1)S(1)} %copy-done.3), channel_id=1, source_target_pairs={{0,2},{1,3},{2,0},{3,1},{4,6},{5,7},{6,4},{7,5},{8,10},{9,11},{10,... | collective-permute-start | bytes 3342344 | tf_op jit(solution)/shard_map/ppermute | solution.py:871
  685.1 24.8 %collective-permute-start.48 = (bf16[544,1024]{1,0:T(8,128)(2,1)S(1)}, bf16[544,1024]{1,0:T(8,128)(2,1)S(1)}, u32[]{:S(2)}, u32[]{:S(2)}) collective-permute-start(bf16[544,1024]{1,0:T(8,128)(2,1)S(1)} %add_convert_fusion.6.refs_0_), channel_id=1, source_target_pairs={{0,2},{1,3},{2,0},{3,1},{4,6},{5,7},{6,4},{7,5},{8,10},{9,11},{10,... | collective-permute-start | bytes 3342344 | tf_op jit(solution)/shard_map/ppermute | solution.py:871
  685.7 26.0 %collective-permute-start.49 = (bf16[544,1024]{1,0:T(8,128)(2,1)S(1)}, bf16[544,1024]{1,0:T(8,128)(2,1)}, u32[]{:S(2)}, u32[]{:S(2)}) collective-permute-start(bf16[544,1024]{1,0:T(8,128)(2,1)S(1)} %add_convert_fusion.6.refs_0_), channel_id=1, source_target_pairs={{0,1},{1,0},{2,3},{3,2},{4,5},{5,4},{6,7},{7,6},{8,9},{9,8},{10,11... | collective-permute-start | bytes 3342344 | tf_op jit(solution)/shard_map/ppermute | solution.py:871
  710.0 4.4 collective-permute-start.50
  710.0 9.9 %collective-permute-start.52 = (bf16[544,1024]{1,0:T(8,128)(2,1)}, bf16[544,1024]{1,0:T(8,128)(2,1)}, u32[]{:S(2)}, u32[]{:S(2)}) collective-permute-start(bf16[544,1024]{1,0:T(8,128)(2,1)} %collective-permute-done.46.refs_1_), channel_id=1, source_target_pairs={{0,1},{1,0},{2,3},{3,2},{4,5},{5,4},{6,7},{7,6},{8,9},{9,8},{10,11... | collective-permute-start | bytes 3342344 | tf_op jit(solution)/shard_map/ppermute | solution.py:871
  710.5 9.4 %collective-permute-start.51 = (bf16[544,1024]{1,0:T(8,128)(2,1)S(1)}, bf16[544,1024]{1,0:T(8,128)(2,1)}, u32[]{:S(2)}, u32[]{:S(2)}) collective-permute-start(bf16[544,1024]{1,0:T(8,128)(2,1)S(1)} %copy-done.3), channel_id=1, source_target_pairs={{0,1},{1,0},{2,3},{3,2},{4,5},{5,4},{6,7},{7,6},{8,9},{9,8},{10,11... | collective-permute-start | bytes 3342344 | tf_op jit(solution)/shard_map/ppermute | solution.py:871
  711.2 15.3 %collective-permute-start.53 = (f32[10,1024]{1,0:T(8,128)S(1)}, f32[10,1024]{1,0:T(8,128)S(1)}, u32[]{:S(2)}, u32[]{:S(2)}) collective-permute-start(f32[10,1024]{1,0:T(8,128)S(1)} %slice_convert_fusion.1), channel_id=1, source_target_pairs={{0,1},{1,0},{2,3},{3,2},{4,5},{5,4},{6,7},{7,6},{8,9},{9,8},{10,11... | collective-permute-start | bytes 122888 | tf_op jit(solution)/shard_map/ppermute | solution.py:871
  727.3 6.3 collective-permute-start.54
  (40 other events, 395.4 us)
Sparse Core Ops, SparseCore 0:
  629.7 50.1 all-gather.1

commit v8 on v7

--- a/solution.py
+++ b/solution.py
@@ -963,7 +963,7 @@
     middle, second_in, gates = middle_of(
         own_block, mixed, head_out_all, block_in, gain_two, router_wide, expert_ids, route_noise
     )
-    *second_all, late_out = pinned(*gathered(second_in), expert_out[0])
+    *second_all, signal, late_out = pinned(*gathered(second_in), signal, expert_out[0])
     w1 = [gathered_from(a, b) for a, b in zip(w1_own, w1_far)]
     w1 = [w1[h][p] for p in range(parts) for h in range(2)]
 
@@ -974,9 +974,7 @@
         return over_experts(x.reshape(experts, slots, width)).reshape(chunk_rows, width)
 
     x = sent(packed_rows(0))
-    w2_far, head_in_t, signal, *outgoing = pinned(
-        far_part(late_out), jnp.swapaxes(head_in, 1, 2), signal, *[packed_rows(n) for n in range(1, CHUNKS)]
-    )
+    w2_far, *outgoing = pinned(far_part(late_out), *[packed_rows(n) for n in range(1, CHUNKS)])
     w2 = gathered_from(expert_out[0], w2_far)
     backs, actives, hidden_grads, rows_grads, arrived, returned = [], [], [], [], [], []
     for n in range(CHUNKS):
@@ -1010,16 +1008,14 @@
     quarter = here // 4
     tile = half_tile(each)
     tiles = each // tile
-    out_far = [far_tile(out_kept, out_other, n, quarter) for n in range(2)]
-    *returned, out_kept, out_far[0] = pinned(*returned, out_kept, out_far[0])
+    out_far = [far_tile(out_kept, out_other, n, here // 2) for n in range(2)]
+    *returned, out_kept = pinned(*returned, out_kept)
 
     second_pieces = unpack(part_of, place, returned, slots, per, each, True)
-    *second_pieces, out_far[1] = pinned(*second_pieces, out_far[1])
-    out_far += [far_tile(out_kept, out_other, n, quarter) for n in range(2, 4)]
     second_kept, second_other = near_sum(second_pieces, near_hop(second_pieces))
-    second_kept, out_far[2] = pinned(second_kept, out_far[2])
-    second_other = after(second_other, second_kept)
-    *hidden_grads, second_kept = pinned(*hidden_grads, second_kept)
+    second_kept, out_far[0] = pinned(second_kept, out_far[0])
+    if paired:
+        second_other, second_kept, *hidden_grads = pinned(second_other, second_kept, *hidden_grads)
     second_far = [far_tile(second_kept, second_other, n, tile) for n in range(tiles)]
     in_parts = []
     for p in range(parts - 2, -1, -2):
@@ -1027,7 +1023,7 @@
         in_parts = list(pair) + in_parts
         if p == parts - 2:
             in_came = near_hop([None] * p + list(pair)) if paired else ()
-            second_far[0], out_far[3], pair = pinned(second_far[0], out_far[3], pair)
+            second_far[0], out_far[1], pair = pinned(second_far[0], out_far[1], pair)
     in_kept, in_other = near_sum(in_parts, in_came)
     second_far[-1], in_kept = pinned(second_far[-1], in_kept)
     in_other = after(in_other, in_kept)
@@ -1044,37 +1040,39 @@
     in_other = after(in_other, *mixed_grad)
     in_far += [far_tile(in_kept, in_other, n, quarter) for n in (1, 2)]
     *pieces, head_in_part, norm_one_part = attend_back(
-        starts, mixed_grad, qkv, logs, first_in, head_in_t, gain_one
+        starts, mixed_grad, qkv, logs, first_in, jnp.swapaxes(head_in, 1, 2), gain_one
     )
     *pieces, combined[-1], in_far[1], in_far[2], head_out_far = pinned(
         *pieces, combined[-1], in_far[1], in_far[2], head_out_far
     )
     first_kept, first_other = near_sum(pieces, near_hop(pieces))
-    first_kept, head_in_part, head_out_far, *combined = pinned(first_kept, head_in_part, head_out_far, *combined)
-    first_other = after(first_other, first_kept)
+    if paired:
+        first_other, first_kept, head_in_part, head_out_far, *combined = pinned(
+            first_other, first_kept, head_in_part, head_out_far, *combined
+        )
     first_far = [far_tile(first_kept, first_other, n, tile) for n in range(tiles)]
     block_pieces = unpack(part_of, place, combined, slots, per, each, False)
-    first_far, block_pieces = pinned(first_far, block_pieces)
+    first_far[0], block_pieces = pinned(first_far[0], block_pieces)
     in_far.append(far_tile(in_kept, after(in_other, block_pieces[0]), 3, quarter))
     block_kept, block_other = near_sum(block_pieces, near_hop(block_pieces))
     input_part = input_back(own_block, first_kept, first_far, block_in, middle_grad, gain_one)
-    input_part, block_kept, in_far[3] = pinned(input_part, block_kept, in_far[3])
-    block_far = far_hop(block_kept, after(block_other, block_kept))
-    out_grad = sum_far(out_kept, out_far, False)
-    in_grad = sum_far(in_kept, in_far, True)
-    input_far, out_grad, in_grad, block_far = pinned(far_part(input_part), out_grad, in_grad, block_far)
-    block_own = (middle + block_kept.astype(F32) + block_far.astype(F32)).astype(BF)
-
-    cols = head_in.shape[2]
+    block_far = far_hop(block_kept, block_other)
     head_out_part = (head_out_kept.astype(F32) + head_out_far.astype(F32)).astype(BF)
     small = jnp.concatenate([norm_one_part, norm_two_part, router_part[:experts]], 0).astype(BF)
+    cols = head_in.shape[2]
     count = 4 * cols + 2 + experts
     total = up_to(count, 16 * groups)
     heads = jnp.concatenate(
         [head_in_part.reshape(3 * cols, width), head_out_part, jnp.pad(small, ((0, total - count), (0, 0)))], 0
     )
     heads = over_experts(heads.reshape(groups, total // groups, width))
-    heads, input_part = pinned(heads, input_part)
+    input_far = far_part(input_part)
+    heads, out_kept = pinned(heads, out_kept)
+    out_grad = sum_far(out_kept, out_far, False)
+    in_grad = sum_far(in_kept, in_far, True)
+    input_far, out_grad, in_grad, block_far = pinned(input_far, out_grad, in_grad, block_far)
+    block_own = (middle + block_kept.astype(F32) + block_far.astype(F32)).astype(BF)
+
     input_grad = assemble(part_of, gathered_from(input_part, input_far), rows_here, F32)
     block_out = assemble(part_of, gathered(block_own), rows_here, BF)
     heads = jnp.sum(heads.astype(F32), 0).astype(BF)

time: 749 us -> 765 us (1.021)
  waiting for transfers between devices: 217 us -> 259 us
  Pallas kernels: 345 us -> 332 us
    all_to_all x8, waiting for transfers between devices: 28 us -> 56.3 us  [over_experts(): return lax.all_to_all(x, 'expert', split_axis=0, concat_axis=0, tiled=True)]
    ppermute x55 -> x53, waiting for transfers between devices: 189 us -> 202 us  [cross(): return lax.ppermute(x, 'tensor', [(n, n ^ k) for n in range(parts)])]
    pallas_call x2, Pallas kernels: 107 us -> 95.2 us  [expert(): pl.pallas_call(functools.partial(expert_kernel, count, slots, per), grid=...]
    convert_element_type x11 -> x10, other arithmetic: 30.1 us -> 26.1 us  [near_sum(): (a.astype(F32) + b.astype(F32)).astype(BF)]
    ppermute x55 -> x53, starting transfers between devices: 34 us -> 32.4 us  [cross(): return lax.ppermute(x, 'tensor', [(n, n ^ k) for n in range(parts)])]
  transfers between devices with their start and end apart: 64 -> 62, of which waited for: 23 -> 19; matrix products, arithmetic and copies ran while one was open for 9% -> 8% of each run, Pallas kernels for 45% -> 42%
where the time goes in v8:
time: 765 us; the launch traced here: 758 us
  Pallas kernels  332 us (43%)
  waiting for transfers between devices  259 us (34%)
  starting transfers between devices  75 us (10%)
  other arithmetic  44 us (6%)
  local copies, waits for them, and re-layouts  33.4 us (4%)
  between operations  15 us (2%)
    ppermute x53, waiting for transfers between devices, cross(): return lax.ppermute(x, 'tensor', [(n, n ^ k) for n in range(parts)])  202 us
    pallas_call x2, Pallas kernels, expert(): pl.pallas_call(functools.partial(expert_kernel, count, slots, per), grid=...  95.2 us
    all_to_all x8, waiting for transfers between devices, over_experts(): return lax.all_to_all(x, 'expert', split_axis=0, concat_axis=0, tiled=True)  56.3 us
    pallas_call x4, Pallas kernels, weight_grad(): pl.pallas_call(functools.partial(weight_kernel, count, steps), grid=(2 *...  55.9 us
    all_to_all x8, starting transfers between devices, over_experts(): return lax.all_to_all(x, 'expert', split_axis=0, concat_axis=0, tiled=True)  42.6 us
    pallas_call x1, Pallas kernels, attend_back(): pl.pallas_call(functools.partial(attend_back_kernel, count), grid_spec=sp...  34.3 us
    pallas_call x2, Pallas kernels, unpack(): pl.pallas_call(functools.partial(unpack_kernel, count, slots, per, graded...  33.6 us
    ppermute x53, starting transfers between devices, cross(): return lax.ppermute(x, 'tensor', [(n, n ^ k) for n in range(parts)])  32.4 us
  transfers between devices with their start and end apart: 62, of which 19 were waited for; matrix products, arithmetic and copies ran while one was open for 8% of the time, Pallas kernels for 42%

profile of v8, /device:TPU:0, one launch (start us, length us, event | category | flops | bytes accessed | tf_op | source)
XLA Modules:
  0.0 758.2 jit_solution(14902549815586299816)
XLA Ops:
  7.2 3.1 slice_bitcast_fusion
  10.3 2.9 collective-permute-start
  13.3 2.3 reduce-window.6
  23.3 17.3 %pack_cotangent.1 = bf16[8,2,112,1152]{3,2,1,0:T(8,128)(2,1)} custom-call(bf16[2167,1024]{1,0:T(8,128)(2,1)} %refs_7_.1, bf16[16,1024]{1,0:T(8,128)(2,1)} %pad.26.tail_ref, s32[2,2176]{1,0:T(2,128)} %copy.103.lp_ref, bf16[2,2176,128]{2,1,0:T(8,128)(2,1)} %fusion.5.side_ref), custom_call_target="tpu_custom_call" | custom-call | flops 11978932224 | bytes 4438016 | tf_op jit(solution)/shard_map/pack_cotangent/pallas_call | solution.py:323
  40.7 6.2 all-to-all-start
  50.3 30.3 %attend.1 = (bf16[11,208,1024]{2,1,0:T(8,128)(2,1)}, bf16[3,11,208,256]{3,2,1,0:T(8,128)(2,1)}, f32[11,208,128]{2,1,0:T(8,128)}, bf16[544,256]{1,0:T(8,128)(2,1)...) custom-call(s32[4]{0:T(128)} %get-tuple-element.327.starts_ref, ...), custom_call_target="tpu_custom_call" | custom-call | flops 9596567552 | bytes 35504128 | tf_op jit(solution)/shard_map/attend/pallas_call | solution.py:180
  80.6 1.9 collective-permute-done.2.refs_5_.refs_15_
  88.5 3.8 collective-permute-done.3.refs_1_.refs_11_
  92.3 5.1 collective-permute-done.5.refs_3_.refs_13_
  98.2 6.8 middle.1
  106.0 26.4 %collective-permute-done.8.refs_1_ = bf16[544,1024]{1,0:T(8,128)(2,1)S(1)} collective-permute-done((bf16[544,1024]{1,0:T(8,128)(2,1)}, bf16[544,1024]{1,0:T(8,128)(2,1)S(1)}, u32[]{:S(2)}, u32[]{:S(2)}) %collective-permute-start.8) | collective-permute-done | bytes 1114144 | tf_op jit(solution)/shard_map/ppermute | solution.py:871
  132.4 2.9 collective-permute-done.10.refs_3_
  135.3 3.1 all-to-all-done.g_ref
  140.0 9.9 %pack_rows.2 = bf16[896,1024]{1,0:T(8,128)(2,1)} custom-call(s32[4]{0:T(128)} %get-tuple-element.328.part_ref, bf16[544,1024]{1,0:T(8,128)(2,1)} %get-tuple-element.180.refs_0_.refs_4_, bf16[544,1024]{1,0:T(8,128)(2,1)} %copy-done.35, bf16[544,1024]{1,0:T(8,128)(2,1)} %copy-done.36, bf16[544,1024]{1,0:T(8,128)(2,1)} %collective-permute-done.10.refs_3_, ...), custom_call_target="tpu_custom_call" | custom-call | flops 5989466112 | bytes 4456448 | tf_op jit(solution)/shard_map/pack_rows/pallas_call | solution.py:359
  149.9 3.7 all-to-all-start.1
  154.1 9.9 %pack_rows.3 = bf16[896,1024]{1,0:T(8,128)(2,1)} custom-call(s32[4]{0:T(128)} %get-tuple-element.328.part_ref, bf16[544,1024]{1,0:T(8,128)(2,1)} %get-tuple-element.180.refs_0_.refs_4_, bf16[544,1024]{1,0:T(8,128)(2,1)} %copy-done.35, bf16[544,1024]{1,0:T(8,128)(2,1)} %copy-done.36, bf16[544,1024]{1,0:T(8,128)(2,1)} %collective-permute-done.10.refs_3_, ...), custom_call_target="tpu_custom_call" | custom-call | flops 5989466112 | bytes 4456448 | tf_op jit(solution)/shard_map/pack_rows/pallas_call | solution.py:359
  164.1 20.6 %collective-permute-done.11.refs_9_ = bf16[1024,1024]{1,0:T(8,128)(2,1)} collective-permute-done((bf16[1024,1024]{1,0:T(8,128)(2,1)}, bf16[1024,1024]{1,0:T(8,128)(2,1)}, u32[]{:S(2)}, u32[]{:S(2)}) %collective-permute-start.11) | collective-permute-done | bytes 2097184 | tf_op jit(solution)/shard_map/ppermute | solution.py:871
  185.7 10.4 %all-to-all-done.1 = bf16[8,112,1024]{2,1,0:T(8,128)(2,1)S(1)} async-done(((bf16[8,112,1024]{2,1,0:T(8,128)(2,1)}), bf16[8,112,1024]{2,1,0:T(8,128)(2,1)S(1)}, u32[]{:S(2)}, u32[]{:S(2)}) %all-to-all-start.1) | async-done | bytes 1835040 | tf_op jit(solution)/shard_map/all_to_all | solution.py:916
  197.3 4.3 all-to-all-start.2
  201.7 47.5 %expert.2 = (bf16[896,1024]{1,0:T(8,128)(2,1)}, bf16[896,4096]{1,0:T(8,128)(2,1)}, bf16[896,4096]{1,0:T(8,128)(2,1)}, bf16[896,1024]{1,0:T(8,128)(2,1)}, bf16[896,1024]{1,0:T(8,128)(2,1)}) custom-call(bf16[896,1024]{1,0:T(8,128)(2,1)} %bitcast.63, bf16[8,2,112,1152]{3,2,1,0:T(8,128)(2,1)} %all-to-all-done.g_ref, ...), custom_call_target="tpu_custom_call" | custom-call | flops 30064771072 | bytes 22020096 | tf_op jit(solution)/shard_map/expert/pallas_call | solution.py:775
  249.2 5.9 all-to-all-start.3
  255.2 47.7 %expert.3 = (bf16[896,1024]{1,0:T(8,128)(2,1)}, bf16[896,4096]{1,0:T(8,128)(2,1)}, bf16[896,4096]{1,0:T(8,128)(2,1)}, bf16[896,1024]{1,0:T(8,128)(2,1)}, bf16[896,1024]{1,0:T(8,128)(2,1)}) custom-call(bf16[896,1024]{1,0:T(8,128)(2,1)} %bitcast.21.x_ref.refs_3_, bf16[8,2,112,1152]{3,2,1,0:T(8,128)(2,1)} %all-to-all-done.g_ref, ...), custom_call_target="tpu_custom_call" | custom-call | flops 30064771072 | bytes 22020096 | tf_op jit(solution)/shard_map/expert/pallas_call | solution.py:775
  304.1 6.0 all-to-all-start.4
  310.1 14.0 %weight_grad.5 = (bf16[1024,1024]{1,0:T(8,128)(2,1)}, bf16[1024,1024]{1,0:T(8,128)(2,1)}) custom-call(bf16[896,4096]{1,0:T(8,128)(2,1)} %get-tuple-element.212.refs_0_, bf16[896,1024]{1,0:T(8,128)(2,1)} %get-tuple-element.213.refs_1_, bf16[896,4096]{1,0:T(8,128)(2,1)} %get-tuple-element.214.refs_2_, bf16[896,1024]{1,0:T(8,128)(2,1)} %get-tuple-element.215.refs_3_), custom_call_target="tpu_custom_call" | custom-call | flops 7516192768 | bytes 8388608 | tf_op jit(solution)/shard_map/weight_grad/pallas_call | solution.py:823
  324.6 14.0 %weight_grad.4 = (bf16[1024,1024]{1,0:T(8,128)(2,1)}, bf16[1024,1024]{1,0:T(8,128)(2,1)}) custom-call(bf16[896,4096]{1,0:T(8,128)(2,1)} %get-tuple-element.212.refs_0_, bf16[896,1024]{1,0:T(8,128)(2,1)} %get-tuple-element.213.refs_1_, bf16[896,4096]{1,0:T(8,128)(2,1)} %get-tuple-element.214.refs_2_, bf16[896,1024]{1,0:T(8,128)(2,1)} %get-tuple-element.215.refs_3_), custom_call_target="tpu_custom_call" | custom-call | flops 7516192768 | bytes 8388608 | tf_op jit(solution)/shard_map/weight_grad/pallas_call | solution.py:823
  338.6 4.5 add_convert_fusion.3.refs_2_
  343.1 8.4 %all-to-all-done.4 = bf16[8,112,1024]{2,1,0:T(8,128)(2,1)} async-done(((bf16[8,112,1024]{2,1,0:T(8,128)(2,1)}), bf16[8,112,1024]{2,1,0:T(8,128)(2,1)}, u32[]{:S(2)}, u32[]{:S(2)}) %all-to-all-start.4) | async-done | bytes 1835040 | tf_op jit(solution)/shard_map/all_to_all | solution.py:916
  351.5 17.5 %unpack_rows.2 = (bf16[544,1152]{1,0:T(8,128)(2,1)}, bf16[544,1152]{1,0:T(8,128)(2,1)}, bf16[544,1152]{1,0:T(8,128)(2,1)}, bf16[544,1152]{1,0:T(8,128)(2,1)}) custom-call(s32[4]{0:T(128)} %get-tuple-element.328.part_ref, s32[2176,2]{1,0:T(8,128)} %copy-done.2, bf16[896,1024]{1,0:T(8,128)(2,1)} %bitcast.67, bf16[896,1024]{1,0:T(8,128)(2,1)} %bitcast.25.refs_1_), custom_call_target="tpu_custom_call" | custom-call | flops 11978932224 | bytes 7340032 | tf_op jit(solution)/shard_map/unpack_rows/pallas_call | solution.py:414
  369.5 4.3 all-to-all-start.5
  373.8 2.6 add_convert_fusion.2
  380.5 1.6 add_convert_fusion.5
  382.1 20.6 %collective-permute-done.22.refs_0_ = bf16[512,1024]{1,0:T(8,128)(2,1)S(1)} collective-permute-done((bf16[512,1024]{1,0:T(8,128)(2,1)S(1)}, bf16[512,1024]{1,0:T(8,128)(2,1)S(1)}, u32[]{:S(2)}, u32[]{:S(2)}) %collective-permute-start.22) | collective-permute-done | bytes 1048608 | tf_op jit(solution)/shard_map/ppermute | solution.py:871
  403.7 13.9 %weight_grad.6 = (bf16[1024,1024]{1,0:T(8,128)(2,1)}, bf16[1024,1024]{1,0:T(8,128)(2,1)}) custom-call(bf16[896,4096]{1,0:T(8,128)(2,1)} %get-tuple-element.241.refs_0_, bf16[896,1024]{1,0:T(8,128)(2,1)} %bitcast.64, bf16[896,4096]{1,0:T(8,128)(2,1)} %get-tuple-element.242.refs_2_, bf16[896,1024]{1,0:T(8,128)(2,1)} %bitcast.21.x_ref.refs_3_), custom_call_target="tpu_custom_call" | custom-call | flops 7516192768 | bytes 8388608 | tf_op jit(solution)/shard_map/weight_grad/pallas_call | solution.py:823
  422.6 14.0 %weight_grad.7 = (bf16[1024,1024]{1,0:T(8,128)(2,1)}, bf16[1024,1024]{1,0:T(8,128)(2,1)}) custom-call(bf16[896,4096]{1,0:T(8,128)(2,1)} %get-tuple-element.241.refs_0_, bf16[896,1024]{1,0:T(8,128)(2,1)} %bitcast.65, bf16[896,4096]{1,0:T(8,128)(2,1)} %get-tuple-element.242.refs_2_, bf16[896,1024]{1,0:T(8,128)(2,1)} %bitcast.21.x_ref.refs_3_), custom_call_target="tpu_custom_call" | custom-call | flops 7516192768 | bytes 8388608 | tf_op jit(solution)/shard_map/weight_grad/pallas_call | solution.py:823
  436.5 7.9 %collective-permute-done.24.refs_1_ = bf16[512,1024]{1,0:T(8,128)(2,1)} collective-permute-done((bf16[512,1024]{1,0:T(8,128)(2,1)}, bf16[512,1024]{1,0:T(8,128)(2,1)}, u32[]{:S(2)}, u32[]{:S(2)}) %collective-permute-start.24) | collective-permute-done | bytes 1048608 | tf_op jit(solution)/shard_map/ppermute | solution.py:871
  444.4 25.9 %collective-permute-done.23.refs_0_ = bf16[272,1152]{1,0:T(8,128)(2,1)S(1)} collective-permute-done((bf16[272,1152]{1,0:T(8,128)(2,1)}, bf16[272,1152]{1,0:T(8,128)(2,1)S(1)}, u32[]{:S(2)}, u32[]{:S(2)}) %collective-permute-start.23) | collective-permute-done | bytes 626720 | tf_op jit(solution)/shard_map/ppermute | solution.py:871
  470.3 5.5 add_convert_fusion.1.refs_4_
  475.8 5.9 all-to-all-start.6
  481.7 3.2 add_convert_fusion
  484.9 1.6 collective-permute-start.28
  486.5 12.4 %middle_back.1 = (f32[544,1024]{1,0:T(8,128)}, f32[128,1024]{1,0:T(8,128)}, f32[1,1024]{1,0:T(1,128)}, bf16[256,1024]{1,0:T(8,128)(2,1)}, bf16[256,1024]{1,0:T(8...) custom-call(s32[1]{0:T(128)} %bitcast.4.at_ref, ...), custom_call_target="tpu_custom_call" | custom-call | flops 4563402752 | bytes 22282240 | tf_op jit(solution)/shard_map/middle_back/pallas_call | solution.py:619
  500.0 1.6 collective-permute-start.31
  501.6 2.6 copy.107
  506.9 2.3 collective-permute-done.29.refs_1_
  509.2 4.3 collective-permute-done.31.refs_3_
  516.7 34.3 %attend_back.1 = (bf16[544,1024]{1,0:T(8,128)(2,1)}, bf16[544,1024]{1,0:T(8,128)(2,1)}, bf16[544,1024]{1,0:T(8,128)(2,1)}, bf16[544,1024]{1,0:T(8,128)(2,1)}, bf...) custom-call(s32[4]{0:T(128)} %get-tuple-element.327.starts_ref, bf16[3,11,208,256]{3,2,1,0:T(8,128)(2,1)} %get-tuple-element.175.qkv_ref, ...), custom_call_target="tpu_custom_call" | custom-call | flops 14394851328 | bytes 46858240 | tf_op jit(solution)/shard_map/attend_back/pallas_call | solution.py:286
  554.7 1.6 collective-permute-done.38
  556.3 2.7 add_convert_fusion.9.refs_2_
  561.6 1.6 pad_maximum_fusion
  563.2 6.3 all-to-all-start.7
  571.1 16.1 %unpack_rows.3 = (bf16[544,1024]{1,0:T(8,128)(2,1)}, bf16[544,1024]{1,0:T(8,128)(2,1)}, bf16[544,1024]{1,0:T(8,128)(2,1)}, bf16[544,1024]{1,0:T(8,128)(2,1)}) custom-call(s32[4]{0:T(128)} %get-tuple-element.328.part_ref, s32[2176,2]{1,0:T(8,128)} %copy-done.2, bf16[896,1024]{1,0:T(8,128)(2,1)} %bitcast.27.refs_0_, bf16[896,1024]{1,0:T(8,128)(2,1)} %bitcast.29.refs_1_), custom_call_target="tpu_custom_call" | custom-call | flops 11978932224 | bytes 7340032 | tf_op jit(solution)/shard_map/unpack_rows/pallas_call | solution.py:414
  589.5 34.4 %all-to-all-done.7 = bf16[8,144,1024]{2,1,0:T(8,128)(2,1)S(1)} async-done(((bf16[8,144,1024]{2,1,0:T(8,128)(2,1)}), bf16[8,144,1024]{2,1,0:T(8,128)(2,1)S(1)}, u32[]{:S(2)}, u32[]{:S(2)}) %all-to-all-start.7) | async-done | bytes 2359328 | tf_op jit(solution)/shard_map/all_to_all | solution.py:916
  625.1 4.7 input_back.1.refs_0_
  630.3 3.1 add_convert_fusion.7
  636.6 54.2 %collective-permute-done.44.refs_3_ = bf16[256,1024]{1,0:T(8,128)(2,1)S(1)} collective-permute-done((bf16[256,1024]{1,0:T(8,128)(2,1)S(1)}, bf16[256,1024]{1,0:T(8,128)(2,1)S(1)}, u32[]{:S(2)}, u32[]{:S(2)}) %collective-permute-start.44) | collective-permute-done | bytes 524320 | tf_op jit(solution)/shard_map/ppermute | solution.py:871
  691.6 5.5 sum_far.3
  697.0 4.3 sum_far.2
  701.4 3.1 add_convert_fusion.6.refs_0_
  705.6 23.7 %collective-permute-done.46.refs_1_ = bf16[544,1024]{1,0:T(8,128)(2,1)S(1)} collective-permute-done((bf16[544,1024]{1,0:T(8,128)(2,1)S(1)}, bf16[544,1024]{1,0:T(8,128)(2,1)S(1)}, u32[]{:S(2)}, u32[]{:S(2)}) %collective-permute-start.46) | collective-permute-done | bytes 1114144 | tf_op jit(solution)/shard_map/ppermute | solution.py:871
  730.6 6.7 assemble.3
  737.4 5.4 assemble.2
  744.2 2.1 slice_convert_fusion
  746.3 1.5 slice.126
  747.8 2.1 copy.110
  (234 shorter events, 63.2 us)
Async XLA Ops:
  10.3 30.4 %collective-permute-start = (bf16[512,1024]{1,0:T(8,128)(2,1)}, bf16[512,1024]{1,0:T(8,128)(2,1)}, u32[]{:S(2)}, u32[]{:S(2)}) collective-permute-start(bf16[512,1024]{1,0:T(8,128)(2,1)} %get-tuple-element.193.refs_0_), channel_id=1, source_target_pairs={{0,2},{1,3},{2,0},{3,1},{4,6},{5,7},{6,4},{7,5},{8,10},{9,11},{10,... | collective-permute-start | bytes 3145736 | tf_op jit(solution)/shard_map/ppermute | solution.py:871
  19.5 119.5 %copy-start.2 = (s32[2176,2]{1,0:T(8,128)}, s32[2176,2]{1,0:T(8,128)S(1)}, u32[]{:S(2)}) copy-start(s32[2176,2]{1,0:T(8,128)S(1)} %get-tuple-element.339.lp_ref) | copy-start | bytes 52228
  40.7 97.7 %all-to-all-start = ((bf16[8,2,112,1152]{3,2,1,0:T(8,128)(2,1)}), bf16[8,2,112,1152]{3,2,1,0:T(8,128)(2,1)}, u32[]{:S(2)}, u32[]{:S(2)}) async-start(bf16[8,2,112,1152]{3,2,1,0:T(8,128)(2,1)} %pack_cotangent.1), calls=%async_computation | async-start | bytes 8257536 | tf_op jit(solution)/shard_map/all_to_all | solution.py:916
  46.9 35.6 %collective-permute-start.1 = (bf16[512,1024]{1,0:T(8,128)(2,1)S(1)}, bf16[512,1024]{1,0:T(8,128)(2,1)}, u32[]{:S(2)}, u32[]{:S(2)}) collective-permute-start(bf16[512,1024]{1,0:T(8,128)(2,1)S(1)} %copy-done.15), channel_id=1, source_target_pairs={{0,2},{1,3},{2,0},{3,1},{4,6},{5,7},{6,4},{7,5},{8,10},{9,11},{10,... | collective-permute-start | bytes 3145736 | tf_op jit(solution)/shard_map/ppermute | solution.py:871
  47.5 35.0 %collective-permute-start.2 = (bf16[256,1024]{1,0:T(8,128)(2,1)S(1)}, bf16[256,1024]{1,0:T(8,128)(2,1)S(1)}, u32[]{:S(2)}, u32[]{:S(2)}) collective-permute-start(bf16[256,1024]{1,0:T(8,128)(2,1)S(1)} %copy-done.19), channel_id=1, source_target_pairs={{0,2},{1,3},{2,0},{3,1},{4,6},{5,7},{6,4},{7,5},{8,10},{9,11},{10,... | collective-permute-start | bytes 1572872 | tf_op jit(solution)/shard_map/ppermute | solution.py:871
  49.0 39.5 %collective-permute-start.6 = (bf16[256,1024]{1,0:T(8,128)(2,1)S(1)}, bf16[256,1024]{1,0:T(8,128)(2,1)}, u32[]{:S(2)}, u32[]{:S(2)}) collective-permute-start(bf16[256,1024]{1,0:T(8,128)(2,1)S(1)} %copy-done.19), channel_id=1, source_target_pairs={{0,1},{1,0},{2,3},{3,2},{4,5},{5,4},{6,7},{7,6},{8,9},{9,8},{10,11... | collective-permute-start | bytes 1572872 | tf_op jit(solution)/shard_map/ppermute | solution.py:871
  82.5 14.9 %collective-permute-start.7 = (bf16[256,1024]{1,0:T(8,128)(2,1)S(1)}, bf16[256,1024]{1,0:T(8,128)(2,1)S(1)}, u32[]{:S(2)}, u32[]{:S(2)}) collective-permute-start(bf16[256,1024]{1,0:T(8,128)(2,1)S(1)} %collective-permute-done.2.refs_5_.refs_15_), channel_id=1, source_target_pairs={{0,1},{1,0},{2,3},{3,2},{4,5},{5,4},{6,7},{7,6},{8,9},{9,8},{10,11... | collective-permute-start | bytes 1572872 | tf_op jit(solution)/shard_map/ppermute | solution.py:871
  82.6 9.7 %collective-permute-start.3 = (bf16[544,256]{1,0:T(8,128)(2,1)}, bf16[544,256]{1,0:T(8,128)(2,1)S(1)}, u32[]{:S(2)}, u32[]{:S(2)}) collective-permute-start(bf16[544,256]{1,0:T(8,128)(2,1)} %get-tuple-element.170), channel_id=1, source_target_pairs={{0,2},{1,3},{2,0},{3,1},{4,6},{5,7},{6,4},{7,5},{8,10},{9,11},{10,... | collective-permute-start | bytes 835592 | tf_op jit(solution)/shard_map/ppermute | solution.py:871
  83.2 9.1 %collective-permute-start.4 = (bf16[544,256]{1,0:T(8,128)(2,1)}, bf16[544,256]{1,0:T(8,128)(2,1)}, u32[]{:S(2)}, u32[]{:S(2)}) collective-permute-start(bf16[544,256]{1,0:T(8,128)(2,1)} %get-tuple-element.171), channel_id=1, source_target_pairs={{0,1},{1,0},{2,3},{3,2},{4,5},{5,4},{6,7},{7,6},{8,9},{9,8},{10,11... | collective-permute-start | bytes 835592 | tf_op jit(solution)/shard_map/ppermute | solution.py:871
  83.3 14.1 %collective-permute-start.5 = (bf16[544,256]{1,0:T(8,128)(2,1)}, bf16[544,256]{1,0:T(8,128)(2,1)}, u32[]{:S(2)}, u32[]{:S(2)}) collective-permute-start(bf16[544,256]{1,0:T(8,128)(2,1)} %get-tuple-element.172), channel_id=1, source_target_pairs={{0,3},{1,2},{2,1},{3,0},{4,7},{5,6},{6,5},{7,4},{8,11},{9,10},{10,... | collective-permute-start | bytes 835592 | tf_op jit(solution)/shard_map/ppermute | solution.py:871
  105.1 27.3 %collective-permute-start.8 = (bf16[544,1024]{1,0:T(8,128)(2,1)}, bf16[544,1024]{1,0:T(8,128)(2,1)S(1)}, u32[]{:S(2)}, u32[]{:S(2)}) collective-permute-start(bf16[544,1024]{1,0:T(8,128)(2,1)} %get-tuple-element.180.refs_0_.refs_4_), channel_id=1, source_target_pairs={{0,2},{1,3},{2,0},{3,1},{4,6},{5,7},{6,4},{7,5},{8,10},{9,11},{10,... | collective-permute-start | bytes 3342344 | tf_op jit(solution)/shard_map/ppermute | solution.py:871
  105.6 26.7 %collective-permute-start.9 = (bf16[544,1024]{1,0:T(8,128)(2,1)}, bf16[544,1024]{1,0:T(8,128)(2,1)S(1)}, u32[]{:S(2)}, u32[]{:S(2)}) collective-permute-start(bf16[544,1024]{1,0:T(8,128)(2,1)} %get-tuple-element.180.refs_0_.refs_4_), channel_id=1, source_target_pairs={{0,1},{1,0},{2,3},{3,2},{4,5},{5,4},{6,7},{7,6},{8,9},{9,8},{10,11... | collective-permute-start | bytes 3342344 | tf_op jit(solution)/shard_map/ppermute | solution.py:871
  132.4 2.9 collective-permute-start.10
  138.4 46.2 %collective-permute-start.11 = (bf16[1024,1024]{1,0:T(8,128)(2,1)}, bf16[1024,1024]{1,0:T(8,128)(2,1)}, u32[]{:S(2)}, u32[]{:S(2)}) collective-permute-start(bf16[1024,1024]{1,0:T(8,128)(2,1)} %bitcast.85), channel_id=1, source_target_pairs={{0,2},{1,3},{2,0},{3,1},{4,6},{5,7},{6,4},{7,5},{8,10},{9,11},{10,... | collective-permute-start | bytes 6291464 | tf_op jit(solution)/shard_map/ppermute | solution.py:871
  149.9 46.2 %all-to-all-start.1 = ((bf16[8,112,1024]{2,1,0:T(8,128)(2,1)}), bf16[8,112,1024]{2,1,0:T(8,128)(2,1)S(1)}, u32[]{:S(2)}, u32[]{:S(2)}) async-start(bf16[8,112,1024]{2,1,0:T(8,128)(2,1)} %bitcast.70), calls=%async_computation.1 | async-start | bytes 3670016 | tf_op jit(solution)/shard_map/all_to_all | solution.py:916
  153.6 31.6 %collective-permute-start.12 = (bf16[512,1024]{1,0:T(8,128)(2,1)}, bf16[512,1024]{1,0:T(8,128)(2,1)}, u32[]{:S(2)}, u32[]{:S(2)}) collective-permute-start(bf16[512,1024]{1,0:T(8,128)(2,1)} %get-tuple-element.193.refs_0_), channel_id=1, source_target_pairs={{0,1},{1,0},{2,3},{3,2},{4,5},{5,4},{6,7},{7,6},{8,9},{9,8},{10,11... | collective-permute-start | bytes 3145736 | tf_op jit(solution)/shard_map/ppermute | solution.py:871
  153.6 48.1 %collective-permute-start.16 = (bf16[1024,1024]{1,0:T(8,128)(2,1)}, bf16[1024,1024]{1,0:T(8,128)(2,1)}, u32[]{:S(2)}, u32[]{:S(2)}) collective-permute-start(bf16[1024,1024]{1,0:T(8,128)(2,1)} %bitcast.86), channel_id=1, source_target_pairs={{0,1},{1,0},{2,3},{3,2},{4,5},{5,4},{6,7},{7,6},{8,9},{9,8},{10,11... | collective-permute-start | bytes 6291464 | tf_op jit(solution)/shard_map/ppermute | solution.py:871
  184.7 17.0 %collective-permute-start.17 = (bf16[1024,1024]{1,0:T(8,128)(2,1)}, bf16[1024,1024]{1,0:T(8,128)(2,1)}, u32[]{:S(2)}, u32[]{:S(2)}) collective-permute-start(bf16[1024,1024]{1,0:T(8,128)(2,1)} %collective-permute-done.11.refs_9_), channel_id=1, source_target_pairs={{0,1},{1,0},{2,3},{3,2},{4,5},{5,4},{6,7},{7,6},{8,9},{9,8},{10,11... | collective-permute-start | bytes 6291464 | tf_op jit(solution)/shard_map/ppermute | solution.py:871
  184.7 17.0 %collective-permute-start.13 = (bf16[512,1024]{1,0:T(8,128)(2,1)S(1)}, bf16[512,1024]{1,0:T(8,128)(2,1)}, u32[]{:S(2)}, u32[]{:S(2)}) collective-permute-start(bf16[512,1024]{1,0:T(8,128)(2,1)S(1)} %copy-done.16), channel_id=1, source_target_pairs={{0,1},{1,0},{2,3},{3,2},{4,5},{5,4},{6,7},{7,6},{8,9},{9,8},{10,11... | collective-permute-start | bytes 3145736 | tf_op jit(solution)/shard_map/ppermute | solution.py:871
  185.2 16.5 %collective-permute-start.15 = (bf16[512,1024]{1,0:T(8,128)(2,1)}, bf16[512,1024]{1,0:T(8,128)(2,1)}, u32[]{:S(2)}, u32[]{:S(2)}) collective-permute-start(bf16[512,1024]{1,0:T(8,128)(2,1)} %collective-permute-done.1.refs_3_), channel_id=1, source_target_pairs={{0,1},{1,0},{2,3},{3,2},{4,5},{5,4},{6,7},{7,6},{8,9},{9,8},{10,11... | collective-permute-start | bytes 3145736 | tf_op jit(solution)/shard_map/ppermute | solution.py:871
  185.2 16.5 %collective-permute-start.14 = (bf16[512,1024]{1,0:T(8,128)(2,1)}, bf16[512,1024]{1,0:T(8,128)(2,1)}, u32[]{:S(2)}, u32[]{:S(2)}) collective-permute-start(bf16[512,1024]{1,0:T(8,128)(2,1)} %collective-permute-done.refs_2_), channel_id=1, source_target_pairs={{0,1},{1,0},{2,3},{3,2},{4,5},{5,4},{6,7},{7,6},{8,9},{9,8},{10,11... | collective-permute-start | bytes 3145736 | tf_op jit(solution)/shard_map/ppermute | solution.py:871
  197.3 51.9 %all-to-all-start.2 = ((bf16[8,112,1024]{2,1,0:T(8,128)(2,1)}), bf16[8,112,1024]{2,1,0:T(8,128)(2,1)}, u32[]{:S(2)}, u32[]{:S(2)}) async-start(bf16[8,112,1024]{2,1,0:T(8,128)(2,1)} %bitcast.68), calls=%async_computation.2 | async-start | bytes 3670016 | tf_op jit(solution)/shard_map/all_to_all | solution.py:916
  249.2 53.6 %all-to-all-start.3 = ((bf16[8,112,1024]{2,1,0:T(8,128)(2,1)}), bf16[8,112,1024]{2,1,0:T(8,128)(2,1)S(1)}, u32[]{:S(2)}, u32[]{:S(2)}) async-start(bf16[8,112,1024]{2,1,0:T(8,128)(2,1)} %bitcast.71), calls=%async_computation.3 | async-start | bytes 3670016 | tf_op jit(solution)/shard_map/all_to_all | solution.py:916
  304.1 47.4 %all-to-all-start.4 = ((bf16[8,112,1024]{2,1,0:T(8,128)(2,1)}), bf16[8,112,1024]{2,1,0:T(8,128)(2,1)}, u32[]{:S(2)}, u32[]{:S(2)}) async-start(bf16[8,112,1024]{2,1,0:T(8,128)(2,1)} %bitcast.69), calls=%async_computation.4 | async-start | bytes 3670016 | tf_op jit(solution)/shard_map/all_to_all | solution.py:916
  324.1 14.5 %collective-permute-start.18 = (bf16[1024,1024]{1,0:T(8,128)(2,1)}, bf16[1024,1024]{1,0:T(8,128)(2,1)}, u32[]{:S(2)}, u32[]{:S(2)}) collective-permute-start(bf16[1024,1024]{1,0:T(8,128)(2,1)} %get-tuple-element.217), channel_id=1, source_target_pairs={{0,1},{1,0},{2,3},{3,2},{4,5},{5,4},{6,7},{7,6},{8,9},{9,8},{10,11... | collective-permute-start | bytes 6291464 | tf_op jit(solution)/shard_map/ppermute | solution.py:871
  324.1 14.5 %collective-permute-start.19 = (bf16[1024,1024]{1,0:T(8,128)(2,1)}, bf16[1024,1024]{1,0:T(8,128)(2,1)S(1)}, u32[]{:S(2)}, u32[]{:S(2)}) collective-permute-start(bf16[1024,1024]{1,0:T(8,128)(2,1)} %get-tuple-element.218), channel_id=1, source_target_pairs={{0,1},{1,0},{2,3},{3,2},{4,5},{5,4},{6,7},{7,6},{8,9},{9,8},{10,11... | collective-permute-start | bytes 6291464 | tf_op jit(solution)/shard_map/ppermute | solution.py:871
  369.0 10.1 %collective-permute-start.20 = (bf16[544,1152]{1,0:T(8,128)(2,1)}, bf16[544,1152]{1,0:T(8,128)(2,1)S(1)}, u32[]{:S(2)}, u32[]{:S(2)}) collective-permute-start(bf16[544,1152]{1,0:T(8,128)(2,1)} %get-tuple-element.223), channel_id=1, source_target_pairs={{0,1},{1,0},{2,3},{3,2},{4,5},{5,4},{6,7},{7,6},{8,9},{9,8},{10,11... | collective-permute-start | bytes 3760136 | tf_op jit(solution)/shard_map/ppermute | solution.py:871
  369.0 10.1 %collective-permute-start.21 = (bf16[544,1152]{1,0:T(8,128)(2,1)}, bf16[544,1152]{1,0:T(8,128)(2,1)}, u32[]{:S(2)}, u32[]{:S(2)}) collective-permute-start(bf16[544,1152]{1,0:T(8,128)(2,1)} %get-tuple-element.224), channel_id=1, source_target_pairs={{0,1},{1,0},{2,3},{3,2},{4,5},{5,4},{6,7},{7,6},{8,9},{9,8},{10,11... | collective-permute-start | bytes 3760136 | tf_op jit(solution)/shard_map/ppermute | solution.py:871
  369.5 106.3 %all-to-all-start.5 = ((bf16[8,112,1024]{2,1,0:T(8,128)(2,1)}), bf16[8,112,1024]{2,1,0:T(8,128)(2,1)}, u32[]{:S(2)}, u32[]{:S(2)}) async-start(bf16[8,112,1024]{2,1,0:T(8,128)(2,1)} %bitcast.66), calls=%async_computation.5 | async-start | bytes 3670016 | tf_op jit(solution)/shard_map/all_to_all | solution.py:916
  377.6 25.1 %collective-permute-start.22 = (bf16[512,1024]{1,0:T(8,128)(2,1)S(1)}, bf16[512,1024]{1,0:T(8,128)(2,1)S(1)}, u32[]{:S(2)}, u32[]{:S(2)}) collective-permute-start(bf16[512,1024]{1,0:T(8,128)(2,1)S(1)} %get-tuple-element.332), channel_id=1, source_target_pairs={{0,2},{1,3},{2,0},{3,1},{4,6},{5,7},{6,4},{7,5},{8,10},{9,11},{10,... | collective-permute-start | bytes 3145736 | tf_op jit(solution)/shard_map/ppermute | solution.py:871
  417.6 52.7 %collective-permute-start.26 = (bf16[1024,1024]{1,0:T(8,128)(2,1)}, bf16[1024,1024]{1,0:T(8,128)(2,1)}, u32[]{:S(2)}, u32[]{:S(2)}) collective-permute-start(bf16[1024,1024]{1,0:T(8,128)(2,1)} %get-tuple-element.238), channel_id=1, source_target_pairs={{0,1},{1,0},{2,3},{3,2},{4,5},{5,4},{6,7},{7,6},{8,9},{9,8},{10,11... | collective-permute-start | bytes 6291464 | tf_op jit(solution)/shard_map/ppermute | solution.py:871
  417.6 52.7 %collective-permute-start.27 = (bf16[1024,1024]{1,0:T(8,128)(2,1)}, bf16[1024,1024]{1,0:T(8,128)(2,1)S(1)}, u32[]{:S(2)}, u32[]{:S(2)}) collective-permute-start(bf16[1024,1024]{1,0:T(8,128)(2,1)} %get-tuple-element.239), channel_id=1, source_target_pairs={{0,1},{1,0},{2,3},{3,2},{4,5},{5,4},{6,7},{7,6},{8,9},{9,8},{10,11... | collective-permute-start | bytes 6291464 | tf_op jit(solution)/shard_map/ppermute | solution.py:871
  418.1 26.3 %collective-permute-start.24 = (bf16[512,1024]{1,0:T(8,128)(2,1)}, bf16[512,1024]{1,0:T(8,128)(2,1)}, u32[]{:S(2)}, u32[]{:S(2)}) collective-permute-start(bf16[512,1024]{1,0:T(8,128)(2,1)} %get-tuple-element.331), channel_id=1, source_target_pairs={{0,2},{1,3},{2,0},{3,1},{4,6},{5,7},{6,4},{7,5},{8,10},{9,11},{10,... | collective-permute-start | bytes 3145736 | tf_op jit(solution)/shard_map/ppermute | solution.py:871
  420.5 55.3 %collective-permute-start.25 = (bf16[272,1152]{1,0:T(8,128)(2,1)S(1)}, bf16[272,1152]{1,0:T(8,128)(2,1)}, u32[]{:S(2)}, u32[]{:S(2)}) collective-permute-start(bf16[272,1152]{1,0:T(8,128)(2,1)S(1)} %get-tuple-element.335), channel_id=1, source_target_pairs={{0,2},{1,3},{2,0},{3,1},{4,6},{5,7},{6,4},{7,5},{8,10},{9,11},{10,... | collective-permute-start | bytes 1880072 | tf_op jit(solution)/shard_map/ppermute | solution.py:871
  421.0 49.3 %collective-permute-start.23 = (bf16[272,1152]{1,0:T(8,128)(2,1)}, bf16[272,1152]{1,0:T(8,128)(2,1)S(1)}, u32[]{:S(2)}, u32[]{:S(2)}) collective-permute-start(bf16[272,1152]{1,0:T(8,128)(2,1)} %get-tuple-element.336), channel_id=1, source_target_pairs={{0,2},{1,3},{2,0},{3,1},{4,6},{5,7},{6,4},{7,5},{8,10},{9,11},{10,... | collective-permute-start | bytes 1880072 | tf_op jit(solution)/shard_map/ppermute | solution.py:871
  475.8 75.2 %all-to-all-start.6 = ((bf16[8,112,1024]{2,1,0:T(8,128)(2,1)}), bf16[8,112,1024]{2,1,0:T(8,128)(2,1)}, u32[]{:S(2)}, u32[]{:S(2)}) async-start(bf16[8,112,1024]{2,1,0:T(8,128)(2,1)} %bitcast.62), calls=%async_computation.6 | async-start | bytes 3670016 | tf_op jit(solution)/shard_map/all_to_all | solution.py:916
  484.9 14.6 %collective-permute-start.28 = (bf16[256,1024]{1,0:T(8,128)(2,1)S(1)}, bf16[256,1024]{1,0:T(8,128)(2,1)}, u32[]{:S(2)}, u32[]{:S(2)}) collective-permute-start(bf16[256,1024]{1,0:T(8,128)(2,1)S(1)} %slice.106), channel_id=1, source_target_pairs={{0,2},{1,3},{2,0},{3,1},{4,6},{5,7},{6,4},{7,5},{8,10},{9,11},{10,... | collective-permute-start | bytes 1572872 | tf_op jit(solution)/shard_map/ppermute | solution.py:871
  498.9 5.3 collective-permute-start.34
  499.0 5.2 collective-permute-start.35
  499.5 9.7 %collective-permute-start.29 = (bf16[544,256]{1,0:T(8,128)(2,1)}, bf16[544,256]{1,0:T(8,128)(2,1)S(1)}, u32[]{:S(2)}, u32[]{:S(2)}) collective-permute-start(bf16[544,256]{1,0:T(8,128)(2,1)} %get-tuple-element.260), channel_id=1, source_target_pairs={{0,2},{1,3},{2,0},{3,1},{4,6},{5,7},{6,4},{7,5},{8,10},{9,11},{10,... | collective-permute-start | bytes 835592 | tf_op jit(solution)/shard_map/ppermute | solution.py:871
  500.0 9.2 %collective-permute-start.30 = (bf16[544,256]{1,0:T(8,128)(2,1)}, bf16[544,256]{1,0:T(8,128)(2,1)}, u32[]{:S(2)}, u32[]{:S(2)}) collective-permute-start(bf16[544,256]{1,0:T(8,128)(2,1)} %get-tuple-element.261), channel_id=1, source_target_pairs={{0,1},{1,0},{2,3},{3,2},{4,5},{5,4},{6,7},{7,6},{8,9},{9,8},{10,11... | collective-permute-start | bytes 835592 | tf_op jit(solution)/shard_map/ppermute | solution.py:871
  500.0 13.5 %collective-permute-start.31 = (bf16[544,256]{1,0:T(8,128)(2,1)}, bf16[544,256]{1,0:T(8,128)(2,1)}, u32[]{:S(2)}, u32[]{:S(2)}) collective-permute-start(bf16[544,256]{1,0:T(8,128)(2,1)} %get-tuple-element.262), channel_id=1, source_target_pairs={{0,3},{1,2},{2,1},{3,0},{4,7},{5,6},{6,5},{7,4},{8,11},{9,10},{10,... | collective-permute-start | bytes 835592 | tf_op jit(solution)/shard_map/ppermute | solution.py:871
  506.2 44.8 %collective-permute-start.36 = (bf16[256,1024]{1,0:T(8,128)(2,1)S(1)}, bf16[256,1024]{1,0:T(8,128)(2,1)S(1)}, u32[]{:S(2)}, u32[]{:S(2)}) collective-permute-start(bf16[256,1024]{1,0:T(8,128)(2,1)S(1)} %add_convert_fusion.13), channel_id=1, source_target_pairs={{0,2},{1,3},{2,0},{3,1},{4,6},{5,7},{6,4},{7,5},{8,10},{9,11},{10,... | collective-permute-start | bytes 1572872 | tf_op jit(solution)/shard_map/ppermute | solution.py:871
  514.7 36.4 %collective-permute-start.32 = (bf16[256,1024]{1,0:T(8,128)(2,1)}, bf16[256,1024]{1,0:T(8,128)(2,1)S(1)}, u32[]{:S(2)}, u32[]{:S(2)}) collective-permute-start(bf16[256,1024]{1,0:T(8,128)(2,1)} %get-tuple-element.330), channel_id=1, source_target_pairs={{0,2},{1,3},{2,0},{3,1},{4,6},{5,7},{6,4},{7,5},{8,10},{9,11},{10,... | collective-permute-start | bytes 1572872 | tf_op jit(solution)/shard_map/ppermute | solution.py:871
  516.0 35.1 %collective-permute-start.33 = (bf16[256,1024]{1,0:T(8,128)(2,1)}, bf16[256,1024]{1,0:T(8,128)(2,1)S(1)}, u32[]{:S(2)}, u32[]{:S(2)}) collective-permute-start(bf16[256,1024]{1,0:T(8,128)(2,1)} %get-tuple-element.329), channel_id=1, source_target_pairs={{0,2},{1,3},{2,0},{3,1},{4,6},{5,7},{6,4},{7,5},{8,10},{9,11},{10,... | collective-permute-start | bytes 1572872 | tf_op jit(solution)/shard_map/ppermute | solution.py:871
  516.7 36.4 %copy-start.34 = (f32[1,1024]{1,0:T(1,128)S(1)}, f32[1,1024]{1,0:T(1,128)}, u32[]{:S(2)}) copy-start(f32[1,1024]{1,0:T(1,128)} %get-tuple-element.304) | copy-start | bytes 12292
  551.1 3.7 collective-permute-start.37
  552.1 4.2 collective-permute-start.38
  563.2 60.7 %all-to-all-start.7 = ((bf16[8,144,1024]{2,1,0:T(8,128)(2,1)}), bf16[8,144,1024]{2,1,0:T(8,128)(2,1)S(1)}, u32[]{:S(2)}, u32[]{:S(2)}) async-start(bf16[8,144,1024]{2,1,0:T(8,128)(2,1)} %bitcast.54), calls=%async_computation.7 | async-start | bytes 4718592 | tf_op jit(solution)/shard_map/all_to_all | solution.py:916
  569.5 159.9 %all-gather.2.cloned.1.call-start = ((), (), s32[]{:S(2)}) async-start(), calls=%async_computation.8 | async-start | bytes 2654208 | tf_op jit(solution)/shard_map/all_gather | solution.py:1079
  570.6 16.6 %collective-permute-start.39 = (bf16[272,1024]{1,0:T(8,128)(2,1)}, bf16[272,1024]{1,0:T(8,128)(2,1)S(1)}, u32[]{:S(2)}, u32[]{:S(2)}) collective-permute-start(bf16[272,1024]{1,0:T(8,128)(2,1)} %get-tuple-element.338), channel_id=1, source_target_pairs={{0,2},{1,3},{2,0},{3,1},{4,6},{5,7},{6,4},{7,5},{8,10},{9,11},{10,... | collective-permute-start | bytes 1671176 | tf_op jit(solution)/shard_map/ppermute | solution.py:871
  587.2 43.1 %collective-permute-start.40 = (bf16[544,1024]{1,0:T(8,128)(2,1)}, bf16[544,1024]{1,0:T(8,128)(2,1)S(1)}, u32[]{:S(2)}, u32[]{:S(2)}) collective-permute-start(bf16[544,1024]{1,0:T(8,128)(2,1)} %get-tuple-element.291), channel_id=1, source_target_pairs={{0,1},{1,0},{2,3},{3,2},{4,5},{5,4},{6,7},{7,6},{8,9},{9,8},{10,11... | collective-permute-start | bytes 3342344 | tf_op jit(solution)/shard_map/ppermute | solution.py:871
  587.3 43.0 %collective-permute-start.41 = (bf16[544,1024]{1,0:T(8,128)(2,1)}, bf16[544,1024]{1,0:T(8,128)(2,1)}, u32[]{:S(2)}, u32[]{:S(2)}) collective-permute-start(bf16[544,1024]{1,0:T(8,128)(2,1)} %get-tuple-element.292), channel_id=1, source_target_pairs={{0,1},{1,0},{2,3},{3,2},{4,5},{5,4},{6,7},{7,6},{8,9},{9,8},{10,11... | collective-permute-start | bytes 3342344 | tf_op jit(solution)/shard_map/ppermute | solution.py:871
  588.0 37.0 %collective-permute-start.42 = (bf16[272,1024]{1,0:T(8,128)(2,1)}, bf16[272,1024]{1,0:T(8,128)(2,1)}, u32[]{:S(2)}, u32[]{:S(2)}) collective-permute-start(bf16[272,1024]{1,0:T(8,128)(2,1)} %get-tuple-element.337), channel_id=1, source_target_pairs={{0,2},{1,3},{2,0},{3,1},{4,6},{5,7},{6,4},{7,5},{8,10},{9,11},{10,... | collective-permute-start | bytes 1671176 | tf_op jit(solution)/shard_map/ppermute | solution.py:871
  629.7 71.6 %collective-permute-start.43 = (bf16[544,1024]{1,0:T(8,128)(2,1)}, bf16[544,1024]{1,0:T(8,128)(2,1)}, u32[]{:S(2)}, u32[]{:S(2)}) collective-permute-start(bf16[544,1024]{1,0:T(8,128)(2,1)} %input_back.1.refs_0_), channel_id=1, source_target_pairs={{0,2},{1,3},{2,0},{3,1},{4,6},{5,7},{6,4},{7,5},{8,10},{9,11},{10,... | collective-permute-start | bytes 3342344 | tf_op jit(solution)/shard_map/ppermute | solution.py:871
  633.4 67.9 %collective-permute-start.45 = (bf16[544,1024]{1,0:T(8,128)(2,1)}, bf16[544,1024]{1,0:T(8,128)(2,1)}, u32[]{:S(2)}, u32[]{:S(2)}) collective-permute-start(bf16[544,1024]{1,0:T(8,128)(2,1)} %add_convert_fusion.7), channel_id=1, source_target_pairs={{0,2},{1,3},{2,0},{3,1},{4,6},{5,7},{6,4},{7,5},{8,10},{9,11},{10,... | collective-permute-start | bytes 3342344 | tf_op jit(solution)/shard_map/ppermute | solution.py:871
  636.0 54.8 %collective-permute-start.44 = (bf16[256,1024]{1,0:T(8,128)(2,1)S(1)}, bf16[256,1024]{1,0:T(8,128)(2,1)S(1)}, u32[]{:S(2)}, u32[]{:S(2)}) collective-permute-start(bf16[256,1024]{1,0:T(8,128)(2,1)S(1)} %slice.112), channel_id=1, source_target_pairs={{0,2},{1,3},{2,0},{3,1},{4,6},{5,7},{6,4},{7,5},{8,10},{9,11},{10,... | collective-permute-start | bytes 1572872 | tf_op jit(solution)/shard_map/ppermute | solution.py:871
  704.5 24.9 %collective-permute-start.46 = (bf16[544,1024]{1,0:T(8,128)(2,1)S(1)}, bf16[544,1024]{1,0:T(8,128)(2,1)S(1)}, u32[]{:S(2)}, u32[]{:S(2)}) collective-permute-start(bf16[544,1024]{1,0:T(8,128)(2,1)S(1)} %add_convert_fusion.6.refs_0_), channel_id=1, source_target_pairs={{0,2},{1,3},{2,0},{3,1},{4,6},{5,7},{6,4},{7,5},{8,10},{9,11},{10,... | collective-permute-start | bytes 3342344 | tf_op jit(solution)/shard_map/ppermute | solution.py:871
  705.1 25.5 %collective-permute-start.49 = (bf16[544,1024]{1,0:T(8,128)(2,1)S(1)}, bf16[544,1024]{1,0:T(8,128)(2,1)}, u32[]{:S(2)}, u32[]{:S(2)}) collective-permute-start(bf16[544,1024]{1,0:T(8,128)(2,1)S(1)} %copy-done.3), channel_id=1, source_target_pairs={{0,1},{1,0},{2,3},{3,2},{4,5},{5,4},{6,7},{7,6},{8,9},{9,8},{10,11... | collective-permute-start | bytes 3342344 | tf_op jit(solution)/shard_map/ppermute | solution.py:871
  705.1 25.5 %collective-permute-start.50 = (bf16[544,1024]{1,0:T(8,128)(2,1)}, bf16[544,1024]{1,0:T(8,128)(2,1)}, u32[]{:S(2)}, u32[]{:S(2)}) collective-permute-start(bf16[544,1024]{1,0:T(8,128)(2,1)} %collective-permute-done.43.refs_1_), channel_id=1, source_target_pairs={{0,1},{1,0},{2,3},{3,2},{4,5},{5,4},{6,7},{7,6},{8,9},{9,8},{10,11... | collective-permute-start | bytes 3342344 | tf_op jit(solution)/shard_map/ppermute | solution.py:871
  705.6 31.7 %collective-permute-start.47 = (bf16[544,1024]{1,0:T(8,128)(2,1)S(1)}, bf16[544,1024]{1,0:T(8,128)(2,1)}, u32[]{:S(2)}, u32[]{:S(2)}) collective-permute-start(bf16[544,1024]{1,0:T(8,128)(2,1)S(1)} %add_convert_fusion.6.refs_0_), channel_id=1, source_target_pairs={{0,1},{1,0},{2,3},{3,2},{4,5},{5,4},{6,7},{7,6},{8,9},{9,8},{10,11... | collective-permute-start | bytes 3342344 | tf_op jit(solution)/shard_map/ppermute | solution.py:871
  729.4 8.0 %collective-permute-start.48 = (bf16[544,1024]{1,0:T(8,128)(2,1)S(1)}, bf16[544,1024]{1,0:T(8,128)(2,1)}, u32[]{:S(2)}, u32[]{:S(2)}) collective-permute-start(bf16[544,1024]{1,0:T(8,128)(2,1)S(1)} %collective-permute-done.46.refs_1_), channel_id=1, source_target_pairs={{0,1},{1,0},{2,3},{3,2},{4,5},{5,4},{6,7},{7,6},{8,9},{9,8},{10,11... | collective-permute-start | bytes 3342344 | tf_op jit(solution)/shard_map/ppermute | solution.py:871
  730.2 12.7 %collective-permute-start.51 = (f32[10,1024]{1,0:T(8,128)S(1)}, f32[10,1024]{1,0:T(8,128)S(1)}, u32[]{:S(2)}, u32[]{:S(2)}) collective-permute-start(f32[10,1024]{1,0:T(8,128)S(1)} %slice_convert_fusion.1), channel_id=1, source_target_pairs={{0,1},{1,0},{2,3},{3,2},{4,5},{5,4},{6,7},{7,6},{8,9},{9,8},{10,11... | collective-permute-start | bytes 122888 | tf_op jit(solution)/shard_map/ppermute | solution.py:871
  743.6 6.3 collective-permute-start.52
  (39 other events, 260.5 us)
Sparse Core Ops, SparseCore 0:
  625.2 50.1 all-gather.1

commit v9 on v5

--- a/solution.py
+++ b/solution.py
@@ -797,7 +797,7 @@
     store_piece(outs, steps, total.astype(BF))
 
 
-def weight_grad(columns, rows, first, here):
+def weight_grad(columns, rows, first, here, parts=2):
     count = len(columns)
     width = rows[0].shape[1]
     step = min(512, here)
@@ -807,15 +807,15 @@
     for a, b in zip(columns, rows):
         specs += [pl.BlockSpec((a.shape[0], step), lambda i: (0, i + offset)), whole(b.shape, True)]
         args += [a, b]
-    out_specs, out_shape = by_piece(2, steps, (step, width), (here, width), BF)
+    out_specs, out_shape = by_piece(parts, steps, (step, width), (here, width), BF)
     return pl.pallas_call(
         functools.partial(weight_kernel, count, steps),
-        grid=(2 * steps,),
+        grid=(parts * steps,),
         in_specs=specs,
         out_specs=out_specs,
         out_shape=out_shape,
         compiler_params=params(),
-        cost_estimate=cost(4 * sum(b.shape[0] for b in rows) * width * here, 8 * here * width),
+        cost_estimate=cost(2 * parts * sum(b.shape[0] for b in rows) * width * here, 4 * parts * here * width),
         name="weight_grad",
     )(*args)
 
@@ -990,9 +990,12 @@
 
     second_pieces = unpack(part_of, place, returned, slots, per, each, True)
     second_kept, second_other = near_sum(second_pieces, near_hop(second_pieces))
-    second_kept, out_far, *hidden_grads = pinned(second_kept, out_far, *hidden_grads)
+    if paired:
+        second_other, second_kept, out_far, *hidden_grads = pinned(
+            second_other, second_kept, out_far, *hidden_grads
+        )
     second_far = far_hop(second_kept, second_other)
-    in_parts = weight_parts(hidden_grads, arrived)
+    in_parts = weight_grad(hidden_grads, arrived, 0, here, parts)
     in_came = near_hop(in_parts)
     second_far, *in_parts = pinned(second_far, *in_parts)
     combined = [sent(item) for item in backs]
@@ -1002,42 +1005,45 @@
     )
     head_out_parts, mixed_grad = pieces[:parts], pieces[parts:]
     *mixed_grad, combined[0] = pinned(*mixed_grad, combined[0])
-    *mixed_grad, in_came = pinned(*swapped(mixed_grad), in_came)
+    *mixed_grad, in_came = pinned(*mixed_grad, in_came)
+    mixed_grad = swapped(mixed_grad)
     in_kept, in_other = near_sum(in_parts, in_came)
+    if paired:
+        in_other = pinned(in_other, *mixed_grad)[0]
     in_far = far_hop(in_kept, in_other)
     head_out_kept, head_out_far = scattered(head_out_parts)
     *pieces, head_in_part, norm_one_part = attend_back(
         starts, mixed_grad, qkv, logs, first_in, jnp.swapaxes(head_in, 1, 2), gain_one
     )
-    *pieces, combined[-1], in_far, head_out_far = pinned(*pieces, combined[-1], in_far, head_out_far)
-    first_kept, first_far = scattered(pieces)
+    *pieces, combined[-1] = pinned(*pieces, combined[-1])
+    first_kept, first_other = near_sum(pieces, near_hop(pieces))
+    if paired:
+        first_other, first_kept, in_far, head_in_part, *combined = pinned(
+            first_other, first_kept, in_far, head_in_part, *combined
+        )
+    first_far = far_hop(first_kept, first_other)
     block_pieces = unpack(part_of, place, combined, slots, per, each, False)
+    *block_pieces, head_out_far = pinned(*block_pieces, head_out_far)
     block_kept, block_other = near_sum(block_pieces, near_hop(block_pieces))
     first_far, block_kept = pinned(first_far, block_kept)
     block_far = far_hop(block_kept, block_other)
     input_part = input_back(own_block, first_kept, first_far, block_in, middle_grad, gain_one)
     out_grad = out_kept.astype(F32) + out_far.astype(F32)
     in_grad = sum_turned(in_kept, in_far)
-    input_far, out_grad, in_grad = pinned(far_part(input_part), out_grad, in_grad)
+    input_far, out_grad, in_grad, block_far = pinned(far_part(input_part), out_grad, in_grad, block_far)
     block_own = (middle + block_kept.astype(F32) + block_far.astype(F32)).astype(BF)
 
-    cols = head_in.shape[2]
+    input_grad = assemble(part_of, gathered_from(input_part, input_far), rows_here, F32)
+    block_out = assemble(part_of, gathered(block_own), rows_here, BF)
+
     head_out_part = (head_out_kept.astype(F32) + head_out_far.astype(F32)).astype(BF)
     small = jnp.concatenate([norm_one_part, norm_two_part, router_part[:experts]], 0).astype(BF)
-    count = 4 * cols + 2 + experts
-    total = up_to(count, 16 * groups)
-    heads = jnp.concatenate(
-        [head_in_part.reshape(3 * cols, width), head_out_part, jnp.pad(small, ((0, total - count), (0, 0)))], 0
-    )
-    heads = over_experts(heads.reshape(groups, total // groups, width))
-    heads, block_own = pinned(heads, block_own)
-    input_grad = assemble(part_of, gathered_from(input_part, input_far), rows_here, F32)
-    block_out = assemble(part_of, gathered(block_own), rows_here, BF)
-    heads = jnp.sum(heads.astype(F32), 0).astype(BF)
-    heads = lax.all_gather(heads, "expert", axis=0, tiled=True)
-    head_in_grad = jnp.swapaxes(heads[: 3 * cols].reshape(3, cols, width), 1, 2).astype(F32)
-    head_out_grad = heads[3 * cols : 4 * cols].astype(F32)
-    small = heads[4 * cols : count].astype(F32)
+    cols, count = head_out.shape[0], 2 + experts
+    rest = jnp.concatenate([head_out_part, jnp.pad(small, ((0, up_to(count, 16) - count), (0, 0)))], 0)
+    head_in_grad, rest = lax.psum((head_in_part, rest), "expert")
+    head_in_grad = jnp.swapaxes(head_in_grad, 1, 2).astype(F32)
+    head_out_grad = rest[:cols].astype(F32)
+    small = rest[cols : cols + count].astype(F32)
     if paired:
         small = small + cross(small, 1)
         small = small + cross(small, 2)

time: 709 us -> 742 us (1.047)
  waiting for transfers between devices: 219 us -> 261 us
    psum x0 -> x1, waiting for transfers between devices: none -> 34 us  [shards(): head_in_grad, rest = lax.psum((head_in_part, rest), 'expert')]
    ppermute x47, waiting for transfers between devices: 194 us -> 206 us  [cross(): return lax.ppermute(x, 'tensor', [(n, n ^ k) for n in range(parts)])]
    all_to_all x8 -> x7, starting transfers between devices: 40.9 us -> 34.9 us  [over_experts(): return lax.all_to_all(x, 'expert', split_axis=0, concat_axis=0, tiled=True)]
    all_to_all x8 -> x7, waiting for transfers between devices: 25.2 us -> 21.7 us  [over_experts(): return lax.all_to_all(x, 'expert', split_axis=0, concat_axis=0, tiled=True)]
    pallas_call x4 -> x3, Pallas kernels: 56 us -> 53 us  [weight_grad(): pl.pallas_call(functools.partial(weight_kernel, count, steps), grid=(part...]
  transfers between devices with their start and end apart: 56 -> 55, of which waited for: 24 -> 24; matrix products, arithmetic and copies ran while one was open for 8% -> 9% of each run, Pallas kernels for 47% -> 41%
where the time goes in v9:
time: 742 us; the launch traced here: 735 us
  Pallas kernels  324 us (44%)
  waiting for transfers between devices  261 us (35%)
  starting transfers between devices  61.8 us (8%)
  other arithmetic  47.1 us (6%)
  local copies, waits for them, and re-layouts  25.6 us (3%)
  between operations  14.9 us (2%)
    ppermute x47, waiting for transfers between devices, cross(): return lax.ppermute(x, 'tensor', [(n, n ^ k) for n in range(parts)])  206 us
    pallas_call x2, Pallas kernels, expert(): pl.pallas_call(functools.partial(expert_kernel, count, slots, per), grid=...  95.1 us
    pallas_call x3, Pallas kernels, weight_grad(): pl.pallas_call(functools.partial(weight_kernel, count, steps), grid=(part...  53 us
    all_to_all x7, starting transfers between devices, over_experts(): return lax.all_to_all(x, 'expert', split_axis=0, concat_axis=0, tiled=True)  34.9 us
    pallas_call x1, Pallas kernels, attend_back(): pl.pallas_call(functools.partial(attend_back_kernel, count), grid_spec=sp...  34.1 us
    psum x1, waiting for transfers between devices, shards(): head_in_grad, rest = lax.psum((head_in_part, rest), 'expert')  34 us
    pallas_call x2, Pallas kernels, unpack(): pl.pallas_call(functools.partial(unpack_kernel, count, slots, per, graded...  33.6 us
    pallas_call x1, Pallas kernels, attend(): pl.pallas_call(functools.partial(attend_kernel, count), grid_spec=spec, o...  30.3 us
  transfers between devices with their start and end apart: 55, of which 24 were waited for; matrix products, arithmetic and copies ran while one was open for 9% of the time, Pallas kernels for 41%

profile of v9, /device:TPU:0, one launch (start us, length us, event | category | flops | bytes accessed | tf_op | source)
XLA Modules:
  0.0 734.8 jit_solution(1625538254152225415)
XLA Ops:
  7.2 3.0 slice_bitcast_fusion
  10.2 2.9 collective-permute-start
  13.3 2.3 reduce-window.6
  23.3 17.3 %pack_cotangent.1 = bf16[8,2,112,1152]{3,2,1,0:T(8,128)(2,1)} custom-call(bf16[2167,1024]{1,0:T(8,128)(2,1)} %refs_6_.1, bf16[16,1024]{1,0:T(8,128)(2,1)} %pad.26.tail_ref, s32[2,2176]{1,0:T(2,128)} %copy.103.lp_ref, bf16[2,2176,128]{2,1,0:T(8,128)(2,1)} %fusion.5.side_ref), custom_call_target="tpu_custom_call" | custom-call | flops 11978932224 | bytes 4438016 | tf_op jit(solution)/shard_map/pack_cotangent/pallas_call | solution.py:323
  40.7 6.2 all-to-all-start
  50.2 30.3 %attend.1 = (bf16[11,208,1024]{2,1,0:T(8,128)(2,1)}, bf16[3,11,208,256]{3,2,1,0:T(8,128)(2,1)}, f32[11,208,128]{2,1,0:T(8,128)}, bf16[544,256]{1,0:T(8,128)(2,1)...) custom-call(s32[4]{0:T(128)} %get-tuple-element.358.starts_ref, ...), custom_call_target="tpu_custom_call" | custom-call | flops 9596567552 | bytes 35504128 | tf_op jit(solution)/shard_map/attend/pallas_call | solution.py:180
  80.6 2.1 collective-permute-done.2.refs_5_.refs_14_
  88.5 3.8 collective-permute-done.3.refs_1_.refs_10_
  92.3 5.2 collective-permute-done.5.refs_3_.refs_12_
  98.4 6.8 middle.1
  106.2 26.4 %collective-permute-done.8.refs_1_ = bf16[544,1024]{1,0:T(8,128)(2,1)S(1)} collective-permute-done((bf16[544,1024]{1,0:T(8,128)(2,1)}, bf16[544,1024]{1,0:T(8,128)(2,1)S(1)}, u32[]{:S(2)}, u32[]{:S(2)}) %collective-permute-start.8) | collective-permute-done | bytes 1114144 | tf_op jit(solution)/shard_map/ppermute | solution.py:859
  132.6 2.9 collective-permute-done.10.refs_3_
  135.5 2.9 all-to-all-done.g_ref
  140.0 9.9 %pack_rows.2 = bf16[896,1024]{1,0:T(8,128)(2,1)} custom-call(s32[4]{0:T(128)} %get-tuple-element.359.part_ref, bf16[544,1024]{1,0:T(8,128)(2,1)} %get-tuple-element.172.refs_0_.refs_3_, bf16[544,1024]{1,0:T(8,128)(2,1)} %copy-done.27, bf16[544,1024]{1,0:T(8,128)(2,1)} %collective-permute-done.9.refs_2_, bf16[544,1024]{1,0:T(8,128)(2,1)} %collective-permute-done.10.refs_3_, ...), custom_call_target="tpu_custom_call" | custom-call | flops 5989466112 | bytes 4456448 | tf_op jit(solution)/shard_map/pack_rows/pallas_call | solution.py:359
  149.9 3.6 all-to-all-start.1
  154.1 9.9 %pack_rows.3 = bf16[896,1024]{1,0:T(8,128)(2,1)} custom-call(s32[4]{0:T(128)} %get-tuple-element.359.part_ref, bf16[544,1024]{1,0:T(8,128)(2,1)} %get-tuple-element.172.refs_0_.refs_3_, bf16[544,1024]{1,0:T(8,128)(2,1)} %copy-done.27, bf16[544,1024]{1,0:T(8,128)(2,1)} %collective-permute-done.9.refs_2_, bf16[544,1024]{1,0:T(8,128)(2,1)} %collective-permute-done.10.refs_3_, ...), custom_call_target="tpu_custom_call" | custom-call | flops 5989466112 | bytes 4456448 | tf_op jit(solution)/shard_map/pack_rows/pallas_call | solution.py:359
  164.0 20.6 %collective-permute-done.11.refs_9_ = bf16[1024,1024]{1,0:T(8,128)(2,1)} collective-permute-done((bf16[1024,1024]{1,0:T(8,128)(2,1)}, bf16[1024,1024]{1,0:T(8,128)(2,1)}, u32[]{:S(2)}, u32[]{:S(2)}) %collective-permute-start.11) | collective-permute-done | bytes 2097184 | tf_op jit(solution)/shard_map/ppermute | solution.py:859
  185.7 10.4 %all-to-all-done.1 = bf16[8,112,1024]{2,1,0:T(8,128)(2,1)S(1)} async-done(((bf16[8,112,1024]{2,1,0:T(8,128)(2,1)}), bf16[8,112,1024]{2,1,0:T(8,128)(2,1)S(1)}, u32[]{:S(2)}, u32[]{:S(2)}) %all-to-all-start.1) | async-done | bytes 1835040 | tf_op jit(solution)/shard_map/all_to_all | solution.py:896
  197.3 4.3 all-to-all-start.2
  201.7 47.5 %expert.2 = (bf16[896,1024]{1,0:T(8,128)(2,1)}, bf16[896,4096]{1,0:T(8,128)(2,1)}, bf16[896,4096]{1,0:T(8,128)(2,1)}, bf16[896,1024]{1,0:T(8,128)(2,1)}, bf16[896,1024]{1,0:T(8,128)(2,1)}) custom-call(bf16[896,1024]{1,0:T(8,128)(2,1)} %bitcast.56, bf16[8,2,112,1152]{3,2,1,0:T(8,128)(2,1)} %all-to-all-done.g_ref, ...), custom_call_target="tpu_custom_call" | custom-call | flops 30064771072 | bytes 22020096 | tf_op jit(solution)/shard_map/expert/pallas_call | solution.py:763
  249.2 5.9 all-to-all-start.3
  255.1 47.6 %expert.3 = (bf16[896,1024]{1,0:T(8,128)(2,1)}, bf16[896,4096]{1,0:T(8,128)(2,1)}, bf16[896,4096]{1,0:T(8,128)(2,1)}, bf16[896,1024]{1,0:T(8,128)(2,1)}, bf16[896,1024]{1,0:T(8,128)(2,1)}) custom-call(bf16[896,1024]{1,0:T(8,128)(2,1)} %bitcast.21.x_ref.refs_3_, bf16[8,2,112,1152]{3,2,1,0:T(8,128)(2,1)} %all-to-all-done.g_ref, ...), custom_call_target="tpu_custom_call" | custom-call | flops 30064771072 | bytes 22020096 | tf_op jit(solution)/shard_map/expert/pallas_call | solution.py:763
  304.0 6.0 all-to-all-start.4
  310.0 14.0 %weight_grad.4 = (bf16[1024,1024]{1,0:T(8,128)(2,1)}, bf16[1024,1024]{1,0:T(8,128)(2,1)}) custom-call(bf16[896,4096]{1,0:T(8,128)(2,1)} %get-tuple-element.204.refs_0_, bf16[896,1024]{1,0:T(8,128)(2,1)} %get-tuple-element.205.refs_1_, bf16[896,4096]{1,0:T(8,128)(2,1)} %get-tuple-element.206.refs_2_, bf16[896,1024]{1,0:T(8,128)(2,1)} %get-tuple-element.207.refs_3_), custom_call_target="tpu_custom_call" | custom-call | flops 7516192768 | bytes 8388608 | tf_op jit(solution)/shard_map/weight_grad/pallas_call | solution.py:811
  324.5 14.0 %weight_grad.3 = (bf16[1024,1024]{1,0:T(8,128)(2,1)}, bf16[1024,1024]{1,0:T(8,128)(2,1)}) custom-call(bf16[896,4096]{1,0:T(8,128)(2,1)} %get-tuple-element.204.refs_0_, bf16[896,1024]{1,0:T(8,128)(2,1)} %get-tuple-element.205.refs_1_, bf16[896,4096]{1,0:T(8,128)(2,1)} %get-tuple-element.206.refs_2_, bf16[896,1024]{1,0:T(8,128)(2,1)} %get-tuple-element.207.refs_3_), custom_call_target="tpu_custom_call" | custom-call | flops 7516192768 | bytes 8388608 | tf_op jit(solution)/shard_map/weight_grad/pallas_call | solution.py:811
  339.9 3.2 add_convert_fusion.3
  343.1 8.4 %all-to-all-done.4 = bf16[8,112,1024]{2,1,0:T(8,128)(2,1)} async-done(((bf16[8,112,1024]{2,1,0:T(8,128)(2,1)}), bf16[8,112,1024]{2,1,0:T(8,128)(2,1)}, u32[]{:S(2)}, u32[]{:S(2)}) %all-to-all-start.4) | async-done | bytes 1835040 | tf_op jit(solution)/shard_map/all_to_all | solution.py:896
  351.4 17.5 %unpack_rows.2 = (bf16[544,1152]{1,0:T(8,128)(2,1)}, bf16[544,1152]{1,0:T(8,128)(2,1)}, bf16[544,1152]{1,0:T(8,128)(2,1)}, bf16[544,1152]{1,0:T(8,128)(2,1)}) custom-call(s32[4]{0:T(128)} %get-tuple-element.359.part_ref, s32[2176,2]{1,0:T(8,128)} %copy-done.1, bf16[896,1024]{1,0:T(8,128)(2,1)} %bitcast.59, bf16[896,1024]{1,0:T(8,128)(2,1)} %bitcast.25.refs_1_), custom_call_target="tpu_custom_call" | custom-call | flops 11978932224 | bytes 7340032 | tf_op jit(solution)/shard_map/unpack_rows/pallas_call | solution.py:414
  369.5 4.5 add_convert_fusion.2
  374.0 1.5 collective-permute-start.22
  375.5 4.5 all-to-all-start.5
  380.0 2.7 add_convert_fusion.4.refs_0_
  382.7 1.6 add_convert_fusion.5
  384.3 37.6 %collective-permute-done.22 = bf16[1024,1024]{1,0:T(8,128)(2,1)} collective-permute-done((bf16[1024,1024]{1,0:T(8,128)(2,1)}, bf16[1024,1024]{1,0:T(8,128)(2,1)}, u32[]{:S(2)}, u32[]{:S(2)}) %collective-permute-start.22) | collective-permute-done | bytes 2097184 | tf_op jit(solution)/shard_map/ppermute | solution.py:859
  421.9 25.0 %weight_grad.5 = (bf16[1024,1024]{1,0:T(8,128)(2,1)}, bf16[1024,1024]{1,0:T(8,128)(2,1)}, bf16[1024,1024]{1,0:T(8,128)(2,1)}, bf16[1024,1024]{1,0:T(8,128)(2,1)}) custom-call(bf16[896,4096]{1,0:T(8,128)(2,1)} %get-tuple-element.226.refs_0_, bf16[896,1024]{1,0:T(8,128)(2,1)} %bitcast.57, bf16[896,4096]{1,0:T(8,128)(2,1)} %get-tuple-element.227.refs_2_, ...), custom_call_target="tpu_custom_call" | custom-call | flops 15032385536 | bytes 16777216 | tf_op jit(solution)/shard_map/weight_grad/pallas_call | solution.py:811
  448.9 4.3 all-to-all-start.6
  453.3 2.8 copy.107
  456.1 21.0 %collective-permute-done.23.refs_1_ = bf16[544,1152]{1,0:T(8,128)(2,1)} collective-permute-done((bf16[544,1152]{1,0:T(8,128)(2,1)S(1)}, bf16[544,1152]{1,0:T(8,128)(2,1)}, u32[]{:S(2)}, u32[]{:S(2)}) %collective-permute-start.23) | collective-permute-done | bytes 1253408 | tf_op jit(solution)/shard_map/ppermute | solution.py:859
  477.1 12.1 %middle_back.1 = (f32[544,1024]{1,0:T(8,128)}, f32[128,1024]{1,0:T(8,128)}, f32[1,1024]{1,0:T(1,128)}, bf16[256,1024]{1,0:T(8,128)(2,1)}, bf16[256,1024]{1,0:T(8...) custom-call(s32[1]{0:T(128)} %bitcast.4.at_ref, ...), custom_call_target="tpu_custom_call" | custom-call | flops 4563402752 | bytes 22282240 | tf_op jit(solution)/shard_map/middle_back/pallas_call | solution.py:609
  489.2 1.6 collective-permute-start.26
  491.4 4.5 add_convert_fusion.1
  495.9 3.2 collective-permute-done.26.refs_1_
  499.1 3.3 collective-permute-done.28.refs_3_
  503.0 34.1 %attend_back.1 = (bf16[544,1024]{1,0:T(8,128)(2,1)}, bf16[544,1024]{1,0:T(8,128)(2,1)}, bf16[544,1024]{1,0:T(8,128)(2,1)}, bf16[544,1024]{1,0:T(8,128)(2,1)}, bf...) custom-call(s32[4]{0:T(128)} %get-tuple-element.358.starts_ref, bf16[3,11,208,256]{3,2,1,0:T(8,128)(2,1)} %get-tuple-element.167.qkv_ref, ...), custom_call_target="tpu_custom_call" | custom-call | flops 14394851328 | bytes 46858240 | tf_op jit(solution)/shard_map/attend_back/pallas_call | solution.py:286
  539.1 4.3 collective-permute-done.33
  546.5 1.5 add_convert_fusion.9.keep_ref
  549.4 1.7 collective-permute-done.31.b_ref
  551.2 16.1 %unpack_rows.3 = (bf16[544,1024]{1,0:T(8,128)(2,1)}, bf16[544,1024]{1,0:T(8,128)(2,1)}, bf16[544,1024]{1,0:T(8,128)(2,1)}, bf16[544,1024]{1,0:T(8,128)(2,1)}) custom-call(s32[4]{0:T(128)} %get-tuple-element.359.part_ref, s32[2176,2]{1,0:T(8,128)} %copy-done.1, bf16[896,1024]{1,0:T(8,128)(2,1)} %bitcast.27.refs_0_, bf16[896,1024]{1,0:T(8,128)(2,1)} %bitcast.29.refs_1_), custom_call_target="tpu_custom_call" | custom-call | flops 11978932224 | bytes 7340032 | tf_op jit(solution)/shard_map/unpack_rows/pallas_call | solution.py:414
  570.3 1.6 collective-permute-done.37
  571.9 2.7 add_convert_fusion.7
  576.0 19.6 %collective-permute-done.32.far_ref = bf16[544,1024]{1,0:T(8,128)(2,1)} collective-permute-done((bf16[544,1024]{1,0:T(8,128)(2,1)}, bf16[544,1024]{1,0:T(8,128)(2,1)}, u32[]{:S(2)}, u32[]{:S(2)}) %collective-permute-start.32) | collective-permute-done | bytes 1114144 | tf_op jit(solution)/shard_map/ppermute | solution.py:859
  595.6 4.3 input_back.1.refs_0_
  603.1 4.7 convert_add_fusion
  607.8 3.9 add_convert_fusion.a_ref
  611.7 5.2 sum_turned.1
  616.8 2.6 collective-permute-done.39
  619.5 23.0 %collective-permute-done.38.refs_1_ = bf16[544,1024]{1,0:T(8,128)(2,1)} collective-permute-done((bf16[544,1024]{1,0:T(8,128)(2,1)}, bf16[544,1024]{1,0:T(8,128)(2,1)}, u32[]{:S(2)}, u32[]{:S(2)}) %collective-permute-start.38) | collective-permute-done | bytes 1114144 | tf_op jit(solution)/shard_map/ppermute | solution.py:859
  642.5 2.5 add_convert_fusion.6.refs_0_
  646.8 24.0 %collective-permute-done.40.refs_1_ = bf16[544,1024]{1,0:T(8,128)(2,1)S(1)} collective-permute-done((bf16[544,1024]{1,0:T(8,128)(2,1)S(1)}, bf16[544,1024]{1,0:T(8,128)(2,1)S(1)}, u32[]{:S(2)}, u32[]{:S(2)}) %collective-permute-start.40) | collective-permute-done | bytes 1114144 | tf_op jit(solution)/shard_map/ppermute | solution.py:859
  670.8 34.0 %all-reduce.10.cloned.1.call-done = (bf16[3,1024,256]{1,2,0:T(8,128)(2,1)}, bf16[272,1024]{1,0:T(8,128)(2,1)}) async-done(((bf16[3,1024,256]{1,2,0:T(8,128)(2,1)}, bf16[272,1024]{1,0:T(8,128)(2,1)}), (bf16[3,1024,256]{1,2,0:T(8,128)(2,1)}, bf16[272,1024]{1,0:T(8,128)(2,1)})) %all-reduce.10.cloned.1.call-update) | async-done | bytes 2129936 | tf_op jit(solution)/shard_map/psum | solution.py:1043
  709.1 2.1 slice_convert_fusion
  711.2 3.1 copy.110
  715.6 6.7 assemble.3
  722.3 5.4 assemble.2
  (196 shorter events, 51.4 us)
Async XLA Ops:
  10.2 30.4 %collective-permute-start = (bf16[512,1024]{1,0:T(8,128)(2,1)}, bf16[512,1024]{1,0:T(8,128)(2,1)}, u32[]{:S(2)}, u32[]{:S(2)}) collective-permute-start(bf16[512,1024]{1,0:T(8,128)(2,1)} %get-tuple-element.185.refs_0_), channel_id=1, source_target_pairs={{0,2},{1,3},{2,0},{3,1},{4,6},{5,7},{6,4},{7,5},{8,10},{9,11},{10,... | collective-permute-start | bytes 3145736 | tf_op jit(solution)/shard_map/ppermute | solution.py:859
  19.4 119.5 %copy-start.1 = (s32[2176,2]{1,0:T(8,128)}, s32[2176,2]{1,0:T(8,128)S(1)}, u32[]{:S(2)}) copy-start(s32[2176,2]{1,0:T(8,128)S(1)} %get-tuple-element.362.lp_ref) | copy-start | bytes 52228
  40.7 8.3 %slice-start = ((bf16[2167,1024]{1,0:T(8,128)(2,1)}), bf16[7,1024]{1,0:T(8,128)(2,1)S(1)}, s32[]{:S(2)}) async-start(bf16[2167,1024]{1,0:T(8,128)(2,1)} %x_ref.4), calls=%async_computation.8 | async-start | bytes 32768 | tf_op jit(solution)/shard_map/slice | solution.py:902
  40.7 97.7 %all-to-all-start = ((bf16[8,2,112,1152]{3,2,1,0:T(8,128)(2,1)}), bf16[8,2,112,1152]{3,2,1,0:T(8,128)(2,1)}, u32[]{:S(2)}, u32[]{:S(2)}) async-start(bf16[8,2,112,1152]{3,2,1,0:T(8,128)(2,1)} %pack_cotangent.1), calls=%async_computation | async-start | bytes 8257536 | tf_op jit(solution)/shard_map/all_to_all | solution.py:896
  46.9 35.7 %collective-permute-start.1 = (bf16[512,1024]{1,0:T(8,128)(2,1)S(1)}, bf16[512,1024]{1,0:T(8,128)(2,1)}, u32[]{:S(2)}, u32[]{:S(2)}) collective-permute-start(bf16[512,1024]{1,0:T(8,128)(2,1)S(1)} %copy-done.13), channel_id=1, source_target_pairs={{0,2},{1,3},{2,0},{3,1},{4,6},{5,7},{6,4},{7,5},{8,10},{9,11},{10,... | collective-permute-start | bytes 3145736 | tf_op jit(solution)/shard_map/ppermute | solution.py:859
  47.5 35.1 %collective-permute-start.2 = (bf16[256,1024]{1,0:T(8,128)(2,1)S(1)}, bf16[256,1024]{1,0:T(8,128)(2,1)}, u32[]{:S(2)}, u32[]{:S(2)}) collective-permute-start(bf16[256,1024]{1,0:T(8,128)(2,1)S(1)} %copy-done.15), channel_id=1, source_target_pairs={{0,2},{1,3},{2,0},{3,1},{4,6},{5,7},{6,4},{7,5},{8,10},{9,11},{10,... | collective-permute-start | bytes 1572872 | tf_op jit(solution)/shard_map/ppermute | solution.py:859
  49.0 39.6 %collective-permute-start.6 = (bf16[256,1024]{1,0:T(8,128)(2,1)S(1)}, bf16[256,1024]{1,0:T(8,128)(2,1)}, u32[]{:S(2)}, u32[]{:S(2)}) collective-permute-start(bf16[256,1024]{1,0:T(8,128)(2,1)S(1)} %copy-done.15), channel_id=1, source_target_pairs={{0,1},{1,0},{2,3},{3,2},{4,5},{5,4},{6,7},{7,6},{8,9},{9,8},{10,11... | collective-permute-start | bytes 1572872 | tf_op jit(solution)/shard_map/ppermute | solution.py:859
  82.6 14.9 %collective-permute-start.7 = (bf16[256,1024]{1,0:T(8,128)(2,1)}, bf16[256,1024]{1,0:T(8,128)(2,1)S(1)}, u32[]{:S(2)}, u32[]{:S(2)}) collective-permute-start(bf16[256,1024]{1,0:T(8,128)(2,1)} %collective-permute-done.2.refs_5_.refs_14_), channel_id=1, source_target_pairs={{0,1},{1,0},{2,3},{3,2},{4,5},{5,4},{6,7},{7,6},{8,9},{9,8},{10,11... | collective-permute-start | bytes 1572872 | tf_op jit(solution)/shard_map/ppermute | solution.py:859
  82.7 9.7 %collective-permute-start.3 = (bf16[544,256]{1,0:T(8,128)(2,1)}, bf16[544,256]{1,0:T(8,128)(2,1)S(1)}, u32[]{:S(2)}, u32[]{:S(2)}) collective-permute-start(bf16[544,256]{1,0:T(8,128)(2,1)} %get-tuple-element.162), channel_id=1, source_target_pairs={{0,2},{1,3},{2,0},{3,1},{4,6},{5,7},{6,4},{7,5},{8,10},{9,11},{10,... | collective-permute-start | bytes 835592 | tf_op jit(solution)/shard_map/ppermute | solution.py:859
  83.2 9.1 %collective-permute-start.4 = (bf16[544,256]{1,0:T(8,128)(2,1)}, bf16[544,256]{1,0:T(8,128)(2,1)S(1)}, u32[]{:S(2)}, u32[]{:S(2)}) collective-permute-start(bf16[544,256]{1,0:T(8,128)(2,1)} %get-tuple-element.163), channel_id=1, source_target_pairs={{0,1},{1,0},{2,3},{3,2},{4,5},{5,4},{6,7},{7,6},{8,9},{9,8},{10,11... | collective-permute-start | bytes 835592 | tf_op jit(solution)/shard_map/ppermute | solution.py:859
  83.4 14.1 %collective-permute-start.5 = (bf16[544,256]{1,0:T(8,128)(2,1)}, bf16[544,256]{1,0:T(8,128)(2,1)S(1)}, u32[]{:S(2)}, u32[]{:S(2)}) collective-permute-start(bf16[544,256]{1,0:T(8,128)(2,1)} %get-tuple-element.164), channel_id=1, source_target_pairs={{0,3},{1,2},{2,1},{3,0},{4,7},{5,6},{6,5},{7,4},{8,11},{9,10},{10,... | collective-permute-start | bytes 835592 | tf_op jit(solution)/shard_map/ppermute | solution.py:859
  105.3 27.3 %collective-permute-start.8 = (bf16[544,1024]{1,0:T(8,128)(2,1)}, bf16[544,1024]{1,0:T(8,128)(2,1)S(1)}, u32[]{:S(2)}, u32[]{:S(2)}) collective-permute-start(bf16[544,1024]{1,0:T(8,128)(2,1)} %get-tuple-element.172.refs_0_.refs_3_), channel_id=1, source_target_pairs={{0,2},{1,3},{2,0},{3,1},{4,6},{5,7},{6,4},{7,5},{8,10},{9,11},{10,... | collective-permute-start | bytes 3342344 | tf_op jit(solution)/shard_map/ppermute | solution.py:859
  105.9 26.8 %collective-permute-start.9 = (bf16[544,1024]{1,0:T(8,128)(2,1)}, bf16[544,1024]{1,0:T(8,128)(2,1)}, u32[]{:S(2)}, u32[]{:S(2)}) collective-permute-start(bf16[544,1024]{1,0:T(8,128)(2,1)} %get-tuple-element.172.refs_0_.refs_3_), channel_id=1, source_target_pairs={{0,1},{1,0},{2,3},{3,2},{4,5},{5,4},{6,7},{7,6},{8,9},{9,8},{10,11... | collective-permute-start | bytes 3342344 | tf_op jit(solution)/shard_map/ppermute | solution.py:859
  132.6 2.9 collective-permute-start.10
  138.4 46.2 %collective-permute-start.11 = (bf16[1024,1024]{1,0:T(8,128)(2,1)}, bf16[1024,1024]{1,0:T(8,128)(2,1)}, u32[]{:S(2)}, u32[]{:S(2)}) collective-permute-start(bf16[1024,1024]{1,0:T(8,128)(2,1)} %bitcast.77), channel_id=1, source_target_pairs={{0,2},{1,3},{2,0},{3,1},{4,6},{5,7},{6,4},{7,5},{8,10},{9,11},{10,... | collective-permute-start | bytes 6291464 | tf_op jit(solution)/shard_map/ppermute | solution.py:859
  149.9 46.2 %all-to-all-start.1 = ((bf16[8,112,1024]{2,1,0:T(8,128)(2,1)}), bf16[8,112,1024]{2,1,0:T(8,128)(2,1)S(1)}, u32[]{:S(2)}, u32[]{:S(2)}) async-start(bf16[8,112,1024]{2,1,0:T(8,128)(2,1)} %bitcast.62), calls=%async_computation.1 | async-start | bytes 3670016 | tf_op jit(solution)/shard_map/all_to_all | solution.py:896
  153.5 31.1 %copy-start.14 = (bf16[512,1024]{1,0:T(8,128)(2,1)S(1)}, bf16[512,1024]{1,0:T(8,128)(2,1)}, u32[]{:S(2)}) copy-start(bf16[512,1024]{1,0:T(8,128)(2,1)} %get-tuple-element.186.refs_1_) | copy-start | bytes 3145732
  153.5 31.6 %collective-permute-start.12 = (bf16[512,1024]{1,0:T(8,128)(2,1)}, bf16[512,1024]{1,0:T(8,128)(2,1)}, u32[]{:S(2)}, u32[]{:S(2)}) collective-permute-start(bf16[512,1024]{1,0:T(8,128)(2,1)} %get-tuple-element.185.refs_0_), channel_id=1, source_target_pairs={{0,1},{1,0},{2,3},{3,2},{4,5},{5,4},{6,7},{7,6},{8,9},{9,8},{10,11... | collective-permute-start | bytes 3145736 | tf_op jit(solution)/shard_map/ppermute | solution.py:859
  153.6 48.0 %collective-permute-start.16 = (bf16[1024,1024]{1,0:T(8,128)(2,1)}, bf16[1024,1024]{1,0:T(8,128)(2,1)}, u32[]{:S(2)}, u32[]{:S(2)}) collective-permute-start(bf16[1024,1024]{1,0:T(8,128)(2,1)} %bitcast.78), channel_id=1, source_target_pairs={{0,1},{1,0},{2,3},{3,2},{4,5},{5,4},{6,7},{7,6},{8,9},{9,8},{10,11... | collective-permute-start | bytes 6291464 | tf_op jit(solution)/shard_map/ppermute | solution.py:859
  184.7 17.0 %collective-permute-start.17 = (bf16[1024,1024]{1,0:T(8,128)(2,1)}, bf16[1024,1024]{1,0:T(8,128)(2,1)}, u32[]{:S(2)}, u32[]{:S(2)}) collective-permute-start(bf16[1024,1024]{1,0:T(8,128)(2,1)} %collective-permute-done.11.refs_9_), channel_id=1, source_target_pairs={{0,1},{1,0},{2,3},{3,2},{4,5},{5,4},{6,7},{7,6},{8,9},{9,8},{10,11... | collective-permute-start | bytes 6291464 | tf_op jit(solution)/shard_map/ppermute | solution.py:859
  184.7 17.0 %collective-permute-start.13 = (bf16[512,1024]{1,0:T(8,128)(2,1)S(1)}, bf16[512,1024]{1,0:T(8,128)(2,1)}, u32[]{:S(2)}, u32[]{:S(2)}) collective-permute-start(bf16[512,1024]{1,0:T(8,128)(2,1)S(1)} %copy-done.14), channel_id=1, source_target_pairs={{0,1},{1,0},{2,3},{3,2},{4,5},{5,4},{6,7},{7,6},{8,9},{9,8},{10,11... | collective-permute-start | bytes 3145736 | tf_op jit(solution)/shard_map/ppermute | solution.py:859
  185.2 16.5 %collective-permute-start.15 = (bf16[512,1024]{1,0:T(8,128)(2,1)}, bf16[512,1024]{1,0:T(8,128)(2,1)}, u32[]{:S(2)}, u32[]{:S(2)}) collective-permute-start(bf16[512,1024]{1,0:T(8,128)(2,1)} %collective-permute-done.1.refs_3_), channel_id=1, source_target_pairs={{0,1},{1,0},{2,3},{3,2},{4,5},{5,4},{6,7},{7,6},{8,9},{9,8},{10,11... | collective-permute-start | bytes 3145736 | tf_op jit(solution)/shard_map/ppermute | solution.py:859
  185.2 16.5 %collective-permute-start.14 = (bf16[512,1024]{1,0:T(8,128)(2,1)}, bf16[512,1024]{1,0:T(8,128)(2,1)}, u32[]{:S(2)}, u32[]{:S(2)}) collective-permute-start(bf16[512,1024]{1,0:T(8,128)(2,1)} %collective-permute-done.refs_2_), channel_id=1, source_target_pairs={{0,1},{1,0},{2,3},{3,2},{4,5},{5,4},{6,7},{7,6},{8,9},{9,8},{10,11... | collective-permute-start | bytes 3145736 | tf_op jit(solution)/shard_map/ppermute | solution.py:859
  197.3 51.9 %all-to-all-start.2 = ((bf16[8,112,1024]{2,1,0:T(8,128)(2,1)}), bf16[8,112,1024]{2,1,0:T(8,128)(2,1)}, u32[]{:S(2)}, u32[]{:S(2)}) async-start(bf16[8,112,1024]{2,1,0:T(8,128)(2,1)} %bitcast.60), calls=%async_computation.2 | async-start | bytes 3670016 | tf_op jit(solution)/shard_map/all_to_all | solution.py:896
  249.2 53.5 %all-to-all-start.3 = ((bf16[8,112,1024]{2,1,0:T(8,128)(2,1)}), bf16[8,112,1024]{2,1,0:T(8,128)(2,1)S(1)}, u32[]{:S(2)}, u32[]{:S(2)}) async-start(bf16[8,112,1024]{2,1,0:T(8,128)(2,1)} %bitcast.63), calls=%async_computation.3 | async-start | bytes 3670016 | tf_op jit(solution)/shard_map/all_to_all | solution.py:896
  304.0 47.4 %all-to-all-start.4 = ((bf16[8,112,1024]{2,1,0:T(8,128)(2,1)}), bf16[8,112,1024]{2,1,0:T(8,128)(2,1)}, u32[]{:S(2)}, u32[]{:S(2)}) async-start(bf16[8,112,1024]{2,1,0:T(8,128)(2,1)} %bitcast.61), calls=%async_computation.4 | async-start | bytes 3670016 | tf_op jit(solution)/shard_map/all_to_all | solution.py:896
  324.0 14.5 %collective-permute-start.18 = (bf16[1024,1024]{1,0:T(8,128)(2,1)}, bf16[1024,1024]{1,0:T(8,128)(2,1)}, u32[]{:S(2)}, u32[]{:S(2)}) collective-permute-start(bf16[1024,1024]{1,0:T(8,128)(2,1)} %get-tuple-element.209), channel_id=1, source_target_pairs={{0,1},{1,0},{2,3},{3,2},{4,5},{5,4},{6,7},{7,6},{8,9},{9,8},{10,11... | collective-permute-start | bytes 6291464 | tf_op jit(solution)/shard_map/ppermute | solution.py:859
  324.0 14.5 %collective-permute-start.19 = (bf16[1024,1024]{1,0:T(8,128)(2,1)}, bf16[1024,1024]{1,0:T(8,128)(2,1)S(1)}, u32[]{:S(2)}, u32[]{:S(2)}) collective-permute-start(bf16[1024,1024]{1,0:T(8,128)(2,1)} %get-tuple-element.210), channel_id=1, source_target_pairs={{0,1},{1,0},{2,3},{3,2},{4,5},{5,4},{6,7},{7,6},{8,9},{9,8},{10,11... | collective-permute-start | bytes 6291464 | tf_op jit(solution)/shard_map/ppermute | solution.py:859
  368.9 11.0 %collective-permute-start.20 = (bf16[544,1152]{1,0:T(8,128)(2,1)}, bf16[544,1152]{1,0:T(8,128)(2,1)}, u32[]{:S(2)}, u32[]{:S(2)}) collective-permute-start(bf16[544,1152]{1,0:T(8,128)(2,1)} %get-tuple-element.215), channel_id=1, source_target_pairs={{0,1},{1,0},{2,3},{3,2},{4,5},{5,4},{6,7},{7,6},{8,9},{9,8},{10,11... | collective-permute-start | bytes 3760136 | tf_op jit(solution)/shard_map/ppermute | solution.py:859
  368.9 11.0 %collective-permute-start.21 = (bf16[544,1152]{1,0:T(8,128)(2,1)}, bf16[544,1152]{1,0:T(8,128)(2,1)}, u32[]{:S(2)}, u32[]{:S(2)}) collective-permute-start(bf16[544,1152]{1,0:T(8,128)(2,1)} %get-tuple-element.216), channel_id=1, source_target_pairs={{0,1},{1,0},{2,3},{3,2},{4,5},{5,4},{6,7},{7,6},{8,9},{9,8},{10,11... | collective-permute-start | bytes 3760136 | tf_op jit(solution)/shard_map/ppermute | solution.py:859
  374.0 47.9 %collective-permute-start.22 = (bf16[1024,1024]{1,0:T(8,128)(2,1)}, bf16[1024,1024]{1,0:T(8,128)(2,1)}, u32[]{:S(2)}, u32[]{:S(2)}) collective-permute-start(bf16[1024,1024]{1,0:T(8,128)(2,1)} %add_convert_fusion.2), channel_id=1, source_target_pairs={{0,2},{1,3},{2,0},{3,1},{4,6},{5,7},{6,4},{7,5},{8,10},{9,11},{10,... | collective-permute-start | bytes 6291464 | tf_op jit(solution)/shard_map/ppermute | solution.py:859
  375.5 73.5 %all-to-all-start.5 = ((bf16[8,112,1024]{2,1,0:T(8,128)(2,1)}), bf16[8,112,1024]{2,1,0:T(8,128)(2,1)}, u32[]{:S(2)}, u32[]{:S(2)}) async-start(bf16[8,112,1024]{2,1,0:T(8,128)(2,1)} %bitcast.58), calls=%async_computation.5 | async-start | bytes 3670016 | tf_op jit(solution)/shard_map/all_to_all | solution.py:896
  446.9 42.3 %collective-permute-start.24 = (bf16[1024,1024]{1,0:T(8,128)(2,1)}, bf16[1024,1024]{1,0:T(8,128)(2,1)}, u32[]{:S(2)}, u32[]{:S(2)}) collective-permute-start(bf16[1024,1024]{1,0:T(8,128)(2,1)} %get-tuple-element.230), channel_id=1, source_target_pairs={{0,1},{1,0},{2,3},{3,2},{4,5},{5,4},{6,7},{7,6},{8,9},{9,8},{10,11... | collective-permute-start | bytes 6291464 | tf_op jit(solution)/shard_map/ppermute | solution.py:859
  446.9 42.3 %collective-permute-start.25 = (bf16[1024,1024]{1,0:T(8,128)(2,1)}, bf16[1024,1024]{1,0:T(8,128)(2,1)}, u32[]{:S(2)}, u32[]{:S(2)}) collective-permute-start(bf16[1024,1024]{1,0:T(8,128)(2,1)} %get-tuple-element.231), channel_id=1, source_target_pairs={{0,1},{1,0},{2,3},{3,2},{4,5},{5,4},{6,7},{7,6},{8,9},{9,8},{10,11... | collective-permute-start | bytes 6291464 | tf_op jit(solution)/shard_map/ppermute | solution.py:859
  447.4 29.6 %collective-permute-start.23 = (bf16[544,1152]{1,0:T(8,128)(2,1)S(1)}, bf16[544,1152]{1,0:T(8,128)(2,1)}, u32[]{:S(2)}, u32[]{:S(2)}) collective-permute-start(bf16[544,1152]{1,0:T(8,128)(2,1)S(1)} %add_convert_fusion.5), channel_id=1, source_target_pairs={{0,2},{1,3},{2,0},{3,1},{4,6},{5,7},{6,4},{7,5},{8,10},{9,11},{10,... | collective-permute-start | bytes 3760136 | tf_op jit(solution)/shard_map/ppermute | solution.py:859
  448.9 88.2 %all-to-all-start.6 = ((bf16[8,112,1024]{2,1,0:T(8,128)(2,1)}), bf16[8,112,1024]{2,1,0:T(8,128)(2,1)}, u32[]{:S(2)}, u32[]{:S(2)}) async-start(bf16[8,112,1024]{2,1,0:T(8,128)(2,1)} %bitcast.55), calls=%async_computation.6 | async-start | bytes 3670016 | tf_op jit(solution)/shard_map/all_to_all | solution.py:896
  453.3 251.6 %all-reduce.10.cloned.1.call-start = ((), (), s32[]{:S(2)}) async-start(), calls=%async_computation.7 | async-start | bytes 4259840 | tf_op jit(solution)/shard_map/psum | solution.py:1043
  489.2 9.9 %collective-permute-start.26 = (bf16[544,256]{1,0:T(8,128)(2,1)}, bf16[544,256]{1,0:T(8,128)(2,1)S(1)}, u32[]{:S(2)}, u32[]{:S(2)}) collective-permute-start(bf16[544,256]{1,0:T(8,128)(2,1)} %get-tuple-element.246), channel_id=1, source_target_pairs={{0,2},{1,3},{2,0},{3,1},{4,6},{5,7},{6,4},{7,5},{8,10},{9,11},{10,... | collective-permute-start | bytes 835592 | tf_op jit(solution)/shard_map/ppermute | solution.py:859
  490.8 8.3 %collective-permute-start.27 = (bf16[544,256]{1,0:T(8,128)(2,1)}, bf16[544,256]{1,0:T(8,128)(2,1)S(1)}, u32[]{:S(2)}, u32[]{:S(2)}) collective-permute-start(bf16[544,256]{1,0:T(8,128)(2,1)} %get-tuple-element.247), channel_id=1, source_target_pairs={{0,1},{1,0},{2,3},{3,2},{4,5},{5,4},{6,7},{7,6},{8,9},{9,8},{10,11... | collective-permute-start | bytes 835592 | tf_op jit(solution)/shard_map/ppermute | solution.py:859
  490.8 11.6 %collective-permute-start.28 = (bf16[544,256]{1,0:T(8,128)(2,1)}, bf16[544,256]{1,0:T(8,128)(2,1)S(1)}, u32[]{:S(2)}, u32[]{:S(2)}) collective-permute-start(bf16[544,256]{1,0:T(8,128)(2,1)} %get-tuple-element.248), channel_id=1, source_target_pairs={{0,3},{1,2},{2,1},{3,0},{4,7},{5,6},{6,5},{7,4},{8,11},{9,10},{10,... | collective-permute-start | bytes 835592 | tf_op jit(solution)/shard_map/ppermute | solution.py:859
  502.3 48.8 %collective-permute-start.31 = (bf16[1024,1024]{1,0:T(8,128)(2,1)}, bf16[1024,1024]{1,0:T(8,128)(2,1)}, u32[]{:S(2)}, u32[]{:S(2)}) collective-permute-start(bf16[1024,1024]{1,0:T(8,128)(2,1)} %add_convert_fusion.1), channel_id=1, source_target_pairs={{0,2},{1,3},{2,0},{3,1},{4,6},{5,7},{6,4},{7,5},{8,10},{9,11},{10,... | collective-permute-start | bytes 6291464 | tf_op jit(solution)/shard_map/ppermute | solution.py:859
  537.1 9.3 %copy-start.11 = (bf16[544,1024]{1,0:T(8,128)(2,1)S(1)}, bf16[544,1024]{1,0:T(8,128)(2,1)}, u32[]{:S(2)}) copy-start(bf16[544,1024]{1,0:T(8,128)(2,1)} %get-tuple-element.258) | copy-start | bytes 3342340
  537.2 9.3 %collective-permute-start.29 = (bf16[544,1024]{1,0:T(8,128)(2,1)}, bf16[544,1024]{1,0:T(8,128)(2,1)S(1)}, u32[]{:S(2)}, u32[]{:S(2)}) collective-permute-start(bf16[544,1024]{1,0:T(8,128)(2,1)} %get-tuple-element.255), channel_id=1, source_target_pairs={{0,1},{1,0},{2,3},{3,2},{4,5},{5,4},{6,7},{7,6},{8,9},{9,8},{10,11... | collective-permute-start | bytes 3342344 | tf_op jit(solution)/shard_map/ppermute | solution.py:859
  538.5 8.0 %collective-permute-start.30 = (bf16[544,1024]{1,0:T(8,128)(2,1)}, bf16[544,1024]{1,0:T(8,128)(2,1)S(1)}, u32[]{:S(2)}, u32[]{:S(2)}) collective-permute-start(bf16[544,1024]{1,0:T(8,128)(2,1)} %get-tuple-element.256), channel_id=1, source_target_pairs={{0,1},{1,0},{2,3},{3,2},{4,5},{5,4},{6,7},{7,6},{8,9},{9,8},{10,11... | collective-permute-start | bytes 3342344 | tf_op jit(solution)/shard_map/ppermute | solution.py:859
  538.5 4.9 collective-permute-start.33
  539.0 5.2 collective-permute-start.34
  545.4 21.9 %collective-permute-start.35 = (bf16[256,1024]{1,0:T(8,128)(2,1)S(1)}, bf16[256,1024]{1,0:T(8,128)(2,1)}, u32[]{:S(2)}, u32[]{:S(2)}) collective-permute-start(bf16[256,1024]{1,0:T(8,128)(2,1)S(1)} %add_convert_fusion.13), channel_id=1, source_target_pairs={{0,2},{1,3},{2,0},{3,1},{4,6},{5,7},{6,4},{7,5},{8,10},{9,11},{10,... | collective-permute-start | bytes 1572872 | tf_op jit(solution)/shard_map/ppermute | solution.py:859
  551.2 18.3 %copy-start.25 = (f32[1,1024]{1,0:T(1,128)S(1)}, f32[1,1024]{1,0:T(1,128)}, u32[]{:S(2)}) copy-start(f32[1,1024]{1,0:T(1,128)} %get-tuple-element.298) | copy-start | bytes 12292
  551.2 18.3 %copy-start.26 = (f32[1,1024]{1,0:T(1,128)S(1)}, f32[1,1024]{1,0:T(1,128)}, u32[]{:S(2)}) copy-start(f32[1,1024]{1,0:T(1,128)} %get-tuple-element.297) | copy-start | bytes 12292
  567.3 3.0 collective-permute-start.36
  567.4 4.5 collective-permute-start.37
  567.9 27.7 %collective-permute-start.32 = (bf16[544,1024]{1,0:T(8,128)(2,1)}, bf16[544,1024]{1,0:T(8,128)(2,1)}, u32[]{:S(2)}, u32[]{:S(2)}) collective-permute-start(bf16[544,1024]{1,0:T(8,128)(2,1)} %add_convert_fusion.10), channel_id=1, source_target_pairs={{0,2},{1,3},{2,0},{3,1},{4,6},{5,7},{6,4},{7,5},{8,10},{9,11},{10,... | collective-permute-start | bytes 3342344 | tf_op jit(solution)/shard_map/ppermute | solution.py:859
  574.6 44.9 %collective-permute-start.39 = (bf16[544,1024]{1,0:T(8,128)(2,1)}, bf16[544,1024]{1,0:T(8,128)(2,1)}, u32[]{:S(2)}, u32[]{:S(2)}) collective-permute-start(bf16[544,1024]{1,0:T(8,128)(2,1)} %add_convert_fusion.7), channel_id=1, source_target_pairs={{0,2},{1,3},{2,0},{3,1},{4,6},{5,7},{6,4},{7,5},{8,10},{9,11},{10,... | collective-permute-start | bytes 3342344 | tf_op jit(solution)/shard_map/ppermute | solution.py:859
  600.0 42.5 %collective-permute-start.38 = (bf16[544,1024]{1,0:T(8,128)(2,1)}, bf16[544,1024]{1,0:T(8,128)(2,1)}, u32[]{:S(2)}, u32[]{:S(2)}) collective-permute-start(bf16[544,1024]{1,0:T(8,128)(2,1)} %input_back.1.refs_0_), channel_id=1, source_target_pairs={{0,2},{1,3},{2,0},{3,1},{4,6},{5,7},{6,4},{7,5},{8,10},{9,11},{10,... | collective-permute-start | bytes 3342344 | tf_op jit(solution)/shard_map/ppermute | solution.py:859
  616.8 29.5 %copy-start.2 = (bf16[544,1024]{1,0:T(8,128)(2,1)S(1)}, bf16[544,1024]{1,0:T(8,128)(2,1)}, u32[]{:S(2)}) copy-start(bf16[544,1024]{1,0:T(8,128)(2,1)} %input_back.1.refs_0_) | copy-start | bytes 3342340
  645.0 69.3 %copy-start = (bf16[544,1024]{1,0:T(8,128)(2,1)}, bf16[544,1024]{1,0:T(8,128)(2,1)S(1)}, u32[]{:S(2)}) copy-start(bf16[544,1024]{1,0:T(8,128)(2,1)S(1)} %add_convert_fusion.6.refs_0_) | copy-start | bytes 3342340
  645.0 25.8 %collective-permute-start.40 = (bf16[544,1024]{1,0:T(8,128)(2,1)S(1)}, bf16[544,1024]{1,0:T(8,128)(2,1)S(1)}, u32[]{:S(2)}, u32[]{:S(2)}) collective-permute-start(bf16[544,1024]{1,0:T(8,128)(2,1)S(1)} %add_convert_fusion.6.refs_0_), channel_id=1, source_target_pairs={{0,2},{1,3},{2,0},{3,1},{4,6},{5,7},{6,4},{7,5},{8,10},{9,11},{10,... | collective-permute-start | bytes 3342344 | tf_op jit(solution)/shard_map/ppermute | solution.py:859
  646.3 69.2 %collective-permute-start.43 = (bf16[544,1024]{1,0:T(8,128)(2,1)S(1)}, bf16[544,1024]{1,0:T(8,128)(2,1)}, u32[]{:S(2)}, u32[]{:S(2)}) collective-permute-start(bf16[544,1024]{1,0:T(8,128)(2,1)S(1)} %copy-done.2), channel_id=1, source_target_pairs={{0,1},{1,0},{2,3},{3,2},{4,5},{5,4},{6,7},{7,6},{8,9},{9,8},{10,11... | collective-permute-start | bytes 3342344 | tf_op jit(solution)/shard_map/ppermute | solution.py:859
  646.3 75.9 %collective-permute-start.41 = (bf16[544,1024]{1,0:T(8,128)(2,1)S(1)}, bf16[544,1024]{1,0:T(8,128)(2,1)}, u32[]{:S(2)}, u32[]{:S(2)}) collective-permute-start(bf16[544,1024]{1,0:T(8,128)(2,1)S(1)} %add_convert_fusion.6.refs_0_), channel_id=1, source_target_pairs={{0,1},{1,0},{2,3},{3,2},{4,5},{5,4},{6,7},{7,6},{8,9},{9,8},{10,11... | collective-permute-start | bytes 3342344 | tf_op jit(solution)/shard_map/ppermute | solution.py:859
  646.8 68.7 %collective-permute-start.44 = (bf16[544,1024]{1,0:T(8,128)(2,1)}, bf16[544,1024]{1,0:T(8,128)(2,1)}, u32[]{:S(2)}, u32[]{:S(2)}) collective-permute-start(bf16[544,1024]{1,0:T(8,128)(2,1)} %collective-permute-done.38.refs_1_), channel_id=1, source_target_pairs={{0,1},{1,0},{2,3},{3,2},{4,5},{5,4},{6,7},{7,6},{8,9},{9,8},{10,11... | collective-permute-start | bytes 3342344 | tf_op jit(solution)/shard_map/ppermute | solution.py:859
  670.8 43.5 %copy-start.9 = (bf16[544,1024]{1,0:T(8,128)(2,1)}, bf16[544,1024]{1,0:T(8,128)(2,1)S(1)}, u32[]{:S(2)}) copy-start(bf16[544,1024]{1,0:T(8,128)(2,1)S(1)} %collective-permute-done.40.refs_1_) | copy-start | bytes 3342340
  670.8 51.4 %collective-permute-start.42 = (bf16[544,1024]{1,0:T(8,128)(2,1)S(1)}, bf16[544,1024]{1,0:T(8,128)(2,1)}, u32[]{:S(2)}, u32[]{:S(2)}) collective-permute-start(bf16[544,1024]{1,0:T(8,128)(2,1)S(1)} %collective-permute-done.40.refs_1_), channel_id=1, source_target_pairs={{0,1},{1,0},{2,3},{3,2},{4,5},{5,4},{6,7},{7,6},{8,9},{9,8},{10,11... | collective-permute-start | bytes 3342344 | tf_op jit(solution)/shard_map/ppermute | solution.py:859
  705.6 1.3 collective-permute-start.45
  707.6 6.7 collective-permute-start.46
  (24 other events, 92.0 us)
Sparse Core Ops, SparseCore 0:
  603.2 101.5 all-reduce.9

commit v10 on v5

--- a/solution.py
+++ b/solution.py
@@ -1009,16 +1009,22 @@
     *pieces, head_in_part, norm_one_part = attend_back(
         starts, mixed_grad, qkv, logs, first_in, jnp.swapaxes(head_in, 1, 2), gain_one
     )
-    *pieces, combined[-1], in_far, head_out_far = pinned(*pieces, combined[-1], in_far, head_out_far)
-    first_kept, first_far = scattered(pieces)
+    *pieces, combined[-1] = pinned(*pieces, combined[-1])
+    first_kept, first_other = near_sum(pieces, near_hop(pieces))
+    if paired:
+        first_other, first_kept, in_far, head_in_part, *combined = pinned(
+            first_other, first_kept, in_far, head_in_part, *combined
+        )
+    first_far = far_hop(first_kept, first_other)
     block_pieces = unpack(part_of, place, combined, slots, per, each, False)
+    *block_pieces, head_out_far = pinned(*block_pieces, head_out_far)
     block_kept, block_other = near_sum(block_pieces, near_hop(block_pieces))
     first_far, block_kept = pinned(first_far, block_kept)
     block_far = far_hop(block_kept, block_other)
     input_part = input_back(own_block, first_kept, first_far, block_in, middle_grad, gain_one)
     out_grad = out_kept.astype(F32) + out_far.astype(F32)
     in_grad = sum_turned(in_kept, in_far)
-    input_far, out_grad, in_grad = pinned(far_part(input_part), out_grad, in_grad)
+    input_far, out_grad, in_grad, block_far = pinned(far_part(input_part), out_grad, in_grad, block_far)
     block_own = (middle + block_kept.astype(F32) + block_far.astype(F32)).astype(BF)
 
     cols = head_in.shape[2]

time: 709 us -> 712 us (level)
    ppermute x47, waiting for transfers between devices: 194 us -> 167 us  [cross(): return lax.ppermute(x, 'tensor', [(n, n ^ k) for n in range(parts)])]
    all_gather x1, waiting for transfers between devices: 0.01 us -> 26.9 us  [shards(): heads = lax.all_gather(heads, 'expert', axis=0, tiled=True)]
    unnamed x81 -> x73, local copies, waits for them, and re-layouts: 13.3 us -> 14.7 us
  transfers between devices with their start and end apart: 56 -> 56, of which waited for: 24 -> 24; matrix products, arithmetic and copies ran while one was open for 8% -> 9% of each run, Pallas kernels for 47% -> 46%
where the time goes in v10:
time: 712 us; the launch traced here: 705 us
  Pallas kernels  327 us (46%)
  waiting for transfers between devices  219 us (31%)
  starting transfers between devices  66 us (9%)
  other arithmetic  47.7 us (7%)
  local copies, waits for them, and re-layouts  30.1 us (4%)
  between operations  15 us (2%)
    ppermute x47, waiting for transfers between devices, cross(): return lax.ppermute(x, 'tensor', [(n, n ^ k) for n in range(parts)])  167 us
    pallas_call x2, Pallas kernels, expert(): pl.pallas_call(functools.partial(expert_kernel, count, slots, per), grid=...  95.1 us
    pallas_call x4, Pallas kernels, weight_grad(): pl.pallas_call(functools.partial(weight_kernel, count, steps), grid=(2 *...  56 us
    all_to_all x8, starting transfers between devices, over_experts(): return lax.all_to_all(x, 'expert', split_axis=0, concat_axis=0, tiled=True)  40.9 us
    pallas_call x1, Pallas kernels, attend_back(): pl.pallas_call(functools.partial(attend_back_kernel, count), grid_spec=sp...  34.5 us
    pallas_call x2, Pallas kernels, unpack(): pl.pallas_call(functools.partial(unpack_kernel, count, slots, per, graded...  33.4 us
    pallas_call x1, Pallas kernels, attend(): pl.pallas_call(functools.partial(attend_kernel, count), grid_spec=spec, o...  30.4 us
    all_gather x1, waiting for transfers between devices, shards(): heads = lax.all_gather(heads, 'expert', axis=0, tiled=True)  26.9 us
  transfers between devices with their start and end apart: 56, of which 24 were waited for; matrix products, arithmetic and copies ran while one was open for 9% of the time, Pallas kernels for 46%

profile of v10, /device:TPU:0, one launch (start us, length us, event | category | flops | bytes accessed | tf_op | source)
XLA Modules:
  0.0 705.1 jit_solution(7528791146077659859)
XLA Ops:
  7.2 3.1 slice_bitcast_fusion
  10.2 2.9 collective-permute-start
  13.3 2.3 reduce-window.6
  23.3 17.3 %pack_cotangent.1 = bf16[8,2,112,1152]{3,2,1,0:T(8,128)(2,1)} custom-call(bf16[2167,1024]{1,0:T(8,128)(2,1)} %refs_6_.1, bf16[16,1024]{1,0:T(8,128)(2,1)} %pad.26.tail_ref, s32[2,2176]{1,0:T(2,128)} %copy.103.lp_ref, bf16[2,2176,128]{2,1,0:T(8,128)(2,1)} %fusion.5.side_ref), custom_call_target="tpu_custom_call" | custom-call | flops 11978932224 | bytes 4438016 | tf_op jit(solution)/shard_map/pack_cotangent/pallas_call | solution.py:323
  40.7 6.2 all-to-all-start
  50.3 30.4 %attend.1 = (bf16[11,208,1024]{2,1,0:T(8,128)(2,1)}, bf16[3,11,208,256]{3,2,1,0:T(8,128)(2,1)}, f32[11,208,128]{2,1,0:T(8,128)}, bf16[544,256]{1,0:T(8,128)(2,1)...) custom-call(s32[4]{0:T(128)} %get-tuple-element.311.starts_ref, ...), custom_call_target="tpu_custom_call" | custom-call | flops 9596567552 | bytes 35504128 | tf_op jit(solution)/shard_map/attend/pallas_call | solution.py:180
  80.7 2.0 collective-permute-done.2.refs_5_.refs_14_
  88.6 3.7 collective-permute-done.3.refs_1_.refs_10_
  92.3 5.3 collective-permute-done.5.refs_3_.refs_12_
  97.6 6.8 middle.1
  105.3 26.4 %collective-permute-done.8.refs_1_ = bf16[544,1024]{1,0:T(8,128)(2,1)S(1)} collective-permute-done((bf16[544,1024]{1,0:T(8,128)(2,1)}, bf16[544,1024]{1,0:T(8,128)(2,1)S(1)}, u32[]{:S(2)}, u32[]{:S(2)}) %collective-permute-start.8) | collective-permute-done | bytes 1114144 | tf_op jit(solution)/shard_map/ppermute | solution.py:859
  132.7 2.9 collective-permute-done.10.refs_3_
  135.6 2.9 all-to-all-done.g_ref
  140.0 9.9 %pack_rows.2 = bf16[896,1024]{1,0:T(8,128)(2,1)} custom-call(s32[4]{0:T(128)} %get-tuple-element.312.part_ref, bf16[544,1024]{1,0:T(8,128)(2,1)} %get-tuple-element.171.refs_0_.refs_3_, bf16[544,1024]{1,0:T(8,128)(2,1)} %copy-done.29, bf16[544,1024]{1,0:T(8,128)(2,1)} %collective-permute-done.9.refs_2_, bf16[544,1024]{1,0:T(8,128)(2,1)} %collective-permute-done.10.refs_3_, ...), custom_call_target="tpu_custom_call" | custom-call | flops 5989466112 | bytes 4456448 | tf_op jit(solution)/shard_map/pack_rows/pallas_call | solution.py:359
  149.9 3.7 all-to-all-start.1
  154.1 9.9 %pack_rows.3 = bf16[896,1024]{1,0:T(8,128)(2,1)} custom-call(s32[4]{0:T(128)} %get-tuple-element.312.part_ref, bf16[544,1024]{1,0:T(8,128)(2,1)} %get-tuple-element.171.refs_0_.refs_3_, bf16[544,1024]{1,0:T(8,128)(2,1)} %copy-done.29, bf16[544,1024]{1,0:T(8,128)(2,1)} %collective-permute-done.9.refs_2_, bf16[544,1024]{1,0:T(8,128)(2,1)} %collective-permute-done.10.refs_3_, ...), custom_call_target="tpu_custom_call" | custom-call | flops 5989466112 | bytes 4456448 | tf_op jit(solution)/shard_map/pack_rows/pallas_call | solution.py:359
  164.0 20.6 %collective-permute-done.11.refs_9_ = bf16[1024,1024]{1,0:T(8,128)(2,1)} collective-permute-done((bf16[1024,1024]{1,0:T(8,128)(2,1)}, bf16[1024,1024]{1,0:T(8,128)(2,1)}, u32[]{:S(2)}, u32[]{:S(2)}) %collective-permute-start.11) | collective-permute-done | bytes 2097184 | tf_op jit(solution)/shard_map/ppermute | solution.py:859
  185.7 10.4 %all-to-all-done.1 = bf16[8,112,1024]{2,1,0:T(8,128)(2,1)S(1)} async-done(((bf16[8,112,1024]{2,1,0:T(8,128)(2,1)}), bf16[8,112,1024]{2,1,0:T(8,128)(2,1)S(1)}, u32[]{:S(2)}, u32[]{:S(2)}) %all-to-all-start.1) | async-done | bytes 1835040 | tf_op jit(solution)/shard_map/all_to_all | solution.py:896
  197.4 4.3 all-to-all-start.2
  201.7 47.5 %expert.2 = (bf16[896,1024]{1,0:T(8,128)(2,1)}, bf16[896,4096]{1,0:T(8,128)(2,1)}, bf16[896,4096]{1,0:T(8,128)(2,1)}, bf16[896,1024]{1,0:T(8,128)(2,1)}, bf16[896,1024]{1,0:T(8,128)(2,1)}) custom-call(bf16[896,1024]{1,0:T(8,128)(2,1)} %bitcast.63, bf16[8,2,112,1152]{3,2,1,0:T(8,128)(2,1)} %all-to-all-done.g_ref, ...), custom_call_target="tpu_custom_call" | custom-call | flops 30064771072 | bytes 22020096 | tf_op jit(solution)/shard_map/expert/pallas_call | solution.py:763
  249.3 5.9 all-to-all-start.3
  255.2 47.6 %expert.3 = (bf16[896,1024]{1,0:T(8,128)(2,1)}, bf16[896,4096]{1,0:T(8,128)(2,1)}, bf16[896,4096]{1,0:T(8,128)(2,1)}, bf16[896,1024]{1,0:T(8,128)(2,1)}, bf16[896,1024]{1,0:T(8,128)(2,1)}) custom-call(bf16[896,1024]{1,0:T(8,128)(2,1)} %bitcast.21.x_ref.refs_3_, bf16[8,2,112,1152]{3,2,1,0:T(8,128)(2,1)} %all-to-all-done.g_ref, ...), custom_call_target="tpu_custom_call" | custom-call | flops 30064771072 | bytes 22020096 | tf_op jit(solution)/shard_map/expert/pallas_call | solution.py:763
  304.1 6.0 all-to-all-start.4
  310.1 14.0 %weight_grad.5 = (bf16[1024,1024]{1,0:T(8,128)(2,1)}, bf16[1024,1024]{1,0:T(8,128)(2,1)}) custom-call(bf16[896,4096]{1,0:T(8,128)(2,1)} %get-tuple-element.203.refs_0_, bf16[896,1024]{1,0:T(8,128)(2,1)} %get-tuple-element.204.refs_1_, bf16[896,4096]{1,0:T(8,128)(2,1)} %get-tuple-element.205.refs_2_, bf16[896,1024]{1,0:T(8,128)(2,1)} %get-tuple-element.206.refs_3_), custom_call_target="tpu_custom_call" | custom-call | flops 7516192768 | bytes 8388608 | tf_op jit(solution)/shard_map/weight_grad/pallas_call | solution.py:811
  324.6 14.0 %weight_grad.4 = (bf16[1024,1024]{1,0:T(8,128)(2,1)}, bf16[1024,1024]{1,0:T(8,128)(2,1)}) custom-call(bf16[896,4096]{1,0:T(8,128)(2,1)} %get-tuple-element.203.refs_0_, bf16[896,1024]{1,0:T(8,128)(2,1)} %get-tuple-element.204.refs_1_, bf16[896,4096]{1,0:T(8,128)(2,1)} %get-tuple-element.205.refs_2_, bf16[896,1024]{1,0:T(8,128)(2,1)} %get-tuple-element.206.refs_3_), custom_call_target="tpu_custom_call" | custom-call | flops 7516192768 | bytes 8388608 | tf_op jit(solution)/shard_map/weight_grad/pallas_call | solution.py:811
  339.9 3.4 add_convert_fusion.2
  344.9 2.3 add_convert_fusion.3
  347.1 4.4 all-to-all-done.4
  351.5 17.5 %unpack_rows.2 = (bf16[544,1152]{1,0:T(8,128)(2,1)}, bf16[544,1152]{1,0:T(8,128)(2,1)}, bf16[544,1152]{1,0:T(8,128)(2,1)}, bf16[544,1152]{1,0:T(8,128)(2,1)}) custom-call(s32[4]{0:T(128)} %get-tuple-element.312.part_ref, s32[2176,2]{1,0:T(8,128)} %copy-done.1, bf16[896,1024]{1,0:T(8,128)(2,1)} %bitcast.67, bf16[896,1024]{1,0:T(8,128)(2,1)} %bitcast.25.refs_1_), custom_call_target="tpu_custom_call" | custom-call | flops 11978932224 | bytes 7340032 | tf_op jit(solution)/shard_map/unpack_rows/pallas_call | solution.py:414
  369.5 4.3 all-to-all-start.5
  374.0 3.5 add_convert_fusion.5.refs_0_
  377.5 13.6 %collective-permute-done.22 = bf16[1024,1024]{1,0:T(8,128)(2,1)} collective-permute-done((bf16[1024,1024]{1,0:T(8,128)(2,1)S(1)}, bf16[1024,1024]{1,0:T(8,128)(2,1)}, u32[]{:S(2)}, u32[]{:S(2)}) %collective-permute-start.22) | collective-permute-done | bytes 2097184 | tf_op jit(solution)/shard_map/ppermute | solution.py:859
  391.1 14.0 %weight_grad.7 = (bf16[1024,1024]{1,0:T(8,128)(2,1)}, bf16[1024,1024]{1,0:T(8,128)(2,1)}) custom-call(bf16[896,4096]{1,0:T(8,128)(2,1)} %get-tuple-element.224.refs_0_, bf16[896,1024]{1,0:T(8,128)(2,1)} %bitcast.64, bf16[896,4096]{1,0:T(8,128)(2,1)} %get-tuple-element.225.refs_2_, bf16[896,1024]{1,0:T(8,128)(2,1)} %bitcast.21.x_ref.refs_3_), custom_call_target="tpu_custom_call" | custom-call | flops 7516192768 | bytes 8388608 | tf_op jit(solution)/shard_map/weight_grad/pallas_call | solution.py:811
  405.6 2.6 add_convert_fusion.4
  409.8 7.2 %all-to-all-done.5 = bf16[8,112,1024]{2,1,0:T(8,128)(2,1)} async-done(((bf16[8,112,1024]{2,1,0:T(8,128)(2,1)}), bf16[8,112,1024]{2,1,0:T(8,128)(2,1)}, u32[]{:S(2)}, u32[]{:S(2)}) %all-to-all-start.5) | async-done | bytes 1835040 | tf_op jit(solution)/shard_map/all_to_all | solution.py:896
  417.0 4.5 all-to-all-start.6
  421.5 14.0 %weight_grad.6 = (bf16[1024,1024]{1,0:T(8,128)(2,1)}, bf16[1024,1024]{1,0:T(8,128)(2,1)}) custom-call(bf16[896,4096]{1,0:T(8,128)(2,1)} %get-tuple-element.224.refs_0_, bf16[896,1024]{1,0:T(8,128)(2,1)} %bitcast.65, bf16[896,4096]{1,0:T(8,128)(2,1)} %get-tuple-element.225.refs_2_, bf16[896,1024]{1,0:T(8,128)(2,1)} %bitcast.21.x_ref.refs_3_), custom_call_target="tpu_custom_call" | custom-call | flops 7516192768 | bytes 8388608 | tf_op jit(solution)/shard_map/weight_grad/pallas_call | solution.py:811
  435.5 2.5 collective-permute-done.23.refs_1_
  439.0 12.1 %middle_back.1 = (f32[544,1024]{1,0:T(8,128)}, f32[128,1024]{1,0:T(8,128)}, f32[1,1024]{1,0:T(1,128)}, bf16[256,1024]{1,0:T(8,128)(2,1)}, bf16[256,1024]{1,0:T(8...) custom-call(s32[1]{0:T(128)} %bitcast.12.at_ref, ...), custom_call_target="tpu_custom_call" | custom-call | flops 4563402752 | bytes 22282240 | tf_op jit(solution)/shard_map/middle_back/pallas_call | solution.py:609
  453.3 2.6 copy.104
  455.9 5.1 collective-permute-done.24.refs_1_
  461.0 3.4 collective-permute-done.26.refs_3_
  464.4 4.6 add_convert_fusion.1
  469.7 34.5 %attend_back.1 = (bf16[544,1024]{1,0:T(8,128)(2,1)}, bf16[544,1024]{1,0:T(8,128)(2,1)}, bf16[544,1024]{1,0:T(8,128)(2,1)}, bf16[544,1024]{1,0:T(8,128)(2,1)}, bf...) custom-call(s32[4]{0:T(128)} %get-tuple-element.311.starts_ref, bf16[3,11,208,256]{3,2,1,0:T(8,128)(2,1)} %get-tuple-element.157.qkv_ref, ...), custom_call_target="tpu_custom_call" | custom-call | flops 14394851328 | bytes 46858240 | tf_op jit(solution)/shard_map/attend_back/pallas_call | solution.py:286
  506.9 4.3 collective-permute-done.32
  515.7 2.2 collective-permute-done.31.b_ref
  517.9 15.9 %unpack_rows.3 = (bf16[544,1024]{1,0:T(8,128)(2,1)}, bf16[544,1024]{1,0:T(8,128)(2,1)}, bf16[544,1024]{1,0:T(8,128)(2,1)}, bf16[544,1024]{1,0:T(8,128)(2,1)}) custom-call(s32[4]{0:T(128)} %get-tuple-element.312.part_ref, s32[2176,2]{1,0:T(8,128)} %copy-done.1, bf16[896,1024]{1,0:T(8,128)(2,1)} %bitcast.27.refs_0_, bf16[896,1024]{1,0:T(8,128)(2,1)} %bitcast.29.refs_1_), custom_call_target="tpu_custom_call" | custom-call | flops 11978932224 | bytes 7340032 | tf_op jit(solution)/shard_map/unpack_rows/pallas_call | solution.py:414
  536.8 6.0 all-to-all-start.7
  543.9 2.0 collective-permute-done.36
  547.5 2.7 add_convert_fusion.7
  552.2 18.9 %collective-permute-done.35.far_ref = bf16[544,1024]{1,0:T(8,128)(2,1)S(1)} collective-permute-done((bf16[544,1024]{1,0:T(8,128)(2,1)}, bf16[544,1024]{1,0:T(8,128)(2,1)S(1)}, u32[]{:S(2)}, u32[]{:S(2)}) %collective-permute-start.35) | collective-permute-done | bytes 1114144 | tf_op jit(solution)/shard_map/ppermute | solution.py:859
  572.1 4.5 input_back.1.refs_0_
  577.1 5.4 convert_add_fusion
  582.5 2.3 add_convert_fusion.a_ref
  584.8 5.2 sum_turned.1
  589.9 5.2 collective-permute-done.39
  595.1 23.0 %collective-permute-done.38.refs_1_ = bf16[544,1024]{1,0:T(8,128)(2,1)} collective-permute-done((bf16[544,1024]{1,0:T(8,128)(2,1)}, bf16[544,1024]{1,0:T(8,128)(2,1)}, u32[]{:S(2)}, u32[]{:S(2)}) %collective-permute-start.38) | collective-permute-done | bytes 1114144 | tf_op jit(solution)/shard_map/ppermute | solution.py:859
  618.1 2.8 add_convert_fusion.6.refs_0_
  623.5 24.4 %collective-permute-done.40.refs_1_ = bf16[544,1024]{1,0:T(8,128)(2,1)S(1)} collective-permute-done((bf16[544,1024]{1,0:T(8,128)(2,1)S(1)}, bf16[544,1024]{1,0:T(8,128)(2,1)S(1)}, u32[]{:S(2)}, u32[]{:S(2)}) %collective-permute-start.40) | collective-permute-done | bytes 1114144 | tf_op jit(solution)/shard_map/ppermute | solution.py:859
  647.9 26.9 %all-gather.2.cloned.1.call-done = bf16[1152,1024]{1,0:T(8,128)(2,1)} async-done(((bf16[144,1024]{1,0:T(8,128)(2,1)}), bf16[1152,1024]{1,0:T(8,128)(2,1)}) %all-gather.2.cloned.1.call-update) | async-done | bytes 2359312 | tf_op jit(solution)/shard_map/all_gather | solution.py:1043
  675.6 6.7 assemble.3
  683.3 5.4 assemble.2
  691.0 2.1 slice_convert_fusion
  694.7 2.1 copy.110
  (207 shorter events, 60.1 us)
Async XLA Ops:
  10.2 30.4 %collective-permute-start = (bf16[512,1024]{1,0:T(8,128)(2,1)}, bf16[512,1024]{1,0:T(8,128)(2,1)}, u32[]{:S(2)}, u32[]{:S(2)}) collective-permute-start(bf16[512,1024]{1,0:T(8,128)(2,1)} %get-tuple-element.184.refs_0_), channel_id=1, source_target_pairs={{0,2},{1,3},{2,0},{3,1},{4,6},{5,7},{6,4},{7,5},{8,10},{9,11},{10,... | collective-permute-start | bytes 3145736 | tf_op jit(solution)/shard_map/ppermute | solution.py:859
  19.4 119.5 %copy-start.1 = (s32[2176,2]{1,0:T(8,128)}, s32[2176,2]{1,0:T(8,128)S(1)}, u32[]{:S(2)}) copy-start(s32[2176,2]{1,0:T(8,128)S(1)} %get-tuple-element.316.lp_ref) | copy-start | bytes 52228
  40.7 97.7 %all-to-all-start = ((bf16[8,2,112,1152]{3,2,1,0:T(8,128)(2,1)}), bf16[8,2,112,1152]{3,2,1,0:T(8,128)(2,1)}, u32[]{:S(2)}, u32[]{:S(2)}) async-start(bf16[8,2,112,1152]{3,2,1,0:T(8,128)(2,1)} %pack_cotangent.1), calls=%async_computation | async-start | bytes 8257536 | tf_op jit(solution)/shard_map/all_to_all | solution.py:896
  46.9 35.7 %collective-permute-start.1 = (bf16[512,1024]{1,0:T(8,128)(2,1)S(1)}, bf16[512,1024]{1,0:T(8,128)(2,1)}, u32[]{:S(2)}, u32[]{:S(2)}) collective-permute-start(bf16[512,1024]{1,0:T(8,128)(2,1)S(1)} %copy-done.19), channel_id=1, source_target_pairs={{0,2},{1,3},{2,0},{3,1},{4,6},{5,7},{6,4},{7,5},{8,10},{9,11},{10,... | collective-permute-start | bytes 3145736 | tf_op jit(solution)/shard_map/ppermute | solution.py:859
  47.5 35.1 %collective-permute-start.2 = (bf16[256,1024]{1,0:T(8,128)(2,1)S(1)}, bf16[256,1024]{1,0:T(8,128)(2,1)}, u32[]{:S(2)}, u32[]{:S(2)}) collective-permute-start(bf16[256,1024]{1,0:T(8,128)(2,1)S(1)} %copy-done.20), channel_id=1, source_target_pairs={{0,2},{1,3},{2,0},{3,1},{4,6},{5,7},{6,4},{7,5},{8,10},{9,11},{10,... | collective-permute-start | bytes 1572872 | tf_op jit(solution)/shard_map/ppermute | solution.py:859
  49.0 39.6 %collective-permute-start.6 = (bf16[256,1024]{1,0:T(8,128)(2,1)S(1)}, bf16[256,1024]{1,0:T(8,128)(2,1)}, u32[]{:S(2)}, u32[]{:S(2)}) collective-permute-start(bf16[256,1024]{1,0:T(8,128)(2,1)S(1)} %copy-done.20), channel_id=1, source_target_pairs={{0,1},{1,0},{2,3},{3,2},{4,5},{5,4},{6,7},{7,6},{8,9},{9,8},{10,11... | collective-permute-start | bytes 1572872 | tf_op jit(solution)/shard_map/ppermute | solution.py:859
  82.7 15.0 %collective-permute-start.7 = (bf16[256,1024]{1,0:T(8,128)(2,1)}, bf16[256,1024]{1,0:T(8,128)(2,1)}, u32[]{:S(2)}, u32[]{:S(2)}) collective-permute-start(bf16[256,1024]{1,0:T(8,128)(2,1)} %collective-permute-done.2.refs_5_.refs_14_), channel_id=1, source_target_pairs={{0,1},{1,0},{2,3},{3,2},{4,5},{5,4},{6,7},{7,6},{8,9},{9,8},{10,11... | collective-permute-start | bytes 1572872 | tf_op jit(solution)/shard_map/ppermute | solution.py:859
  82.7 9.7 %collective-permute-start.3 = (bf16[544,256]{1,0:T(8,128)(2,1)}, bf16[544,256]{1,0:T(8,128)(2,1)S(1)}, u32[]{:S(2)}, u32[]{:S(2)}) collective-permute-start(bf16[544,256]{1,0:T(8,128)(2,1)} %get-tuple-element.165), channel_id=1, source_target_pairs={{0,2},{1,3},{2,0},{3,1},{4,6},{5,7},{6,4},{7,5},{8,10},{9,11},{10,... | collective-permute-start | bytes 835592 | tf_op jit(solution)/shard_map/ppermute | solution.py:859
  83.2 9.1 %collective-permute-start.4 = (bf16[544,256]{1,0:T(8,128)(2,1)}, bf16[544,256]{1,0:T(8,128)(2,1)}, u32[]{:S(2)}, u32[]{:S(2)}) collective-permute-start(bf16[544,256]{1,0:T(8,128)(2,1)} %get-tuple-element.166), channel_id=1, source_target_pairs={{0,1},{1,0},{2,3},{3,2},{4,5},{5,4},{6,7},{7,6},{8,9},{9,8},{10,11... | collective-permute-start | bytes 835592 | tf_op jit(solution)/shard_map/ppermute | solution.py:859
  83.4 14.2 %collective-permute-start.5 = (bf16[544,256]{1,0:T(8,128)(2,1)}, bf16[544,256]{1,0:T(8,128)(2,1)}, u32[]{:S(2)}, u32[]{:S(2)}) collective-permute-start(bf16[544,256]{1,0:T(8,128)(2,1)} %get-tuple-element.167), channel_id=1, source_target_pairs={{0,3},{1,2},{2,1},{3,0},{4,7},{5,6},{6,5},{7,4},{8,11},{9,10},{10,... | collective-permute-start | bytes 835592 | tf_op jit(solution)/shard_map/ppermute | solution.py:859
  104.5 27.2 %collective-permute-start.8 = (bf16[544,1024]{1,0:T(8,128)(2,1)}, bf16[544,1024]{1,0:T(8,128)(2,1)S(1)}, u32[]{:S(2)}, u32[]{:S(2)}) collective-permute-start(bf16[544,1024]{1,0:T(8,128)(2,1)} %get-tuple-element.171.refs_0_.refs_3_), channel_id=1, source_target_pairs={{0,2},{1,3},{2,0},{3,1},{4,6},{5,7},{6,4},{7,5},{8,10},{9,11},{10,... | collective-permute-start | bytes 3342344 | tf_op jit(solution)/shard_map/ppermute | solution.py:859
  105.1 27.6 %collective-permute-start.9 = (bf16[544,1024]{1,0:T(8,128)(2,1)}, bf16[544,1024]{1,0:T(8,128)(2,1)}, u32[]{:S(2)}, u32[]{:S(2)}) collective-permute-start(bf16[544,1024]{1,0:T(8,128)(2,1)} %get-tuple-element.171.refs_0_.refs_3_), channel_id=1, source_target_pairs={{0,1},{1,0},{2,3},{3,2},{4,5},{5,4},{6,7},{7,6},{8,9},{9,8},{10,11... | collective-permute-start | bytes 3342344 | tf_op jit(solution)/shard_map/ppermute | solution.py:859
  132.7 2.9 collective-permute-start.10
  138.4 46.2 %collective-permute-start.11 = (bf16[1024,1024]{1,0:T(8,128)(2,1)}, bf16[1024,1024]{1,0:T(8,128)(2,1)}, u32[]{:S(2)}, u32[]{:S(2)}) collective-permute-start(bf16[1024,1024]{1,0:T(8,128)(2,1)} %bitcast.85), channel_id=1, source_target_pairs={{0,2},{1,3},{2,0},{3,1},{4,6},{5,7},{6,4},{7,5},{8,10},{9,11},{10,... | collective-permute-start | bytes 6291464 | tf_op jit(solution)/shard_map/ppermute | solution.py:859
  149.9 46.2 %all-to-all-start.1 = ((bf16[8,112,1024]{2,1,0:T(8,128)(2,1)}), bf16[8,112,1024]{2,1,0:T(8,128)(2,1)S(1)}, u32[]{:S(2)}, u32[]{:S(2)}) async-start(bf16[8,112,1024]{2,1,0:T(8,128)(2,1)} %bitcast.70), calls=%async_computation.1 | async-start | bytes 3670016 | tf_op jit(solution)/shard_map/all_to_all | solution.py:896
  153.5 31.6 %collective-permute-start.12 = (bf16[512,1024]{1,0:T(8,128)(2,1)}, bf16[512,1024]{1,0:T(8,128)(2,1)}, u32[]{:S(2)}, u32[]{:S(2)}) collective-permute-start(bf16[512,1024]{1,0:T(8,128)(2,1)} %get-tuple-element.184.refs_0_), channel_id=1, source_target_pairs={{0,1},{1,0},{2,3},{3,2},{4,5},{5,4},{6,7},{7,6},{8,9},{9,8},{10,11... | collective-permute-start | bytes 3145736 | tf_op jit(solution)/shard_map/ppermute | solution.py:859
  153.6 48.1 %collective-permute-start.16 = (bf16[1024,1024]{1,0:T(8,128)(2,1)}, bf16[1024,1024]{1,0:T(8,128)(2,1)}, u32[]{:S(2)}, u32[]{:S(2)}) collective-permute-start(bf16[1024,1024]{1,0:T(8,128)(2,1)} %bitcast.86), channel_id=1, source_target_pairs={{0,1},{1,0},{2,3},{3,2},{4,5},{5,4},{6,7},{7,6},{8,9},{9,8},{10,11... | collective-permute-start | bytes 6291464 | tf_op jit(solution)/shard_map/ppermute | solution.py:859
  184.7 17.1 %collective-permute-start.17 = (bf16[1024,1024]{1,0:T(8,128)(2,1)}, bf16[1024,1024]{1,0:T(8,128)(2,1)}, u32[]{:S(2)}, u32[]{:S(2)}) collective-permute-start(bf16[1024,1024]{1,0:T(8,128)(2,1)} %collective-permute-done.11.refs_9_), channel_id=1, source_target_pairs={{0,1},{1,0},{2,3},{3,2},{4,5},{5,4},{6,7},{7,6},{8,9},{9,8},{10,11... | collective-permute-start | bytes 6291464 | tf_op jit(solution)/shard_map/ppermute | solution.py:859
  184.7 17.0 %collective-permute-start.13 = (bf16[512,1024]{1,0:T(8,128)(2,1)S(1)}, bf16[512,1024]{1,0:T(8,128)(2,1)}, u32[]{:S(2)}, u32[]{:S(2)}) collective-permute-start(bf16[512,1024]{1,0:T(8,128)(2,1)S(1)} %copy-done.19), channel_id=1, source_target_pairs={{0,1},{1,0},{2,3},{3,2},{4,5},{5,4},{6,7},{7,6},{8,9},{9,8},{10,11... | collective-permute-start | bytes 3145736 | tf_op jit(solution)/shard_map/ppermute | solution.py:859
  185.2 16.5 %collective-permute-start.15 = (bf16[512,1024]{1,0:T(8,128)(2,1)}, bf16[512,1024]{1,0:T(8,128)(2,1)}, u32[]{:S(2)}, u32[]{:S(2)}) collective-permute-start(bf16[512,1024]{1,0:T(8,128)(2,1)} %collective-permute-done.1.refs_3_), channel_id=1, source_target_pairs={{0,1},{1,0},{2,3},{3,2},{4,5},{5,4},{6,7},{7,6},{8,9},{9,8},{10,11... | collective-permute-start | bytes 3145736 | tf_op jit(solution)/shard_map/ppermute | solution.py:859
  185.2 16.5 %collective-permute-start.14 = (bf16[512,1024]{1,0:T(8,128)(2,1)}, bf16[512,1024]{1,0:T(8,128)(2,1)}, u32[]{:S(2)}, u32[]{:S(2)}) collective-permute-start(bf16[512,1024]{1,0:T(8,128)(2,1)} %collective-permute-done.refs_2_), channel_id=1, source_target_pairs={{0,1},{1,0},{2,3},{3,2},{4,5},{5,4},{6,7},{7,6},{8,9},{9,8},{10,11... | collective-permute-start | bytes 3145736 | tf_op jit(solution)/shard_map/ppermute | solution.py:859
  197.4 51.9 %all-to-all-start.2 = ((bf16[8,112,1024]{2,1,0:T(8,128)(2,1)}), bf16[8,112,1024]{2,1,0:T(8,128)(2,1)}, u32[]{:S(2)}, u32[]{:S(2)}) async-start(bf16[8,112,1024]{2,1,0:T(8,128)(2,1)} %bitcast.69), calls=%async_computation.2 | async-start | bytes 3670016 | tf_op jit(solution)/shard_map/all_to_all | solution.py:896
  249.3 53.6 %all-to-all-start.3 = ((bf16[8,112,1024]{2,1,0:T(8,128)(2,1)}), bf16[8,112,1024]{2,1,0:T(8,128)(2,1)S(1)}, u32[]{:S(2)}, u32[]{:S(2)}) async-start(bf16[8,112,1024]{2,1,0:T(8,128)(2,1)} %bitcast.71), calls=%async_computation.3 | async-start | bytes 3670016 | tf_op jit(solution)/shard_map/all_to_all | solution.py:896
  304.1 47.4 %all-to-all-start.4 = ((bf16[8,112,1024]{2,1,0:T(8,128)(2,1)}), bf16[8,112,1024]{2,1,0:T(8,128)(2,1)}, u32[]{:S(2)}, u32[]{:S(2)}) async-start(bf16[8,112,1024]{2,1,0:T(8,128)(2,1)} %bitcast.68), calls=%async_computation.4 | async-start | bytes 3670016 | tf_op jit(solution)/shard_map/all_to_all | solution.py:896
  324.1 14.5 %collective-permute-start.18 = (bf16[1024,1024]{1,0:T(8,128)(2,1)}, bf16[1024,1024]{1,0:T(8,128)(2,1)S(1)}, u32[]{:S(2)}, u32[]{:S(2)}) collective-permute-start(bf16[1024,1024]{1,0:T(8,128)(2,1)} %get-tuple-element.208), channel_id=1, source_target_pairs={{0,1},{1,0},{2,3},{3,2},{4,5},{5,4},{6,7},{7,6},{8,9},{9,8},{10,11... | collective-permute-start | bytes 6291464 | tf_op jit(solution)/shard_map/ppermute | solution.py:859
  324.1 14.5 %collective-permute-start.19 = (bf16[1024,1024]{1,0:T(8,128)(2,1)}, bf16[1024,1024]{1,0:T(8,128)(2,1)}, u32[]{:S(2)}, u32[]{:S(2)}) collective-permute-start(bf16[1024,1024]{1,0:T(8,128)(2,1)} %get-tuple-element.209), channel_id=1, source_target_pairs={{0,1},{1,0},{2,3},{3,2},{4,5},{5,4},{6,7},{7,6},{8,9},{9,8},{10,11... | collective-permute-start | bytes 6291464 | tf_op jit(solution)/shard_map/ppermute | solution.py:859
  343.3 47.8 %collective-permute-start.22 = (bf16[1024,1024]{1,0:T(8,128)(2,1)S(1)}, bf16[1024,1024]{1,0:T(8,128)(2,1)}, u32[]{:S(2)}, u32[]{:S(2)}) collective-permute-start(bf16[1024,1024]{1,0:T(8,128)(2,1)S(1)} %add_convert_fusion.2), channel_id=1, source_target_pairs={{0,2},{1,3},{2,0},{3,1},{4,6},{5,7},{6,4},{7,5},{8,10},{9,11},{10,... | collective-permute-start | bytes 6291464 | tf_op jit(solution)/shard_map/ppermute | solution.py:859
  369.0 4.8 collective-permute-start.20
  369.0 5.0 collective-permute-start.21
  369.5 47.5 %all-to-all-start.5 = ((bf16[8,112,1024]{2,1,0:T(8,128)(2,1)}), bf16[8,112,1024]{2,1,0:T(8,128)(2,1)}, u32[]{:S(2)}, u32[]{:S(2)}) async-start(bf16[8,112,1024]{2,1,0:T(8,128)(2,1)} %bitcast.66), calls=%async_computation.5 | async-start | bytes 3670016 | tf_op jit(solution)/shard_map/all_to_all | solution.py:896
  391.1 14.6 %copy-start.11 = (bf16[544,1152]{1,0:T(8,128)(2,1)S(1)}, bf16[544,1152]{1,0:T(8,128)(2,1)}, u32[]{:S(2)}) copy-start(bf16[544,1152]{1,0:T(8,128)(2,1)} %get-tuple-element.222) | copy-start | bytes 3760132
  405.1 50.8 %collective-permute-start.27 = (bf16[1024,1024]{1,0:T(8,128)(2,1)}, bf16[1024,1024]{1,0:T(8,128)(2,1)S(1)}, u32[]{:S(2)}, u32[]{:S(2)}) collective-permute-start(bf16[1024,1024]{1,0:T(8,128)(2,1)} %get-tuple-element.228), channel_id=1, source_target_pairs={{0,1},{1,0},{2,3},{3,2},{4,5},{5,4},{6,7},{7,6},{8,9},{9,8},{10,11... | collective-permute-start | bytes 6291464 | tf_op jit(solution)/shard_map/ppermute | solution.py:859
  405.1 50.8 %collective-permute-start.28 = (bf16[1024,1024]{1,0:T(8,128)(2,1)}, bf16[1024,1024]{1,0:T(8,128)(2,1)}, u32[]{:S(2)}, u32[]{:S(2)}) collective-permute-start(bf16[1024,1024]{1,0:T(8,128)(2,1)} %get-tuple-element.229), channel_id=1, source_target_pairs={{0,1},{1,0},{2,3},{3,2},{4,5},{5,4},{6,7},{7,6},{8,9},{9,8},{10,11... | collective-permute-start | bytes 6291464 | tf_op jit(solution)/shard_map/ppermute | solution.py:859
  408.3 29.7 %collective-permute-start.23 = (bf16[544,1152]{1,0:T(8,128)(2,1)}, bf16[544,1152]{1,0:T(8,128)(2,1)S(1)}, u32[]{:S(2)}, u32[]{:S(2)}) collective-permute-start(bf16[544,1152]{1,0:T(8,128)(2,1)} %add_convert_fusion.4), channel_id=1, source_target_pairs={{0,2},{1,3},{2,0},{3,1},{4,6},{5,7},{6,4},{7,5},{8,10},{9,11},{10,... | collective-permute-start | bytes 3760136 | tf_op jit(solution)/shard_map/ppermute | solution.py:859
  417.0 87.2 %all-to-all-start.6 = ((bf16[8,112,1024]{2,1,0:T(8,128)(2,1)}), bf16[8,112,1024]{2,1,0:T(8,128)(2,1)}, u32[]{:S(2)}, u32[]{:S(2)}) async-start(bf16[8,112,1024]{2,1,0:T(8,128)(2,1)} %bitcast.62), calls=%async_computation.6 | async-start | bytes 3670016 | tf_op jit(solution)/shard_map/all_to_all | solution.py:896
  451.1 9.9 %collective-permute-start.24 = (bf16[544,256]{1,0:T(8,128)(2,1)}, bf16[544,256]{1,0:T(8,128)(2,1)S(1)}, u32[]{:S(2)}, u32[]{:S(2)}) collective-permute-start(bf16[544,256]{1,0:T(8,128)(2,1)} %get-tuple-element.239), channel_id=1, source_target_pairs={{0,2},{1,3},{2,0},{3,1},{4,6},{5,7},{6,4},{7,5},{8,10},{9,11},{10,... | collective-permute-start | bytes 835592 | tf_op jit(solution)/shard_map/ppermute | solution.py:859
  452.7 8.3 %collective-permute-start.25 = (bf16[544,256]{1,0:T(8,128)(2,1)}, bf16[544,256]{1,0:T(8,128)(2,1)S(1)}, u32[]{:S(2)}, u32[]{:S(2)}) collective-permute-start(bf16[544,256]{1,0:T(8,128)(2,1)} %get-tuple-element.240), channel_id=1, source_target_pairs={{0,1},{1,0},{2,3},{3,2},{4,5},{5,4},{6,7},{7,6},{8,9},{9,8},{10,11... | collective-permute-start | bytes 835592 | tf_op jit(solution)/shard_map/ppermute | solution.py:859
  452.7 11.7 %collective-permute-start.26 = (bf16[544,256]{1,0:T(8,128)(2,1)}, bf16[544,256]{1,0:T(8,128)(2,1)S(1)}, u32[]{:S(2)}, u32[]{:S(2)}) collective-permute-start(bf16[544,256]{1,0:T(8,128)(2,1)} %get-tuple-element.241), channel_id=1, source_target_pairs={{0,3},{1,2},{2,1},{3,0},{4,7},{5,6},{6,5},{7,4},{8,11},{9,10},{10,... | collective-permute-start | bytes 835592 | tf_op jit(solution)/shard_map/ppermute | solution.py:859
  469.0 48.9 %collective-permute-start.31 = (bf16[1024,1024]{1,0:T(8,128)(2,1)}, bf16[1024,1024]{1,0:T(8,128)(2,1)}, u32[]{:S(2)}, u32[]{:S(2)}) collective-permute-start(bf16[1024,1024]{1,0:T(8,128)(2,1)} %add_convert_fusion.1), channel_id=1, source_target_pairs={{0,2},{1,3},{2,0},{3,1},{4,6},{5,7},{6,4},{7,5},{8,10},{9,11},{10,... | collective-permute-start | bytes 6291464 | tf_op jit(solution)/shard_map/ppermute | solution.py:859
  469.7 36.3 %copy-start.30 = (bf16[256,1024]{1,0:T(8,128)(2,1)S(1)}, bf16[256,1024]{1,0:T(8,128)(2,1)}, u32[]{:S(2)}) copy-start(bf16[256,1024]{1,0:T(8,128)(2,1)} %get-tuple-element.267) | copy-start | bytes 1572868
  469.7 37.2 %copy-start.27 = (f32[1,1024]{1,0:T(1,128)S(1)}, f32[1,1024]{1,0:T(1,128)}, u32[]{:S(2)}) copy-start(f32[1,1024]{1,0:T(1,128)} %get-tuple-element.279) | copy-start | bytes 12292
  469.7 41.5 %copy-start.21 = (bf16[256,1024]{1,0:T(8,128)(2,1)S(1)}, bf16[256,1024]{1,0:T(8,128)(2,1)}, u32[]{:S(2)}) copy-start(bf16[256,1024]{1,0:T(8,128)(2,1)} %get-tuple-element.275) | copy-start | bytes 1572868
  504.2 8.6 %collective-permute-start.29 = (bf16[544,1024]{1,0:T(8,128)(2,1)}, bf16[544,1024]{1,0:T(8,128)(2,1)S(1)}, u32[]{:S(2)}, u32[]{:S(2)}) collective-permute-start(bf16[544,1024]{1,0:T(8,128)(2,1)} %get-tuple-element.254), channel_id=1, source_target_pairs={{0,1},{1,0},{2,3},{3,2},{4,5},{5,4},{6,7},{7,6},{8,9},{9,8},{10,11... | collective-permute-start | bytes 3342344 | tf_op jit(solution)/shard_map/ppermute | solution.py:859
  505.5 7.2 %collective-permute-start.30 = (bf16[544,1024]{1,0:T(8,128)(2,1)}, bf16[544,1024]{1,0:T(8,128)(2,1)S(1)}, u32[]{:S(2)}, u32[]{:S(2)}) collective-permute-start(bf16[544,1024]{1,0:T(8,128)(2,1)} %get-tuple-element.255), channel_id=1, source_target_pairs={{0,1},{1,0},{2,3},{3,2},{4,5},{5,4},{6,7},{7,6},{8,9},{9,8},{10,11... | collective-permute-start | bytes 3342344 | tf_op jit(solution)/shard_map/ppermute | solution.py:859
  505.6 5.6 collective-permute-start.32
  506.1 5.2 collective-permute-start.33
  511.4 22.4 %collective-permute-start.34 = (bf16[256,1024]{1,0:T(8,128)(2,1)S(1)}, bf16[256,1024]{1,0:T(8,128)(2,1)S(1)}, u32[]{:S(2)}, u32[]{:S(2)}) collective-permute-start(bf16[256,1024]{1,0:T(8,128)(2,1)S(1)} %add_convert_fusion.12), channel_id=1, source_target_pairs={{0,2},{1,3},{2,0},{3,1},{4,6},{5,7},{6,4},{7,5},{8,10},{9,11},{10,... | collective-permute-start | bytes 1572872 | tf_op jit(solution)/shard_map/ppermute | solution.py:859
  517.9 15.9 %copy-start.22 = (bf16[256,1024]{1,0:T(8,128)(2,1)S(1)}, bf16[256,1024]{1,0:T(8,128)(2,1)}, u32[]{:S(2)}) copy-start(bf16[256,1024]{1,0:T(8,128)(2,1)} %get-tuple-element.265) | copy-start | bytes 1572868
  536.8 84.1 %all-to-all-start.7 = ((bf16[8,144,1024]{2,1,0:T(8,128)(2,1)}), bf16[8,144,1024]{2,1,0:T(8,128)(2,1)S(1)}, u32[]{:S(2)}, u32[]{:S(2)}) async-start(bf16[8,144,1024]{2,1,0:T(8,128)(2,1)} %bitcast.54), calls=%async_computation.7 | async-start | bytes 4718592 | tf_op jit(solution)/shard_map/all_to_all | solution.py:896
  542.8 132.0 %all-gather.2.cloned.1.call-start = ((), (), s32[]{:S(2)}) async-start(), calls=%async_computation.8 | async-start | bytes 2654208 | tf_op jit(solution)/shard_map/all_gather | solution.py:1043
  542.9 3.0 collective-permute-start.36
  543.0 4.5 collective-permute-start.37
  543.5 27.6 %collective-permute-start.35 = (bf16[544,1024]{1,0:T(8,128)(2,1)}, bf16[544,1024]{1,0:T(8,128)(2,1)S(1)}, u32[]{:S(2)}, u32[]{:S(2)}) collective-permute-start(bf16[544,1024]{1,0:T(8,128)(2,1)} %add_convert_fusion.10), channel_id=1, source_target_pairs={{0,2},{1,3},{2,0},{3,1},{4,6},{5,7},{6,4},{7,5},{8,10},{9,11},{10,... | collective-permute-start | bytes 3342344 | tf_op jit(solution)/shard_map/ppermute | solution.py:859
  550.3 44.8 %collective-permute-start.39 = (bf16[544,1024]{1,0:T(8,128)(2,1)}, bf16[544,1024]{1,0:T(8,128)(2,1)}, u32[]{:S(2)}, u32[]{:S(2)}) collective-permute-start(bf16[544,1024]{1,0:T(8,128)(2,1)} %add_convert_fusion.7), channel_id=1, source_target_pairs={{0,2},{1,3},{2,0},{3,1},{4,6},{5,7},{6,4},{7,5},{8,10},{9,11},{10,... | collective-permute-start | bytes 3342344 | tf_op jit(solution)/shard_map/ppermute | solution.py:859
  576.6 41.5 %collective-permute-start.38 = (bf16[544,1024]{1,0:T(8,128)(2,1)}, bf16[544,1024]{1,0:T(8,128)(2,1)}, u32[]{:S(2)}, u32[]{:S(2)}) collective-permute-start(bf16[544,1024]{1,0:T(8,128)(2,1)} %input_back.1.refs_0_), channel_id=1, source_target_pairs={{0,2},{1,3},{2,0},{3,1},{4,6},{5,7},{6,4},{7,5},{8,10},{9,11},{10,... | collective-permute-start | bytes 3342344 | tf_op jit(solution)/shard_map/ppermute | solution.py:859
  620.9 61.4 %copy-start = (bf16[544,1024]{1,0:T(8,128)(2,1)}, bf16[544,1024]{1,0:T(8,128)(2,1)S(1)}, u32[]{:S(2)}) copy-start(bf16[544,1024]{1,0:T(8,128)(2,1)S(1)} %add_convert_fusion.6.refs_0_) | copy-start | bytes 3342340
  622.1 25.8 %collective-permute-start.40 = (bf16[544,1024]{1,0:T(8,128)(2,1)S(1)}, bf16[544,1024]{1,0:T(8,128)(2,1)S(1)}, u32[]{:S(2)}, u32[]{:S(2)}) collective-permute-start(bf16[544,1024]{1,0:T(8,128)(2,1)S(1)} %add_convert_fusion.6.refs_0_), channel_id=1, source_target_pairs={{0,2},{1,3},{2,0},{3,1},{4,6},{5,7},{6,4},{7,5},{8,10},{9,11},{10,... | collective-permute-start | bytes 3342344 | tf_op jit(solution)/shard_map/ppermute | solution.py:859
  623.0 52.5 %collective-permute-start.43 = (bf16[544,1024]{1,0:T(8,128)(2,1)}, bf16[544,1024]{1,0:T(8,128)(2,1)}, u32[]{:S(2)}, u32[]{:S(2)}) collective-permute-start(bf16[544,1024]{1,0:T(8,128)(2,1)} %input_back.1.refs_0_), channel_id=1, source_target_pairs={{0,1},{1,0},{2,3},{3,2},{4,5},{5,4},{6,7},{7,6},{8,9},{9,8},{10,11... | collective-permute-start | bytes 3342344 | tf_op jit(solution)/shard_map/ppermute | solution.py:859
  623.0 52.6 %collective-permute-start.44 = (bf16[544,1024]{1,0:T(8,128)(2,1)}, bf16[544,1024]{1,0:T(8,128)(2,1)}, u32[]{:S(2)}, u32[]{:S(2)}) collective-permute-start(bf16[544,1024]{1,0:T(8,128)(2,1)} %collective-permute-done.38.refs_1_), channel_id=1, source_target_pairs={{0,1},{1,0},{2,3},{3,2},{4,5},{5,4},{6,7},{7,6},{8,9},{9,8},{10,11... | collective-permute-start | bytes 3342344 | tf_op jit(solution)/shard_map/ppermute | solution.py:859
  623.5 58.8 %collective-permute-start.41 = (bf16[544,1024]{1,0:T(8,128)(2,1)S(1)}, bf16[544,1024]{1,0:T(8,128)(2,1)S(1)}, u32[]{:S(2)}, u32[]{:S(2)}) collective-permute-start(bf16[544,1024]{1,0:T(8,128)(2,1)S(1)} %add_convert_fusion.6.refs_0_), channel_id=1, source_target_pairs={{0,1},{1,0},{2,3},{3,2},{4,5},{5,4},{6,7},{7,6},{8,9},{9,8},{10,11... | collective-permute-start | bytes 3342344 | tf_op jit(solution)/shard_map/ppermute | solution.py:859
  647.9 34.4 %copy-start.13 = (bf16[544,1024]{1,0:T(8,128)(2,1)}, bf16[544,1024]{1,0:T(8,128)(2,1)S(1)}, u32[]{:S(2)}) copy-start(bf16[544,1024]{1,0:T(8,128)(2,1)S(1)} %collective-permute-done.40.refs_1_) | copy-start | bytes 3342340
  647.9 34.4 %collective-permute-start.42 = (bf16[544,1024]{1,0:T(8,128)(2,1)S(1)}, bf16[544,1024]{1,0:T(8,128)(2,1)}, u32[]{:S(2)}, u32[]{:S(2)}) collective-permute-start(bf16[544,1024]{1,0:T(8,128)(2,1)S(1)} %collective-permute-done.40.refs_1_), channel_id=1, source_target_pairs={{0,1},{1,0},{2,3},{3,2},{4,5},{5,4},{6,7},{7,6},{8,9},{9,8},{10,11... | collective-permute-start | bytes 3342344 | tf_op jit(solution)/shard_map/ppermute | solution.py:859
  675.6 13.2 %collective-permute-start.45 = (f32[10,1024]{1,0:T(8,128)S(1)}, f32[10,1024]{1,0:T(8,128)S(1)}, u32[]{:S(2)}, u32[]{:S(2)}) collective-permute-start(f32[10,1024]{1,0:T(8,128)S(1)} %slice_convert_fusion.1), channel_id=1, source_target_pairs={{0,1},{1,0},{2,3},{3,2},{4,5},{5,4},{6,7},{7,6},{8,9},{9,8},{10,11... | collective-permute-start | bytes 122888 | tf_op jit(solution)/shard_map/ppermute | solution.py:859
  689.5 7.2 %collective-permute-start.46 = (f32[10,1024]{1,0:T(8,128)S(1)}, f32[10,1024]{1,0:T(8,128)S(1)}, u32[]{:S(2)}, u32[]{:S(2)}) collective-permute-start(f32[10,1024]{1,0:T(8,128)S(1)} %fusion.12), channel_id=1, source_target_pairs={{0,2},{1,3},{2,0},{3,1},{4,6},{5,7},{6,4},{7,5},{8,10},{9,11},{10,... | collective-permute-start | bytes 122888 | tf_op jit(solution)/shard_map/ppermute | solution.py:859
  (28 other events, 130.4 us)
Sparse Core Ops, SparseCore 0:
  622.3 52.4 all-gather.1
